TPU v7x, 32 devices: a whole 2x2x4 slice. The times are simulated.
32 devices in a mesh: role: 2 (over x), seq: 8 (over z, core), head: 2 (over y).
Axes of the slice: x: 2, y: 2, z: 4, core: 2. Of those that a mesh axis runs over, the one named last changes fastest.
Arguments:
- hidden_rows: bfloat16 [3072, 5120], P('seq'), may hold values from -6 to 6
- gen_weight: bfloat16 [5120, 5120], P(None, ('role', 'head')), may hold values from -0.078125 to 0.078125
- noise: bfloat16 [3072, 5120], P('seq'), may hold values from -6 to 6
- timesteps: int32 [48], P('seq'), may hold values from 20 to 979
- qkv_weight: bfloat16 [2, 5120, 9216], P('role', 'seq', 'head'), may hold values from -0.078125 to 0.078125
- out_weight: bfloat16 [2, 3072, 5120], P('role', 'head'), may hold values from -0.109375 to 0.109375
- qk_gain: float32 [2, 2, 24], P('role', None, 'head'), may hold values from 0.6 to 9
- block_keys: int32 [24, 48, 8], P('head', 'seq'), may hold values from 0 to 47, as said below
- block_count: int32 [24, 48], P('head', 'seq'), may hold values from 1 to 8, as said below
Outputs:
- score_grad: float32 [3072, 5120], P('seq', ('role', 'head'))
Inputs may be any that keep to these rules, and one draw needn't show every extreme that they name: `block_keys`: entry 0 of each list is the query block itself; the entries of one list are distinct. For each head, all entries of the lists of one index of seq name at most 2 distinct blocks of any other index of seq, and every index names exactly 2 blocks of the next index. `block_count`: in every draw the lists of some sequence shards are all full, those of others shorter.
All inputs are finite; a program needn't handle non-finite values.
Results may differ from a plain program's by a relative error of at most 0.018.
The roundings to bfloat16 on the way count: a program that leaves them out, or rounds other values in their place, can miss the bound.
Values may be sent and summed in bfloat16 or wider, within the bound.
No kernel may reach another device: no remote copies, remote signals or barrier semaphores. Data moves between devices by JAX's collectives and lax.ppermute only.
A program may use at most 192 MiB of HBM per device.

v0:
```python
import math

import jax
import jax.numpy as jnp
from jax import lax
from jax.sharding import PartitionSpec as P

HEAD_DIM = 128
BLOCK = 64
KMAX = 8
CAP = 2


def rms_rows(values):
    return values * lax.rsqrt(jnp.mean(values * values, axis=-1, keepdims=True) + 1e-06)


def block_attention(queries, key_table, value_table, key_list, key_count):
    picked_keys = key_table[key_list]
    picked_values = value_table[key_list]
    scale = 1.0 / math.sqrt(HEAD_DIM)
    scores = (
        jnp.einsum("nqe,nkbe->nqkb", queries, picked_keys, preferred_element_type=jnp.float32)
        * scale
    )
    live = lax.broadcasted_iota(jnp.int32, (key_list.shape[0], KMAX), 1) < key_count[:, None]
    scores = jnp.where(live[:, None, :, None], scores, -jnp.inf)
    highest = jnp.max(scores, axis=(2, 3), keepdims=True)
    raised = jnp.exp(scores - highest)
    summed = jnp.sum(raised, axis=(2, 3), keepdims=True)
    weights = (raised / summed).astype(jnp.bfloat16)
    mixed = jnp.einsum("nqkb,nkbe->nqe", weights, picked_values, preferred_element_type=jnp.float32)
    return mixed.astype(jnp.bfloat16)


def pick_blocks(table, wanted):
    return table[wanted]


def per_device(
    hidden_rows,
    gen_weight,
    noise,
    timesteps,
    qkv_weight,
    out_weight,
    qk_gain,
    block_keys,
    block_count,
):
    generated = jnp.dot(hidden_rows, gen_weight, preferred_element_type=jnp.float32).astype(
        jnp.bfloat16
    )
    forked = lax.all_gather(generated, ("role", "head"), axis=1, tiled=True)
    row_count = forked.shape[0]
    width = forked.shape[1]
    local_blocks = timesteps.shape[0]
    angle_blocks = (timesteps.astype(jnp.float32) * (math.pi / 2000.0))[:, None, None]
    noisy = jnp.cos(angle_blocks) * forked.astype(jnp.float32).reshape(local_blocks, BLOCK, width)
    noisy = noisy + jnp.sin(angle_blocks) * noise.astype(jnp.float32).reshape(
        local_blocks, BLOCK, width
    )
    normed = rms_rows(noisy).reshape(row_count, width).astype(jnp.bfloat16)
    weight_here = qkv_weight[0]
    projected = jnp.dot(
        normed,
        lax.all_gather(weight_here, "seq", axis=0, tiled=True),
        preferred_element_type=jnp.float32,
    )
    heads_here = projected.shape[1] // (3 * HEAD_DIM)
    head_parts = projected.reshape(row_count, heads_here, 3, HEAD_DIM)
    gain_here = qk_gain[0]
    queries = (rms_rows(head_parts[:, :, 0]) * gain_here[0][None, :, None]).astype(jnp.bfloat16)
    key_local = (rms_rows(head_parts[:, :, 1]) * gain_here[1][None, :, None]).astype(jnp.bfloat16)
    value_local = head_parts[:, :, 2].astype(jnp.bfloat16)
    query_table = queries.reshape(local_blocks, BLOCK, heads_here, HEAD_DIM).transpose(2, 0, 1, 3)
    shard_count = lax.axis_size("seq")
    shard_here = lax.axis_index("seq")
    all_blocks = shard_count * local_blocks
    key_heads = key_local.reshape(local_blocks, BLOCK, heads_here, HEAD_DIM).transpose(2, 0, 1, 3)
    value_heads = value_local.reshape(local_blocks, BLOCK, heads_here, HEAD_DIM).transpose(
        2, 0, 1, 3
    )
    block_ids = lax.broadcasted_iota(jnp.int32, (1, 1, 1, all_blocks), 3)
    matches = block_keys[:, :, :, None] == block_ids
    remote = block_ids // local_blocks != shard_here
    needed = jnp.any(jnp.logical_and(matches, remote), axis=(1, 2))
    needed = needed.reshape(heads_here, shard_count, local_blocks)
    slot_of = jnp.cumsum(needed.astype(jnp.int32), axis=2) - 1
    slot_ids = lax.broadcasted_iota(jnp.int32, (1, 1, 1, CAP), 3)
    within_ids = lax.broadcasted_iota(jnp.int32, (1, 1, local_blocks, 1), 2)
    chosen_slot = jnp.logical_and(needed[..., None], slot_of[..., None] == slot_ids)
    requests = jnp.sum(jnp.where(chosen_slot, within_ids, 0), axis=2)
    asked = lax.all_to_all(
        requests.transpose(1, 0, 2), "seq", split_axis=0, concat_axis=0, tiled=True
    )
    sent_keys = jax.vmap(pick_blocks, in_axes=(0, 1), out_axes=1)(key_heads, asked)
    sent_values = jax.vmap(pick_blocks, in_axes=(0, 1), out_axes=1)(value_heads, asked)
    got_keys, got_values = (
        lax.all_to_all(sent_keys, "seq", split_axis=0, concat_axis=0, tiled=True),
        lax.all_to_all(sent_values, "seq", split_axis=0, concat_axis=0, tiled=True),
    )
    fetched_keys = got_keys.transpose(1, 0, 2, 3, 4).reshape(
        heads_here, shard_count * CAP, BLOCK, HEAD_DIM
    )
    fetched_values = got_values.transpose(1, 0, 2, 3, 4).reshape(
        heads_here, shard_count * CAP, BLOCK, HEAD_DIM
    )
    key_table = jnp.concatenate([key_heads, fetched_keys], axis=1)
    value_table = jnp.concatenate([value_heads, fetched_values], axis=1)
    local_ids = lax.broadcasted_iota(jnp.int32, (1, shard_count, local_blocks), 2)
    owner_grid = lax.broadcasted_iota(jnp.int32, (1, shard_count, local_blocks), 1)
    position = jnp.where(
        owner_grid == shard_here, local_ids, local_blocks + owner_grid * CAP + slot_of
    )
    position = position.reshape(heads_here, all_blocks)
    key_lists = jnp.sum(jnp.where(matches, position[:, None, None, :], 0), axis=3)
    attended = jax.vmap(block_attention)(
        query_table, key_table, value_table, key_lists, block_count
    )
    attended = attended.transpose(1, 2, 0, 3).reshape(row_count, heads_here * HEAD_DIM)
    contribution = jnp.dot(attended, out_weight[0], preferred_element_type=jnp.float32)
    signed = (2.0 * lax.axis_index("role").astype(jnp.float32) - 1.0) * contribution
    return lax.psum_scatter(
        signed.astype(jnp.bfloat16), ("role", "head"), scatter_dimension=1, tiled=True
    ).astype(jnp.float32)


def solution(mesh):
    placed = (
        P("seq", None),
        P(None, ("role", "head")),
        P("seq", None),
        P("seq"),
        P("role", "seq", "head"),
        P("role", "head", None),
        P("role", None, "head"),
        P("head", "seq", None),
        P("head", "seq"),
    )
    return jax.shard_map(
        per_device,
        mesh=mesh,
        in_specs=placed,
        out_specs=P("seq", ("role", "head")),
        check_vma=False,
    )
```

profile of v0, /device:TPU:0, one launch (start us, length us, event | category | flops | bytes accessed | tf_op | source)
XLA Modules:
  0.0 852.0 jit_solution(16642412005860158354)
XLA Ops:
  6.5 11.5 %convolution_convert_fusion = bf16[384,1280]{1,0:T(8,128)(2,1)} fusion(bf16[384,5120]{1,0:T(8,128)(2,1)} %param.9, bf16[5120,1280]{1,0:T(8,128)(2,1)} %param.10), kind=kOutput, calls=%fused_computation.23 | convolution fusion | flops 5033656320 | bytes 18022400 | tf_op jit(solution)/shard_map/dot_general | solution.py:51
  22.1 6.3 all-to-all-start
  28.8 5.2 all-to-all-done
  34.3 37.2 %all-gather.4.cloned.1.call-done = bf16[384,5120]{1,0:T(8,128)(2,1)} async-done(((bf16[384,1280]{1,0:T(8,128)(2,1)}), bf16[384,5120]{1,0:T(8,128)(2,1)}) %all-gather.4.cloned.1.call-update) | async-done | bytes 3932176 | tf_op jit(solution)/shard_map/all_gather | solution.py:54
  71.5 5.3 multiply_reduce_fusion
  76.8 398.2 %all-gather.6.cloned.1.call-done = bf16[1,5120,4608]{2,1,0:T(8,128)(2,1)} async-done(((bf16[1,640,4608]{2,1,0:T(8,128)(2,1)}), bf16[1,5120,4608]{2,1,0:T(8,128)(2,1)}) %all-gather.6.cloned.1.call-update) | async-done | bytes 47185936 | tf_op jit(solution)/shard_map/all_gather | solution.py:67
  475.0 54.8 %copy.46 = bf16[4608,5120]{1,0:T(8,128)(2,1)} copy(bf16[4608,5120]{0,1:T(8,128)(2,1)} %bitcast.85) | data formatting | bytes 94371840 | tf_op jit(solution)/shard_map/dot_general | solution.py:65
  529.7 30.7 %fusion.8 = f32[384,12,3,128]{3,0,2,1:T(8,128)} fusion(bf16[12,3,128,5120]{3,2,1,0:T(8,128)(2,1)} %bitcast.86, bf16[384,5120]{1,0:T(8,128)(2,1)} %param.11, bf16[384,5120]{1,0:T(8,128)(2,1)} %all-gather.4.cloned.1.call-done, f32[384]{0:T(512)S(1)} %add_rsqrt_fusion.2, f32[384]{0:T(512)S(1)} %mul.118, f32[384]{0:T(512)S(1)} %mul.114), kind=kOutput, calls=%fused_computation.19 | convolution fusion | flops 18133155840 | bytes 62132736 | tf_op jit(solution)/shard_map/dot_general | solution.py:65
  560.4 5.1 multiply_reduce_fusion.2
  567.7 3.7 gather_fusion
  571.4 4.9 copy.55
  576.3 4.7 all-to-all-start.1
  582.9 3.7 gather_fusion.2
  586.5 4.8 copy.59
  591.4 60.9 %all-to-all-done.1 = bf16[8,12,2,64,128]{4,3,2,1,0:T(8,128)(2,1)} async-done(((bf16[8,12,2,64,128]{4,3,2,1,0:T(8,128)(2,1)}), bf16[8,12,2,64,128]{4,3,2,1,0:T(8,128)(2,1)}, u32[]{:S(2)}, u32[]{:S(2)}) %all-to-all-start.1) | async-done | bytes 3145760 | tf_op jit(solution)/shard_map/all_to_all | solution.py:100
  652.3 4.4 all-to-all-start.2
  664.4 63.9 %all-to-all-done.2 = bf16[8,12,2,64,128]{4,3,2,1,0:T(8,128)(2,1)} async-done(((bf16[8,12,2,64,128]{4,3,2,1,0:T(8,128)(2,1)}), bf16[8,12,2,64,128]{4,3,2,1,0:T(8,128)(2,1)}, u32[]{:S(2)}, u32[]{:S(2)}) %all-to-all-start.2) | async-done | bytes 3145760 | tf_op jit(solution)/shard_map/all_to_all | solution.py:101
  733.2 10.0 %gather_fusion.3 = bf16[576,64,128]{2,1,0:T(8,128)(2,1)} fusion(bf16[12,22,64,128]{3,2,1,0:T(8,128)(2,1)} %pad_maximum_fusion.1, s32[576]{0:T(1024)S(1)} %reshape.171), kind=kCustom, calls=%fused_computation.3 | custom fusion | bytes 18878976 | tf_op jit(solution)/shard_map/vmap()/gather | solution.py:20
  743.2 10.0 %gather_fusion.1 = bf16[576,64,128]{2,1,0:T(8,128)(2,1)} fusion(bf16[12,22,64,128]{3,2,1,0:T(8,128)(2,1)} %pad_maximum_fusion, s32[576]{0:T(1024)S(1)} %reshape.171), kind=kCustom, calls=%fused_computation.1 | custom fusion | bytes 18878976 | tf_op jit(solution)/shard_map/vmap()/gather | solution.py:19
  753.1 7.1 fusion
  760.3 5.1 fusion.3
  766.7 12.2 %fusion.13 = bf16[6,64,12,128]{3,1,0,2:T(8,128)(2,1)S(1)} fusion(bf16[12,6,8,64,128]{4,3,2,1,0:T(8,128)(2,1)} %bitcast.94, f32[12,6,64,8,64]{2,4,3,1,0:T(8,128)} %copy-done, f32[12,6,64]{2,1,0:T(8,128)S(1)} %fusion.3, f32[12,6,64]{2,1,0:T(8,128)S(1)} %get-tuple-element.13, pred[12,6,8]{2,1,0:T(8,128)(4,1)S(1)} %iota_compare_fusion.2), kind=kOutput, calls=%fused_computation.30 | convolution fusion | flops 616366080 | bytes 20091456 | tf_op jit(solution)/shard_map/vmap(nqkb,nkbe->nqe)/dot_general | solution.py:32
  779.7 13.6 %multiply_convert_fusion = bf16[384,5120]{1,0:T(8,128)(2,1)} fusion(bf16[1,1536,5120]{2,1,0:T(8,128)(2,1)} %param.14, f32[]{:T(128)S(6)} %sub.23, bf16[48,8,12,128]{3,2,1,0:T(8,128)(2,1)S(1)} %bitcast.96), kind=kOutput, calls=%fused_computation.12 | convolution fusion | flops 6043729920 | bytes 20840452 | tf_op jit(solution)/shard_map/dot_general | solution.py:122
  793.3 49.5 %reduce-scatter.2.cloned.1.call-done = bf16[384,1280]{1,0:T(8,128)(2,1)} async-done(((bf16[384,5120]{1,0:T(8,128)(2,1)}), bf16[384,1280]{1,0:T(8,128)(2,1)}) %reduce-scatter.2.cloned.1.call-update) | async-done | bytes 983056 | tf_op jit(solution)/shard_map/reduce_scatter | solution.py:124
  (65 shorter events, 26.0 us)
Async XLA Ops:
  6.5 65.0 %all-gather.4.cloned.1.call-start = ((), (), s32[]{:S(2)}) async-start(), calls=%async_computation.4 | async-start | bytes 4915200 | tf_op jit(solution)/shard_map/all_gather | solution.py:54
  18.1 0.8 copy-start.1
  18.1 10.4 %copy-start.3 = (f32[1,2,12]{2,1,0:T(2,128)S(1)}, f32[1,2,12]{2,1,0:T(2,128)}, u32[]{:S(2)}) copy-start(f32[1,2,12]{2,1,0:T(2,128)} %param.15) | copy-start | bytes 292
  18.1 10.4 %copy-start.4 = (s32[6]{0:T(128)S(1)}, s32[6]{0:T(128)}, u32[]{:S(2)}) copy-start(s32[6]{0:T(128)} %param.12) | copy-start | bytes 76
  18.1 456.9 %all-gather.6.cloned.1.call-start = ((), (), s32[]{:S(2)}) async-start(), calls=%async_computation.6 | async-start | bytes 53084160 | tf_op jit(solution)/shard_map/all_gather | solution.py:67
  22.1 11.9 %all-to-all-start = ((s32[8,12,2]{1,2,0:T(2,128)}), s32[8,12,2]{1,2,0:T(2,128)S(1)}, u32[]{:S(2)}, u32[]{:S(2)}) async-start(s32[8,12,2]{1,2,0:T(2,128)} %copy.50), calls=%async_computation | async-start | bytes 16384 | tf_op jit(solution)/shard_map/all_to_all | solution.py:94
  576.3 76.0 %all-to-all-start.1 = ((bf16[8,12,2,64,128]{4,3,2,1,0:T(8,128)(2,1)}), bf16[8,12,2,64,128]{4,3,2,1,0:T(8,128)(2,1)}, u32[]{:S(2)}, u32[]{:S(2)}) async-start(bf16[8,12,2,64,128]{4,3,2,1,0:T(8,128)(2,1)} %copy.55), calls=%async_computation.1 | async-start | bytes 6291456 | tf_op jit(solution)/shard_map/all_to_all | solution.py:100
  591.4 65.9 %copy-start.2 = (s32[12,6]{0,1:T(8,128)S(1)}, s32[12,6]{0,1:T(8,128)}, u32[]{:S(2)}) copy-start(s32[12,6]{0,1:T(8,128)} %param.17) | copy-start | bytes 868
  652.3 76.0 %all-to-all-start.2 = ((bf16[8,12,2,64,128]{4,3,2,1,0:T(8,128)(2,1)}), bf16[8,12,2,64,128]{4,3,2,1,0:T(8,128)(2,1)}, u32[]{:S(2)}, u32[]{:S(2)}) async-start(bf16[8,12,2,64,128]{4,3,2,1,0:T(8,128)(2,1)} %copy.59), calls=%async_computation.2 | async-start | bytes 6291456 | tf_op jit(solution)/shard_map/all_to_all | solution.py:101
  656.7 186.1 %reduce-scatter.2.cloned.1.call-start = ((), (), s32[]{:S(2)}) async-start(), calls=%async_computation.5 | async-start | bytes 4915200 | tf_op jit(solution)/shard_map/reduce_scatter | solution.py:124
  760.2 6.5 copy-start
Sparse Core Ops, SparseCore 0:
  18.2 53.2 all-gather.3
  73.2 401.7 all-gather.5
  793.4 49.3 reduce-scatter.1
where the time goes:
time: 854 us; the launch traced here: 852 us
  waiting for transfers between devices  616 us (72%)
  local copies, waits for them, and re-layouts  104 us (12%)
  matrix products  75 us (9%)
  other arithmetic  28.7 us (3%)
  starting transfers between devices  15.5 us (2%)
  between operations  13.3 us (2%)
    all_gather x1, waiting for transfers between devices, per_device(): lax.all_gather(weight_here, 'seq', axis=0, tiled=True)  398 us
    all_to_all x1, waiting for transfers between devices, per_device(): lax.all_to_all(sent_values, 'seq', split_axis=0, concat_axis=0, tiled=True)  63.9 us
    all_to_all x1, waiting for transfers between devices, per_device(): lax.all_to_all(sent_keys, 'seq', split_axis=0, concat_axis=0, tiled=True)  60.9 us
    dot_general x1, local copies, waits for them, and re-layouts, per_device(): jnp.dot(normed, lax.all_gather(weight_here, 'seq', axis=0, tiled=True), p...  54.8 us
    reduce_scatter x1, waiting for transfers between devices, per_device(): lax.psum_scatter(signed.astype(jnp.bfloat16), ('role', 'head'), scatter_d...  49.5 us
    all_gather x1, waiting for transfers between devices, per_device(): forked = lax.all_gather(generated, ('role', 'head'), axis=1, tiled=True)  37.2 us
    dot_general x1, matrix products, per_device(): jnp.dot(normed, lax.all_gather(weight_here, 'seq', axis=0, tiled=True), p...  30.7 us
  transfers between devices with their start and end apart: 6, of which 6 were waited for; matrix products, arithmetic and copies ran while one was open for 3% of the time, Pallas kernels for 0%

commit v1 on v0

--- a/solution.py
+++ b/solution.py
@@ -3,6 +3,9 @@
 import jax
 import jax.numpy as jnp
 from jax import lax
+from jax.experimental import pallas as pl
+from jax.experimental.pallas import tpu as pltpu
+from jax.sharding import Mesh
 from jax.sharding import PartitionSpec as P
 
 HEAD_DIM = 128
@@ -37,7 +40,7 @@
     return table[wanted]
 
 
-def per_device(
+def per_device_by_tokens(
     hidden_rows,
     gen_weight,
     noise,
@@ -126,22 +129,360 @@
     ).astype(jnp.float32)
 
 
+VMEM_BYTES = 56 * 1024 * 1024
+CORES = 2
+
+
+def whole_in_vmem():
+    return pl.BlockSpec(memory_space=pltpu.VMEM)
+
+
+def in_hbm():
+    return pl.BlockSpec(memory_space=pl.ANY)
+
+
+def in_smem():
+    return pl.BlockSpec(memory_space=pltpu.SMEM)
+
+
+def project_heads(places, gains, rounds, weight_own, weight_other):
+    slabs, depth, columns = weight_own.shape
+    tokens, features = rounds[0][0].shape
+    half = rounds[0][3].shape[0]
+    heads = columns // (3 * HEAD_DIM)
+    pieces = [piece for one in rounds for piece in one]
+    per_round = len(rounds[0])
+    dtype = weight_own.dtype
+
+    def body(places_ref, gains_ref, own_ref, other_ref, *refs):
+        piece_refs = refs[: len(pieces)]
+        query_ref, kv_ref = refs[len(pieces) : len(pieces) + 2]
+        table, rows, weight_sems, row_sems = refs[len(pieces) + 2 :]
+        core = places_ref[4]
+        weight_copies = []
+        for slab in range(slabs):
+            for side, ref in enumerate((own_ref, other_ref)):
+                place = core if side == 0 else 1 - core
+                copy = pltpu.make_async_copy(
+                    ref.at[slab], table.at[slab, place], weight_sems.at[slab, side]
+                )
+                copy.start()
+                weight_copies.append(copy)
+        row_copies = []
+        for turn in range(len(rounds)):
+            for which in range(per_round):
+                ref = piece_refs[turn * per_round + which]
+                if which < 3:
+                    target = rows.at[turn, which]
+                else:
+                    target = rows.at[turn, 3, pl.ds((which - 3) * half, half)]
+                copy = pltpu.make_async_copy(ref, target, row_sems.at[turn, which])
+                copy.start()
+                row_copies.append(copy)
+        for copy in weight_copies:
+            copy.wait()
+        for turn in range(len(rounds)):
+            for which in range(per_round):
+                row_copies[turn * per_round + which].wait()
+            total = None
+            for which in range(4):
+                weight = table[places_ref[which]].reshape(CORES * depth, columns)
+                part = jnp.dot(rows[turn, which], weight, preferred_element_type=jnp.float32)
+                total = part if total is None else total + part
+            for head in range(heads):
+                at = 3 * head * HEAD_DIM
+                for part in range(2):
+                    block = total[:, at + part * HEAD_DIM : at + (part + 1) * HEAD_DIM]
+                    normal = rms_rows(block) * gains_ref[part, head]
+                    if part == 0:
+                        query_ref[head, turn] = normal.astype(dtype)
+                    else:
+                        kv_ref[head, 0, turn] = normal.astype(dtype)
+                block = total[:, at + 2 * HEAD_DIM : at + 3 * HEAD_DIM]
+                kv_ref[head, 1, turn] = block.astype(dtype)
+
+    return pl.pallas_call(
+        body,
+        in_specs=[in_smem(), in_smem(), in_hbm(), in_hbm()] + [in_hbm()] * len(pieces),
+        out_specs=(whole_in_vmem(), whole_in_vmem()),
+        out_shape=(
+            jax.ShapeDtypeStruct((heads, len(rounds), tokens, HEAD_DIM), dtype),
+            jax.ShapeDtypeStruct((heads, 2, len(rounds), tokens, HEAD_DIM), dtype),
+        ),
+        scratch_shapes=[
+            pltpu.VMEM((slabs, CORES, depth, columns), dtype),
+            pltpu.VMEM((len(rounds), 4, tokens, features), dtype),
+            pltpu.SemaphoreType.DMA((slabs, 2)),
+            pltpu.SemaphoreType.DMA((len(rounds), per_round)),
+        ],
+        compiler_params=pltpu.CompilerParams(vmem_limit_bytes=VMEM_BYTES),
+        name="project_heads",
+    )(places, gains, weight_own, weight_other, *pieces)
+
+
+def attend(key_slots, counts, query_slots, queries, kv_own, kv_other):
+    blocks = queries.shape[0]
+    most = key_slots.shape[1]
+    scale = 1.0 / math.sqrt(HEAD_DIM)
+    together = 4 if blocks % 4 == 0 else 1
+
+    def body(slots_ref, counts_ref, from_ref, query_ref, own_ref, other_ref, out_ref, table, sems):
+        copies = []
+        for side, ref in enumerate((own_ref, other_ref)):
+            for part in range(2):
+                copy = pltpu.make_async_copy(
+                    ref.at[part], table.at[part, pl.ds(side * blocks, blocks)], sems.at[side, part]
+                )
+                copy.start()
+                copies.append(copy)
+        for copy in copies:
+            copy.wait()
+
+        def step(at, carry):
+            for inner in range(together):
+                block = at * together + inner
+                slots = [slots_ref[block, entry] for entry in range(most)]
+                keys = jnp.concatenate([table[0, slot] for slot in slots], axis=0)
+                values = jnp.concatenate([table[1, slot] for slot in slots], axis=0)
+                scores = (
+                    lax.dot_general(
+                        query_ref[from_ref[block]],
+                        keys,
+                        (((1,), (1,)), ((), ())),
+                        preferred_element_type=jnp.float32,
+                    )
+                    * scale
+                )
+                column = lax.broadcasted_iota(jnp.int32, scores.shape, 1)
+                scores = jnp.where(column < counts_ref[block] * BLOCK, scores, -jnp.inf)
+                highest = jnp.max(scores, axis=1, keepdims=True)
+                raised = jnp.exp(scores - highest)
+                summed = jnp.sum(raised, axis=1, keepdims=True)
+                weights = (raised / summed).astype(values.dtype)
+                mixed = jnp.dot(weights, values, preferred_element_type=jnp.float32)
+                out_ref[block] = mixed.astype(out_ref.dtype)
+            return carry
+
+        lax.fori_loop(0, blocks // together, step, 0)
+
+    return pl.pallas_call(
+        body,
+        in_specs=[in_smem(), in_smem(), in_smem(), whole_in_vmem(), in_hbm(), in_hbm()],
+        out_specs=whole_in_vmem(),
+        out_shape=jax.ShapeDtypeStruct(queries.shape, queries.dtype),
+        scratch_shapes=[
+            pltpu.VMEM((2, CORES * blocks, BLOCK, HEAD_DIM), queries.dtype),
+            pltpu.SemaphoreType.DMA((2, 2)),
+        ],
+        compiler_params=pltpu.CompilerParams(vmem_limit_bytes=VMEM_BYTES),
+        name="attend",
+    )(key_slots, counts, query_slots, queries, kv_own, kv_other)
+
+
+def out_blocks(which, sign, attended, out_weight, dtype, steps):
+    groups, tokens, _ = attended[0].shape
+    count = len(attended)
+    depth, features = out_weight.shape
+    wanted = which.shape[0]
+    width = features // steps
+    split = 1 if (width // 2) % HEAD_DIM else 2
+    tile = width // split
+
+    def body(which_ref, sign_ref, *refs):
+        parts, weight_ref, out_ref, joined = refs[:count], refs[count], refs[count + 1], refs[count + 2]
+
+        @pl.when(jnp.logical_and(pl.program_id(0) == 0, pl.program_id(1) == 0))
+        def _():
+            for group in range(groups):
+                for chunk in range(count):
+                    at = (group * count + chunk) * HEAD_DIM
+                    joined[:, at : at + HEAD_DIM] = parts[chunk][group]
+
+        total = jnp.dot(joined[...], weight_ref[...], preferred_element_type=jnp.float32)
+        out_ref[0] = (total * sign_ref[0].astype(jnp.float32)).astype(dtype)
+
+    return pl.pallas_call(
+        body,
+        grid_spec=pltpu.PrefetchScalarGridSpec(
+            num_scalar_prefetch=2,
+            grid=(wanted, split),
+            in_specs=[pl.BlockSpec((groups, tokens, HEAD_DIM), lambda i, k, w, s: (0, 0, 0))] * count
+            + [pl.BlockSpec((depth, tile), lambda i, k, w, s: (0, w[i] * split + k))],
+            out_specs=pl.BlockSpec((1, tokens, tile), lambda i, k, w, s: (i, 0, k)),
+            scratch_shapes=[pltpu.VMEM((tokens, depth), attended[0].dtype)],
+        ),
+        out_shape=jax.ShapeDtypeStruct((wanted, tokens, width), dtype),
+        compiler_params=pltpu.CompilerParams(vmem_limit_bytes=VMEM_BYTES),
+        name="out_blocks",
+    )(which, sign, *attended, out_weight)
+
+
+def per_device_by_heads(
+    hidden_rows,
+    gen_weight,
+    noise,
+    timesteps,
+    qkv_weight,
+    out_weight,
+    qk_gain,
+    block_keys,
+    block_count,
+):
+    role, head = lax.axis_index("role"), lax.axis_index("head")
+    chip, core = lax.axis_index("chip"), lax.axis_index("core")
+    chips = lax.axis_size("chip")
+    local_heads, local_blocks, most = block_keys.shape
+    heads = local_heads // chips
+    tokens = hidden_rows.shape[0]
+    width = hidden_rows.shape[1]
+    features = gen_weight.shape[1]
+    all_blocks = chips * local_blocks
+    swap = [(0, 1), (1, 0)]
+    ring = [(at, (at + 1) % chips) for at in range(chips)]
+
+    def exchange(array):
+        return lax.all_to_all(array, "chip", split_axis=0, concat_axis=0, tiled=True)
+
+    weight_rows = qkv_weight.shape[1]
+    by_chip = qkv_weight[0].reshape(weight_rows, chips, heads, 3 * HEAD_DIM)
+    weights_own = [exchange(by_chip[:, :, at].transpose(1, 0, 2)) for at in range(heads)]
+    weights_other = [lax.ppermute(one, "core", swap) for one in weights_own]
+
+    mine = role * lax.axis_size("head") + head
+    generated = jnp.dot(hidden_rows, gen_weight, preferred_element_type=jnp.float32).astype(
+        jnp.bfloat16
+    )
+    angle_blocks = (timesteps.astype(jnp.float32) * (math.pi / 2000.0))[:, None, None]
+    noise_here = lax.dynamic_slice_in_dim(noise, mine * features, features, axis=1)
+    noisy = jnp.cos(angle_blocks) * generated.astype(jnp.float32).reshape(
+        local_blocks, BLOCK, features
+    )
+    noisy = noisy + jnp.sin(angle_blocks) * noise_here.astype(jnp.float32).reshape(
+        local_blocks, BLOCK, features
+    )
+    squares = jnp.sum(noisy * noisy, axis=-1)
+    squares = squares + lax.ppermute(squares, "role", swap)
+    squares = squares + lax.ppermute(squares, "head", swap)
+    normed = (noisy * lax.rsqrt(squares / width + 1e-06)[:, :, None]).astype(jnp.bfloat16)
+    normed = normed.reshape(tokens, features)
+
+    shards = [normed]
+    for _ in range(chips - 1):
+        shards.append(lax.ppermute(shards[-1], "chip", ring))
+    rounds = []
+    for shard in shards:
+        over_role = lax.ppermute(shard, "role", swap)
+        over_head = lax.ppermute(shard, "head", swap)
+        first = lax.ppermute(over_head[: tokens // 2], "role", swap)
+        second = lax.ppermute(over_role[tokens // 2 :], "head", swap)
+        rounds.append((shard, over_role, over_head, first, second))
+
+    lists = jnp.concatenate([block_keys, block_count[:, :, None]], axis=2)
+    lists = exchange(lists.reshape(chips, heads, local_blocks, most + 1))
+    lists = lists.transpose(1, 0, 2, 3).reshape(heads, all_blocks, most + 1)
+    owner = lists[:, :, :most] // local_blocks
+    turn = (chip - owner // CORES) % chips
+    far = (owner % CORES != core).astype(jnp.int32)
+    key_slots = far * all_blocks + turn * local_blocks + lists[:, :, :most] % local_blocks
+    counts = lists[:, :, most]
+    spot = jnp.arange(all_blocks, dtype=jnp.int32)
+    query_slots = (chip - spot // local_blocks) % chips * local_blocks + spot % local_blocks
+
+    sides = lax.axis_size("head")
+    peers = jnp.stack(
+        [
+            role * sides + head,
+            (1 - role) * sides + head,
+            role * sides + 1 - head,
+            (1 - role) * sides + 1 - head,
+        ]
+    ).astype(jnp.int32)
+    places = jnp.concatenate([peers, core[None].astype(jnp.int32)])
+    gains = lax.dynamic_slice_in_dim(qk_gain[0], chip * heads, heads, axis=1)
+
+    attended = []
+    for at in range(heads):
+        queries, kv = project_heads(
+            places, gains[:, at : at + 1], rounds, weights_own[at], weights_other[at]
+        )
+        kv = kv.reshape(2, all_blocks, BLOCK, HEAD_DIM)
+        kv_other = lax.ppermute(kv, "core", swap)
+        mixed = attend(
+            key_slots[at],
+            counts[at],
+            query_slots,
+            queries.reshape(all_blocks, BLOCK, HEAD_DIM),
+            kv,
+            kv_other,
+        )
+        attended.append(exchange(mixed.reshape(chips, tokens, HEAD_DIM)))
+
+    sign = (2 * role - 1).astype(jnp.int32)[None]
+    blocks = sides * lax.axis_size("role")
+    diagonal = out_blocks(peers[3:4], sign, attended, out_weight[0], jnp.bfloat16, blocks)
+    sides_two = out_blocks(peers[1:3], sign, attended, out_weight[0], jnp.bfloat16, blocks)
+    own = out_blocks(peers[0:1], sign, attended, out_weight[0], jnp.float32, blocks)
+    far_swap = [(0, 3), (1, 2), (2, 1), (3, 0)]
+    from_diagonal = lax.ppermute(diagonal[0], ("role", "head"), far_swap)
+    from_role = lax.ppermute(sides_two[0], "role", swap)
+    from_head = lax.ppermute(sides_two[1], "head", swap)
+    return own[0] + (
+        from_role.astype(jnp.float32)
+        + from_head.astype(jnp.float32)
+        + from_diagonal.astype(jnp.float32)
+    )
+
+
+def splits_heads(mesh, qkv_weight, hidden_rows):
+    role, seq, head = (mesh.shape[name] for name in ("role", "seq", "head"))
+    if role != 2 or head != 2 or seq % CORES != 0:
+        return False
+    chips = seq // CORES
+    heads = qkv_weight.shape[2] // (3 * HEAD_DIM * head)
+    width = hidden_rows.shape[1]
+    tokens = hidden_rows.shape[0] // seq
+    return (
+        heads % chips == 0
+        and chips == role * head
+        and width % (role * head * 256) == 0
+        and width % (seq * 16) == 0
+        and tokens % (2 * BLOCK) == 0
+    )
+
+
 def solution(mesh):
-    placed = (
-        P("seq", None),
-        P(None, ("role", "head")),
-        P("seq", None),
-        P("seq"),
-        P("role", "seq", "head"),
-        P("role", "head", None),
-        P("role", None, "head"),
-        P("head", "seq", None),
-        P("head", "seq"),
-    )
-    return jax.shard_map(
-        per_device,
-        mesh=mesh,
-        in_specs=placed,
-        out_specs=P("seq", ("role", "head")),
-        check_vma=False,
-    )
+    def call(*arrays):
+        if splits_heads(mesh, arrays[4], arrays[0]):
+            per_device = per_device_by_heads
+            seq = ("chip", "core")
+            shape = mesh.devices.shape
+            names = mesh.axis_names
+            at = names.index("seq")
+            layout = Mesh(
+                mesh.devices.reshape(shape[:at] + (shape[at] // CORES, CORES) + shape[at + 1 :]),
+                names[:at] + seq + names[at + 1 :],
+            )
+        else:
+            per_device = per_device_by_tokens
+            seq = "seq"
+            layout = mesh
+        placed = (
+            P(seq, None),
+            P(None, ("role", "head")),
+            P(seq, None),
+            P(seq),
+            P("role", seq, "head"),
+            P("role", "head", None),
+            P("role", None, "head"),
+            P("head", seq, None),
+            P("head", seq),
+        )
+        return jax.shard_map(
+            per_device,
+            mesh=layout,
+            in_specs=placed,
+            out_specs=P(seq, ("role", "head")),
+            check_vma=False,
+        )(*arrays)
+
+    return call

time: 854 us -> 470 us (0.55)
  waiting for transfers between devices: 616 us -> 221 us
  Pallas kernels: 0 us -> 108 us
  starting transfers between devices: 15.5 us -> 79.9 us
  matrix products: 75 us -> 11.5 us
  local copies, waits for them, and re-layouts: 104 us -> 42.3 us
  other arithmetic: 28.7 us -> 5.55 us
  between operations: 13.3 us -> 0.37 us
    all_gather x2 -> x0, waiting for transfers between devices: 435 us -> none  [the longest x1 398 us: per_device(): lax.all_gather(weight_here, 'seq', axis=0, tiled=True)]
    ppermute x0 -> x30, waiting for transfers between devices: none -> 150 us  [the longest x3 53.3 us: per_device_by_heads(): shards.append(lax.ppermute(shards[-1], 'chip', ring))]
    pallas_call x0 -> x9, Pallas kernels: none -> 108 us  [the longest x3 52.7 us: project_heads(): pl.pallas_call(body, in_specs=[in_smem(), in_smem(), in_hbm(), in_hbm()]...]
    dot_general x5 -> x1, matrix products: 75 us -> 11.5 us  [per_device_by_heads(): jnp.dot(hidden_rows, gen_weight, preferred_element_type=jnp.float32)]
    all_to_all x3 -> x7, waiting for transfers between devices: 130 us -> 70.8 us  [exchange(): lax.all_to_all(array, 'chip', split_axis=0, concat_axis=0, tiled=True)]
    dot_general x1 -> x0, local copies, waits for them, and re-layouts: 54.8 us -> none  [per_device(): jnp.dot(normed, lax.all_gather(weight_here, 'seq', axis=0, tiled=True), p...]
    reduce_scatter x1 -> x0, waiting for transfers between devices: 49.5 us -> none  [per_device(): lax.psum_scatter(signed.astype(jnp.bfloat16), ('role', 'head'), scatter_d...]
    ppermute x0 -> x30, starting transfers between devices: none -> 39.3 us  [the longest x3 12 us: per_device_by_heads(): shards.append(lax.ppermute(shards[-1], 'chip', ring))]
  transfers between devices with their start and end apart: 6 -> 37, of which waited for: 6 -> 17; matrix products, arithmetic and copies ran while one was open for 3% -> 7% of each run, Pallas kernels for 0% -> 22%
where the time goes in v1:
time: 470 us; the launch traced here: 469 us
  waiting for transfers between devices  221 us (47%)
  Pallas kernels  108 us (23%)
  starting transfers between devices  79.9 us (17%)
  local copies, waits for them, and re-layouts  42.3 us (9%)
  matrix products  11.5 us (2%)
  other arithmetic  5.55 us (1%)
    all_to_all x7, waiting for transfers between devices, exchange(): lax.all_to_all(array, 'chip', split_axis=0, concat_axis=0, tiled=True)  70.8 us
    ppermute x3, waiting for transfers between devices, per_device_by_heads(): shards.append(lax.ppermute(shards[-1], 'chip', ring))  53.3 us
    pallas_call x3, Pallas kernels, project_heads(): pl.pallas_call(body, in_specs=[in_smem(), in_smem(), in_hbm(), in_hbm()]...  52.7 us
    all_to_all x7, starting transfers between devices, exchange(): lax.all_to_all(array, 'chip', split_axis=0, concat_axis=0, tiled=True)  40.6 us
    ppermute x4, waiting for transfers between devices, per_device_by_heads(): second = lax.ppermute(over_role[tokens // 2:], 'head', swap)  37.2 us
    pallas_call x3, Pallas kernels, attend(): pl.pallas_call(body, in_specs=[in_smem(), in_smem(), in_smem(), whole_in_...  36.1 us
    unnamed x58, local copies, waits for them, and re-layouts  25.5 us
    ppermute x4, waiting for transfers between devices, per_device_by_heads(): first = lax.ppermute(over_head[:tokens // 2], 'role', swap)  22.2 us
  transfers between devices with their start and end apart: 37, of which 17 were waited for; matrix products, arithmetic and copies ran while one was open for 7% of the time, Pallas kernels for 22%

profile of v1, /device:TPU:0, one launch (start us, length us, event | category | flops | bytes accessed | tf_op | source)
XLA Modules:
  0.0 468.7 jit_solution(9020909790510785347)
XLA Ops:
  0.0 8.8 %copy.18 = bf16[1,640,4608]{1,2,0:T(8,128)(2,1)} copy(bf16[1,640,4608]{2,1,0:T(8,128)(2,1)} %param.13) | data formatting | bytes 11796480 | tf_op args[4]
  27.5 42.7 %all-to-all-done.1.own_ref = bf16[4,640,384]{2,1,0:T(8,128)(2,1)} async-done(((bf16[4,640,384]{2,1,0:T(8,128)(2,1)}), bf16[4,640,384]{2,1,0:T(8,128)(2,1)}, u32[]{:S(2)}, u32[]{:S(2)}) %all-to-all-start.1) | async-done | bytes 1966112 | tf_op jit(solution)/shard_map/all_to_all | solution.py:344
  74.7 11.5 %multiply_reduce_fusion = (f32[384]{0:T(512)S(1)}, f32[384,1280]{1,0:T(8,128)S(1)}) fusion(bf16[384,5120]{1,0:T(8,128)(2,1)} %param.11, s32[]{:T(128)S(6)} %select_n.53, f32[384]{0:T(512)S(1)} %mul.88, bf16[384,5120]{1,0:T(8,128)(2,1)} %param.9, bf16[5120,1280]{1,0:T(8,128)(2,1)} %param.10, f32[384]{0:T(512)S(1)} %mul.84), kind=kOutput, calls=%fused_computation.6 | convolution fusion | flops 5037096448 | bytes 19993092 | tf_op jit(solution)/shard_map/dot_general | solution.py:352
  97.4 33.8 %collective-permute-done.7.refs_5_ = bf16[384,1280]{1,0:T(8,128)(2,1)} collective-permute-done((bf16[384,1280]{1,0:T(8,128)(2,1)S(1)}, bf16[384,1280]{1,0:T(8,128)(2,1)}, u32[]{:S(2)}, u32[]{:S(2)}) %collective-permute-start.7) | collective-permute-done | bytes 983072 | tf_op jit(solution)/shard_map/ppermute | solution.py:371
  131.2 8.1 %collective-permute-start.12 = (bf16[384,1280]{1,0:T(8,128)(2,1)}, bf16[384,1280]{1,0:T(8,128)(2,1)}, u32[]{:S(2)}, u32[]{:S(2)}) collective-permute-start(bf16[384,1280]{1,0:T(8,128)(2,1)} %collective-permute-done.7.refs_5_), channel_id=1, source_target_pairs={{0,4},{4,8},{8,12},{12,0},{1,5},{5,9},{9,13},{13,1},{2,6},{6,10},{... | collective-permute-start | bytes 2949128 | tf_op jit(solution)/shard_map/ppermute | solution.py:371
  144.8 16.9 %all-to-all-done.3.own_ref = bf16[4,640,384]{2,1,0:T(8,128)(2,1)} async-done(((bf16[4,640,384]{2,1,0:T(8,128)(2,1)}), bf16[4,640,384]{2,1,0:T(8,128)(2,1)}, u32[]{:S(2)}, u32[]{:S(2)}) %all-to-all-start.3) | async-done | bytes 1966112 | tf_op jit(solution)/shard_map/all_to_all | solution.py:344
  172.4 9.6 %collective-permute-done.5.refs_3_ = bf16[192,1280]{1,0:T(8,128)(2,1)S(1)} collective-permute-done((bf16[192,1280]{1,0:T(8,128)(2,1)S(1)}, bf16[192,1280]{1,0:T(8,128)(2,1)S(1)}, u32[]{:S(2)}, u32[]{:S(2)}) %collective-permute-start.5) | collective-permute-done | bytes 491552 | tf_op jit(solution)/shard_map/ppermute | solution.py:376
  183.6 7.6 %collective-permute-done.9.refs_7_ = bf16[384,1280]{1,0:T(8,128)(2,1)S(1)} collective-permute-done((bf16[384,1280]{1,0:T(8,128)(2,1)}, bf16[384,1280]{1,0:T(8,128)(2,1)S(1)}, u32[]{:S(2)}, u32[]{:S(2)}) %collective-permute-start.9) | collective-permute-done | bytes 983072 | tf_op jit(solution)/shard_map/ppermute | solution.py:375
  192.7 9.0 %collective-permute-done.6.refs_4_ = bf16[192,1280]{1,0:T(8,128)(2,1)S(1)} collective-permute-done((bf16[192,1280]{1,0:T(8,128)(2,1)S(1)}, bf16[192,1280]{1,0:T(8,128)(2,1)S(1)}, u32[]{:S(2)}, u32[]{:S(2)}) %collective-permute-start.6) | collective-permute-done | bytes 491552 | tf_op jit(solution)/shard_map/ppermute | solution.py:377
  203.2 19.5 %collective-permute-done.17.refs_15_ = bf16[384,1280]{1,0:T(8,128)(2,1)} collective-permute-done((bf16[384,1280]{1,0:T(8,128)(2,1)}, bf16[384,1280]{1,0:T(8,128)(2,1)}, u32[]{:S(2)}, u32[]{:S(2)}) %collective-permute-start.17) | collective-permute-done | bytes 983072 | tf_op jit(solution)/shard_map/ppermute | solution.py:371
  224.2 10.6 %collective-permute-done.10.refs_8_ = bf16[192,1280]{1,0:T(8,128)(2,1)} collective-permute-done((bf16[192,1280]{1,0:T(8,128)(2,1)S(1)}, bf16[192,1280]{1,0:T(8,128)(2,1)}, u32[]{:S(2)}, u32[]{:S(2)}) %collective-permute-start.10) | collective-permute-done | bytes 491552 | tf_op jit(solution)/shard_map/ppermute | solution.py:376
  238.7 26.3 %collective-permute-done.11.refs_9_ = bf16[192,1280]{1,0:T(8,128)(2,1)S(1)} collective-permute-done((bf16[192,1280]{1,0:T(8,128)(2,1)S(1)}, bf16[192,1280]{1,0:T(8,128)(2,1)S(1)}, u32[]{:S(2)}, u32[]{:S(2)}) %collective-permute-start.11) | collective-permute-done | bytes 491552 | tf_op jit(solution)/shard_map/ppermute | solution.py:377
  279.2 8.5 %all-to-all-start = ((s32[4,1,162]{2,1,0:T(1,128)}), s32[4,1,162]{2,1,0:T(1,128)S(1)}, u32[]{:S(2)}, u32[]{:S(2)}) async-start(s32[4,1,162]{2,1,0:T(1,128)} %reshape.67), calls=%async_computation | async-start | bytes 8192 | tf_op jit(solution)/shard_map/all_to_all | solution.py:344
  289.8 17.6 %project_heads.3 = (bf16[1,4,384,128]{3,2,1,0:T(8,128)(2,1)}, bf16[1,2,4,384,128]{4,3,2,1,0:T(8,128)(2,1)}) custom-call(s32[5]{0:T(128)} %concatenate.16.places_ref, f32[2,1]{1,0:T(2,128)} %get-tuple-element.30.gains_ref, bf16[4,640,384]{2,1,0:T(8,128)(2,1)} %all-to-all-done.1.own_ref, bf16[4,640,384]{2,1,0:T(8,128)(2,1)} %collective-permute-done.other_ref, ...), custom_call_target="tpu_custom_call" | custom-call | tf_op jit(solution)/shard_map/project_heads/pallas_call | solution.py:204
  310.4 17.6 %project_heads.4 = (bf16[1,4,384,128]{3,2,1,0:T(8,128)(2,1)}, bf16[1,2,4,384,128]{4,3,2,1,0:T(8,128)(2,1)}) custom-call(s32[5]{0:T(128)} %concatenate.16.places_ref, f32[2,1]{1,0:T(2,128)} %get-tuple-element.29.gains_ref, bf16[4,640,384]{2,1,0:T(8,128)(2,1)} %all-to-all-done.3.own_ref, bf16[4,640,384]{2,1,0:T(8,128)(2,1)} %collective-permute-done.23.other_ref, ...), custom_call_target="tpu_custom_call" | custom-call | tf_op jit(solution)/shard_map/project_heads/pallas_call | solution.py:204
  330.1 12.0 %attend.3 = bf16[24,64,128]{2,1,0:T(8,128)(2,1)} custom-call(s32[24,8]{1,0:T(8,128)} %get-tuple-element.24.slots_ref, s32[24]{0:T(128)} %get-tuple-element.27.counts_ref, s32[24]{0:T(128)} %fusion.12.from_ref, bf16[24,64,128]{2,1,0:T(8,128)(2,1)} %bitcast.71, bf16[2,24,64,128]{3,2,1,0:T(8,128)(2,1)} %bitcast.67, bf16[2,24,64,128]{3,2,1,0:T(8,128)(2,1)} %copy-done.20), custom_call_target="tpu_custom_call" | custom-call | tf_op jit(solution)/shard_map/attend/pallas_call | solution.py:268
  342.1 6.7 %all-to-all-start.2 = ((bf16[4,384,128]{2,1,0:T(8,128)(2,1)}), bf16[4,384,128]{2,1,0:T(8,128)(2,1)S(1)}, u32[]{:S(2)}, u32[]{:S(2)}) async-start(bf16[4,384,128]{2,1,0:T(8,128)(2,1)} %bitcast.60), calls=%async_computation.2 | async-start | bytes 786432 | tf_op jit(solution)/shard_map/all_to_all | solution.py:344
  348.8 17.6 %project_heads.5 = (bf16[1,4,384,128]{3,2,1,0:T(8,128)(2,1)}, bf16[1,2,4,384,128]{4,3,2,1,0:T(8,128)(2,1)}) custom-call(s32[5]{0:T(128)} %concatenate.16.places_ref, f32[2,1]{1,0:T(2,128)} %get-tuple-element.28.gains_ref, bf16[4,640,384]{2,1,0:T(8,128)(2,1)} %all-to-all-done.5.own_ref, bf16[4,640,384]{2,1,0:T(8,128)(2,1)} %collective-permute-done.25.other_ref, ...), custom_call_target="tpu_custom_call" | custom-call | tf_op jit(solution)/shard_map/project_heads/pallas_call | solution.py:204
  367.3 12.0 %attend.4 = bf16[24,64,128]{2,1,0:T(8,128)(2,1)} custom-call(s32[24,8]{1,0:T(8,128)} %get-tuple-element.23.slots_ref, s32[24]{0:T(128)} %get-tuple-element.26.counts_ref, s32[24]{0:T(128)} %fusion.12.from_ref, bf16[24,64,128]{2,1,0:T(8,128)(2,1)} %bitcast.70, bf16[2,24,64,128]{3,2,1,0:T(8,128)(2,1)} %bitcast.65, bf16[2,24,64,128]{3,2,1,0:T(8,128)(2,1)} %copy-done.19), custom_call_target="tpu_custom_call" | custom-call | tf_op jit(solution)/shard_map/attend/pallas_call | solution.py:268
  385.4 12.0 %attend.5 = bf16[24,64,128]{2,1,0:T(8,128)(2,1)} custom-call(s32[24,8]{1,0:T(8,128)} %get-tuple-element.22.slots_ref, s32[24]{0:T(128)} %get-tuple-element.25.counts_ref, s32[24]{0:T(128)} %fusion.12.from_ref, bf16[24,64,128]{2,1,0:T(8,128)(2,1)} %bitcast.72, bf16[2,24,64,128]{3,2,1,0:T(8,128)(2,1)} %bitcast.69, bf16[2,24,64,128]{3,2,1,0:T(8,128)(2,1)} %copy-done.21), custom_call_target="tpu_custom_call" | custom-call | tf_op jit(solution)/shard_map/attend/pallas_call | solution.py:268
  403.2 11.2 %all-to-all-done.6.refs_2_ = bf16[4,384,128]{2,1,0:T(8,128)(2,1)S(1)} async-done(((bf16[4,384,128]{2,1,0:T(8,128)(2,1)}), bf16[4,384,128]{2,1,0:T(8,128)(2,1)S(1)}, u32[]{:S(2)}, u32[]{:S(2)}) %all-to-all-start.6) | async-done | bytes 393248 | tf_op jit(solution)/shard_map/all_to_all | solution.py:344
  422.0 8.7 %out_blocks.4 = bf16[2,384,1280]{2,1,0:T(8,128)(2,1)} custom-call(s32[2]{0:T(128)} %pad_add_fusion.1.which_ref, s32[1]{0:T(128)} %bitcast.1.sign_ref, bf16[4,384,128]{2,1,0:T(8,128)(2,1)} %copy-done.10, bf16[4,384,128]{2,1,0:T(8,128)(2,1)} %copy-done.11, bf16[4,384,128]{2,1,0:T(8,128)(2,1)} %copy-done.12, bf16[1536,5120]{1,0:T(8,128)(2,1)} %bitcast.56), custom_call_target="tpu_custom_call" | custom-call | tf_op jit(solution)/shard_map/out_blocks/pallas_call | solution.py:304
  439.2 6.8 %collective-permute-done.29 = bf16[384,1280]{1,0:T(8,128)(2,1)S(1)} collective-permute-done((bf16[384,1280]{1,0:T(8,128)(2,1)}, bf16[384,1280]{1,0:T(8,128)(2,1)S(1)}, u32[]{:S(2)}, u32[]{:S(2)}) %collective-permute-start.29) | collective-permute-done | bytes 983072 | tf_op jit(solution)/shard_map/ppermute | solution.py:426
  446.0 19.1 %collective-permute-done.28 = bf16[384,1280]{1,0:T(8,128)(2,1)S(1)} collective-permute-done((bf16[384,1280]{1,0:T(8,128)(2,1)S(1)}, bf16[384,1280]{1,0:T(8,128)(2,1)S(1)}, u32[]{:S(2)}, u32[]{:S(2)}) %collective-permute-start.28) | collective-permute-done | bytes 983072 | tf_op jit(solution)/shard_map/ppermute | solution.py:428
  (155 shorter events, 114.3 us)
Async XLA Ops:
  18.3 51.9 %all-to-all-start.1 = ((bf16[4,640,384]{2,1,0:T(8,128)(2,1)}), bf16[4,640,384]{2,1,0:T(8,128)(2,1)}, u32[]{:S(2)}, u32[]{:S(2)}) async-start(bf16[4,640,384]{2,1,0:T(8,128)(2,1)} %bitcast.13), calls=%async_computation.1 | async-start | bytes 3932160 | tf_op jit(solution)/shard_map/all_to_all | solution.py:344
  70.2 91.5 %all-to-all-start.3 = ((bf16[4,640,384]{2,1,0:T(8,128)(2,1)}), bf16[4,640,384]{2,1,0:T(8,128)(2,1)}, u32[]{:S(2)}, u32[]{:S(2)}) async-start(bf16[4,640,384]{2,1,0:T(8,128)(2,1)} %bitcast.20), calls=%async_computation.3 | async-start | bytes 3932160 | tf_op jit(solution)/shard_map/all_to_all | solution.py:344
  93.7 37.5 %collective-permute-start.7 = (bf16[384,1280]{1,0:T(8,128)(2,1)S(1)}, bf16[384,1280]{1,0:T(8,128)(2,1)}, u32[]{:S(2)}, u32[]{:S(2)}) collective-permute-start(bf16[384,1280]{1,0:T(8,128)(2,1)S(1)} %multiply_convert_fusion.refs_0_), channel_id=1, source_target_pairs={{0,4},{4,8},{8,12},{12,0},{1,5},{5,9},{9,13},{13,1},{2,6},{6,10},{... | collective-permute-start | bytes 2949128 | tf_op jit(solution)/shard_map/ppermute | solution.py:371
  95.8 72.0 %collective-permute-start.4 = (bf16[384,1280]{1,0:T(8,128)(2,1)S(1)}, bf16[384,1280]{1,0:T(8,128)(2,1)S(1)}, u32[]{:S(2)}, u32[]{:S(2)}) collective-permute-start(bf16[384,1280]{1,0:T(8,128)(2,1)S(1)} %multiply_convert_fusion.refs_0_), channel_id=1, source_target_pairs={{0,1},{1,0},{2,3},{3,2},{4,5},{5,4},{6,7},{7,6},{8,9},{9,8},{10,11... | collective-permute-start | bytes 2949128 | tf_op jit(solution)/shard_map/ppermute | solution.py:375
  131.2 38.2 %collective-permute-start.12 = (bf16[384,1280]{1,0:T(8,128)(2,1)}, bf16[384,1280]{1,0:T(8,128)(2,1)}, u32[]{:S(2)}, u32[]{:S(2)}) collective-permute-start(bf16[384,1280]{1,0:T(8,128)(2,1)} %collective-permute-done.7.refs_5_), channel_id=1, source_target_pairs={{0,4},{4,8},{8,12},{12,0},{1,5},{5,9},{9,13},{13,1},{2,6},{6,10},{... | collective-permute-start | bytes 2949128 | tf_op jit(solution)/shard_map/ppermute | solution.py:371
  143.3 28.5 %collective-permute-start.3 = (bf16[384,1280]{1,0:T(8,128)(2,1)S(1)}, bf16[384,1280]{1,0:T(8,128)(2,1)S(1)}, u32[]{:S(2)}, u32[]{:S(2)}) collective-permute-start(bf16[384,1280]{1,0:T(8,128)(2,1)S(1)} %multiply_convert_fusion.refs_0_), channel_id=1, source_target_pairs={{0,16},{16,0},{1,17},{17,1},{2,18},{18,2},{3,19},{19,3},{4,20},{20... | collective-permute-start | bytes 2949128 | tf_op jit(solution)/shard_map/ppermute | solution.py:374
  161.7 106.7 %all-to-all-start.5 = ((bf16[4,640,384]{2,1,0:T(8,128)(2,1)}), bf16[4,640,384]{2,1,0:T(8,128)(2,1)}, u32[]{:S(2)}, u32[]{:S(2)}) async-start(bf16[4,640,384]{2,1,0:T(8,128)(2,1)} %bitcast.59), calls=%async_computation.5 | async-start | bytes 3932160 | tf_op jit(solution)/shard_map/all_to_all | solution.py:344
  169.4 53.3 %collective-permute-start.17 = (bf16[384,1280]{1,0:T(8,128)(2,1)}, bf16[384,1280]{1,0:T(8,128)(2,1)}, u32[]{:S(2)}, u32[]{:S(2)}) collective-permute-start(bf16[384,1280]{1,0:T(8,128)(2,1)} %collective-permute-done.12.refs_10_), channel_id=1, source_target_pairs={{0,4},{4,8},{8,12},{12,0},{1,5},{5,9},{9,13},{13,1},{2,6},{6,10},{... | collective-permute-start | bytes 2949128 | tf_op jit(solution)/shard_map/ppermute | solution.py:371
  171.3 52.9 %collective-permute-start.8 = (bf16[384,1280]{1,0:T(8,128)(2,1)}, bf16[384,1280]{1,0:T(8,128)(2,1)S(1)}, u32[]{:S(2)}, u32[]{:S(2)}) collective-permute-start(bf16[384,1280]{1,0:T(8,128)(2,1)} %collective-permute-done.7.refs_5_), channel_id=1, source_target_pairs={{0,16},{16,0},{1,17},{17,1},{2,18},{18,2},{3,19},{19,3},{4,20},{20... | collective-permute-start | bytes 2949128 | tf_op jit(solution)/shard_map/ppermute | solution.py:374
  171.9 29.8 %collective-permute-start.6 = (bf16[192,1280]{1,0:T(8,128)(2,1)S(1)}, bf16[192,1280]{1,0:T(8,128)(2,1)S(1)}, u32[]{:S(2)}, u32[]{:S(2)}) collective-permute-start(bf16[192,1280]{1,0:T(8,128)(2,1)S(1)} %slice.107), channel_id=1, source_target_pairs={{0,1},{1,0},{2,3},{3,2},{4,5},{5,4},{6,7},{7,6},{8,9},{9,8},{10,11... | collective-permute-start | bytes 1474568 | tf_op jit(solution)/shard_map/ppermute | solution.py:377
  182.0 53.3 %collective-permute-start.13 = (bf16[384,1280]{1,0:T(8,128)(2,1)}, bf16[384,1280]{1,0:T(8,128)(2,1)S(1)}, u32[]{:S(2)}, u32[]{:S(2)}) collective-permute-start(bf16[384,1280]{1,0:T(8,128)(2,1)} %collective-permute-done.12.refs_10_), channel_id=1, source_target_pairs={{0,16},{16,0},{1,17},{17,1},{2,18},{18,2},{3,19},{19,3},{4,20},{20... | collective-permute-start | bytes 2949128 | tf_op jit(solution)/shard_map/ppermute | solution.py:374
  191.2 45.8 %collective-permute-start.14 = (bf16[384,1280]{1,0:T(8,128)(2,1)}, bf16[384,1280]{1,0:T(8,128)(2,1)S(1)}, u32[]{:S(2)}, u32[]{:S(2)}) collective-permute-start(bf16[384,1280]{1,0:T(8,128)(2,1)} %collective-permute-done.12.refs_10_), channel_id=1, source_target_pairs={{0,1},{1,0},{2,3},{3,2},{4,5},{5,4},{6,7},{7,6},{8,9},{9,8},{10,11... | collective-permute-start | bytes 2949128 | tf_op jit(solution)/shard_map/ppermute | solution.py:375
  201.7 33.1 %collective-permute-start.10 = (bf16[192,1280]{1,0:T(8,128)(2,1)S(1)}, bf16[192,1280]{1,0:T(8,128)(2,1)}, u32[]{:S(2)}, u32[]{:S(2)}) collective-permute-start(bf16[192,1280]{1,0:T(8,128)(2,1)S(1)} %slice.108), channel_id=1, source_target_pairs={{0,16},{16,0},{1,17},{17,1},{2,18},{18,2},{3,19},{19,3},{4,20},{20... | collective-permute-start | bytes 1474568 | tf_op jit(solution)/shard_map/ppermute | solution.py:376
  222.7 44.2 %collective-permute-start.18 = (bf16[384,1280]{1,0:T(8,128)(2,1)}, bf16[384,1280]{1,0:T(8,128)(2,1)S(1)}, u32[]{:S(2)}, u32[]{:S(2)}) collective-permute-start(bf16[384,1280]{1,0:T(8,128)(2,1)} %collective-permute-done.17.refs_15_), channel_id=1, source_target_pairs={{0,16},{16,0},{1,17},{17,1},{2,18},{18,2},{3,19},{19,3},{4,20},{20... | collective-permute-start | bytes 2949128 | tf_op jit(solution)/shard_map/ppermute | solution.py:374
  224.2 64.8 %collective-permute-start = (bf16[4,640,384]{2,1,0:T(8,128)(2,1)}, bf16[4,640,384]{2,1,0:T(8,128)(2,1)}, u32[]{:S(2)}, u32[]{:S(2)}) collective-permute-start(bf16[4,640,384]{2,1,0:T(8,128)(2,1)} %all-to-all-done.1.own_ref), channel_id=1, source_target_pairs={{0,2},{2,0},{1,3},{3,1},{4,6},{6,4},{5,7},{7,5},{8,10},{10,8},{9,1... | collective-permute-start | bytes 5898248 | tf_op jit(solution)/shard_map/ppermute | solution.py:349
  234.8 33.6 %collective-permute-start.19 = (bf16[384,1280]{1,0:T(8,128)(2,1)}, bf16[384,1280]{1,0:T(8,128)(2,1)}, u32[]{:S(2)}, u32[]{:S(2)}) collective-permute-start(bf16[384,1280]{1,0:T(8,128)(2,1)} %collective-permute-done.17.refs_15_), channel_id=1, source_target_pairs={{0,1},{1,0},{2,3},{3,2},{4,5},{5,4},{6,7},{7,6},{8,9},{9,8},{10,11... | collective-permute-start | bytes 2949128 | tf_op jit(solution)/shard_map/ppermute | solution.py:375
  235.4 29.6 %collective-permute-start.11 = (bf16[192,1280]{1,0:T(8,128)(2,1)S(1)}, bf16[192,1280]{1,0:T(8,128)(2,1)S(1)}, u32[]{:S(2)}, u32[]{:S(2)}) collective-permute-start(bf16[192,1280]{1,0:T(8,128)(2,1)S(1)} %slice.109), channel_id=1, source_target_pairs={{0,1},{1,0},{2,3},{3,2},{4,5},{5,4},{6,7},{7,6},{8,9},{9,8},{10,11... | collective-permute-start | bytes 1474568 | tf_op jit(solution)/shard_map/ppermute | solution.py:377
  237.0 73.4 %collective-permute-start.23 = (bf16[4,640,384]{2,1,0:T(8,128)(2,1)}, bf16[4,640,384]{2,1,0:T(8,128)(2,1)}, u32[]{:S(2)}, u32[]{:S(2)}) collective-permute-start(bf16[4,640,384]{2,1,0:T(8,128)(2,1)} %all-to-all-done.3.own_ref), channel_id=1, source_target_pairs={{0,2},{2,0},{1,3},{3,1},{4,6},{6,4},{5,7},{7,5},{8,10},{10,8},{9,1... | collective-permute-start | bytes 5898248 | tf_op jit(solution)/shard_map/ppermute | solution.py:349
  268.4 80.3 %collective-permute-start.25 = (bf16[4,640,384]{2,1,0:T(8,128)(2,1)}, bf16[4,640,384]{2,1,0:T(8,128)(2,1)}, u32[]{:S(2)}, u32[]{:S(2)}) collective-permute-start(bf16[4,640,384]{2,1,0:T(8,128)(2,1)} %all-to-all-done.5.own_ref), channel_id=1, source_target_pairs={{0,2},{2,0},{1,3},{3,1},{4,6},{6,4},{5,7},{7,5},{8,10},{10,8},{9,1... | collective-permute-start | bytes 5898248 | tf_op jit(solution)/shard_map/ppermute | solution.py:349
  279.2 28.8 %all-to-all-start = ((s32[4,1,162]{2,1,0:T(1,128)}), s32[4,1,162]{2,1,0:T(1,128)S(1)}, u32[]{:S(2)}, u32[]{:S(2)}) async-start(s32[4,1,162]{2,1,0:T(1,128)} %reshape.67), calls=%async_computation | async-start | bytes 8192 | tf_op jit(solution)/shard_map/all_to_all | solution.py:344
  328.0 38.4 %collective-permute-start.24 = (bf16[2,24,64,128]{3,2,1,0:T(8,128)(2,1)}, bf16[2,24,64,128]{3,2,1,0:T(8,128)(2,1)S(1)}, u32[]{:S(2)}, u32[]{:S(2)}) collective-permute-start(bf16[2,24,64,128]{3,2,1,0:T(8,128)(2,1)} %bitcast.64), channel_id=1, source_target_pairs={{0,2},{2,0},{1,3},{3,1},{4,6},{6,4},{5,7},{7,5},{8,10},{10,8},{9,1... | collective-permute-start | bytes 2359304 | tf_op jit(solution)/shard_map/ppermute | solution.py:409
  342.1 37.3 %all-to-all-start.2 = ((bf16[4,384,128]{2,1,0:T(8,128)(2,1)}), bf16[4,384,128]{2,1,0:T(8,128)(2,1)S(1)}, u32[]{:S(2)}, u32[]{:S(2)}) async-start(bf16[4,384,128]{2,1,0:T(8,128)(2,1)} %bitcast.60), calls=%async_computation.2 | async-start | bytes 786432 | tf_op jit(solution)/shard_map/all_to_all | solution.py:344
  432.3 32.7 %collective-permute-start.28 = (bf16[384,1280]{1,0:T(8,128)(2,1)S(1)}, bf16[384,1280]{1,0:T(8,128)(2,1)S(1)}, u32[]{:S(2)}, u32[]{:S(2)}) collective-permute-start(bf16[384,1280]{1,0:T(8,128)(2,1)S(1)} %get-tuple-element.21), channel_id=1, source_target_pairs={{0,1},{1,0},{2,3},{3,2},{4,5},{5,4},{6,7},{7,6},{8,9},{9,8},{10,11... | collective-permute-start | bytes 2949128 | tf_op jit(solution)/shard_map/ppermute | solution.py:428
  432.7 32.7 %collective-permute-start.27 = (bf16[384,1280]{1,0:T(8,128)(2,1)S(1)}, bf16[384,1280]{1,0:T(8,128)(2,1)S(1)}, u32[]{:S(2)}, u32[]{:S(2)}) collective-permute-start(bf16[384,1280]{1,0:T(8,128)(2,1)S(1)} %get-tuple-element.20), channel_id=1, source_target_pairs={{0,16},{16,0},{1,17},{17,1},{2,18},{18,2},{3,19},{19,3},{4,20},{20... | collective-permute-start | bytes 2949128 | tf_op jit(solution)/shard_map/ppermute | solution.py:427
  (38 other events, 1159.5 us)

commit v2 on v1

--- a/solution.py
+++ b/solution.py
@@ -145,6 +145,32 @@
     return pl.BlockSpec(memory_space=pltpu.SMEM)
 
 
+def cut_columns(weight, chips, first, heads, chip_heads):
+    rows = weight.shape[0]
+    wide = 3 * HEAD_DIM
+
+    def body(weight_ref, out_ref, sems):
+        copies = []
+        for chip in range(chips):
+            at = (chip * chip_heads + first) * wide
+            copy = pltpu.make_async_copy(
+                weight_ref.at[:, pl.ds(at, heads * wide)], out_ref.at[chip], sems.at[chip]
+            )
+            copy.start()
+            copies.append(copy)
+        for copy in copies:
+            copy.wait()
+
+    return pl.pallas_call(
+        body,
+        in_specs=[in_hbm()],
+        out_specs=in_hbm(),
+        out_shape=jax.ShapeDtypeStruct((chips, rows, heads * wide), weight.dtype),
+        scratch_shapes=[pltpu.SemaphoreType.DMA((chips,))],
+        name="cut_columns",
+    )(weight)
+
+
 def project_heads(places, gains, rounds, weight_own, weight_other):
     slabs, depth, columns = weight_own.shape
     tokens, features = rounds[0][0].shape
@@ -152,7 +178,10 @@
     heads = columns // (3 * HEAD_DIM)
     pieces = [piece for one in rounds for piece in one]
     per_round = len(rounds[0])
+    turns = len(rounds)
     dtype = weight_own.dtype
+    width = CORES * slabs * depth
+    pair = 2 if turns % 2 == 0 else 1
 
     def body(places_ref, gains_ref, own_ref, other_ref, *refs):
         piece_refs = refs[: len(pieces)]
@@ -164,89 +193,105 @@
             for side, ref in enumerate((own_ref, other_ref)):
                 place = core if side == 0 else 1 - core
                 copy = pltpu.make_async_copy(
-                    ref.at[slab], table.at[slab, place], weight_sems.at[slab, side]
+                    ref.at[places_ref[slab]], table.at[slab, place], weight_sems.at[slab, side]
                 )
                 copy.start()
                 weight_copies.append(copy)
         row_copies = []
-        for turn in range(len(rounds)):
+        for turn in range(turns):
             for which in range(per_round):
                 ref = piece_refs[turn * per_round + which]
-                if which < 3:
-                    target = rows.at[turn, which]
-                else:
-                    target = rows.at[turn, 3, pl.ds((which - 3) * half, half)]
-                copy = pltpu.make_async_copy(ref, target, row_sems.at[turn, which])
+                column = min(which, 3) * features
+                first = turn * tokens + max(which - 3, 0) * half
+                count = tokens if which < 3 else half
+                copy = pltpu.make_async_copy(
+                    ref,
+                    rows.at[pl.ds(first, count), pl.ds(column, features)],
+                    row_sems.at[turn, which],
+                )
                 copy.start()
                 row_copies.append(copy)
         for copy in weight_copies:
             copy.wait()
-        for turn in range(len(rounds)):
-            for which in range(per_round):
-                row_copies[turn * per_round + which].wait()
-            total = None
-            for which in range(4):
-                weight = table[places_ref[which]].reshape(CORES * depth, columns)
-                part = jnp.dot(rows[turn, which], weight, preferred_element_type=jnp.float32)
-                total = part if total is None else total + part
-            for head in range(heads):
-                at = 3 * head * HEAD_DIM
-                for part in range(2):
-                    block = total[:, at + part * HEAD_DIM : at + (part + 1) * HEAD_DIM]
-                    normal = rms_rows(block) * gains_ref[part, head]
-                    if part == 0:
-                        query_ref[head, turn] = normal.astype(dtype)
-                    else:
-                        kv_ref[head, 0, turn] = normal.astype(dtype)
-                block = total[:, at + 2 * HEAD_DIM : at + 3 * HEAD_DIM]
-                kv_ref[head, 1, turn] = block.astype(dtype)
+        for begin in range(0, turns, pair):
+            for copy in row_copies[begin * per_round : (begin + pair) * per_round]:
+                copy.wait()
+            total = jnp.dot(
+                rows[begin * tokens : (begin + pair) * tokens],
+                table[...].reshape(width, columns),
+                preferred_element_type=jnp.float32,
+            )
+            for turn in range(pair):
+                for head in range(heads):
+                    at = 3 * head * HEAD_DIM
+                    here = total[turn * tokens : (turn + 1) * tokens]
+                    for part in range(2):
+                        block = here[:, at + part * HEAD_DIM : at + (part + 1) * HEAD_DIM]
+                        normal = (rms_rows(block) * gains_ref[part, head]).astype(dtype)
+                        if part == 0:
+                            query_ref[head, begin + turn] = normal
+                        else:
+                            kv_ref[head, 0, begin + turn] = normal
+                    block = here[:, at + 2 * HEAD_DIM : at + 3 * HEAD_DIM]
+                    kv_ref[head, 1, begin + turn] = block.astype(dtype)
 
     return pl.pallas_call(
         body,
         in_specs=[in_smem(), in_smem(), in_hbm(), in_hbm()] + [in_hbm()] * len(pieces),
         out_specs=(whole_in_vmem(), whole_in_vmem()),
         out_shape=(
-            jax.ShapeDtypeStruct((heads, len(rounds), tokens, HEAD_DIM), dtype),
-            jax.ShapeDtypeStruct((heads, 2, len(rounds), tokens, HEAD_DIM), dtype),
+            jax.ShapeDtypeStruct((heads, turns, tokens, HEAD_DIM), dtype),
+            jax.ShapeDtypeStruct((heads, 2, turns, tokens, HEAD_DIM), dtype),
         ),
         scratch_shapes=[
             pltpu.VMEM((slabs, CORES, depth, columns), dtype),
-            pltpu.VMEM((len(rounds), 4, tokens, features), dtype),
+            pltpu.VMEM((turns * tokens, 4 * features), dtype),
             pltpu.SemaphoreType.DMA((slabs, 2)),
-            pltpu.SemaphoreType.DMA((len(rounds), per_round)),
+            pltpu.SemaphoreType.DMA((turns, per_round)),
         ],
         compiler_params=pltpu.CompilerParams(vmem_limit_bytes=VMEM_BYTES),
         name="project_heads",
     )(places, gains, weight_own, weight_other, *pieces)
 
 
-def attend(key_slots, counts, query_slots, queries, kv_own, kv_other):
-    blocks = queries.shape[0]
-    most = key_slots.shape[1]
+def attend(key_slots, counts, query_slots, group_most, queries, kv_own, kv_other):
+    heads, blocks, most = key_slots.shape
+    groups = group_most.shape[1]
+    together = blocks // groups
+    parts = len(queries)
+    sizes = [one.shape[1] for one in queries]
+    starts = [sum(sizes[:at]) for at in range(parts)]
     scale = 1.0 / math.sqrt(HEAD_DIM)
-    together = 4 if blocks % 4 == 0 else 1
-
-    def body(slots_ref, counts_ref, from_ref, query_ref, own_ref, other_ref, out_ref, table, sems):
+    dtype = queries[0].dtype
+
+    def body(slots_ref, counts_ref, from_ref, most_ref, *refs):
+        query_refs = refs[:parts]
+        own_refs = refs[parts : 2 * parts]
+        other_refs = refs[2 * parts : 3 * parts]
+        out_ref, query_table, table, query_sems, sems = refs[3 * parts :]
         copies = []
-        for side, ref in enumerate((own_ref, other_ref)):
-            for part in range(2):
-                copy = pltpu.make_async_copy(
-                    ref.at[part], table.at[part, pl.ds(side * blocks, blocks)], sems.at[side, part]
-                )
-                copy.start()
-                copies.append(copy)
+        for at in range(parts):
+            span = pl.ds(starts[at], sizes[at])
+            copies.append(
+                pltpu.make_async_copy(query_refs[at], query_table.at[:, span], query_sems.at[at])
+            )
+            for side, ref in enumerate((own_refs[at], other_refs[at])):
+                span = pl.ds(side * blocks + starts[at], sizes[at])
+                copies.append(pltpu.make_async_copy(ref, table.at[:, :, span], sems.at[at, side]))
+        for copy in copies:
+            copy.start()
         for copy in copies:
             copy.wait()
 
-        def step(at, carry):
+        def run(head, group, listed):
             for inner in range(together):
-                block = at * together + inner
-                slots = [slots_ref[block, entry] for entry in range(most)]
-                keys = jnp.concatenate([table[0, slot] for slot in slots], axis=0)
-                values = jnp.concatenate([table[1, slot] for slot in slots], axis=0)
+                block = group * together + inner
+                slots = [slots_ref[head, block, entry] for entry in range(listed)]
+                keys = jnp.concatenate([table[head, 0, slot] for slot in slots], axis=0)
+                values = jnp.concatenate([table[head, 1, slot] for slot in slots], axis=0)
                 scores = (
                     lax.dot_general(
-                        query_ref[from_ref[block]],
+                        query_table[head, from_ref[block]],
                         keys,
                         (((1,), (1,)), ((), ())),
                         preferred_element_type=jnp.float32,
@@ -254,67 +299,82 @@
                     * scale
                 )
                 column = lax.broadcasted_iota(jnp.int32, scores.shape, 1)
-                scores = jnp.where(column < counts_ref[block] * BLOCK, scores, -jnp.inf)
+                scores = jnp.where(column < counts_ref[head, block] * BLOCK, scores, -jnp.inf)
                 highest = jnp.max(scores, axis=1, keepdims=True)
                 raised = jnp.exp(scores - highest)
                 summed = jnp.sum(raised, axis=1, keepdims=True)
-                weights = (raised / summed).astype(values.dtype)
+                weights = (raised * (1.0 / summed)).astype(dtype)
                 mixed = jnp.dot(weights, values, preferred_element_type=jnp.float32)
-                out_ref[block] = mixed.astype(out_ref.dtype)
+                out_ref[head, block] = mixed.astype(dtype)
+
+        def step(at, carry):
+            head, group = at // groups, at % groups
+            few = most_ref[head, group] <= most // 2
+
+            @pl.when(few)
+            def _():
+                run(head, group, most // 2)
+
+            @pl.when(jnp.logical_not(few))
+            def _():
+                run(head, group, most)
+
             return carry
 
-        lax.fori_loop(0, blocks // together, step, 0)
+        lax.fori_loop(0, heads * groups, step, 0)
 
     return pl.pallas_call(
         body,
-        in_specs=[in_smem(), in_smem(), in_smem(), whole_in_vmem(), in_hbm(), in_hbm()],
+        in_specs=[in_smem()] * 4 + [in_hbm()] * (3 * parts),
         out_specs=whole_in_vmem(),
-        out_shape=jax.ShapeDtypeStruct(queries.shape, queries.dtype),
+        out_shape=jax.ShapeDtypeStruct((heads, blocks, BLOCK, HEAD_DIM), dtype),
         scratch_shapes=[
-            pltpu.VMEM((2, CORES * blocks, BLOCK, HEAD_DIM), queries.dtype),
-            pltpu.SemaphoreType.DMA((2, 2)),
+            pltpu.VMEM((heads, blocks, BLOCK, HEAD_DIM), dtype),
+            pltpu.VMEM((heads, 2, CORES * blocks, BLOCK, HEAD_DIM), dtype),
+            pltpu.SemaphoreType.DMA((parts,)),
+            pltpu.SemaphoreType.DMA((parts, 2)),
         ],
         compiler_params=pltpu.CompilerParams(vmem_limit_bytes=VMEM_BYTES),
         name="attend",
-    )(key_slots, counts, query_slots, queries, kv_own, kv_other)
-
-
-def out_blocks(which, sign, attended, out_weight, dtype, steps):
-    groups, tokens, _ = attended[0].shape
+    )(key_slots, counts, query_slots, group_most, *queries, *kv_own, *kv_other)
+
+
+def out_blocks(which, sign, attended, out_weight, dtype, blocks):
+    groups, _, tokens, _ = attended[0].shape
+    sizes = [one.shape[1] for one in attended]
     count = len(attended)
     depth, features = out_weight.shape
-    wanted = which.shape[0]
-    width = features // steps
-    split = 1 if (width // 2) % HEAD_DIM else 2
-    tile = width // split
+    width = features // blocks
 
     def body(which_ref, sign_ref, *refs):
-        parts, weight_ref, out_ref, joined = refs[:count], refs[count], refs[count + 1], refs[count + 2]
-
-        @pl.when(jnp.logical_and(pl.program_id(0) == 0, pl.program_id(1) == 0))
-        def _():
-            for group in range(groups):
-                for chunk in range(count):
-                    at = (group * count + chunk) * HEAD_DIM
-                    joined[:, at : at + HEAD_DIM] = parts[chunk][group]
-
-        total = jnp.dot(joined[...], weight_ref[...], preferred_element_type=jnp.float32)
-        out_ref[0] = (total * sign_ref[0].astype(jnp.float32)).astype(dtype)
+        parts, weight_ref, out_ref = refs[:count], refs[count], refs[count + 1]
+        columns = []
+        for group in range(groups):
+            for chunk in range(count):
+                for head in range(sizes[chunk]):
+                    columns.append(parts[chunk][group, head])
+        joined = jnp.concatenate(columns, axis=1)
+        total = jnp.dot(joined, weight_ref[...], preferred_element_type=jnp.float32)
+        out_ref[...] = (total * sign_ref[0].astype(jnp.float32)).astype(dtype)
 
     return pl.pallas_call(
         body,
         grid_spec=pltpu.PrefetchScalarGridSpec(
             num_scalar_prefetch=2,
-            grid=(wanted, split),
-            in_specs=[pl.BlockSpec((groups, tokens, HEAD_DIM), lambda i, k, w, s: (0, 0, 0))] * count
-            + [pl.BlockSpec((depth, tile), lambda i, k, w, s: (0, w[i] * split + k))],
-            out_specs=pl.BlockSpec((1, tokens, tile), lambda i, k, w, s: (i, 0, k)),
-            scratch_shapes=[pltpu.VMEM((tokens, depth), attended[0].dtype)],
+            grid=(1,),
+            in_specs=[pl.BlockSpec(one.shape, lambda i, w, s: (0, 0, 0, 0)) for one in attended]
+            + [pl.BlockSpec((depth, width), lambda i, w, s: (0, w[0]))],
+            out_specs=pl.BlockSpec((tokens, width), lambda i, w, s: (0, 0)),
         ),
-        out_shape=jax.ShapeDtypeStruct((wanted, tokens, width), dtype),
+        out_shape=jax.ShapeDtypeStruct((tokens, width), dtype),
         compiler_params=pltpu.CompilerParams(vmem_limit_bytes=VMEM_BYTES),
         name="out_blocks",
     )(which, sign, *attended, out_weight)
+
+
+def chunk_sizes(heads):
+    last = max(1, heads // 3)
+    return [heads - last, last] if heads > last else [heads]
 
 
 def per_device_by_heads(
@@ -343,20 +403,20 @@
     def exchange(array):
         return lax.all_to_all(array, "chip", split_axis=0, concat_axis=0, tiled=True)
 
-    weight_rows = qkv_weight.shape[1]
-    by_chip = qkv_weight[0].reshape(weight_rows, chips, heads, 3 * HEAD_DIM)
-    weights_own = [exchange(by_chip[:, :, at].transpose(1, 0, 2)) for at in range(heads)]
-    weights_other = [lax.ppermute(one, "core", swap) for one in weights_own]
+    chunks = chunk_sizes(heads)
+    weight_here = qkv_weight[0]
+    cuts = [
+        cut_columns(weight_here, chips, sum(chunks[:at]), chunks[at], heads)
+        for at in range(len(chunks))
+    ]
+    weights_own = [exchange(cuts[0])]
 
     mine = role * lax.axis_size("head") + head
-    generated = jnp.dot(hidden_rows, gen_weight, preferred_element_type=jnp.float32).astype(
-        jnp.bfloat16
-    )
+    generated = jnp.dot(hidden_rows, gen_weight, preferred_element_type=jnp.float32)
+    generated = lax.reduce_precision(generated, 8, 7)
     angle_blocks = (timesteps.astype(jnp.float32) * (math.pi / 2000.0))[:, None, None]
     noise_here = lax.dynamic_slice_in_dim(noise, mine * features, features, axis=1)
-    noisy = jnp.cos(angle_blocks) * generated.astype(jnp.float32).reshape(
-        local_blocks, BLOCK, features
-    )
+    noisy = jnp.cos(angle_blocks) * generated.reshape(local_blocks, BLOCK, features)
     noisy = noisy + jnp.sin(angle_blocks) * noise_here.astype(jnp.float32).reshape(
         local_blocks, BLOCK, features
     )
@@ -365,6 +425,10 @@
     squares = squares + lax.ppermute(squares, "head", swap)
     normed = (noisy * lax.rsqrt(squares / width + 1e-06)[:, :, None]).astype(jnp.bfloat16)
     normed = normed.reshape(tokens, features)
+    for cut in cuts[1:]:
+        held, _ = lax.optimization_barrier((cut, normed))
+        weights_own.append(exchange(held))
+    weights_other = [lax.ppermute(one, "core", swap) for one in weights_own]
 
     shards = [normed]
     for _ in range(chips - 1):
@@ -378,13 +442,14 @@
         rounds.append((shard, over_role, over_head, first, second))
 
     lists = jnp.concatenate([block_keys, block_count[:, :, None]], axis=2)
-    lists = exchange(lists.reshape(chips, heads, local_blocks, most + 1))
-    lists = lists.transpose(1, 0, 2, 3).reshape(heads, all_blocks, most + 1)
+    lists = lax.all_gather(lists, "chip", axis=1, tiled=True)
+    lists = lax.dynamic_slice_in_dim(lists, chip * heads, heads, axis=0)
     owner = lists[:, :, :most] // local_blocks
     turn = (chip - owner // CORES) % chips
     far = (owner % CORES != core).astype(jnp.int32)
     key_slots = far * all_blocks + turn * local_blocks + lists[:, :, :most] % local_blocks
     counts = lists[:, :, most]
+    group_most = jnp.max(counts.reshape(heads, chips, local_blocks), axis=2)
     spot = jnp.arange(all_blocks, dtype=jnp.int32)
     query_slots = (chip - spot // local_blocks) % chips * local_blocks + spot % local_blocks
 
@@ -401,32 +466,44 @@
     gains = lax.dynamic_slice_in_dim(qk_gain[0], chip * heads, heads, axis=1)
 
     attended = []
-    for at in range(heads):
-        queries, kv = project_heads(
-            places, gains[:, at : at + 1], rounds, weights_own[at], weights_other[at]
-        )
-        kv = kv.reshape(2, all_blocks, BLOCK, HEAD_DIM)
-        kv_other = lax.ppermute(kv, "core", swap)
+    held_places = places
+    for at, size in enumerate(chunks):
+        span = slice(sum(chunks[:at]), sum(chunks[: at + 1]))
+        last = at == len(chunks) - 1
+        parts = [rounds] if last else [rounds[: chips // 2], rounds[chips // 2 :]]
+        queries, kv_own, kv_other = [], [], []
+        for part in parts:
+            query, kv = project_heads(
+                held_places, gains[:, span], part, weights_own[at], weights_other[at]
+            )
+            here = len(part) * local_blocks
+            queries.append(query.reshape(size, here, BLOCK, HEAD_DIM))
+            kv_own.append(kv.reshape(size, 2, here, BLOCK, HEAD_DIM))
+            kv_other.append(lax.ppermute(kv_own[-1], "core", swap))
+            held_places, _ = lax.optimization_barrier((places, kv))
         mixed = attend(
-            key_slots[at],
-            counts[at],
+            key_slots[span],
+            counts[span],
             query_slots,
-            queries.reshape(all_blocks, BLOCK, HEAD_DIM),
-            kv,
+            group_most[span],
+            queries,
+            kv_own,
             kv_other,
         )
-        attended.append(exchange(mixed.reshape(chips, tokens, HEAD_DIM)))
+        mixed = mixed.reshape(size, chips, tokens, HEAD_DIM).transpose(1, 0, 2, 3)
+        attended.append(exchange(mixed))
 
     sign = (2 * role - 1).astype(jnp.int32)[None]
     blocks = sides * lax.axis_size("role")
-    diagonal = out_blocks(peers[3:4], sign, attended, out_weight[0], jnp.bfloat16, blocks)
-    sides_two = out_blocks(peers[1:3], sign, attended, out_weight[0], jnp.bfloat16, blocks)
-    own = out_blocks(peers[0:1], sign, attended, out_weight[0], jnp.float32, blocks)
+
+    def block_of(at, dtype):
+        return out_blocks(peers[at : at + 1], sign, attended, out_weight[0], dtype, blocks)
+
     far_swap = [(0, 3), (1, 2), (2, 1), (3, 0)]
-    from_diagonal = lax.ppermute(diagonal[0], ("role", "head"), far_swap)
-    from_role = lax.ppermute(sides_two[0], "role", swap)
-    from_head = lax.ppermute(sides_two[1], "head", swap)
-    return own[0] + (
+    from_diagonal = lax.ppermute(block_of(3, jnp.bfloat16), ("role", "head"), far_swap)
+    from_role = lax.ppermute(block_of(1, jnp.bfloat16), "role", swap)
+    from_head = lax.ppermute(block_of(2, jnp.bfloat16), "head", swap)
+    return block_of(0, jnp.float32) + (
         from_role.astype(jnp.float32)
         + from_head.astype(jnp.float32)
         + from_diagonal.astype(jnp.float32)

time: 470 us -> 580 us (1.23)
  Pallas kernels: 108 us -> 280 us
  waiting for transfers between devices: 221 us -> 184 us
  local copies, waits for them, and re-layouts: 42.3 us -> 22.2 us
  starting transfers between devices: 79.9 us -> 61.4 us
  blocking collectives: 0 us -> 13.6 us
    pallas_call x3 -> x4, Pallas kernels: 36.1 us -> 214 us  [the longest x2 181 us: cut_columns(): pl.pallas_call(body, in_specs=[in_hbm()], out_specs=in_hbm(), out_shape=j...]
    ppermute x4, waiting for transfers between devices: 0.01 us -> 38.3 us  [per_device_by_heads(): over_role = lax.ppermute(shard, 'role', swap)]
    ppermute x4, waiting for transfers between devices: 37.2 us -> 0.89 us  [per_device_by_heads(): second = lax.ppermute(over_role[tokens // 2:], 'head', swap)]
    all_to_all x7 -> x4, waiting for transfers between devices: 70.8 us -> 45.6 us  [exchange(): lax.all_to_all(array, 'chip', split_axis=0, concat_axis=0, tiled=True)]
    unnamed x58 -> x49, local copies, waits for them, and re-layouts: 25.5 us -> 2.96 us
    ppermute x4, waiting for transfers between devices: 22.2 us -> 0.01 us  [per_device_by_heads(): first = lax.ppermute(over_head[:tokens // 2], 'role', swap)]
    all_to_all x7 -> x4, starting transfers between devices: 40.6 us -> 18.8 us  [exchange(): lax.all_to_all(array, 'chip', split_axis=0, concat_axis=0, tiled=True)]
    all_gather x0 -> x1, blocking collectives: none -> 13.6 us  [per_device_by_heads(): lists = lax.all_gather(lists, 'chip', axis=1, tiled=True)]
  transfers between devices with their start and end apart: 37 -> 33, of which waited for: 17 -> 14; matrix products, arithmetic and copies ran while one was open for 7% -> 6% of each run, Pallas kernels for 22% -> 24%
where the time goes in v2:
time: 580 us; the launch traced here: 578 us
  Pallas kernels  280 us (48%)
  waiting for transfers between devices  184 us (32%)
  starting transfers between devices  61.4 us (11%)
  local copies, waits for them, and re-layouts  22.2 us (4%)
  blocking collectives  13.6 us (2%)
  matrix products  11.5 us (2%)
    pallas_call x2, Pallas kernels, cut_columns(): pl.pallas_call(body, in_specs=[in_hbm()], out_specs=in_hbm(), out_shape=j...  181 us
    all_to_all x4, waiting for transfers between devices, exchange(): lax.all_to_all(array, 'chip', split_axis=0, concat_axis=0, tiled=True)  45.6 us
    pallas_call x3, Pallas kernels, project_heads(): pl.pallas_call(body, in_specs=[in_smem(), in_smem(), in_hbm(), in_hbm()]...  45 us
    ppermute x3, waiting for transfers between devices, per_device_by_heads(): shards.append(lax.ppermute(shards[-1], 'chip', ring))  44.8 us
    ppermute x4, waiting for transfers between devices, per_device_by_heads(): over_role = lax.ppermute(shard, 'role', swap)  38.3 us
    pallas_call x2, Pallas kernels, attend(): pl.pallas_call(body, in_specs=[in_smem()] * 4 + [in_hbm()] * (3 * parts),...  33.3 us
    ppermute x1, waiting for transfers between devices, per_device_by_heads(): from_head = lax.ppermute(block_of(2, jnp.bfloat16), 'head', swap)  25.6 us
    pallas_call x4, Pallas kernels, out_blocks(): pl.pallas_call(body, grid_spec=pltpu.PrefetchScalarGridSpec(num_scalar_pr...  20.8 us
  transfers between devices with their start and end apart: 33, of which 14 were waited for; matrix products, arithmetic and copies ran while one was open for 6% of the time, Pallas kernels for 24%

profile of v2, /device:TPU:0, one launch (start us, length us, event | category | flops | bytes accessed | tf_op | source)
XLA Modules:
  0.0 578.4 jit_solution(16966699514036919730)
XLA Ops:
  0.0 120.2 %cut_columns.2 = bf16[4,640,768]{2,1,0:T(8,128)(2,1)} custom-call(bf16[640,4608]{1,0:T(8,128)(2,1)} %bitcast.34), custom_call_target="tpu_custom_call" | custom-call | tf_op jit(solution)/shard_map/cut_columns/pallas_call | solution.py:164
  120.3 6.3 %all-to-all-start = ((bf16[4,640,768]{2,1,0:T(8,128)(2,1)}), bf16[4,640,768]{2,1,0:T(8,128)(2,1)}, u32[]{:S(2)}, u32[]{:S(2)}) async-start(bf16[4,640,768]{2,1,0:T(8,128)(2,1)} %cut_columns.2), calls=%async_computation | async-start | bytes 7864320 | tf_op jit(solution)/shard_map/all_to_all | solution.py:404
  126.9 11.5 %multiply_reduce_fusion = (f32[384]{0:T(512)S(1)}, f32[384,1280]{1,0:T(8,128)S(1)}) fusion(bf16[384,5120]{1,0:T(8,128)(2,1)} %param.11, s32[]{:T(128)S(6)} %select_n.54, f32[384]{0:T(512)S(1)} %mul.89, bf16[384,5120]{1,0:T(8,128)(2,1)} %param.9, bf16[5120,1280]{1,0:T(8,128)(2,1)} %param.10, f32[384]{0:T(512)S(1)} %mul.85), kind=kOutput, calls=%fused_computation.5 | convolution fusion | flops 5036604928 | bytes 19993092 | tf_op jit(solution)/shard_map/dot_general | solution.py:415
  148.1 60.7 %cut_columns.3 = bf16[4,640,384]{2,1,0:T(8,128)(2,1)} custom-call(bf16[640,4608]{1,0:T(8,128)(2,1)} %bitcast.35), custom_call_target="tpu_custom_call" | custom-call | tf_op jit(solution)/shard_map/cut_columns/pallas_call | solution.py:164
  208.8 26.6 %all-to-all-done.own_ref = bf16[4,640,768]{2,1,0:T(8,128)(2,1)} async-done(((bf16[4,640,768]{2,1,0:T(8,128)(2,1)}), bf16[4,640,768]{2,1,0:T(8,128)(2,1)}, u32[]{:S(2)}, u32[]{:S(2)}) %all-to-all-start) | async-done | bytes 3932192 | tf_op jit(solution)/shard_map/all_to_all | solution.py:404
  244.1 19.2 %collective-permute-done.4.refs_2_ = bf16[384,1280]{1,0:T(8,128)(2,1)S(1)} collective-permute-done((bf16[384,1280]{1,0:T(8,128)(2,1)S(1)}, bf16[384,1280]{1,0:T(8,128)(2,1)S(1)}, u32[]{:S(2)}, u32[]{:S(2)}) %collective-permute-start.4) | collective-permute-done | bytes 983072 | tf_op jit(solution)/shard_map/ppermute | solution.py:439
  266.5 29.0 %collective-permute-done.12.refs_0_.refs_10_ = bf16[384,1280]{1,0:T(8,128)(2,1)} collective-permute-done((bf16[384,1280]{1,0:T(8,128)(2,1)}, bf16[384,1280]{1,0:T(8,128)(2,1)}, u32[]{:S(2)}, u32[]{:S(2)}) %collective-permute-start.12) | collective-permute-done | bytes 983072 | tf_op jit(solution)/shard_map/ppermute | solution.py:435
  295.5 8.2 %collective-permute-start.17 = (bf16[384,1280]{1,0:T(8,128)(2,1)}, bf16[384,1280]{1,0:T(8,128)(2,1)}, u32[]{:S(2)}, u32[]{:S(2)}) collective-permute-start(bf16[384,1280]{1,0:T(8,128)(2,1)} %collective-permute-done.12.refs_0_.refs_10_), channel_id=1, source_target_pairs={{0,4},{4,8},{8,12},{12,0},{1,5},{5,9},{9,13},{13,1},{2,6},{6,10},{... | collective-permute-start | bytes 2949128 | tf_op jit(solution)/shard_map/ppermute | solution.py:435
  307.4 15.8 %collective-permute-done.17.refs_5_.refs_15_ = bf16[384,1280]{1,0:T(8,128)(2,1)} collective-permute-done((bf16[384,1280]{1,0:T(8,128)(2,1)}, bf16[384,1280]{1,0:T(8,128)(2,1)}, u32[]{:S(2)}, u32[]{:S(2)}) %collective-permute-start.17) | collective-permute-done | bytes 983072 | tf_op jit(solution)/shard_map/ppermute | solution.py:435
  332.9 16.9 %collective-permute-done.13.refs_1_.refs_11_ = bf16[384,1280]{1,0:T(8,128)(2,1)} collective-permute-done((bf16[384,1280]{1,0:T(8,128)(2,1)}, bf16[384,1280]{1,0:T(8,128)(2,1)}, u32[]{:S(2)}, u32[]{:S(2)}) %collective-permute-start.13) | collective-permute-done | bytes 983072 | tf_op jit(solution)/shard_map/ppermute | solution.py:438
  352.9 17.9 %collective-permute-done.18.refs_6_.refs_16_ = bf16[384,1280]{1,0:T(8,128)(2,1)} collective-permute-done((bf16[384,1280]{1,0:T(8,128)(2,1)}, bf16[384,1280]{1,0:T(8,128)(2,1)}, u32[]{:S(2)}, u32[]{:S(2)}) %collective-permute-start.18) | collective-permute-done | bytes 983072 | tf_op jit(solution)/shard_map/ppermute | solution.py:438
  385.9 13.9 %project_heads.3 = (bf16[2,2,384,128]{3,2,1,0:T(8,128)(2,1)}, bf16[2,2,2,384,128]{4,3,2,1,0:T(8,128)(2,1)}) custom-call(s32[5]{0:T(128)} %concatenate.7.places_ref, f32[2,2]{1,0:T(2,128)} %bitcast.48, bf16[4,640,768]{2,1,0:T(8,128)(2,1)} %all-to-all-done.own_ref, bf16[4,640,768]{2,1,0:T(8,128)(2,1)} %collective-permute-done.other_ref, ...), custom_call_target="tpu_custom_call" | custom-call | tf_op jit(solution)/shard_map/project_heads/pallas_call | solution.py:238
  400.8 13.7 %project_heads.4 = (bf16[2,2,384,128]{3,2,1,0:T(8,128)(2,1)}, bf16[2,2,2,384,128]{4,3,2,1,0:T(8,128)(2,1)}) custom-call(s32[5]{0:T(128)} %concatenate.7.places_ref, f32[2,2]{1,0:T(2,128)} %bitcast.49, bf16[4,640,768]{2,1,0:T(8,128)(2,1)} %all-to-all-done.own_ref, bf16[4,640,768]{2,1,0:T(8,128)(2,1)} %collective-permute-done.other_ref, ...), custom_call_target="tpu_custom_call" | custom-call | tf_op jit(solution)/shard_map/project_heads/pallas_call | solution.py:238
  414.5 17.4 %project_heads.5 = (bf16[1,4,384,128]{3,2,1,0:T(8,128)(2,1)}, bf16[1,2,4,384,128]{4,3,2,1,0:T(8,128)(2,1)}) custom-call(s32[5]{0:T(128)} %concatenate.7.places_ref, f32[2,1]{1,0:T(2,128)} %slice.83.gains_ref, bf16[4,640,384]{2,1,0:T(8,128)(2,1)} %copy-done.5, bf16[4,640,384]{2,1,0:T(8,128)(2,1)} %collective-permute-done.24.other_ref, ...), custom_call_target="tpu_custom_call" | custom-call | tf_op jit(solution)/shard_map/project_heads/pallas_call | solution.py:238
  432.4 13.6 %all_gather.3 = s32[12,24,9]{2,0,1:T(8,128)S(1)} all-gather(s32[12,6,9]{2,0,1:T(8,128)S(1)} %pad_add_fusion), channel_id=1, replica_groups=mesh['role'=2,'chip'=4,'core'=2,'head'=2] {'chip'}, dimensions={1}, use_global_device_ids=true | all-gather | bytes 12960 | tf_op jit(solution)/shard_map/all_gather | solution.py:445
  450.1 11.8 %attend.3 = bf16[1,24,64,128]{3,2,1,0:T(8,128)(2,1)} custom-call(s32[1,24,8]{2,1,0:T(8,128)} %slice.93.slots_ref, s32[1,24]{1,0:T(1,128)} %bitcast.51, s32[24]{0:T(128)} %fusion.12.from_ref, s32[1,4]{1,0:T(1,128)} %slice.82.most_ref, bf16[1,24,64,128]{3,2,1,0:T(8,128)(2,1)} %bitcast.46, bf16[1,2,24,64,128]{4,3,2,1,0:T(8,128)(2,1)} %bitcast.43, ...), custom_call_target="tpu_custom_call" | custom-call | tf_op jit(solution)/shard_map/attend/pallas_call | solution.py:326
  471.0 21.5 %attend.2 = bf16[2,24,64,128]{3,2,1,0:T(8,128)(2,1)} custom-call(s32[2,24,8]{2,1,0:T(8,128)} %slice.84.slots_ref, s32[2,24]{1,0:T(2,128)} %copy.24.counts_ref, s32[24]{0:T(128)} %fusion.12.from_ref, s32[2,4]{1,0:T(2,128)} %slice.69.most_ref, bf16[2,12,64,128]{3,2,1,0:T(8,128)(2,1)} %bitcast.44, bf16[2,12,64,128]{3,2,1,0:T(8,128)(2,1)} %bitcast.45, ...), custom_call_target="tpu_custom_call" | custom-call | tf_op jit(solution)/shard_map/attend/pallas_call | solution.py:326
  499.6 19.0 %all-to-all-done.1.refs_0_ = bf16[4,2,384,128]{3,2,1,0:T(8,128)(2,1)S(1)} async-done(((bf16[4,2,384,128]{3,2,1,0:T(8,128)(2,1)}), bf16[4,2,384,128]{3,2,1,0:T(8,128)(2,1)S(1)}, u32[]{:S(2)}, u32[]{:S(2)}) %all-to-all-start.1) | async-done | bytes 786464 | tf_op jit(solution)/shard_map/all_to_all | solution.py:404
  519.5 5.1 out_blocks.5
  526.3 5.1 out_blocks.6
  532.9 5.1 out_blocks.7
  538.4 5.5 out_blocks.4
  543.8 5.7 collective-permute-done.26
  549.6 25.6 %collective-permute-done.27 = bf16[384,1280]{1,0:T(8,128)(2,1)S(1)} collective-permute-done((bf16[384,1280]{1,0:T(8,128)(2,1)}, bf16[384,1280]{1,0:T(8,128)(2,1)S(1)}, u32[]{:S(2)}, u32[]{:S(2)}) %collective-permute-start.27) | collective-permute-done | bytes 983072 | tf_op jit(solution)/shard_map/ppermute | solution.py:505
  (142 shorter events, 82.8 us)
Async XLA Ops:
  120.3 115.1 %all-to-all-start = ((bf16[4,640,768]{2,1,0:T(8,128)(2,1)}), bf16[4,640,768]{2,1,0:T(8,128)(2,1)}, u32[]{:S(2)}, u32[]{:S(2)}) async-start(bf16[4,640,768]{2,1,0:T(8,128)(2,1)} %cut_columns.2), calls=%async_computation | async-start | bytes 7864320 | tf_op jit(solution)/shard_map/all_to_all | solution.py:404
  146.1 94.7 %collective-permute-start.7 = (bf16[384,1280]{1,0:T(8,128)(2,1)S(1)}, bf16[384,1280]{1,0:T(8,128)(2,1)}, u32[]{:S(2)}, u32[]{:S(2)}) collective-permute-start(bf16[384,1280]{1,0:T(8,128)(2,1)S(1)} %multiply_convert_fusion.refs_0_), channel_id=1, source_target_pairs={{0,4},{4,8},{8,12},{12,0},{1,5},{5,9},{9,13},{13,1},{2,6},{6,10},{... | collective-permute-start | bytes 2949128 | tf_op jit(solution)/shard_map/ppermute | solution.py:435
  235.4 94.9 %all-to-all-start.2 = ((bf16[4,640,384]{2,1,0:T(8,128)(2,1)}), bf16[4,640,384]{2,1,0:T(8,128)(2,1)S(1)}, u32[]{:S(2)}, u32[]{:S(2)}) async-start(bf16[4,640,384]{2,1,0:T(8,128)(2,1)} %cut_columns.3), calls=%async_computation.2 | async-start | bytes 3932160 | tf_op jit(solution)/shard_map/all_to_all | solution.py:404
  239.0 145.3 %collective-permute-start = (bf16[4,640,768]{2,1,0:T(8,128)(2,1)}, bf16[4,640,768]{2,1,0:T(8,128)(2,1)}, u32[]{:S(2)}, u32[]{:S(2)}) collective-permute-start(bf16[4,640,768]{2,1,0:T(8,128)(2,1)} %all-to-all-done.own_ref), channel_id=1, source_target_pairs={{0,2},{2,0},{1,3},{3,1},{4,6},{6,4},{5,7},{7,5},{8,10},{10,8},{9,1... | collective-permute-start | bytes 11796488 | tf_op jit(solution)/shard_map/ppermute | solution.py:431
  239.1 24.2 %collective-permute-start.4 = (bf16[384,1280]{1,0:T(8,128)(2,1)S(1)}, bf16[384,1280]{1,0:T(8,128)(2,1)S(1)}, u32[]{:S(2)}, u32[]{:S(2)}) collective-permute-start(bf16[384,1280]{1,0:T(8,128)(2,1)S(1)} %multiply_convert_fusion.refs_0_), channel_id=1, source_target_pairs={{0,1},{1,0},{2,3},{3,2},{4,5},{5,4},{6,7},{7,6},{8,9},{9,8},{10,11... | collective-permute-start | bytes 2949128 | tf_op jit(solution)/shard_map/ppermute | solution.py:439
  240.8 54.7 %collective-permute-start.12 = (bf16[384,1280]{1,0:T(8,128)(2,1)}, bf16[384,1280]{1,0:T(8,128)(2,1)}, u32[]{:S(2)}, u32[]{:S(2)}) collective-permute-start(bf16[384,1280]{1,0:T(8,128)(2,1)} %collective-permute-done.7.refs_5_), channel_id=1, source_target_pairs={{0,4},{4,8},{8,12},{12,0},{1,5},{5,9},{9,13},{13,1},{2,6},{6,10},{... | collective-permute-start | bytes 2949128 | tf_op jit(solution)/shard_map/ppermute | solution.py:435
  242.6 61.0 %collective-permute-start.3 = (bf16[384,1280]{1,0:T(8,128)(2,1)S(1)}, bf16[384,1280]{1,0:T(8,128)(2,1)S(1)}, u32[]{:S(2)}, u32[]{:S(2)}) collective-permute-start(bf16[384,1280]{1,0:T(8,128)(2,1)S(1)} %multiply_convert_fusion.refs_0_), channel_id=1, source_target_pairs={{0,16},{16,0},{1,17},{17,1},{2,18},{18,2},{3,19},{19,3},{4,20},{20... | collective-permute-start | bytes 2949128 | tf_op jit(solution)/shard_map/ppermute | solution.py:438
  263.3 42.0 %collective-permute-start.5 = (bf16[192,1280]{1,0:T(8,128)(2,1)S(1)}, bf16[192,1280]{1,0:T(8,128)(2,1)S(1)}, u32[]{:S(2)}, u32[]{:S(2)}) collective-permute-start(bf16[192,1280]{1,0:T(8,128)(2,1)S(1)} %slice.85), channel_id=1, source_target_pairs={{0,16},{16,0},{1,17},{17,1},{2,18},{18,2},{3,19},{19,3},{4,20},{20... | collective-permute-start | bytes 1474568 | tf_op jit(solution)/shard_map/ppermute | solution.py:440
  264.9 41.9 %collective-permute-start.9 = (bf16[384,1280]{1,0:T(8,128)(2,1)}, bf16[384,1280]{1,0:T(8,128)(2,1)S(1)}, u32[]{:S(2)}, u32[]{:S(2)}) collective-permute-start(bf16[384,1280]{1,0:T(8,128)(2,1)} %collective-permute-done.7.refs_5_), channel_id=1, source_target_pairs={{0,1},{1,0},{2,3},{3,2},{4,5},{5,4},{6,7},{7,6},{8,9},{9,8},{10,11... | collective-permute-start | bytes 2949128 | tf_op jit(solution)/shard_map/ppermute | solution.py:439
  295.5 27.7 %collective-permute-start.17 = (bf16[384,1280]{1,0:T(8,128)(2,1)}, bf16[384,1280]{1,0:T(8,128)(2,1)}, u32[]{:S(2)}, u32[]{:S(2)}) collective-permute-start(bf16[384,1280]{1,0:T(8,128)(2,1)} %collective-permute-done.12.refs_0_.refs_10_), channel_id=1, source_target_pairs={{0,4},{4,8},{8,12},{12,0},{1,5},{5,9},{9,13},{13,1},{2,6},{6,10},{... | collective-permute-start | bytes 2949128 | tf_op jit(solution)/shard_map/ppermute | solution.py:435
  303.6 24.9 %collective-permute-start.8 = (bf16[384,1280]{1,0:T(8,128)(2,1)}, bf16[384,1280]{1,0:T(8,128)(2,1)S(1)}, u32[]{:S(2)}, u32[]{:S(2)}) collective-permute-start(bf16[384,1280]{1,0:T(8,128)(2,1)} %collective-permute-done.7.refs_5_), channel_id=1, source_target_pairs={{0,16},{16,0},{1,17},{17,1},{2,18},{18,2},{3,19},{19,3},{4,20},{20... | collective-permute-start | bytes 2949128 | tf_op jit(solution)/shard_map/ppermute | solution.py:438
  305.3 25.0 %collective-permute-start.14 = (bf16[384,1280]{1,0:T(8,128)(2,1)}, bf16[384,1280]{1,0:T(8,128)(2,1)}, u32[]{:S(2)}, u32[]{:S(2)}) collective-permute-start(bf16[384,1280]{1,0:T(8,128)(2,1)} %collective-permute-done.12.refs_0_.refs_10_), channel_id=1, source_target_pairs={{0,1},{1,0},{2,3},{3,2},{4,5},{5,4},{6,7},{7,6},{8,9},{9,8},{10,11... | collective-permute-start | bytes 2949128 | tf_op jit(solution)/shard_map/ppermute | solution.py:439
  306.8 42.9 %collective-permute-start.13 = (bf16[384,1280]{1,0:T(8,128)(2,1)}, bf16[384,1280]{1,0:T(8,128)(2,1)}, u32[]{:S(2)}, u32[]{:S(2)}) collective-permute-start(bf16[384,1280]{1,0:T(8,128)(2,1)} %collective-permute-done.12.refs_0_.refs_10_), channel_id=1, source_target_pairs={{0,16},{16,0},{1,17},{17,1},{2,18},{18,2},{3,19},{19,3},{4,20},{20... | collective-permute-start | bytes 2949128 | tf_op jit(solution)/shard_map/ppermute | solution.py:438
  323.2 28.3 %collective-permute-start.19 = (bf16[384,1280]{1,0:T(8,128)(2,1)}, bf16[384,1280]{1,0:T(8,128)(2,1)}, u32[]{:S(2)}, u32[]{:S(2)}) collective-permute-start(bf16[384,1280]{1,0:T(8,128)(2,1)} %collective-permute-done.17.refs_5_.refs_15_), channel_id=1, source_target_pairs={{0,1},{1,0},{2,3},{3,2},{4,5},{5,4},{6,7},{7,6},{8,9},{9,8},{10,11... | collective-permute-start | bytes 2949128 | tf_op jit(solution)/shard_map/ppermute | solution.py:439
  328.5 42.2 %collective-permute-start.18 = (bf16[384,1280]{1,0:T(8,128)(2,1)}, bf16[384,1280]{1,0:T(8,128)(2,1)}, u32[]{:S(2)}, u32[]{:S(2)}) collective-permute-start(bf16[384,1280]{1,0:T(8,128)(2,1)} %collective-permute-done.17.refs_5_.refs_15_), channel_id=1, source_target_pairs={{0,16},{16,0},{1,17},{17,1},{2,18},{18,2},{3,19},{19,3},{4,20},{20... | collective-permute-start | bytes 2949128 | tf_op jit(solution)/shard_map/ppermute | solution.py:438
  330.3 84.2 %collective-permute-start.24 = (bf16[4,640,384]{2,1,0:T(8,128)(2,1)S(1)}, bf16[4,640,384]{2,1,0:T(8,128)(2,1)}, u32[]{:S(2)}, u32[]{:S(2)}) collective-permute-start(bf16[4,640,384]{2,1,0:T(8,128)(2,1)S(1)} %all-to-all-done.2.own_ref), channel_id=1, source_target_pairs={{0,2},{2,0},{1,3},{3,1},{4,6},{6,4},{5,7},{7,5},{8,10},{10,8},{9,1... | collective-permute-start | bytes 5898248 | tf_op jit(solution)/shard_map/ppermute | solution.py:431
  349.7 30.1 %collective-permute-start.6 = (bf16[192,1280]{1,0:T(8,128)(2,1)S(1)}, bf16[192,1280]{1,0:T(8,128)(2,1)}, u32[]{:S(2)}, u32[]{:S(2)}) collective-permute-start(bf16[192,1280]{1,0:T(8,128)(2,1)S(1)} %slice.86), channel_id=1, source_target_pairs={{0,1},{1,0},{2,3},{3,2},{4,5},{5,4},{6,7},{7,6},{8,9},{9,8},{10,11... | collective-permute-start | bytes 1474568 | tf_op jit(solution)/shard_map/ppermute | solution.py:441
  351.4 29.9 %collective-permute-start.10 = (bf16[192,1280]{1,0:T(8,128)(2,1)S(1)}, bf16[192,1280]{1,0:T(8,128)(2,1)}, u32[]{:S(2)}, u32[]{:S(2)}) collective-permute-start(bf16[192,1280]{1,0:T(8,128)(2,1)S(1)} %slice.87), channel_id=1, source_target_pairs={{0,16},{16,0},{1,17},{17,1},{2,18},{18,2},{3,19},{19,3},{4,20},{20... | collective-permute-start | bytes 1474568 | tf_op jit(solution)/shard_map/ppermute | solution.py:440
  446.0 23.9 %collective-permute-start.23 = (bf16[2,2,12,64,128]{4,3,2,1,0:T(8,128)(2,1)S(1)}, bf16[2,2,12,64,128]{4,3,2,1,0:T(8,128)(2,1)S(1)}, u32[]{:S(2)}, u32[]{:S(2)}) collective-permute-start(bf16[2,2,12,64,128]{4,3,2,1,0:T(8,128)(2,1)S(1)} %bitcast.41), channel_id=1, source_target_pairs={{0,2},{2,0},{1,3},{3,1},{4,6},{6,4},{5,7},{7,5},{8,10},{10,8},{9,1... | collective-permute-start | bytes 2359304 | tf_op jit(solution)/shard_map/ppermute | solution.py:482
  462.0 32.6 %all-to-all-start.3 = ((bf16[4,1,384,128]{3,2,1,0:T(8,128)(2,1)}), bf16[4,1,384,128]{3,2,1,0:T(8,128)(2,1)S(1)}, u32[]{:S(2)}, u32[]{:S(2)}) async-start(bf16[4,1,384,128]{3,2,1,0:T(8,128)(2,1)} %bitcast.37), calls=%async_computation.3 | async-start | bytes 786432 | tf_op jit(solution)/shard_map/all_to_all | solution.py:404
  494.6 24.0 %all-to-all-start.1 = ((bf16[4,2,384,128]{3,2,1,0:T(8,128)(2,1)}), bf16[4,2,384,128]{3,2,1,0:T(8,128)(2,1)S(1)}, u32[]{:S(2)}, u32[]{:S(2)}) async-start(bf16[4,2,384,128]{3,2,1,0:T(8,128)(2,1)} %copy_bitcast_fusion), calls=%async_computation.1 | async-start | bytes 1572864 | tf_op jit(solution)/shard_map/all_to_all | solution.py:404
  524.7 24.9 %collective-permute-start.26 = (bf16[384,1280]{1,0:T(8,128)(2,1)}, bf16[384,1280]{1,0:T(8,128)(2,1)S(1)}, u32[]{:S(2)}, u32[]{:S(2)}) collective-permute-start(bf16[384,1280]{1,0:T(8,128)(2,1)} %out_blocks.5), channel_id=1, source_target_pairs={{0,16},{16,0},{1,17},{17,1},{2,18},{18,2},{3,19},{19,3},{4,20},{20... | collective-permute-start | bytes 2949128 | tf_op jit(solution)/shard_map/ppermute | solution.py:504
  531.4 43.7 %collective-permute-start.27 = (bf16[384,1280]{1,0:T(8,128)(2,1)}, bf16[384,1280]{1,0:T(8,128)(2,1)S(1)}, u32[]{:S(2)}, u32[]{:S(2)}) collective-permute-start(bf16[384,1280]{1,0:T(8,128)(2,1)} %out_blocks.6), channel_id=1, source_target_pairs={{0,1},{1,0},{2,3},{3,2},{4,5},{5,4},{6,7},{7,6},{8,9},{9,8},{10,11... | collective-permute-start | bytes 2949128 | tf_op jit(solution)/shard_map/ppermute | solution.py:505
  538.1 37.1 %collective-permute-start.28 = (bf16[384,1280]{1,0:T(8,128)(2,1)}, bf16[384,1280]{1,0:T(8,128)(2,1)S(1)}, u32[]{:S(2)}, u32[]{:S(2)}) collective-permute-start(bf16[384,1280]{1,0:T(8,128)(2,1)} %out_blocks.7), channel_id=1, source_target_pairs={{0,17},{1,16},{16,1},{17,0},{2,19},{3,18},{18,3},{19,2},{4,21},{5,... | collective-permute-start | bytes 2949128 | tf_op jit(solution)/shard_map/ppermute | solution.py:503
  (32 other events, 1111.3 us)

commit v3 on v2

--- a/solution.py
+++ b/solution.py
@@ -145,113 +145,108 @@
     return pl.BlockSpec(memory_space=pltpu.SMEM)
 
 
-def cut_columns(weight, chips, first, heads, chip_heads):
-    rows = weight.shape[0]
+def cut_columns(weight, chips, head):
+    rows, columns = weight.shape
     wide = 3 * HEAD_DIM
-
-    def body(weight_ref, out_ref, sems):
-        copies = []
-        for chip in range(chips):
-            at = (chip * chip_heads + first) * wide
-            copy = pltpu.make_async_copy(
-                weight_ref.at[:, pl.ds(at, heads * wide)], out_ref.at[chip], sems.at[chip]
-            )
-            copy.start()
-            copies.append(copy)
-        for copy in copies:
-            copy.wait()
+    chip_heads = columns // (chips * wide)
+
+    def body(weight_ref, out_ref):
+        out_ref[0] = weight_ref[...]
 
     return pl.pallas_call(
         body,
-        in_specs=[in_hbm()],
-        out_specs=in_hbm(),
-        out_shape=jax.ShapeDtypeStruct((chips, rows, heads * wide), weight.dtype),
-        scratch_shapes=[pltpu.SemaphoreType.DMA((chips,))],
+        grid=(chips,),
+        in_specs=[pl.BlockSpec((rows, wide), lambda chip: (0, chip * chip_heads + head))],
+        out_specs=pl.BlockSpec((1, rows, wide), lambda chip: (chip, 0, 0)),
+        out_shape=jax.ShapeDtypeStruct((chips, rows, wide), weight.dtype),
         name="cut_columns",
     )(weight)
 
 
-def project_heads(places, gains, rounds, weight_own, weight_other):
-    slabs, depth, columns = weight_own.shape
+def project_heads(places, gains, rounds, weights_own, weights_other):
+    heads = len(weights_own)
+    slabs, depth, columns = weights_own[0].shape
     tokens, features = rounds[0][0].shape
-    half = rounds[0][3].shape[0]
-    heads = columns // (3 * HEAD_DIM)
     pieces = [piece for one in rounds for piece in one]
-    per_round = len(rounds[0])
     turns = len(rounds)
-    dtype = weight_own.dtype
-    width = CORES * slabs * depth
-    pair = 2 if turns % 2 == 0 else 1
-
-    def body(places_ref, gains_ref, own_ref, other_ref, *refs):
-        piece_refs = refs[: len(pieces)]
-        query_ref, kv_ref = refs[len(pieces) : len(pieces) + 2]
-        table, rows, weight_sems, row_sems = refs[len(pieces) + 2 :]
-        core = places_ref[4]
-        weight_copies = []
+    dtype = weights_own[0].dtype
+
+    def body(places_ref, gains_ref, *refs):
+        own_refs, other_refs = refs[:heads], refs[heads : 2 * heads]
+        piece_refs = refs[2 * heads : 2 * heads + len(pieces)]
+        query_ref, kv_ref = refs[2 * heads + len(pieces) : 2 * heads + len(pieces) + 2]
+        table, rows, total, weight_sems, row_sems = refs[2 * heads + len(pieces) + 2 :]
+        core = places_ref[slabs]
+        copies = []
         for slab in range(slabs):
-            for side, ref in enumerate((own_ref, other_ref)):
-                place = core if side == 0 else 1 - core
-                copy = pltpu.make_async_copy(
-                    ref.at[places_ref[slab]], table.at[slab, place], weight_sems.at[slab, side]
+            here = []
+            for head in range(heads):
+                for side, ref in enumerate((own_refs[head], other_refs[head])):
+                    place = core if side == 0 else 1 - core
+                    here.append(
+                        pltpu.make_async_copy(
+                            ref.at[places_ref[slab]],
+                            table.at[slab, place, :, pl.ds(head * columns, columns)],
+                            weight_sems.at[slab, head, side],
+                        )
+                    )
+            for turn in range(turns):
+                here.append(
+                    pltpu.make_async_copy(
+                        piece_refs[turn * slabs + slab],
+                        rows.at[slab, pl.ds(turn * tokens, tokens)],
+                        row_sems.at[slab, turn],
+                    )
                 )
+            for copy in here:
                 copy.start()
-                weight_copies.append(copy)
-        row_copies = []
-        for turn in range(turns):
-            for which in range(per_round):
-                ref = piece_refs[turn * per_round + which]
-                column = min(which, 3) * features
-                first = turn * tokens + max(which - 3, 0) * half
-                count = tokens if which < 3 else half
-                copy = pltpu.make_async_copy(
-                    ref,
-                    rows.at[pl.ds(first, count), pl.ds(column, features)],
-                    row_sems.at[turn, which],
-                )
-                copy.start()
-                row_copies.append(copy)
-        for copy in weight_copies:
-            copy.wait()
-        for begin in range(0, turns, pair):
-            for copy in row_copies[begin * per_round : (begin + pair) * per_round]:
+            copies.append(here)
+        for slab in range(slabs):
+            for copy in copies[slab]:
                 copy.wait()
-            total = jnp.dot(
-                rows[begin * tokens : (begin + pair) * tokens],
-                table[...].reshape(width, columns),
+            part = jnp.dot(
+                rows[slab],
+                table[slab].reshape(CORES * depth, heads * columns),
                 preferred_element_type=jnp.float32,
             )
-            for turn in range(pair):
-                for head in range(heads):
-                    at = 3 * head * HEAD_DIM
-                    here = total[turn * tokens : (turn + 1) * tokens]
-                    for part in range(2):
-                        block = here[:, at + part * HEAD_DIM : at + (part + 1) * HEAD_DIM]
-                        normal = (rms_rows(block) * gains_ref[part, head]).astype(dtype)
-                        if part == 0:
-                            query_ref[head, begin + turn] = normal
-                        else:
-                            kv_ref[head, 0, begin + turn] = normal
-                    block = here[:, at + 2 * HEAD_DIM : at + 3 * HEAD_DIM]
-                    kv_ref[head, 1, begin + turn] = block.astype(dtype)
+            if slab == 0:
+                total[...] = part
+            elif slab < slabs - 1:
+                total[...] += part
+            else:
+                part = total[...] + part
+        for turn in range(turns):
+            here = part[turn * tokens : (turn + 1) * tokens]
+            for head in range(heads):
+                at = head * columns
+                for which in range(2):
+                    block = here[:, at + which * HEAD_DIM : at + (which + 1) * HEAD_DIM]
+                    normal = (rms_rows(block) * gains_ref[which, head]).astype(dtype)
+                    if which == 0:
+                        query_ref[head, turn] = normal
+                    else:
+                        kv_ref[head, 0, turn] = normal
+                block = here[:, at + 2 * HEAD_DIM : at + 3 * HEAD_DIM]
+                kv_ref[head, 1, turn] = block.astype(dtype)
 
     return pl.pallas_call(
         body,
-        in_specs=[in_smem(), in_smem(), in_hbm(), in_hbm()] + [in_hbm()] * len(pieces),
+        in_specs=[in_smem(), in_smem()] + [in_hbm()] * (2 * heads + len(pieces)),
         out_specs=(whole_in_vmem(), whole_in_vmem()),
         out_shape=(
             jax.ShapeDtypeStruct((heads, turns, tokens, HEAD_DIM), dtype),
             jax.ShapeDtypeStruct((heads, 2, turns, tokens, HEAD_DIM), dtype),
         ),
         scratch_shapes=[
-            pltpu.VMEM((slabs, CORES, depth, columns), dtype),
-            pltpu.VMEM((turns * tokens, 4 * features), dtype),
-            pltpu.SemaphoreType.DMA((slabs, 2)),
-            pltpu.SemaphoreType.DMA((turns, per_round)),
+            pltpu.VMEM((slabs, CORES, depth, heads * columns), dtype),
+            pltpu.VMEM((slabs, turns * tokens, features), dtype),
+            pltpu.VMEM((turns * tokens, heads * columns), jnp.float32),
+            pltpu.SemaphoreType.DMA((slabs, heads, 2)),
+            pltpu.SemaphoreType.DMA((slabs, turns)),
         ],
         compiler_params=pltpu.CompilerParams(vmem_limit_bytes=VMEM_BYTES),
         name="project_heads",
-    )(places, gains, weight_own, weight_other, *pieces)
+    )(places, gains, *weights_own, *weights_other, *pieces)
 
 
 def attend(key_slots, counts, query_slots, group_most, queries, kv_own, kv_other):
@@ -283,29 +278,36 @@
         for copy in copies:
             copy.wait()
 
-        def run(head, group, listed):
-            for inner in range(together):
-                block = group * together + inner
-                slots = [slots_ref[head, block, entry] for entry in range(listed)]
-                keys = jnp.concatenate([table[head, 0, slot] for slot in slots], axis=0)
-                values = jnp.concatenate([table[head, 1, slot] for slot in slots], axis=0)
-                scores = (
-                    lax.dot_general(
-                        query_table[head, from_ref[block]],
-                        keys,
-                        (((1,), (1,)), ((), ())),
-                        preferred_element_type=jnp.float32,
+        def run(head, group, listed, batch):
+            for first in range(0, together, batch):
+                spots = [group * together + at for at in range(first, min(first + batch, together))]
+                slots = [[slots_ref[head, at, entry] for entry in range(listed)] for at in spots]
+                scores = []
+                for at, listing in zip(spots, slots):
+                    keys = jnp.concatenate([table[head, 0, slot] for slot in listing], axis=0)
+                    scores.append(
+                        lax.dot_general(
+                            query_table[head, from_ref[at]],
+                            keys,
+                            (((1,), (1,)), ((), ())),
+                            preferred_element_type=jnp.float32,
+                        )
                     )
-                    * scale
-                )
-                column = lax.broadcasted_iota(jnp.int32, scores.shape, 1)
-                scores = jnp.where(column < counts_ref[head, block] * BLOCK, scores, -jnp.inf)
-                highest = jnp.max(scores, axis=1, keepdims=True)
-                raised = jnp.exp(scores - highest)
-                summed = jnp.sum(raised, axis=1, keepdims=True)
-                weights = (raised * (1.0 / summed)).astype(dtype)
-                mixed = jnp.dot(weights, values, preferred_element_type=jnp.float32)
-                out_ref[head, block] = mixed.astype(dtype)
+                column = lax.broadcasted_iota(jnp.int32, (1, listed * BLOCK), 1)
+                scores = [
+                    jnp.where(column < counts_ref[head, at] * BLOCK, one * scale, -jnp.inf)
+                    for at, one in zip(spots, scores)
+                ]
+                highest = [jnp.max(one, axis=1, keepdims=True) for one in scores]
+                raised = [jnp.exp(one - top) for one, top in zip(scores, highest)]
+                inverse = [1.0 / jnp.sum(one, axis=1, keepdims=True) for one in raised]
+                weights = [(one * by).astype(dtype) for one, by in zip(raised, inverse)]
+                mixed = []
+                for one, listing in zip(weights, slots):
+                    values = jnp.concatenate([table[head, 1, slot] for slot in listing], axis=0)
+                    mixed.append(jnp.dot(one, values, preferred_element_type=jnp.float32))
+                for at, one in zip(spots, mixed):
+                    out_ref[head, at] = one.astype(dtype)
 
         def step(at, carry):
             head, group = at // groups, at % groups
@@ -313,11 +315,11 @@
 
             @pl.when(few)
             def _():
-                run(head, group, most // 2)
+                run(head, group, most // 2, 6)
 
             @pl.when(jnp.logical_not(few))
             def _():
-                run(head, group, most)
+                run(head, group, most, 3)
 
             return carry
 
@@ -345,6 +347,8 @@
     count = len(attended)
     depth, features = out_weight.shape
     width = features // blocks
+    tile = 2 * HEAD_DIM
+    steps = width // tile
 
     def body(which_ref, sign_ref, *refs):
         parts, weight_ref, out_ref = refs[:count], refs[count], refs[count + 1]
@@ -361,10 +365,10 @@
         body,
         grid_spec=pltpu.PrefetchScalarGridSpec(
             num_scalar_prefetch=2,
-            grid=(1,),
+            grid=(steps,),
             in_specs=[pl.BlockSpec(one.shape, lambda i, w, s: (0, 0, 0, 0)) for one in attended]
-            + [pl.BlockSpec((depth, width), lambda i, w, s: (0, w[0]))],
-            out_specs=pl.BlockSpec((tokens, width), lambda i, w, s: (0, 0)),
+            + [pl.BlockSpec((depth, tile), lambda i, w, s: (0, w[0] * steps + i))],
+            out_specs=pl.BlockSpec((tokens, tile), lambda i, w, s: (0, i)),
         ),
         out_shape=jax.ShapeDtypeStruct((tokens, width), dtype),
         compiler_params=pltpu.CompilerParams(vmem_limit_bytes=VMEM_BYTES),
@@ -398,17 +402,17 @@
     features = gen_weight.shape[1]
     all_blocks = chips * local_blocks
     swap = [(0, 1), (1, 0)]
-    ring = [(at, (at + 1) % chips) for at in range(chips)]
+    upward = [(at, (at + 1) % chips) for at in range(chips)]
+    downward = [((at + 1) % chips, at) for at in range(chips)]
+
+    def turn_of(behind):
+        return jnp.where(behind <= chips // 2, jnp.maximum(2 * behind - 1, 0), 2 * (chips - behind))
 
     def exchange(array):
         return lax.all_to_all(array, "chip", split_axis=0, concat_axis=0, tiled=True)
 
-    chunks = chunk_sizes(heads)
     weight_here = qkv_weight[0]
-    cuts = [
-        cut_columns(weight_here, chips, sum(chunks[:at]), chunks[at], heads)
-        for at in range(len(chunks))
-    ]
+    cuts = [cut_columns(weight_here, chips, at) for at in range(heads)]
     weights_own = [exchange(cuts[0])]
 
     mine = role * lax.axis_size("head") + head
@@ -425,33 +429,48 @@
     squares = squares + lax.ppermute(squares, "head", swap)
     normed = (noisy * lax.rsqrt(squares / width + 1e-06)[:, :, None]).astype(jnp.bfloat16)
     normed = normed.reshape(tokens, features)
-    for cut in cuts[1:]:
-        held, _ = lax.optimization_barrier((cut, normed))
+
+    shards = [normed]
+    up = down = normed
+    for at in range(1, chips):
+        if at % 2 == 1:
+            up = lax.ppermute(up, "chip", upward)
+            shards.append(up)
+        else:
+            down = lax.ppermute(down, "chip", downward)
+            shards.append(down)
+    rounds = []
+    for at, shard in enumerate(shards):
+        over_role = lax.ppermute(shard, "role", swap)
+        over_head = lax.ppermute(shard, "head", swap)
+        if at % 2 == 0:
+            diagonal = lax.ppermute(over_head, "role", swap)
+        else:
+            diagonal = lax.ppermute(over_role, "head", swap)
+        rounds.append((shard, over_role, over_head, diagonal))
+
+    lists = jnp.concatenate([block_keys, block_count[:, :, None]], axis=2)
+    lists, _ = lax.optimization_barrier((lists, normed))
+    lists = lax.all_gather(lists, "chip", axis=1, tiled=True)
+    lists = lax.dynamic_slice_in_dim(lists, chip * heads, heads, axis=0)
+
+    for at in range(1, heads):
+        if at == 1:
+            held, _ = lax.optimization_barrier((cuts[at], (lists, shards[1:3])))
+        else:
+            held, _ = lax.optimization_barrier((cuts[at], weights_own[-1]))
         weights_own.append(exchange(held))
     weights_other = [lax.ppermute(one, "core", swap) for one in weights_own]
 
-    shards = [normed]
-    for _ in range(chips - 1):
-        shards.append(lax.ppermute(shards[-1], "chip", ring))
-    rounds = []
-    for shard in shards:
-        over_role = lax.ppermute(shard, "role", swap)
-        over_head = lax.ppermute(shard, "head", swap)
-        first = lax.ppermute(over_head[: tokens // 2], "role", swap)
-        second = lax.ppermute(over_role[tokens // 2 :], "head", swap)
-        rounds.append((shard, over_role, over_head, first, second))
-
-    lists = jnp.concatenate([block_keys, block_count[:, :, None]], axis=2)
-    lists = lax.all_gather(lists, "chip", axis=1, tiled=True)
-    lists = lax.dynamic_slice_in_dim(lists, chip * heads, heads, axis=0)
     owner = lists[:, :, :most] // local_blocks
-    turn = (chip - owner // CORES) % chips
+    turn = turn_of((chip - owner // CORES) % chips)
     far = (owner % CORES != core).astype(jnp.int32)
     key_slots = far * all_blocks + turn * local_blocks + lists[:, :, :most] % local_blocks
     counts = lists[:, :, most]
     group_most = jnp.max(counts.reshape(heads, chips, local_blocks), axis=2)
     spot = jnp.arange(all_blocks, dtype=jnp.int32)
-    query_slots = (chip - spot // local_blocks) % chips * local_blocks + spot % local_blocks
+    query_slots = turn_of((chip - spot // local_blocks) % chips)
+    query_slots = query_slots * local_blocks + spot % local_blocks
 
     sides = lax.axis_size("head")
     peers = jnp.stack(
@@ -467,14 +486,15 @@
 
     attended = []
     held_places = places
+    chunks = chunk_sizes(heads)
     for at, size in enumerate(chunks):
         span = slice(sum(chunks[:at]), sum(chunks[: at + 1]))
         last = at == len(chunks) - 1
-        parts = [rounds] if last else [rounds[: chips // 2], rounds[chips // 2 :]]
+        parts = [rounds] if last else [rounds[:-1], rounds[-1:]]
         queries, kv_own, kv_other = [], [], []
         for part in parts:
             query, kv = project_heads(
-                held_places, gains[:, span], part, weights_own[at], weights_other[at]
+                held_places, gains[:, span], part, weights_own[span], weights_other[span]
             )
             here = len(part) * local_blocks
             queries.append(query.reshape(size, here, BLOCK, HEAD_DIM))
@@ -490,6 +510,7 @@
             kv_own,
             kv_other,
         )
+        held_places, _ = lax.optimization_barrier((places, mixed))
         mixed = mixed.reshape(size, chips, tokens, HEAD_DIM).transpose(1, 0, 2, 3)
         attended.append(exchange(mixed))
 

time: 580 us -> 439 us (0.76)
  Pallas kernels: 280 us -> 98.8 us
  blocking collectives: 13.6 us -> 45.6 us
  waiting for transfers between devices: 184 us -> 204 us
  local copies, waits for them, and re-layouts: 22.2 us -> 13 us
    pallas_call x5 -> x6, Pallas kernels: 226 us -> 55.8 us  [the longest x3 44.5 us: project_heads(): pl.pallas_call(body, in_specs=[in_smem(), in_smem()] + [in_hbm()] * (2 *...]
    all_to_all x4 -> x5, waiting for transfers between devices: 45.6 us -> 86 us  [exchange(): lax.all_to_all(array, 'chip', split_axis=0, concat_axis=0, tiled=True)]
    all_gather x1, blocking collectives: 13.6 us -> 45.6 us  [per_device_by_heads(): lists = lax.all_gather(lists, 'chip', axis=1, tiled=True)]
    ppermute x4, waiting for transfers between devices: 38.3 us -> 11.1 us  [per_device_by_heads(): over_role = lax.ppermute(shard, 'role', swap)]
    ppermute x4, waiting for transfers between devices: 19.3 us -> 38 us  [per_device_by_heads(): over_head = lax.ppermute(shard, 'head', swap)]
    pallas_call x2, Pallas kernels: 33.3 us -> 18.5 us  [attend(): pl.pallas_call(body, in_specs=[in_smem()] * 4 + [in_hbm()] * (3 * parts),...]
    ppermute x11 -> x7, starting transfers between devices: 23.3 us -> 10.4 us  [the longest x2 3.9 us: per_device_by_heads(): up = lax.ppermute(up, 'chip', upward)]
    all_to_all x4 -> x5, starting transfers between devices: 18.8 us -> 28.9 us  [exchange(): lax.all_to_all(array, 'chip', split_axis=0, concat_axis=0, tiled=True)]
  transfers between devices with their start and end apart: 33 -> 31, of which waited for: 14 -> 14; matrix products, arithmetic and copies ran while one was open for 6% -> 2% of each run, Pallas kernels for 24% -> 21%
where the time goes in v3:
time: 439 us; the launch traced here: 437 us
  waiting for transfers between devices  204 us (46%)
  Pallas kernels  98.8 us (23%)
  starting transfers between devices  59.3 us (14%)
  blocking collectives  45.6 us (10%)
  local copies, waits for them, and re-layouts  13 us (3%)
  matrix products  11.5 us (3%)
  other arithmetic  5.06 us (1%)
    all_to_all x5, waiting for transfers between devices, exchange(): lax.all_to_all(array, 'chip', split_axis=0, concat_axis=0, tiled=True)  86 us
    all_gather x1, blocking collectives, per_device_by_heads(): lists = lax.all_gather(lists, 'chip', axis=1, tiled=True)  45.6 us
    pallas_call x3, Pallas kernels, project_heads(): pl.pallas_call(body, in_specs=[in_smem(), in_smem()] + [in_hbm()] * (2 *...  44.5 us
    ppermute x4, waiting for transfers between devices, per_device_by_heads(): over_head = lax.ppermute(shard, 'head', swap)  38 us
    all_to_all x5, starting transfers between devices, exchange(): lax.all_to_all(array, 'chip', split_axis=0, concat_axis=0, tiled=True)  28.9 us
    ppermute x1, waiting for transfers between devices, per_device_by_heads(): from_head = lax.ppermute(block_of(2, jnp.bfloat16), 'head', swap)  24.8 us
    pallas_call x4, Pallas kernels, out_blocks(): pl.pallas_call(body, grid_spec=pltpu.PrefetchScalarGridSpec(num_scalar_pr...  24.6 us
    pallas_call x2, Pallas kernels, attend(): pl.pallas_call(body, in_specs=[in_smem()] * 4 + [in_hbm()] * (3 * parts),...  18.5 us
  transfers between devices with their start and end apart: 31, of which 14 were waited for; matrix products, arithmetic and copies ran while one was open for 2% of the time, Pallas kernels for 21%

profile of v3, /device:TPU:0, one launch (start us, length us, event | category | flops | bytes accessed | tf_op | source)
XLA Modules:
  0.0 437.2 jit_solution(8188471397024510759)
XLA Ops:
  1.0 11.5 %multiply_reduce_fusion = (f32[384]{0:T(512)S(1)}, f32[384,1280]{1,0:T(8,128)S(1)}) fusion(bf16[384,5120]{1,0:T(8,128)(2,1)} %param.11, s32[]{:T(128)S(6)} %select_n.51, f32[384]{0:T(512)S(1)} %mul.95, bf16[384,5120]{1,0:T(8,128)(2,1)} %param.9, bf16[5120,1280]{1,0:T(8,128)(2,1)} %param.10, f32[384]{0:T(512)S(1)} %mul.91), kind=kOutput, calls=%fused_computation.5 | convolution fusion | flops 5036604928 | bytes 19993092 | tf_op jit(solution)/shard_map/dot_general | solution.py:419
  29.4 45.6 %all_gather.3 = s32[12,24,9]{2,0,1:T(8,128)S(1)} all-gather(s32[12,6,9]{2,0,1:T(8,128)S(1)} %pad_add_fusion), channel_id=1, replica_groups=mesh['role'=2,'chip'=4,'core'=2,'head'=2] {'chip'}, dimensions={1}, use_global_device_ids=true | all-gather | bytes 12960 | tf_op jit(solution)/shard_map/all_gather | solution.py:454
  83.7 38.0 %all-to-all-done.1.refs_1_ = bf16[4,640,384]{2,1,0:T(8,128)(2,1)S(1)} async-done(((bf16[4,640,384]{2,1,0:T(8,128)(2,1)}), bf16[4,640,384]{2,1,0:T(8,128)(2,1)S(1)}, u32[]{:S(2)}, u32[]{:S(2)}) %all-to-all-start.1) | async-done | bytes 1966112 | tf_op jit(solution)/shard_map/all_to_all | solution.py:412
  121.7 4.4 %all-to-all-start = ((bf16[4,640,384]{2,1,0:T(8,128)(2,1)}), bf16[4,640,384]{2,1,0:T(8,128)(2,1)}, u32[]{:S(2)}, u32[]{:S(2)}) async-start(bf16[4,640,384]{2,1,0:T(8,128)(2,1)} %cut_columns.3), calls=%async_computation | async-start | bytes 3932160 | tf_op jit(solution)/shard_map/all_to_all | solution.py:412
  133.7 37.4 %all-to-all-done.refs_0_ = bf16[4,640,384]{2,1,0:T(8,128)(2,1)} async-done(((bf16[4,640,384]{2,1,0:T(8,128)(2,1)}), bf16[4,640,384]{2,1,0:T(8,128)(2,1)}, u32[]{:S(2)}, u32[]{:S(2)}) %all-to-all-start) | async-done | bytes 1966112 | tf_op jit(solution)/shard_map/all_to_all | solution.py:412
  181.5 18.9 %collective-permute-done.13.refs_14_.refs_12_ = bf16[384,1280]{1,0:T(8,128)(2,1)S(1)} collective-permute-done((bf16[384,1280]{1,0:T(8,128)(2,1)}, bf16[384,1280]{1,0:T(8,128)(2,1)S(1)}, u32[]{:S(2)}, u32[]{:S(2)}) %collective-permute-start.13) | collective-permute-done | bytes 983072 | tf_op jit(solution)/shard_map/ppermute | solution.py:445
  200.5 19.1 %collective-permute-done.10.refs_10_.refs_8_ = bf16[384,1280]{1,0:T(8,128)(2,1)S(1)} collective-permute-done((bf16[384,1280]{1,0:T(8,128)(2,1)}, bf16[384,1280]{1,0:T(8,128)(2,1)S(1)}, u32[]{:S(2)}, u32[]{:S(2)}) %collective-permute-start.10) | collective-permute-done | bytes 983072 | tf_op jit(solution)/shard_map/ppermute | solution.py:445
  221.3 10.6 %collective-permute-done.15.refs_4_.refs_14_ = bf16[384,1280]{1,0:T(8,128)(2,1)S(1)} collective-permute-done((bf16[384,1280]{1,0:T(8,128)(2,1)}, bf16[384,1280]{1,0:T(8,128)(2,1)S(1)}, u32[]{:S(2)}, u32[]{:S(2)}) %collective-permute-start.15) | collective-permute-done | bytes 983072 | tf_op jit(solution)/shard_map/ppermute | solution.py:437
  234.0 9.9 %collective-permute-done.11.refs_11_.refs_9_ = bf16[384,1280]{1,0:T(8,128)(2,1)S(1)} collective-permute-done((bf16[384,1280]{1,0:T(8,128)(2,1)}, bf16[384,1280]{1,0:T(8,128)(2,1)S(1)}, u32[]{:S(2)}, u32[]{:S(2)}) %collective-permute-start.11) | collective-permute-done | bytes 983072 | tf_op jit(solution)/shard_map/ppermute | solution.py:449
  245.6 11.1 %collective-permute-done.16.refs_5_.refs_15_ = bf16[384,1280]{1,0:T(8,128)(2,1)} collective-permute-done((bf16[384,1280]{1,0:T(8,128)(2,1)S(1)}, bf16[384,1280]{1,0:T(8,128)(2,1)}, u32[]{:S(2)}, u32[]{:S(2)}) %collective-permute-start.16) | collective-permute-done | bytes 983072 | tf_op jit(solution)/shard_map/ppermute | solution.py:444
  258.4 16.5 %collective-permute-done.14.refs_15_.refs_13_ = bf16[384,1280]{1,0:T(8,128)(2,1)} collective-permute-done((bf16[384,1280]{1,0:T(8,128)(2,1)S(1)}, bf16[384,1280]{1,0:T(8,128)(2,1)}, u32[]{:S(2)}, u32[]{:S(2)}) %collective-permute-start.14) | collective-permute-done | bytes 983072 | tf_op jit(solution)/shard_map/ppermute | solution.py:447
  276.2 19.4 %project_heads.3 = (bf16[2,3,384,128]{3,2,1,0:T(8,128)(2,1)}, bf16[2,2,3,384,128]{4,3,2,1,0:T(8,128)(2,1)}) custom-call(s32[5]{0:T(128)} %concatenate.7.places_ref, f32[2,2]{1,0:T(2,128)} %bitcast.47, bf16[4,640,384]{2,1,0:T(8,128)(2,1)} %all-to-all-done.refs_0_, bf16[4,640,384]{2,1,0:T(8,128)(2,1)} %copy-done.3, ...), custom_call_target="tpu_custom_call" | custom-call | tf_op jit(solution)/shard_map/project_heads/pallas_call | solution.py:232
  296.7 9.9 %project_heads.4 = (bf16[2,1,384,128]{3,2,1,0:T(8,128)(2,1)}, bf16[2,2,1,384,128]{4,3,2,1,0:T(8,128)(2,1)}) custom-call(s32[5]{0:T(128)} %concatenate.7.places_ref, f32[2,2]{1,0:T(2,128)} %bitcast.48, bf16[4,640,384]{2,1,0:T(8,128)(2,1)} %all-to-all-done.refs_0_, bf16[4,640,384]{2,1,0:T(8,128)(2,1)} %copy-done.3, ...), custom_call_target="tpu_custom_call" | custom-call | tf_op jit(solution)/shard_map/project_heads/pallas_call | solution.py:232
  310.4 11.6 %attend.2 = bf16[2,24,64,128]{3,2,1,0:T(8,128)(2,1)} custom-call(s32[2,24,8]{2,1,0:T(8,128)} %slice.53.slots_ref, s32[2,24]{1,0:T(2,128)} %slice_reduce_fusion.1.counts_ref, s32[24]{0:T(128)} %fusion.9.from_ref, s32[2,4]{1,0:T(2,128)} %slice.45.most_ref, bf16[2,18,64,128]{3,2,1,0:T(8,128)(2,1)} %bitcast.42, bf16[2,6,64,128]{3,2,1,0:T(8,128)(2,1)} %bitcast.46, ...), custom_call_target="tpu_custom_call" | custom-call | tf_op jit(solution)/shard_map/attend/pallas_call | solution.py:328
  324.1 11.4 %all-to-all-start.2 = ((bf16[4,2,384,128]{3,2,1,0:T(8,128)(2,1)}), bf16[4,2,384,128]{3,2,1,0:T(8,128)(2,1)S(1)}, u32[]{:S(2)}, u32[]{:S(2)}) async-start(bf16[4,2,384,128]{3,2,1,0:T(8,128)(2,1)} %copy_bitcast_fusion), calls=%async_computation.2 | async-start | bytes 1572864 | tf_op jit(solution)/shard_map/all_to_all | solution.py:412
  336.1 15.2 %project_heads.5 = (bf16[1,4,384,128]{3,2,1,0:T(8,128)(2,1)}, bf16[1,2,4,384,128]{4,3,2,1,0:T(8,128)(2,1)}) custom-call(s32[5]{0:T(128)} %concatenate.7.places_ref, f32[2,1]{1,0:T(2,128)} %slice.51.gains_ref, bf16[4,640,384]{2,1,0:T(8,128)(2,1)} %all-to-all-done.3.refs_0_, bf16[4,640,384]{2,1,0:T(8,128)(2,1)} %collective-permute-done.21.refs_1_, ...), custom_call_target="tpu_custom_call" | custom-call | tf_op jit(solution)/shard_map/project_heads/pallas_call | solution.py:232
  354.8 6.9 %attend.3 = bf16[1,24,64,128]{3,2,1,0:T(8,128)(2,1)} custom-call(s32[1,24,8]{2,1,0:T(8,128)} %slice.56.slots_ref, s32[1,24]{1,0:T(1,128)} %bitcast.50, s32[24]{0:T(128)} %fusion.9.from_ref, s32[1,4]{1,0:T(1,128)} %slice.50.most_ref, bf16[1,24,64,128]{3,2,1,0:T(8,128)(2,1)} %bitcast.43, bf16[1,2,24,64,128]{4,3,2,1,0:T(8,128)(2,1)} %bitcast.41, ...), custom_call_target="tpu_custom_call" | custom-call | tf_op jit(solution)/shard_map/attend/pallas_call | solution.py:328
  361.7 5.1 %all-to-all-start.4 = ((bf16[4,1,384,128]{3,2,1,0:T(8,128)(2,1)}), bf16[4,1,384,128]{3,2,1,0:T(8,128)(2,1)S(1)}, u32[]{:S(2)}, u32[]{:S(2)}) async-start(bf16[4,1,384,128]{3,2,1,0:T(8,128)(2,1)} %bitcast.37), calls=%async_computation.4 | async-start | bytes 786432 | tf_op jit(solution)/shard_map/all_to_all | solution.py:412
  366.8 10.6 %all-to-all-done.4.refs_1_ = bf16[4,1,384,128]{3,2,1,0:T(8,128)(2,1)S(1)} async-done(((bf16[4,1,384,128]{3,2,1,0:T(8,128)(2,1)}), bf16[4,1,384,128]{3,2,1,0:T(8,128)(2,1)S(1)}, u32[]{:S(2)}, u32[]{:S(2)}) %all-to-all-start.4) | async-done | bytes 393248 | tf_op jit(solution)/shard_map/all_to_all | solution.py:412
  378.2 6.1 %out_blocks.5 = bf16[384,1280]{1,0:T(8,128)(2,1)} custom-call(s32[1]{0:T(128)} %bitcast.3.which_ref, s32[1]{0:T(128)} %bitcast.1.sign_ref, bf16[4,2,384,128]{3,2,1,0:T(8,128)(2,1)} %copy-done.2, bf16[4,1,384,128]{3,2,1,0:T(8,128)(2,1)} %copy-done.4, bf16[1536,5120]{1,0:T(8,128)(2,1)} %bitcast.29), custom_call_target="tpu_custom_call" | custom-call | tf_op jit(solution)/shard_map/out_blocks/pallas_call | solution.py:364
  385.9 6.1 %out_blocks.6 = bf16[384,1280]{1,0:T(8,128)(2,1)} custom-call(s32[1]{0:T(128)} %bitcast.4.which_ref, s32[1]{0:T(128)} %bitcast.1.sign_ref, bf16[4,2,384,128]{3,2,1,0:T(8,128)(2,1)} %copy-done.2, bf16[4,1,384,128]{3,2,1,0:T(8,128)(2,1)} %copy-done.4, bf16[1536,5120]{1,0:T(8,128)(2,1)} %bitcast.30), custom_call_target="tpu_custom_call" | custom-call | tf_op jit(solution)/shard_map/out_blocks/pallas_call | solution.py:364
  393.4 6.1 %out_blocks.7 = bf16[384,1280]{1,0:T(8,128)(2,1)} custom-call(s32[1]{0:T(128)} %bitcast.5.which_ref, s32[1]{0:T(128)} %bitcast.1.sign_ref, bf16[4,2,384,128]{3,2,1,0:T(8,128)(2,1)} %copy-done.2, bf16[4,1,384,128]{3,2,1,0:T(8,128)(2,1)} %copy-done.4, bf16[1536,5120]{1,0:T(8,128)(2,1)} %bitcast.31), custom_call_target="tpu_custom_call" | custom-call | tf_op jit(solution)/shard_map/out_blocks/pallas_call | solution.py:364
  400.0 6.3 %out_blocks.4 = f32[384,1280]{1,0:T(8,128)} custom-call(s32[1]{0:T(128)} %bitcast.which_ref, s32[1]{0:T(128)} %bitcast.1.sign_ref, bf16[4,2,384,128]{3,2,1,0:T(8,128)(2,1)} %copy-done.2, bf16[4,1,384,128]{3,2,1,0:T(8,128)(2,1)} %copy-done.4, bf16[1536,5120]{1,0:T(8,128)(2,1)} %bitcast.32), custom_call_target="tpu_custom_call" | custom-call | tf_op jit(solution)/shard_map/out_blocks/pallas_call | solution.py:364
  409.2 24.8 %collective-permute-done.24 = bf16[384,1280]{1,0:T(8,128)(2,1)S(1)} collective-permute-done((bf16[384,1280]{1,0:T(8,128)(2,1)}, bf16[384,1280]{1,0:T(8,128)(2,1)S(1)}, u32[]{:S(2)}, u32[]{:S(2)}) %collective-permute-start.24) | collective-permute-done | bytes 983072 | tf_op jit(solution)/shard_map/ppermute | solution.py:526
  (123 shorter events, 74.5 us)
Async XLA Ops:
  21.2 53.8 %collective-permute-start.2 = (bf16[384,1280]{1,0:T(8,128)(2,1)S(1)}, bf16[384,1280]{1,0:T(8,128)(2,1)S(1)}, u32[]{:S(2)}, u32[]{:S(2)}) collective-permute-start(bf16[384,1280]{1,0:T(8,128)(2,1)S(1)} %multiply_convert_fusion.refs_4_.refs_2_), channel_id=1, source_target_pairs={{0,4},{4,8},{8,12},{12,0},{1,5},{5,9},{9,13},{13,1},{2,6},{6,10},{... | collective-permute-start | bytes 2949128 | tf_op jit(solution)/shard_map/ppermute | solution.py:437
  23.2 51.9 %collective-permute-start.3 = (bf16[384,1280]{1,0:T(8,128)(2,1)S(1)}, bf16[384,1280]{1,0:T(8,128)(2,1)S(1)}, u32[]{:S(2)}, u32[]{:S(2)}) collective-permute-start(bf16[384,1280]{1,0:T(8,128)(2,1)S(1)} %multiply_convert_fusion.refs_4_.refs_2_), channel_id=1, source_target_pairs={{4,0},{8,4},{12,8},{0,12},{5,1},{9,5},{13,9},{1,13},{6,2},{10,6},{... | collective-permute-start | bytes 2949128 | tf_op jit(solution)/shard_map/ppermute | solution.py:440
  76.3 45.3 %all-to-all-start.1 = ((bf16[4,640,384]{2,1,0:T(8,128)(2,1)}), bf16[4,640,384]{2,1,0:T(8,128)(2,1)S(1)}, u32[]{:S(2)}, u32[]{:S(2)}) async-start(bf16[4,640,384]{2,1,0:T(8,128)(2,1)} %cut_columns.4), calls=%async_computation.1 | async-start | bytes 3932160 | tf_op jit(solution)/shard_map/all_to_all | solution.py:412
  121.7 49.4 %all-to-all-start = ((bf16[4,640,384]{2,1,0:T(8,128)(2,1)}), bf16[4,640,384]{2,1,0:T(8,128)(2,1)}, u32[]{:S(2)}, u32[]{:S(2)}) async-start(bf16[4,640,384]{2,1,0:T(8,128)(2,1)} %cut_columns.3), calls=%async_computation | async-start | bytes 3932160 | tf_op jit(solution)/shard_map/all_to_all | solution.py:412
  126.1 51.5 %collective-permute-start.7 = (bf16[384,1280]{1,0:T(8,128)(2,1)S(1)}, bf16[384,1280]{1,0:T(8,128)(2,1)}, u32[]{:S(2)}, u32[]{:S(2)}) collective-permute-start(bf16[384,1280]{1,0:T(8,128)(2,1)S(1)} %multiply_convert_fusion.refs_4_.refs_2_), channel_id=1, source_target_pairs={{0,1},{1,0},{2,3},{3,2},{4,5},{5,4},{6,7},{7,6},{8,9},{9,8},{10,11... | collective-permute-start | bytes 2949128 | tf_op jit(solution)/shard_map/ppermute | solution.py:445
  127.9 51.3 %collective-permute-start.6 = (bf16[384,1280]{1,0:T(8,128)(2,1)S(1)}, bf16[384,1280]{1,0:T(8,128)(2,1)}, u32[]{:S(2)}, u32[]{:S(2)}) collective-permute-start(bf16[384,1280]{1,0:T(8,128)(2,1)S(1)} %multiply_convert_fusion.refs_4_.refs_2_), channel_id=1, source_target_pairs={{0,16},{16,0},{1,17},{17,1},{2,18},{18,2},{3,19},{19,3},{4,20},{20... | collective-permute-start | bytes 2949128 | tf_op jit(solution)/shard_map/ppermute | solution.py:444
  133.0 48.1 %collective-permute-start.9 = (bf16[384,1280]{1,0:T(8,128)(2,1)}, bf16[384,1280]{1,0:T(8,128)(2,1)}, u32[]{:S(2)}, u32[]{:S(2)}) collective-permute-start(bf16[384,1280]{1,0:T(8,128)(2,1)} %copy-done.6), channel_id=1, source_target_pairs={{0,16},{16,0},{1,17},{17,1},{2,18},{18,2},{3,19},{19,3},{4,20},{20... | collective-permute-start | bytes 2949128 | tf_op jit(solution)/shard_map/ppermute | solution.py:444
  171.1 103.8 %all-to-all-start.3 = ((bf16[4,640,384]{2,1,0:T(8,128)(2,1)}), bf16[4,640,384]{2,1,0:T(8,128)(2,1)}, u32[]{:S(2)}, u32[]{:S(2)}) async-start(bf16[4,640,384]{2,1,0:T(8,128)(2,1)} %cut_columns.5), calls=%async_computation.3 | async-start | bytes 3932160 | tf_op jit(solution)/shard_map/all_to_all | solution.py:412
  175.5 25.0 %collective-permute-start.13 = (bf16[384,1280]{1,0:T(8,128)(2,1)}, bf16[384,1280]{1,0:T(8,128)(2,1)S(1)}, u32[]{:S(2)}, u32[]{:S(2)}) collective-permute-start(bf16[384,1280]{1,0:T(8,128)(2,1)} %copy-done.7), channel_id=1, source_target_pairs={{0,1},{1,0},{2,3},{3,2},{4,5},{5,4},{6,7},{7,6},{8,9},{9,8},{10,11... | collective-permute-start | bytes 2949128 | tf_op jit(solution)/shard_map/ppermute | solution.py:445
  177.2 42.3 %collective-permute-start.10 = (bf16[384,1280]{1,0:T(8,128)(2,1)}, bf16[384,1280]{1,0:T(8,128)(2,1)S(1)}, u32[]{:S(2)}, u32[]{:S(2)}) collective-permute-start(bf16[384,1280]{1,0:T(8,128)(2,1)} %copy-done.6), channel_id=1, source_target_pairs={{0,1},{1,0},{2,3},{3,2},{4,5},{5,4},{6,7},{7,6},{8,9},{9,8},{10,11... | collective-permute-start | bytes 2949128 | tf_op jit(solution)/shard_map/ppermute | solution.py:445
  177.6 42.0 %collective-permute-start.12 = (bf16[384,1280]{1,0:T(8,128)(2,1)}, bf16[384,1280]{1,0:T(8,128)(2,1)S(1)}, u32[]{:S(2)}, u32[]{:S(2)}) collective-permute-start(bf16[384,1280]{1,0:T(8,128)(2,1)} %copy-done.7), channel_id=1, source_target_pairs={{0,16},{16,0},{1,17},{17,1},{2,18},{18,2},{3,19},{19,3},{4,20},{20... | collective-permute-start | bytes 2949128 | tf_op jit(solution)/shard_map/ppermute | solution.py:444
  179.2 52.8 %collective-permute-start.15 = (bf16[384,1280]{1,0:T(8,128)(2,1)}, bf16[384,1280]{1,0:T(8,128)(2,1)S(1)}, u32[]{:S(2)}, u32[]{:S(2)}) collective-permute-start(bf16[384,1280]{1,0:T(8,128)(2,1)} %copy-done.6), channel_id=1, source_target_pairs={{0,4},{4,8},{8,12},{12,0},{1,5},{5,9},{9,13},{13,1},{2,6},{6,10},{... | collective-permute-start | bytes 2949128 | tf_op jit(solution)/shard_map/ppermute | solution.py:437
  181.1 52.4 %collective-permute-start.8 = (bf16[384,1280]{1,0:T(8,128)(2,1)}, bf16[384,1280]{1,0:T(8,128)(2,1)S(1)}, u32[]{:S(2)}, u32[]{:S(2)}) collective-permute-start(bf16[384,1280]{1,0:T(8,128)(2,1)} %collective-permute-done.7.refs_6_.refs_4_), channel_id=1, source_target_pairs={{0,16},{16,0},{1,17},{17,1},{2,18},{18,2},{3,19},{19,3},{4,20},{20... | collective-permute-start | bytes 2949128 | tf_op jit(solution)/shard_map/ppermute | solution.py:447
  200.5 75.7 %collective-permute-start.4 = (bf16[4,640,384]{2,1,0:T(8,128)(2,1)}, bf16[4,640,384]{2,1,0:T(8,128)(2,1)}, u32[]{:S(2)}, u32[]{:S(2)}) collective-permute-start(bf16[4,640,384]{2,1,0:T(8,128)(2,1)} %all-to-all-done.refs_0_), channel_id=1, source_target_pairs={{0,2},{2,0},{1,3},{3,1},{4,6},{6,4},{5,7},{7,5},{8,10},{10,8},{9,1... | collective-permute-start | bytes 5898248 | tf_op jit(solution)/shard_map/ppermute | solution.py:463
  219.6 56.7 %collective-permute-start.5 = (bf16[4,640,384]{2,1,0:T(8,128)(2,1)S(1)}, bf16[4,640,384]{2,1,0:T(8,128)(2,1)}, u32[]{:S(2)}, u32[]{:S(2)}) collective-permute-start(bf16[4,640,384]{2,1,0:T(8,128)(2,1)S(1)} %all-to-all-done.1.refs_1_), channel_id=1, source_target_pairs={{0,2},{2,0},{1,3},{3,1},{4,6},{6,4},{5,7},{7,5},{8,10},{10,8},{9,1... | collective-permute-start | bytes 5898248 | tf_op jit(solution)/shard_map/ppermute | solution.py:463
  231.9 24.8 %collective-permute-start.16 = (bf16[384,1280]{1,0:T(8,128)(2,1)S(1)}, bf16[384,1280]{1,0:T(8,128)(2,1)}, u32[]{:S(2)}, u32[]{:S(2)}) collective-permute-start(bf16[384,1280]{1,0:T(8,128)(2,1)S(1)} %collective-permute-done.15.refs_4_.refs_14_), channel_id=1, source_target_pairs={{0,16},{16,0},{1,17},{17,1},{2,18},{18,2},{3,19},{19,3},{4,20},{20... | collective-permute-start | bytes 2949128 | tf_op jit(solution)/shard_map/ppermute | solution.py:444
  233.5 41.4 %collective-permute-start.14 = (bf16[384,1280]{1,0:T(8,128)(2,1)S(1)}, bf16[384,1280]{1,0:T(8,128)(2,1)}, u32[]{:S(2)}, u32[]{:S(2)}) collective-permute-start(bf16[384,1280]{1,0:T(8,128)(2,1)S(1)} %collective-permute-done.13.refs_14_.refs_12_), channel_id=1, source_target_pairs={{0,16},{16,0},{1,17},{17,1},{2,18},{18,2},{3,19},{19,3},{4,20},{20... | collective-permute-start | bytes 2949128 | tf_op jit(solution)/shard_map/ppermute | solution.py:447
  244.0 52.8 %collective-permute-start.17 = (bf16[384,1280]{1,0:T(8,128)(2,1)S(1)}, bf16[384,1280]{1,0:T(8,128)(2,1)}, u32[]{:S(2)}, u32[]{:S(2)}) collective-permute-start(bf16[384,1280]{1,0:T(8,128)(2,1)S(1)} %collective-permute-done.15.refs_4_.refs_14_), channel_id=1, source_target_pairs={{0,1},{1,0},{2,3},{3,2},{4,5},{5,4},{6,7},{7,6},{8,9},{9,8},{10,11... | collective-permute-start | bytes 2949128 | tf_op jit(solution)/shard_map/ppermute | solution.py:445
  256.7 40.0 %collective-permute-start.18 = (bf16[384,1280]{1,0:T(8,128)(2,1)}, bf16[384,1280]{1,0:T(8,128)(2,1)}, u32[]{:S(2)}, u32[]{:S(2)}) collective-permute-start(bf16[384,1280]{1,0:T(8,128)(2,1)} %collective-permute-done.16.refs_5_.refs_15_), channel_id=1, source_target_pairs={{0,1},{1,0},{2,3},{3,2},{4,5},{5,4},{6,7},{7,6},{8,9},{9,8},{10,11... | collective-permute-start | bytes 2949128 | tf_op jit(solution)/shard_map/ppermute | solution.py:449
  274.9 61.3 %collective-permute-start.21 = (bf16[4,640,384]{2,1,0:T(8,128)(2,1)}, bf16[4,640,384]{2,1,0:T(8,128)(2,1)}, u32[]{:S(2)}, u32[]{:S(2)}) collective-permute-start(bf16[4,640,384]{2,1,0:T(8,128)(2,1)} %all-to-all-done.3.refs_0_), channel_id=1, source_target_pairs={{0,2},{2,0},{1,3},{3,1},{4,6},{6,4},{5,7},{7,5},{8,10},{10,8},{9,1... | collective-permute-start | bytes 5898248 | tf_op jit(solution)/shard_map/ppermute | solution.py:463
  324.1 37.6 %all-to-all-start.2 = ((bf16[4,2,384,128]{3,2,1,0:T(8,128)(2,1)}), bf16[4,2,384,128]{3,2,1,0:T(8,128)(2,1)S(1)}, u32[]{:S(2)}, u32[]{:S(2)}) async-start(bf16[4,2,384,128]{3,2,1,0:T(8,128)(2,1)} %copy_bitcast_fusion), calls=%async_computation.2 | async-start | bytes 1572864 | tf_op jit(solution)/shard_map/all_to_all | solution.py:412
  384.3 24.9 %collective-permute-start.23 = (bf16[384,1280]{1,0:T(8,128)(2,1)}, bf16[384,1280]{1,0:T(8,128)(2,1)S(1)}, u32[]{:S(2)}, u32[]{:S(2)}) collective-permute-start(bf16[384,1280]{1,0:T(8,128)(2,1)} %out_blocks.5), channel_id=1, source_target_pairs={{0,16},{16,0},{1,17},{17,1},{2,18},{18,2},{3,19},{19,3},{4,20},{20... | collective-permute-start | bytes 2949128 | tf_op jit(solution)/shard_map/ppermute | solution.py:525
  392.0 42.0 %collective-permute-start.24 = (bf16[384,1280]{1,0:T(8,128)(2,1)}, bf16[384,1280]{1,0:T(8,128)(2,1)S(1)}, u32[]{:S(2)}, u32[]{:S(2)}) collective-permute-start(bf16[384,1280]{1,0:T(8,128)(2,1)} %out_blocks.6), channel_id=1, source_target_pairs={{0,1},{1,0},{2,3},{3,2},{4,5},{5,4},{6,7},{7,6},{8,9},{9,8},{10,11... | collective-permute-start | bytes 2949128 | tf_op jit(solution)/shard_map/ppermute | solution.py:526
  399.5 34.5 %collective-permute-start.25 = (bf16[384,1280]{1,0:T(8,128)(2,1)}, bf16[384,1280]{1,0:T(8,128)(2,1)S(1)}, u32[]{:S(2)}, u32[]{:S(2)}) collective-permute-start(bf16[384,1280]{1,0:T(8,128)(2,1)} %out_blocks.7), channel_id=1, source_target_pairs={{0,17},{1,16},{16,1},{17,0},{2,19},{3,18},{18,3},{19,2},{4,21},{5,... | collective-permute-start | bytes 2949128 | tf_op jit(solution)/shard_map/ppermute | solution.py:524
  (27 other events, 818.4 us)

commit v4 on v3

--- a/solution.py
+++ b/solution.py
@@ -169,6 +169,8 @@
     tokens, features = rounds[0][0].shape
     pieces = [piece for one in rounds for piece in one]
     turns = len(rounds)
+    per_round = len(rounds[0])
+    half = tokens // 2
     dtype = weights_own[0].dtype
 
     def body(places_ref, gains_ref, *refs):
@@ -191,13 +193,16 @@
                         )
                     )
             for turn in range(turns):
-                here.append(
-                    pltpu.make_async_copy(
-                        piece_refs[turn * slabs + slab],
-                        rows.at[slab, pl.ds(turn * tokens, tokens)],
-                        row_sems.at[slab, turn],
+                for which in [slab] if slab < slabs - 1 else [slab, slab + 1]:
+                    first = turn * tokens + max(which - slabs + 1, 0) * half
+                    count = tokens if slab < slabs - 1 else half
+                    here.append(
+                        pltpu.make_async_copy(
+                            piece_refs[turn * per_round + which],
+                            rows.at[slab, pl.ds(first, count)],
+                            row_sems.at[which, turn],
+                        )
                     )
-                )
             for copy in here:
                 copy.start()
             copies.append(here)
@@ -242,7 +247,7 @@
             pltpu.VMEM((slabs, turns * tokens, features), dtype),
             pltpu.VMEM((turns * tokens, heads * columns), jnp.float32),
             pltpu.SemaphoreType.DMA((slabs, heads, 2)),
-            pltpu.SemaphoreType.DMA((slabs, turns)),
+            pltpu.SemaphoreType.DMA((per_round, turns)),
         ],
         compiler_params=pltpu.CompilerParams(vmem_limit_bytes=VMEM_BYTES),
         name="project_heads",
@@ -341,17 +346,16 @@
     )(key_slots, counts, query_slots, group_most, *queries, *kv_own, *kv_other)
 
 
-def out_blocks(which, sign, attended, out_weight, dtype, blocks):
+def out_blocks(which, sign, attended, out_weight, dtypes, blocks):
     groups, _, tokens, _ = attended[0].shape
     sizes = [one.shape[1] for one in attended]
     count = len(attended)
     depth, features = out_weight.shape
     width = features // blocks
-    tile = 2 * HEAD_DIM
-    steps = width // tile
+    wanted = len(dtypes)
 
     def body(which_ref, sign_ref, *refs):
-        parts, weight_ref, out_ref = refs[:count], refs[count], refs[count + 1]
+        parts, weight_ref, out_refs = refs[:count], refs[count], refs[count + 1 :]
         columns = []
         for group in range(groups):
             for chunk in range(count):
@@ -359,21 +363,38 @@
                     columns.append(parts[chunk][group, head])
         joined = jnp.concatenate(columns, axis=1)
         total = jnp.dot(joined, weight_ref[...], preferred_element_type=jnp.float32)
-        out_ref[...] = (total * sign_ref[0].astype(jnp.float32)).astype(dtype)
+        total = total * sign_ref[0].astype(jnp.float32)
+        for at in range(wanted):
+
+            @pl.when(pl.program_id(0) == at)
+            def _(at=at):
+                out_refs[at][...] = total.astype(dtypes[at])
 
     return pl.pallas_call(
         body,
         grid_spec=pltpu.PrefetchScalarGridSpec(
             num_scalar_prefetch=2,
-            grid=(steps,),
+            grid=(wanted,),
             in_specs=[pl.BlockSpec(one.shape, lambda i, w, s: (0, 0, 0, 0)) for one in attended]
-            + [pl.BlockSpec((depth, tile), lambda i, w, s: (0, w[0] * steps + i))],
-            out_specs=pl.BlockSpec((tokens, tile), lambda i, w, s: (0, i)),
+            + [pl.BlockSpec((depth, width), lambda i, w, s: (0, w[i]))],
+            out_specs=[pl.BlockSpec((tokens, width), lambda i, w, s: (0, 0))] * wanted,
         ),
-        out_shape=jax.ShapeDtypeStruct((tokens, width), dtype),
+        out_shape=[jax.ShapeDtypeStruct((tokens, width), dtype) for dtype in dtypes],
         compiler_params=pltpu.CompilerParams(vmem_limit_bytes=VMEM_BYTES),
         name="out_blocks",
     )(which, sign, *attended, out_weight)
+
+
+def nearest(chips):
+    order = [
+        sorted((at for at in range(chips) if at != here), key=lambda at: (abs(at - here), at))
+        for here in range(chips)
+    ]
+    turns = [
+        [0 if at == here else order[here].index(at) + 1 for at in range(chips)]
+        for here in range(chips)
+    ]
+    return order, turns
 
 
 def chunk_sizes(heads):
@@ -402,17 +423,24 @@
     features = gen_weight.shape[1]
     all_blocks = chips * local_blocks
     swap = [(0, 1), (1, 0)]
-    upward = [(at, (at + 1) % chips) for at in range(chips)]
-    downward = [((at + 1) % chips, at) for at in range(chips)]
-
-    def turn_of(behind):
-        return jnp.where(behind <= chips // 2, jnp.maximum(2 * behind - 1, 0), 2 * (chips - behind))
+    order, turns = nearest(chips)
+    turn_here = jnp.asarray(turns, dtype=jnp.int32)[chip]
+
+    def pick(index, options):
+        picked = options[0]
+        for at in range(1, len(options)):
+            picked = jnp.where(index == at, options[at], picked)
+        return picked
+
+    def turn_of(other):
+        return pick(other, [turn_here[at] for at in range(chips)])
 
     def exchange(array):
         return lax.all_to_all(array, "chip", split_axis=0, concat_axis=0, tiled=True)
 
     weight_here = qkv_weight[0]
     cuts = [cut_columns(weight_here, chips, at) for at in range(heads)]
+    hidden_rows, cuts[0] = lax.optimization_barrier((hidden_rows, cuts[0]))
     weights_own = [exchange(cuts[0])]
 
     mine = role * lax.axis_size("head") + head
@@ -430,46 +458,72 @@
     normed = (noisy * lax.rsqrt(squares / width + 1e-06)[:, :, None]).astype(jnp.bfloat16)
     normed = normed.reshape(tokens, features)
 
-    shards = [normed]
-    up = down = normed
-    for at in range(1, chips):
-        if at % 2 == 1:
-            up = lax.ppermute(up, "chip", upward)
-            shards.append(up)
-        else:
-            down = lax.ppermute(down, "chip", downward)
-            shards.append(down)
+    lists = jnp.concatenate([block_keys, block_count[:, :, None]], axis=2)
+    half = tokens // 2
     rounds = []
-    for at, shard in enumerate(shards):
-        over_role = lax.ppermute(shard, "role", swap)
-        over_head = lax.ppermute(shard, "head", swap)
-        if at % 2 == 0:
-            diagonal = lax.ppermute(over_head, "role", swap)
-        else:
-            diagonal = lax.ppermute(over_role, "head", swap)
-        rounds.append((shard, over_role, over_head, diagonal))
-
-    lists = jnp.concatenate([block_keys, block_count[:, :, None]], axis=2)
-    lists, _ = lax.optimization_barrier((lists, normed))
-    lists = lax.all_gather(lists, "chip", axis=1, tiled=True)
-    lists = lax.dynamic_slice_in_dim(lists, chip * heads, heads, axis=0)
-
-    for at in range(1, heads):
-        if at == 1:
-            held, _ = lax.optimization_barrier((cuts[at], (lists, shards[1:3])))
-        else:
-            held, _ = lax.optimization_barrier((cuts[at], weights_own[-1]))
-        weights_own.append(exchange(held))
+    straight = None
+    shard, up, down = normed, normed, normed
+    ups, downs = [None], [None]
+    gathered = [lists]
+    for phase in range(chips + 1):
+        sent = {}
+        if phase < chips:
+            sent["role"] = lax.ppermute(shard, "role", swap)
+            sent["head"] = lax.ppermute(shard, "head", swap)
+        if straight is not None:
+            sent["first"] = lax.ppermute(straight[2][:half], "role", swap)
+            sent["second"] = lax.ppermute(straight[1][half:], "head", swap)
+        step = phase + 1
+        if step < chips:
+            sent["up"] = lax.ppermute(
+                up, "chip", [(at, at + 1) for at in range(step - 1, chips - 1)]
+            )
+            sent["down"] = lax.ppermute(
+                down, "chip", [(at + 1, at) for at in range(chips - step)]
+            )
+        if phase == 1:
+            for shift in range(1, chips):
+                pairs = [(at, (at + shift) % chips) for at in range(chips)]
+                sent["lists" + str(shift)] = lax.ppermute(lists, "chip", pairs)
+        if phase == 0:
+            sent["weights"] = weights_own.pop()
+        sent, (shard, straight) = lax.optimization_barrier((sent, (shard, straight)))
+        if phase == 0:
+            weights_own.append(sent["weights"])
+        if phase == 1:
+            gathered += [sent["lists" + str(shift)] for shift in range(1, chips)]
+        if straight is not None:
+            rounds.append(straight + (sent["first"], sent["second"]))
+        if phase < chips:
+            straight = (shard, sent["role"], sent["head"])
+        if step < chips:
+            up, down = sent["up"], sent["down"]
+            ups.append(up)
+            downs.append(down)
+            options = []
+            for here in range(chips):
+                source = order[here][step - 1]
+                options.append(ups[here - source] if source < here else downs[source - here])
+            shard = pick(chip, options)
+        if phase % 2 == 0 and len(weights_own) < heads:
+            held, _ = lax.optimization_barrier((cuts[len(weights_own)], sent))
+            weights_own.append(exchange(held))
+    while len(weights_own) < heads:
+        weights_own.append(exchange(cuts[len(weights_own)]))
     weights_other = [lax.ppermute(one, "core", swap) for one in weights_own]
 
+    gathered = [lax.dynamic_slice_in_dim(one, chip * heads, heads, axis=0) for one in gathered]
+    lists = jnp.concatenate(
+        [pick((chip - at) % chips, gathered) for at in range(chips)], axis=1
+    )
     owner = lists[:, :, :most] // local_blocks
-    turn = turn_of((chip - owner // CORES) % chips)
+    turn = turn_of(owner // CORES)
     far = (owner % CORES != core).astype(jnp.int32)
     key_slots = far * all_blocks + turn * local_blocks + lists[:, :, :most] % local_blocks
     counts = lists[:, :, most]
     group_most = jnp.max(counts.reshape(heads, chips, local_blocks), axis=2)
     spot = jnp.arange(all_blocks, dtype=jnp.int32)
-    query_slots = turn_of((chip - spot // local_blocks) % chips)
+    query_slots = turn_of(spot // local_blocks)
     query_slots = query_slots * local_blocks + spot % local_blocks
 
     sides = lax.axis_size("head")
@@ -517,14 +571,17 @@
     sign = (2 * role - 1).astype(jnp.int32)[None]
     blocks = sides * lax.axis_size("role")
 
-    def block_of(at, dtype):
-        return out_blocks(peers[at : at + 1], sign, attended, out_weight[0], dtype, blocks)
+    def blocks_of(first, second, dtypes):
+        which = jnp.stack([peers[first], peers[second]])
+        return out_blocks(which, sign, attended, out_weight[0], dtypes, blocks)
 
     far_swap = [(0, 3), (1, 2), (2, 1), (3, 0)]
-    from_diagonal = lax.ppermute(block_of(3, jnp.bfloat16), ("role", "head"), far_swap)
-    from_role = lax.ppermute(block_of(1, jnp.bfloat16), "role", swap)
-    from_head = lax.ppermute(block_of(2, jnp.bfloat16), "head", swap)
-    return block_of(0, jnp.float32) + (
+    diagonal, over_head = blocks_of(3, 2, (jnp.bfloat16, jnp.bfloat16))
+    over_role, own = blocks_of(1, 0, (jnp.bfloat16, jnp.float32))
+    from_diagonal = lax.ppermute(diagonal, ("role", "head"), far_swap)
+    from_head = lax.ppermute(over_head, "head", swap)
+    from_role = lax.ppermute(over_role, "role", swap)
+    return own + (
         from_role.astype(jnp.float32)
         + from_head.astype(jnp.float32)
         + from_diagonal.astype(jnp.float32)

time: 439 us -> 407 us (0.927)
  blocking collectives: 45.6 us -> 0 us
  starting transfers between devices: 59.3 us -> 97.7 us
  waiting for transfers between devices: 204 us -> 167 us
  other arithmetic: 5.06 us -> 19.2 us
  Pallas kernels: 98.8 us -> 88.3 us
  local copies, waits for them, and re-layouts: 13 us -> 20.7 us
    all_to_all x5, waiting for transfers between devices: 86 us -> 16.1 us  [exchange(): lax.all_to_all(array, 'chip', split_axis=0, concat_axis=0, tiled=True)]
    all_gather x1 -> x0, blocking collectives: 45.6 us -> none  [per_device_by_heads(): lists = lax.all_gather(lists, 'chip', axis=1, tiled=True)]
    ppermute x18 -> x28, waiting for transfers between devices: 114 us -> 147 us  [the longest x4 62.2 us: per_device_by_heads(): sent['second'] = lax.ppermute(straight[1][half:], 'head', swap)]
    ppermute x18 -> x28, starting transfers between devices: 24.5 us -> 54.6 us  [the longest x3 15.9 us: per_device_by_heads(): sent['lists' + str(shift)] = lax.ppermute(lists, 'chip', pairs)]
    all_to_all x5, starting transfers between devices: 28.9 us -> 38.2 us  [exchange(): lax.all_to_all(array, 'chip', split_axis=0, concat_axis=0, tiled=True)]
    pallas_call x4 -> x2, Pallas kernels: 24.6 us -> 16.3 us  [out_blocks(): pl.pallas_call(body, grid_spec=pltpu.PrefetchScalarGridSpec(num_scalar_pr...]
    slice x0 -> x9, local copies, waits for them, and re-layouts: none -> 7.56 us  [the longest x4 4.77 us: per_device_by_heads(): sent['second'] = lax.ppermute(straight[1][half:], 'head', swap)]
    select_n x0 -> x5, other arithmetic: none -> 7.21 us  [pick(): picked = jnp.where(index == at, options[at], picked)]
  transfers between devices with their start and end apart: 31 -> 41, of which waited for: 14 -> 18; matrix products, arithmetic and copies ran while one was open for 2% -> 11% of each run, Pallas kernels for 21% -> 19%
where the time goes in v4:
time: 407 us; the launch traced here: 406 us
  waiting for transfers between devices  167 us (41%)
  starting transfers between devices  97.7 us (24%)
  Pallas kernels  88.3 us (22%)
  local copies, waits for them, and re-layouts  20.7 us (5%)
  other arithmetic  19.2 us (5%)
  matrix products  12.8 us (3%)
    ppermute x4, waiting for transfers between devices, per_device_by_heads(): sent['second'] = lax.ppermute(straight[1][half:], 'head', swap)  62.2 us
    pallas_call x3, Pallas kernels, project_heads(): pl.pallas_call(body, in_specs=[in_smem(), in_smem()] + [in_hbm()] * (2 *...  45 us
    all_to_all x5, starting transfers between devices, exchange(): lax.all_to_all(array, 'chip', split_axis=0, concat_axis=0, tiled=True)  38.2 us
    ppermute x3, waiting for transfers between devices, per_device_by_heads(): lax.ppermute(down, 'chip', [(at + 1, at) for at in range(chips - step)])  33 us
    ppermute x1, waiting for transfers between devices, per_device_by_heads(): from_head = lax.ppermute(over_head, 'head', swap)  19.1 us
    ppermute x4, waiting for transfers between devices, per_device_by_heads(): sent['first'] = lax.ppermute(straight[2][:half], 'role', swap)  18.3 us
    pallas_call x2, Pallas kernels, out_blocks(): pl.pallas_call(body, grid_spec=pltpu.PrefetchScalarGridSpec(num_scalar_pr...  16.3 us
    all_to_all x5, waiting for transfers between devices, exchange(): lax.all_to_all(array, 'chip', split_axis=0, concat_axis=0, tiled=True)  16.1 us
  transfers between devices with their start and end apart: 41, of which 18 were waited for; matrix products, arithmetic and copies ran while one was open for 11% of the time, Pallas kernels for 19%

profile of v4, /device:TPU:0, one launch (start us, length us, event | category | flops | bytes accessed | tf_op | source)
XLA Modules:
  0.0 406.3 jit_solution(17694044490479998165)
XLA Ops:
  3.8 6.4 %all-to-all-start = ((bf16[4,640,384]{2,1,0:T(8,128)(2,1)}), bf16[4,640,384]{2,1,0:T(8,128)(2,1)S(1)}, u32[]{:S(2)}, u32[]{:S(2)}) async-start(bf16[4,640,384]{2,1,0:T(8,128)(2,1)} %cut_columns.3), calls=%async_computation | async-start | bytes 3932160 | tf_op jit(solution)/shard_map/all_to_all | solution.py:439
  10.6 12.8 %multiply_reduce_fusion = (f32[384]{0:T(512)S(1)}, f32[384,1280]{1,0:T(8,128)}) fusion(bf16[384,5120]{1,0:T(8,128)(2,1)} %param.12, s32[]{:T(128)S(6)} %select_n.207, f32[384]{0:T(512)S(1)} %mul.87, bf16[384,5120]{1,0:T(8,128)(2,1)} %param.10, bf16[5120,1280]{1,0:T(8,128)(2,1)} %param.11, f32[384]{0:T(512)S(1)} %mul.83), kind=kOutput, calls=%fused_computation.5 | convolution fusion | flops 5036604928 | bytes 19993092 | tf_op jit(solution)/shard_map/dot_general | solution.py:447
  36.8 5.5 %collective-permute-start.5 = (bf16[384,1280]{1,0:T(8,128)(2,1)S(1)}, bf16[384,1280]{1,0:T(8,128)(2,1)}, u32[]{:S(2)}, u32[]{:S(2)}) collective-permute-start(bf16[384,1280]{1,0:T(8,128)(2,1)S(1)} %multiply_convert_fusion.refs_4_.refs_2_), channel_id=1, source_target_pairs={{0,4},{4,8},{8,12},{1,5},{5,9},{9,13},{2,6},{6,10},{10,14},{3,7},{... | collective-permute-start | bytes 2949128 | tf_op jit(solution)/shard_map/ppermute | solution.py:478
  48.1 18.1 %collective-permute-done.2 = bf16[384,1280]{1,0:T(8,128)(2,1)} collective-permute-done((bf16[384,1280]{1,0:T(8,128)(2,1)S(1)}, bf16[384,1280]{1,0:T(8,128)(2,1)}, u32[]{:S(2)}, u32[]{:S(2)}) %collective-permute-start.2) | collective-permute-done | bytes 983072 | tf_op jit(solution)/shard_map/ppermute | solution.py:481
  66.2 11.3 %collective-permute-start.10 = (s32[12,6,9]{2,1,0:T(8,128)}, s32[12,6,9]{2,1,0:T(8,128)}, u32[]{:S(2)}, u32[]{:S(2)}) collective-permute-start(s32[12,6,9]{2,1,0:T(8,128)} %pad_add_fusion), channel_id=1, source_target_pairs={{0,8},{4,12},{8,0},{12,4},{1,9},{5,13},{9,1},{13,5},{2,10},{6,14},... | collective-permute-start | bytes 7784 | tf_op jit(solution)/shard_map/ppermute | solution.py:487
  99.2 24.1 %collective-permute-done.13.refs_8_.refs_6_ = bf16[192,1280]{1,0:T(8,128)(2,1)S(1)} collective-permute-done((bf16[192,1280]{1,0:T(8,128)(2,1)S(1)}, bf16[192,1280]{1,0:T(8,128)(2,1)S(1)}, u32[]{:S(2)}, u32[]{:S(2)}) %collective-permute-start.13) | collective-permute-done | bytes 491552 | tf_op jit(solution)/shard_map/ppermute | solution.py:475
  133.4 5.6 %collective-permute-done.18.refs_12_.refs_10_ = bf16[192,1280]{1,0:T(8,128)(2,1)} collective-permute-done((bf16[192,1280]{1,0:T(8,128)(2,1)S(1)}, bf16[192,1280]{1,0:T(8,128)(2,1)}, u32[]{:S(2)}, u32[]{:S(2)}) %collective-permute-start.18) | collective-permute-done | bytes 491552 | tf_op jit(solution)/shard_map/ppermute | solution.py:474
  144.3 15.0 %collective-permute-done.21.refs_13_.refs_11_ = bf16[192,1280]{1,0:T(8,128)(2,1)} collective-permute-done((bf16[192,1280]{1,0:T(8,128)(2,1)}, bf16[192,1280]{1,0:T(8,128)(2,1)}, u32[]{:S(2)}, u32[]{:S(2)}) %collective-permute-start.21) | collective-permute-done | bytes 491552 | tf_op jit(solution)/shard_map/ppermute | solution.py:475
  159.3 14.9 %collective-permute-done.17 = bf16[384,1280]{1,0:T(8,128)(2,1)} collective-permute-done((bf16[384,1280]{1,0:T(8,128)(2,1)}, bf16[384,1280]{1,0:T(8,128)(2,1)}, u32[]{:S(2)}, u32[]{:S(2)}) %collective-permute-start.17) | collective-permute-done | bytes 983072 | tf_op jit(solution)/shard_map/ppermute | solution.py:481
  174.3 18.8 %all-to-all-start.3 = ((bf16[4,640,384]{2,1,0:T(8,128)(2,1)}), bf16[4,640,384]{2,1,0:T(8,128)(2,1)}, u32[]{:S(2)}, u32[]{:S(2)}) async-start(bf16[4,640,384]{2,1,0:T(8,128)(2,1)} %cut_columns.5), calls=%async_computation.3 | async-start | bytes 3932160 | tf_op jit(solution)/shard_map/all_to_all | solution.py:439
  200.6 7.2 %collective-permute-done.23.refs_17_.refs_15_ = bf16[192,1280]{1,0:T(8,128)(2,1)S(1)} collective-permute-done((bf16[192,1280]{1,0:T(8,128)(2,1)S(1)}, bf16[192,1280]{1,0:T(8,128)(2,1)S(1)}, u32[]{:S(2)}, u32[]{:S(2)}) %collective-permute-start.23) | collective-permute-done | bytes 491552 | tf_op jit(solution)/shard_map/ppermute | solution.py:474
  210.0 20.8 %collective-permute-done.26.refs_18_.refs_16_ = bf16[192,1280]{1,0:T(8,128)(2,1)} collective-permute-done((bf16[192,1280]{1,0:T(8,128)(2,1)}, bf16[192,1280]{1,0:T(8,128)(2,1)}, u32[]{:S(2)}, u32[]{:S(2)}) %collective-permute-start.26) | collective-permute-done | bytes 491552 | tf_op jit(solution)/shard_map/ppermute | solution.py:475
  230.8 4.6 %all-to-all-done.3.refs_0_ = bf16[4,640,384]{2,1,0:T(8,128)(2,1)} async-done(((bf16[4,640,384]{2,1,0:T(8,128)(2,1)}), bf16[4,640,384]{2,1,0:T(8,128)(2,1)}, u32[]{:S(2)}, u32[]{:S(2)}) %all-to-all-start.3) | async-done | bytes 1966112 | tf_op jit(solution)/shard_map/all_to_all | solution.py:439
  236.1 19.1 %project_heads.3 = (bf16[2,3,384,128]{3,2,1,0:T(8,128)(2,1)}, bf16[2,2,3,384,128]{4,3,2,1,0:T(8,128)(2,1)}) custom-call(s32[5]{0:T(128)} %concatenate.11.places_ref, f32[2,2]{1,0:T(2,128)} %bitcast.49, bf16[4,640,384]{2,1,0:T(8,128)(2,1)} %copy-done.2, bf16[4,640,384]{2,1,0:T(8,128)(2,1)} %all-to-all-done.1.refs_1_, ...), custom_call_target="tpu_custom_call" | custom-call | tf_op jit(solution)/shard_map/project_heads/pallas_call | solution.py:237
  274.5 9.7 %project_heads.4 = (bf16[2,1,384,128]{3,2,1,0:T(8,128)(2,1)}, bf16[2,2,1,384,128]{4,3,2,1,0:T(8,128)(2,1)}) custom-call(s32[5]{0:T(128)} %concatenate.11.places_ref, f32[2,2]{1,0:T(2,128)} %bitcast.50, bf16[4,640,384]{2,1,0:T(8,128)(2,1)} %copy-done.2, bf16[4,640,384]{2,1,0:T(8,128)(2,1)} %all-to-all-done.1.refs_1_, ...), custom_call_target="tpu_custom_call" | custom-call | tf_op jit(solution)/shard_map/project_heads/pallas_call | solution.py:237
  290.3 9.8 %attend.2 = bf16[2,24,64,128]{3,2,1,0:T(8,128)(2,1)} custom-call(s32[2,24,8]{2,1,0:T(8,128)} %slice.109.slots_ref, s32[2,24]{1,0:T(2,128)} %slice_reduce_fusion.1.counts_ref, s32[24]{0:T(128)} %fusion.10.from_ref, s32[2,4]{1,0:T(2,128)} %slice.95.most_ref, bf16[2,18,64,128]{3,2,1,0:T(8,128)(2,1)} %bitcast.44, bf16[2,6,64,128]{3,2,1,0:T(8,128)(2,1)} %bitcast.48, ...), custom_call_target="tpu_custom_call" | custom-call | tf_op jit(solution)/shard_map/attend/pallas_call | solution.py:333
  306.4 16.1 %project_heads.5 = (bf16[1,4,384,128]{3,2,1,0:T(8,128)(2,1)}, bf16[1,2,4,384,128]{4,3,2,1,0:T(8,128)(2,1)}) custom-call(s32[5]{0:T(128)} %concatenate.11.places_ref, f32[2,1]{1,0:T(2,128)} %slice.107.gains_ref, bf16[4,640,384]{2,1,0:T(8,128)(2,1)} %all-to-all-done.3.refs_0_, bf16[4,640,384]{2,1,0:T(8,128)(2,1)} %collective-permute-done.31.refs_1_, ...), custom_call_target="tpu_custom_call" | custom-call | tf_op jit(solution)/shard_map/project_heads/pallas_call | solution.py:237
  326.1 6.0 %attend.3 = bf16[1,24,64,128]{3,2,1,0:T(8,128)(2,1)} custom-call(s32[1,24,8]{2,1,0:T(8,128)} %slice.112.slots_ref, s32[1,24]{1,0:T(1,128)} %bitcast.52, s32[24]{0:T(128)} %fusion.10.from_ref, s32[1,4]{1,0:T(1,128)} %slice.106.most_ref, bf16[1,24,64,128]{3,2,1,0:T(8,128)(2,1)} %bitcast.45, bf16[1,2,24,64,128]{4,3,2,1,0:T(8,128)(2,1)} %bitcast.43, ...), custom_call_target="tpu_custom_call" | custom-call | tf_op jit(solution)/shard_map/attend/pallas_call | solution.py:333
  332.1 4.9 %all-to-all-start.4 = ((bf16[4,1,384,128]{3,2,1,0:T(8,128)(2,1)}), bf16[4,1,384,128]{3,2,1,0:T(8,128)(2,1)S(1)}, u32[]{:S(2)}, u32[]{:S(2)}) async-start(bf16[4,1,384,128]{3,2,1,0:T(8,128)(2,1)} %bitcast.39), calls=%async_computation.4 | async-start | bytes 786432 | tf_op jit(solution)/shard_map/all_to_all | solution.py:439
  337.6 11.5 %all-to-all-done.4.refs_1_ = bf16[4,1,384,128]{3,2,1,0:T(8,128)(2,1)S(1)} async-done(((bf16[4,1,384,128]{3,2,1,0:T(8,128)(2,1)}), bf16[4,1,384,128]{3,2,1,0:T(8,128)(2,1)S(1)}, u32[]{:S(2)}, u32[]{:S(2)}) %all-to-all-start.4) | async-done | bytes 393248 | tf_op jit(solution)/shard_map/all_to_all | solution.py:439
  349.9 8.0 %out_blocks.3 = (bf16[384,1280]{1,0:T(8,128)(2,1)}, bf16[384,1280]{1,0:T(8,128)(2,1)}) custom-call(s32[2]{0:T(128)} %get-tuple-element.135.which_ref, s32[1]{0:T(128)} %bitcast.2.sign_ref, bf16[4,2,384,128]{3,2,1,0:T(8,128)(2,1)} %copy-done.6, bf16[4,1,384,128]{3,2,1,0:T(8,128)(2,1)} %copy-done.10, bf16[1536,5120]{1,0:T(8,128)(2,1)} %bitcast.33), custom_call_target="tpu_custom_call" | custom-call | tf_op jit(solution)/shard_map/out_blocks/pallas_call | solution.py:373
  359.8 8.3 %out_blocks.2 = (bf16[384,1280]{1,0:T(8,128)(2,1)}, f32[384,1280]{1,0:T(8,128)}) custom-call(s32[2]{0:T(128)} %get-tuple-element.134.which_ref, s32[1]{0:T(128)} %bitcast.2.sign_ref, bf16[4,2,384,128]{3,2,1,0:T(8,128)(2,1)} %copy-done.6, bf16[4,1,384,128]{3,2,1,0:T(8,128)(2,1)} %copy-done.10, bf16[1536,5120]{1,0:T(8,128)(2,1)} %bitcast.34), custom_call_target="tpu_custom_call" | custom-call | tf_op jit(solution)/shard_map/out_blocks/pallas_call | solution.py:373
  369.7 14.0 %collective-permute-done.35 = bf16[384,1280]{1,0:T(8,128)(2,1)S(1)} collective-permute-done((bf16[384,1280]{1,0:T(8,128)(2,1)}, bf16[384,1280]{1,0:T(8,128)(2,1)S(1)}, u32[]{:S(2)}, u32[]{:S(2)}) %collective-permute-start.35) | collective-permute-done | bytes 983072 | tf_op jit(solution)/shard_map/ppermute | solution.py:581
  383.7 19.1 %collective-permute-done.34 = bf16[384,1280]{1,0:T(8,128)(2,1)S(1)} collective-permute-done((bf16[384,1280]{1,0:T(8,128)(2,1)}, bf16[384,1280]{1,0:T(8,128)(2,1)S(1)}, u32[]{:S(2)}, u32[]{:S(2)}) %collective-permute-start.34) | collective-permute-done | bytes 983072 | tf_op jit(solution)/shard_map/ppermute | solution.py:582
  (165 shorter events, 114.0 us)
Async XLA Ops:
  3.8 77.3 %all-to-all-start = ((bf16[4,640,384]{2,1,0:T(8,128)(2,1)}), bf16[4,640,384]{2,1,0:T(8,128)(2,1)S(1)}, u32[]{:S(2)}, u32[]{:S(2)}) async-start(bf16[4,640,384]{2,1,0:T(8,128)(2,1)} %cut_columns.3), calls=%async_computation | async-start | bytes 3932160 | tf_op jit(solution)/shard_map/all_to_all | solution.py:439
  32.4 33.8 %collective-permute-start.2 = (bf16[384,1280]{1,0:T(8,128)(2,1)S(1)}, bf16[384,1280]{1,0:T(8,128)(2,1)}, u32[]{:S(2)}, u32[]{:S(2)}) collective-permute-start(bf16[384,1280]{1,0:T(8,128)(2,1)S(1)} %multiply_convert_fusion.refs_4_.refs_2_), channel_id=1, source_target_pairs={{4,0},{8,4},{12,8},{5,1},{9,5},{13,9},{6,2},{10,6},{14,10},{7,3},{... | collective-permute-start | bytes 2949128 | tf_op jit(solution)/shard_map/ppermute | solution.py:481
  33.7 43.8 %collective-permute-start.3 = (bf16[384,1280]{1,0:T(8,128)(2,1)S(1)}, bf16[384,1280]{1,0:T(8,128)(2,1)}, u32[]{:S(2)}, u32[]{:S(2)}) collective-permute-start(bf16[384,1280]{1,0:T(8,128)(2,1)S(1)} %multiply_convert_fusion.refs_4_.refs_2_), channel_id=1, source_target_pairs={{0,1},{1,0},{2,3},{3,2},{4,5},{5,4},{6,7},{7,6},{8,9},{9,8},{10,11... | collective-permute-start | bytes 2949128 | tf_op jit(solution)/shard_map/ppermute | solution.py:472
  35.5 45.6 %collective-permute-start.4 = (bf16[384,1280]{1,0:T(8,128)(2,1)S(1)}, bf16[384,1280]{1,0:T(8,128)(2,1)}, u32[]{:S(2)}, u32[]{:S(2)}) collective-permute-start(bf16[384,1280]{1,0:T(8,128)(2,1)S(1)} %multiply_convert_fusion.refs_4_.refs_2_), channel_id=1, source_target_pairs={{0,16},{16,0},{1,17},{17,1},{2,18},{18,2},{3,19},{19,3},{4,20},{20... | collective-permute-start | bytes 2949128 | tf_op jit(solution)/shard_map/ppermute | solution.py:471
  36.8 44.3 %collective-permute-start.5 = (bf16[384,1280]{1,0:T(8,128)(2,1)S(1)}, bf16[384,1280]{1,0:T(8,128)(2,1)}, u32[]{:S(2)}, u32[]{:S(2)}) collective-permute-start(bf16[384,1280]{1,0:T(8,128)(2,1)S(1)} %multiply_convert_fusion.refs_4_.refs_2_), channel_id=1, source_target_pairs={{0,4},{4,8},{8,12},{1,5},{5,9},{9,13},{2,6},{6,10},{10,14},{3,7},{... | collective-permute-start | bytes 2949128 | tf_op jit(solution)/shard_map/ppermute | solution.py:478
  43.3 47.8 %collective-permute-start.9 = (s32[12,6,9]{2,1,0:T(8,128)}, s32[12,6,9]{2,1,0:T(8,128)}, u32[]{:S(2)}, u32[]{:S(2)}) collective-permute-start(s32[12,6,9]{2,1,0:T(8,128)} %pad_add_fusion), channel_id=1, source_target_pairs={{0,4},{4,8},{8,12},{12,0},{1,5},{5,9},{9,13},{13,1},{2,6},{6,10},{... | collective-permute-start | bytes 7784 | tf_op jit(solution)/shard_map/ppermute | solution.py:487
  81.1 42.2 %collective-permute-start.6 = (bf16[384,1280]{1,0:T(8,128)(2,1)}, bf16[384,1280]{1,0:T(8,128)(2,1)}, u32[]{:S(2)}, u32[]{:S(2)}) collective-permute-start(bf16[384,1280]{1,0:T(8,128)(2,1)} %collective-permute-done.2), channel_id=1, source_target_pairs={{4,0},{8,4},{5,1},{9,5},{6,2},{10,6},{7,3},{11,7},{20,16},{24,20},... | collective-permute-start | bytes 2949128 | tf_op jit(solution)/shard_map/ppermute | solution.py:481
  85.0 89.3 %all-to-all-start.1 = ((bf16[4,640,384]{2,1,0:T(8,128)(2,1)}), bf16[4,640,384]{2,1,0:T(8,128)(2,1)}, u32[]{:S(2)}, u32[]{:S(2)}) async-start(bf16[4,640,384]{2,1,0:T(8,128)(2,1)} %cut_columns.4), calls=%async_computation.1 | async-start | bytes 3932160 | tf_op jit(solution)/shard_map/all_to_all | solution.py:439
  91.1 32.2 %collective-permute-start.8 = (bf16[384,1280]{1,0:T(8,128)(2,1)S(1)}, bf16[384,1280]{1,0:T(8,128)(2,1)S(1)}, u32[]{:S(2)}, u32[]{:S(2)}) collective-permute-start(bf16[384,1280]{1,0:T(8,128)(2,1)S(1)} %select_select_fusion.1.refs_9_.refs_7_), channel_id=1, source_target_pairs={{0,1},{1,0},{2,3},{3,2},{4,5},{5,4},{6,7},{7,6},{8,9},{9,8},{10,11... | collective-permute-start | bytes 2949128 | tf_op jit(solution)/shard_map/ppermute | solution.py:472
  92.7 30.7 %collective-permute-start.12 = (bf16[384,1280]{1,0:T(8,128)(2,1)S(1)}, bf16[384,1280]{1,0:T(8,128)(2,1)S(1)}, u32[]{:S(2)}, u32[]{:S(2)}) collective-permute-start(bf16[384,1280]{1,0:T(8,128)(2,1)S(1)} %select_select_fusion.1.refs_9_.refs_7_), channel_id=1, source_target_pairs={{0,16},{16,0},{1,17},{17,1},{2,18},{18,2},{3,19},{19,3},{4,20},{20... | collective-permute-start | bytes 2949128 | tf_op jit(solution)/shard_map/ppermute | solution.py:471
  93.2 30.1 %collective-permute-start.14 = (bf16[384,1280]{1,0:T(8,128)(2,1)}, bf16[384,1280]{1,0:T(8,128)(2,1)}, u32[]{:S(2)}, u32[]{:S(2)}) collective-permute-start(bf16[384,1280]{1,0:T(8,128)(2,1)} %collective-permute-done.5), channel_id=1, source_target_pairs={{4,8},{8,12},{5,9},{9,13},{6,10},{10,14},{7,11},{11,15},{20,24},{2... | collective-permute-start | bytes 2949128 | tf_op jit(solution)/shard_map/ppermute | solution.py:478
  123.4 50.9 %collective-permute-start.17 = (bf16[384,1280]{1,0:T(8,128)(2,1)}, bf16[384,1280]{1,0:T(8,128)(2,1)}, u32[]{:S(2)}, u32[]{:S(2)}) collective-permute-start(bf16[384,1280]{1,0:T(8,128)(2,1)} %collective-permute-done.6), channel_id=1, source_target_pairs={{4,0},{5,1},{6,2},{7,3},{20,16},{21,17},{22,18},{23,19}} | collective-permute-start | bytes 2949128 | tf_op jit(solution)/shard_map/ppermute | solution.py:481
  128.0 46.3 %collective-permute-start.19 = (bf16[384,1280]{1,0:T(8,128)(2,1)}, bf16[384,1280]{1,0:T(8,128)(2,1)S(1)}, u32[]{:S(2)}, u32[]{:S(2)}) collective-permute-start(bf16[384,1280]{1,0:T(8,128)(2,1)} %fusion.2.refs_14_.refs_12_), channel_id=1, source_target_pairs={{0,1},{1,0},{2,3},{3,2},{4,5},{5,4},{6,7},{7,6},{8,9},{9,8},{10,11... | collective-permute-start | bytes 2949128 | tf_op jit(solution)/shard_map/ppermute | solution.py:472
  129.5 44.8 %collective-permute-start.20 = (bf16[384,1280]{1,0:T(8,128)(2,1)}, bf16[384,1280]{1,0:T(8,128)(2,1)}, u32[]{:S(2)}, u32[]{:S(2)}) collective-permute-start(bf16[384,1280]{1,0:T(8,128)(2,1)} %fusion.2.refs_14_.refs_12_), channel_id=1, source_target_pairs={{0,16},{16,0},{1,17},{17,1},{2,18},{18,2},{3,19},{19,3},{4,20},{20... | collective-permute-start | bytes 2949128 | tf_op jit(solution)/shard_map/ppermute | solution.py:471
  131.0 43.3 %collective-permute-start.22 = (bf16[384,1280]{1,0:T(8,128)(2,1)}, bf16[384,1280]{1,0:T(8,128)(2,1)}, u32[]{:S(2)}, u32[]{:S(2)}) collective-permute-start(bf16[384,1280]{1,0:T(8,128)(2,1)} %collective-permute-done.14), channel_id=1, source_target_pairs={{8,12},{9,13},{10,14},{11,15},{24,28},{25,29},{26,30},{27,31}} | collective-permute-start | bytes 2949128 | tf_op jit(solution)/shard_map/ppermute | solution.py:478
  174.3 61.1 %all-to-all-start.3 = ((bf16[4,640,384]{2,1,0:T(8,128)(2,1)}), bf16[4,640,384]{2,1,0:T(8,128)(2,1)}, u32[]{:S(2)}, u32[]{:S(2)}) async-start(bf16[4,640,384]{2,1,0:T(8,128)(2,1)} %cut_columns.5), calls=%async_computation.3 | async-start | bytes 3932160 | tf_op jit(solution)/shard_map/all_to_all | solution.py:439
  193.1 42.9 %collective-permute-start.15 = (bf16[4,640,384]{2,1,0:T(8,128)(2,1)S(1)}, bf16[4,640,384]{2,1,0:T(8,128)(2,1)}, u32[]{:S(2)}, u32[]{:S(2)}) collective-permute-start(bf16[4,640,384]{2,1,0:T(8,128)(2,1)S(1)} %all-to-all-done.refs_0_), channel_id=1, source_target_pairs={{0,2},{2,0},{1,3},{3,1},{4,6},{6,4},{5,7},{7,5},{8,10},{10,8},{9,1... | collective-permute-start | bytes 5898248 | tf_op jit(solution)/shard_map/ppermute | solution.py:513
  193.1 42.9 %collective-permute-start.16 = (bf16[4,640,384]{2,1,0:T(8,128)(2,1)}, bf16[4,640,384]{2,1,0:T(8,128)(2,1)}, u32[]{:S(2)}, u32[]{:S(2)}) collective-permute-start(bf16[4,640,384]{2,1,0:T(8,128)(2,1)} %all-to-all-done.1.refs_1_), channel_id=1, source_target_pairs={{0,2},{2,0},{1,3},{3,1},{4,6},{6,4},{5,7},{7,5},{8,10},{10,8},{9,1... | collective-permute-start | bytes 5898248 | tf_op jit(solution)/shard_map/ppermute | solution.py:513
  196.6 39.4 %collective-permute-start.24 = (bf16[384,1280]{1,0:T(8,128)(2,1)S(1)}, bf16[384,1280]{1,0:T(8,128)(2,1)}, u32[]{:S(2)}, u32[]{:S(2)}) collective-permute-start(bf16[384,1280]{1,0:T(8,128)(2,1)S(1)} %select_select_fusion.2.refs_4_.refs_17_), channel_id=1, source_target_pairs={{0,1},{1,0},{2,3},{3,2},{4,5},{5,4},{6,7},{7,6},{8,9},{9,8},{10,11... | collective-permute-start | bytes 2949128 | tf_op jit(solution)/shard_map/ppermute | solution.py:472
  198.2 37.8 %collective-permute-start.25 = (bf16[384,1280]{1,0:T(8,128)(2,1)S(1)}, bf16[384,1280]{1,0:T(8,128)(2,1)}, u32[]{:S(2)}, u32[]{:S(2)}) collective-permute-start(bf16[384,1280]{1,0:T(8,128)(2,1)S(1)} %select_select_fusion.2.refs_4_.refs_17_), channel_id=1, source_target_pairs={{0,16},{16,0},{1,17},{17,1},{2,18},{18,2},{3,19},{19,3},{4,20},{20... | collective-permute-start | bytes 2949128 | tf_op jit(solution)/shard_map/ppermute | solution.py:471
  235.4 71.0 %collective-permute-start.31 = (bf16[4,640,384]{2,1,0:T(8,128)(2,1)}, bf16[4,640,384]{2,1,0:T(8,128)(2,1)}, u32[]{:S(2)}, u32[]{:S(2)}) collective-permute-start(bf16[4,640,384]{2,1,0:T(8,128)(2,1)} %all-to-all-done.3.refs_0_), channel_id=1, source_target_pairs={{0,2},{2,0},{1,3},{3,1},{4,6},{6,4},{5,7},{7,5},{8,10},{10,8},{9,1... | collective-permute-start | bytes 5898248 | tf_op jit(solution)/shard_map/ppermute | solution.py:513
  255.2 33.9 %collective-permute-start.29 = (bf16[2,2,18,64,128]{4,3,2,1,0:T(8,128)(2,1)}, bf16[2,2,18,64,128]{4,3,2,1,0:T(8,128)(2,1)S(1)}, u32[]{:S(2)}, u32[]{:S(2)}) collective-permute-start(bf16[2,2,18,64,128]{4,3,2,1,0:T(8,128)(2,1)} %bitcast.40), channel_id=1, source_target_pairs={{0,2},{2,0},{1,3},{3,1},{4,6},{6,4},{5,7},{7,5},{8,10},{10,8},{9,1... | collective-permute-start | bytes 3538952 | tf_op jit(solution)/shard_map/ppermute | solution.py:556
  359.3 43.5 %collective-permute-start.34 = (bf16[384,1280]{1,0:T(8,128)(2,1)}, bf16[384,1280]{1,0:T(8,128)(2,1)S(1)}, u32[]{:S(2)}, u32[]{:S(2)}) collective-permute-start(bf16[384,1280]{1,0:T(8,128)(2,1)} %get-tuple-element.119), channel_id=1, source_target_pairs={{0,1},{1,0},{2,3},{3,2},{4,5},{5,4},{6,7},{7,6},{8,9},{9,8},{10,11... | collective-permute-start | bytes 2949128 | tf_op jit(solution)/shard_map/ppermute | solution.py:582
  368.2 34.7 %collective-permute-start.33 = (bf16[384,1280]{1,0:T(8,128)(2,1)}, bf16[384,1280]{1,0:T(8,128)(2,1)S(1)}, u32[]{:S(2)}, u32[]{:S(2)}) collective-permute-start(bf16[384,1280]{1,0:T(8,128)(2,1)} %get-tuple-element.118), channel_id=1, source_target_pairs={{0,16},{16,0},{1,17},{17,1},{2,18},{18,2},{3,19},{19,3},{4,20},{20... | collective-permute-start | bytes 2949128 | tf_op jit(solution)/shard_map/ppermute | solution.py:583
  (42 other events, 926.6 us)

commit v5 on v4

--- a/solution.py
+++ b/solution.py
@@ -465,14 +465,18 @@
     shard, up, down = normed, normed, normed
     ups, downs = [None], [None]
     gathered = [lists]
+    late = None
     for phase in range(chips + 1):
         sent = {}
         if phase < chips:
             sent["role"] = lax.ppermute(shard, "role", swap)
             sent["head"] = lax.ppermute(shard, "head", swap)
+        diagonal = None
         if straight is not None:
-            sent["first"] = lax.ppermute(straight[2][:half], "role", swap)
-            sent["second"] = lax.ppermute(straight[1][half:], "head", swap)
+            diagonal = straight + (
+                lax.ppermute(straight[2][:half], "role", swap),
+                lax.ppermute(straight[1][half:], "head", swap),
+            )
         step = phase + 1
         if step < chips:
             sent["up"] = lax.ppermute(
@@ -481,19 +485,19 @@
             sent["down"] = lax.ppermute(
                 down, "chip", [(at + 1, at) for at in range(chips - step)]
             )
-        if phase == 1:
+        if phase == chips - 1:
             for shift in range(1, chips):
                 pairs = [(at, (at + shift) % chips) for at in range(chips)]
-                sent["lists" + str(shift)] = lax.ppermute(lists, "chip", pairs)
+                gathered.append(lax.ppermute(lists, "chip", pairs))
         if phase == 0:
             sent["weights"] = weights_own.pop()
-        sent, (shard, straight) = lax.optimization_barrier((sent, (shard, straight)))
+        if phase < chips:
+            sent, shard, late = lax.optimization_barrier((sent, shard, late))
         if phase == 0:
             weights_own.append(sent["weights"])
-        if phase == 1:
-            gathered += [sent["lists" + str(shift)] for shift in range(1, chips)]
-        if straight is not None:
-            rounds.append(straight + (sent["first"], sent["second"]))
+        if late is not None:
+            rounds.append(late)
+        late = diagonal
         if phase < chips:
             straight = (shard, sent["role"], sent["head"])
         if step < chips:
@@ -505,9 +509,10 @@
                 source = order[here][step - 1]
                 options.append(ups[here - source] if source < here else downs[source - here])
             shard = pick(chip, options)
-        if phase % 2 == 0 and len(weights_own) < heads:
+        if 1 <= phase < chips - 1 and len(weights_own) < heads:
             held, _ = lax.optimization_barrier((cuts[len(weights_own)], sent))
             weights_own.append(exchange(held))
+    rounds.append(late)
     while len(weights_own) < heads:
         weights_own.append(exchange(cuts[len(weights_own)]))
     weights_other = [lax.ppermute(one, "core", swap) for one in weights_own]
@@ -538,15 +543,15 @@
     places = jnp.concatenate([peers, core[None].astype(jnp.int32)])
     gains = lax.dynamic_slice_in_dim(qk_gain[0], chip * heads, heads, axis=1)
 
-    attended = []
-    held_places = places
     chunks = chunk_sizes(heads)
-    for at, size in enumerate(chunks):
-        span = slice(sum(chunks[:at]), sum(chunks[: at + 1]))
-        last = at == len(chunks) - 1
-        parts = [rounds] if last else [rounds[:-1], rounds[-1:]]
-        queries, kv_own, kv_other = [], [], []
-        for part in parts:
+    spans = [slice(sum(chunks[:at]), sum(chunks[: at + 1])) for at in range(len(chunks))]
+    middle = (chips + 1) // 2
+    projected = [([], [], []) for _ in chunks]
+    tables = (key_slots, counts, query_slots, group_most)
+    held_places, tables = lax.optimization_barrier((places, tables))
+    key_slots, counts, query_slots, group_most = tables
+    for part in (rounds[:middle], rounds[middle:]):
+        for span, size, (queries, kv_own, kv_other) in zip(spans, chunks, projected):
             query, kv = project_heads(
                 held_places, gains[:, span], part, weights_own[span], weights_other[span]
             )
@@ -555,16 +560,13 @@
             kv_own.append(kv.reshape(size, 2, here, BLOCK, HEAD_DIM))
             kv_other.append(lax.ppermute(kv_own[-1], "core", swap))
             held_places, _ = lax.optimization_barrier((places, kv))
+    attended = []
+    held = counts
+    for span, size, (queries, kv_own, kv_other) in zip(spans, chunks, projected):
         mixed = attend(
-            key_slots[span],
-            counts[span],
-            query_slots,
-            group_most[span],
-            queries,
-            kv_own,
-            kv_other,
+            key_slots[span], held[span], query_slots, group_most[span], queries, kv_own, kv_other
         )
-        held_places, _ = lax.optimization_barrier((places, mixed))
+        held, _ = lax.optimization_barrier((counts, mixed))
         mixed = mixed.reshape(size, chips, tokens, HEAD_DIM).transpose(1, 0, 2, 3)
         attended.append(exchange(mixed))
 

time: 407 us -> 433 us (1.064)
  waiting for transfers between devices: 167 us -> 213 us
  starting transfers between devices: 97.7 us -> 62.9 us
  local copies, waits for them, and re-layouts: 20.7 us -> 28.5 us
    ppermute x3, waiting for transfers between devices: 33 us -> 58.7 us  [per_device_by_heads(): lax.ppermute(down, 'chip', [(at + 1, at) for at in range(chips - step)])]
    ppermute x4, waiting for transfers between devices: 0.01 us -> 20 us  [per_device_by_heads(): sent['head'] = lax.ppermute(shard, 'head', swap)]
    all_to_all x5, starting transfers between devices: 38.2 us -> 20.6 us  [exchange(): lax.all_to_all(array, 'chip', split_axis=0, concat_axis=0, tiled=True)]
    ppermute x11, starting transfers between devices: 28.3 us -> 10.9 us  [the longest x3 4.96 us: per_device_by_heads(): gathered.append(lax.ppermute(lists, 'chip', pairs))]
    ppermute x1, waiting for transfers between devices: 14 us -> 0.01 us  [per_device_by_heads(): from_diagonal = lax.ppermute(diagonal, ('role', 'head'), far_swap)]
    ppermute x1, waiting for transfers between devices: 19.1 us -> 32 us  [per_device_by_heads(): from_head = lax.ppermute(over_head, 'head', swap)]
    ppermute x11, waiting for transfers between devices: 80.5 us -> 67.7 us  [the longest x3 38 us: per_device_by_heads(): gathered.append(lax.ppermute(lists, 'chip', pairs))]
    all_to_all x5, waiting for transfers between devices: 16.1 us -> 27.6 us  [exchange(): lax.all_to_all(array, 'chip', split_axis=0, concat_axis=0, tiled=True)]
  transfers between devices with their start and end apart: 41 -> 42, of which waited for: 18 -> 18; matrix products, arithmetic and copies ran while one was open for 11% -> 11% of each run, Pallas kernels for 19% -> 17%
where the time goes in v5:
time: 433 us; the launch traced here: 430 us
  waiting for transfers between devices  213 us (49%)
  Pallas kernels  91.8 us (21%)
  starting transfers between devices  62.9 us (15%)
  local copies, waits for them, and re-layouts  28.5 us (7%)
  other arithmetic  20.5 us (5%)
  matrix products  12.7 us (3%)
    ppermute x3, waiting for transfers between devices, per_device_by_heads(): lax.ppermute(down, 'chip', [(at + 1, at) for at in range(chips - step)])  58.7 us
    pallas_call x4, Pallas kernels, project_heads(): pl.pallas_call(body, in_specs=[in_smem(), in_smem()] + [in_hbm()] * (2 *...  45.7 us
    ppermute x3, waiting for transfers between devices, per_device_by_heads(): gathered.append(lax.ppermute(lists, 'chip', pairs))  38 us
    ppermute x1, waiting for transfers between devices, per_device_by_heads(): from_head = lax.ppermute(over_head, 'head', swap)  32 us
    all_to_all x5, waiting for transfers between devices, exchange(): lax.all_to_all(array, 'chip', split_axis=0, concat_axis=0, tiled=True)  27.6 us
    ppermute x4, waiting for transfers between devices, per_device_by_heads(): lax.ppermute(straight[1][half:], 'head', swap)  24.6 us
    all_to_all x5, starting transfers between devices, exchange(): lax.all_to_all(array, 'chip', split_axis=0, concat_axis=0, tiled=True)  20.6 us
    ppermute x4, waiting for transfers between devices, per_device_by_heads(): sent['head'] = lax.ppermute(shard, 'head', swap)  20 us
  transfers between devices with their start and end apart: 42, of which 18 were waited for; matrix products, arithmetic and copies ran while one was open for 11% of the time, Pallas kernels for 17%

profile of v5, /device:TPU:0, one launch (start us, length us, event | category | flops | bytes accessed | tf_op | source)
XLA Modules:
  0.0 429.7 jit_solution(15395198589839788857)
XLA Ops:
  3.8 6.4 %all-to-all-start = ((bf16[4,640,384]{2,1,0:T(8,128)(2,1)}), bf16[4,640,384]{2,1,0:T(8,128)(2,1)S(1)}, u32[]{:S(2)}, u32[]{:S(2)}) async-start(bf16[4,640,384]{2,1,0:T(8,128)(2,1)} %cut_columns.3), calls=%async_computation | async-start | bytes 3932160 | tf_op jit(solution)/shard_map/all_to_all | solution.py:439
  10.6 12.7 %multiply_reduce_fusion = (f32[384]{0:T(512)S(1)}, f32[384,1280]{1,0:T(8,128)}) fusion(bf16[384,5120]{1,0:T(8,128)(2,1)} %param.12, s32[]{:T(128)S(6)} %select_n.247, f32[384]{0:T(512)S(1)} %mul.92, bf16[384,5120]{1,0:T(8,128)(2,1)} %param.10, bf16[5120,1280]{1,0:T(8,128)(2,1)} %param.11, f32[384]{0:T(512)S(1)} %mul.88), kind=kOutput, calls=%fused_computation.5 | convolution fusion | flops 5036604928 | bytes 19993092 | tf_op jit(solution)/shard_map/dot_general | solution.py:447
  36.8 5.5 %collective-permute-start.8 = (bf16[384,1280]{1,0:T(8,128)(2,1)S(1)}, bf16[384,1280]{1,0:T(8,128)(2,1)}, u32[]{:S(2)}, u32[]{:S(2)}) collective-permute-start(bf16[384,1280]{1,0:T(8,128)(2,1)S(1)} %multiply_convert_fusion.refs_4_.refs_2_), channel_id=1, source_target_pairs={{0,4},{4,8},{8,12},{1,5},{5,9},{9,13},{2,6},{6,10},{10,14},{3,7},{... | collective-permute-start | bytes 2949128 | tf_op jit(solution)/shard_map/ppermute | solution.py:482
  42.3 23.7 %collective-permute-done.5 = bf16[384,1280]{1,0:T(8,128)(2,1)} collective-permute-done((bf16[384,1280]{1,0:T(8,128)(2,1)S(1)}, bf16[384,1280]{1,0:T(8,128)(2,1)}, u32[]{:S(2)}, u32[]{:S(2)}) %collective-permute-start.5) | collective-permute-done | bytes 983072 | tf_op jit(solution)/shard_map/ppermute | solution.py:485
  79.0 11.8 %collective-permute-done.10.refs_11_.refs_9_ = bf16[384,1280]{1,0:T(8,128)(2,1)} collective-permute-done((bf16[384,1280]{1,0:T(8,128)(2,1)}, bf16[384,1280]{1,0:T(8,128)(2,1)}, u32[]{:S(2)}, u32[]{:S(2)}) %collective-permute-start.10) | collective-permute-done | bytes 983072 | tf_op jit(solution)/shard_map/ppermute | solution.py:473
  92.1 16.9 %collective-permute-done.9 = bf16[384,1280]{1,0:T(8,128)(2,1)} collective-permute-done((bf16[384,1280]{1,0:T(8,128)(2,1)}, bf16[384,1280]{1,0:T(8,128)(2,1)}, u32[]{:S(2)}, u32[]{:S(2)}) %collective-permute-start.9) | collective-permute-done | bytes 983072 | tf_op jit(solution)/shard_map/ppermute | solution.py:485
  122.8 5.1 %collective-permute-done.19.refs_7_.refs_5_ = bf16[192,1280]{1,0:T(8,128)(2,1)S(1)} collective-permute-done((bf16[192,1280]{1,0:T(8,128)(2,1)S(1)}, bf16[192,1280]{1,0:T(8,128)(2,1)S(1)}, u32[]{:S(2)}, u32[]{:S(2)}) %collective-permute-start.19) | collective-permute-done | bytes 491552 | tf_op jit(solution)/shard_map/ppermute | solution.py:477
  132.2 15.0 %collective-permute-done.20.refs_8_.refs_6_ = bf16[192,1280]{1,0:T(8,128)(2,1)} collective-permute-done((bf16[192,1280]{1,0:T(8,128)(2,1)}, bf16[192,1280]{1,0:T(8,128)(2,1)}, u32[]{:S(2)}, u32[]{:S(2)}) %collective-permute-start.20) | collective-permute-done | bytes 491552 | tf_op jit(solution)/shard_map/ppermute | solution.py:478
  147.2 18.1 %collective-permute-done.15 = bf16[384,1280]{1,0:T(8,128)(2,1)} collective-permute-done((bf16[384,1280]{1,0:T(8,128)(2,1)}, bf16[384,1280]{1,0:T(8,128)(2,1)}, u32[]{:S(2)}, u32[]{:S(2)}) %collective-permute-start.15) | collective-permute-done | bytes 983072 | tf_op jit(solution)/shard_map/ppermute | solution.py:485
  179.8 22.8 %collective-permute-done = s32[12,6,9]{2,1,0:T(8,128)S(1)} collective-permute-done((s32[12,6,9]{2,1,0:T(8,128)S(1)}, s32[12,6,9]{2,1,0:T(8,128)S(1)}, u32[]{:S(2)}, u32[]{:S(2)}) %collective-permute-start) | collective-permute-done | bytes 2624 | tf_op jit(solution)/shard_map/ppermute | solution.py:491
  203.2 15.1 %collective-permute-done.1 = s32[12,6,9]{2,1,0:T(8,128)S(1)} collective-permute-done((s32[12,6,9]{2,1,0:T(8,128)S(1)}, s32[12,6,9]{2,1,0:T(8,128)S(1)}, u32[]{:S(2)}, u32[]{:S(2)}) %collective-permute-start.1) | collective-permute-done | bytes 2624 | tf_op jit(solution)/shard_map/ppermute | solution.py:491
  223.2 9.6 %collective-permute-done.24.refs_13_.refs_11_ = bf16[192,1280]{1,0:T(8,128)(2,1)} collective-permute-done((bf16[192,1280]{1,0:T(8,128)(2,1)}, bf16[192,1280]{1,0:T(8,128)(2,1)}, u32[]{:S(2)}, u32[]{:S(2)}) %collective-permute-start.24) | collective-permute-done | bytes 491552 | tf_op jit(solution)/shard_map/ppermute | solution.py:478
  243.7 8.2 %collective-permute-done.21.refs_11_.refs_9_ = bf16[384,1280]{1,0:T(8,128)(2,1)} collective-permute-done((bf16[384,1280]{1,0:T(8,128)(2,1)S(1)}, bf16[384,1280]{1,0:T(8,128)(2,1)}, u32[]{:S(2)}, u32[]{:S(2)}) %collective-permute-start.21) | collective-permute-done | bytes 983072 | tf_op jit(solution)/shard_map/ppermute | solution.py:473
  263.6 14.2 %project_heads.4 = (bf16[2,2,384,128]{3,2,1,0:T(8,128)(2,1)}, bf16[2,2,2,384,128]{4,3,2,1,0:T(8,128)(2,1)}) custom-call(s32[5]{0:T(128)} %concatenate.9.places_ref, f32[2,2]{1,0:T(2,128)} %bitcast.53, bf16[4,640,384]{2,1,0:T(8,128)(2,1)} %copy-done.3, bf16[4,640,384]{2,1,0:T(8,128)(2,1)} %copy-done.4, bf16[4,640,384]{2,1,0:T(8,128)(2,1)} %collective-permute-done.13.refs_2_, ...), custom_call_target="tpu_custom_call" | custom-call | tf_op jit(solution)/shard_map/project_heads/pallas_call | solution.py:237
  278.0 8.5 %project_heads.5 = (bf16[1,2,384,128]{3,2,1,0:T(8,128)(2,1)}, bf16[1,2,2,384,128]{4,3,2,1,0:T(8,128)(2,1)}) custom-call(s32[5]{0:T(128)} %concatenate.9.places_ref, f32[2,1]{1,0:T(2,128)} %slice.91.gains_ref, bf16[4,640,384]{2,1,0:T(8,128)(2,1)} %copy-done.2, bf16[4,640,384]{2,1,0:T(8,128)(2,1)} %collective-permute-done.25.refs_1_, ...), custom_call_target="tpu_custom_call" | custom-call | tf_op jit(solution)/shard_map/project_heads/pallas_call | solution.py:237
  288.1 14.5 %project_heads.6 = (bf16[2,2,384,128]{3,2,1,0:T(8,128)(2,1)}, bf16[2,2,2,384,128]{4,3,2,1,0:T(8,128)(2,1)}) custom-call(s32[5]{0:T(128)} %concatenate.9.places_ref, f32[2,2]{1,0:T(2,128)} %bitcast.54, bf16[4,640,384]{2,1,0:T(8,128)(2,1)} %copy-done.3, bf16[4,640,384]{2,1,0:T(8,128)(2,1)} %copy-done.4, bf16[4,640,384]{2,1,0:T(8,128)(2,1)} %collective-permute-done.13.refs_2_, ...), custom_call_target="tpu_custom_call" | custom-call | tf_op jit(solution)/shard_map/project_heads/pallas_call | solution.py:237
  303.2 8.5 %project_heads.7 = (bf16[1,2,384,128]{3,2,1,0:T(8,128)(2,1)}, bf16[1,2,2,384,128]{4,3,2,1,0:T(8,128)(2,1)}) custom-call(s32[5]{0:T(128)} %concatenate.9.places_ref, f32[2,1]{1,0:T(2,128)} %slice.91.gains_ref, bf16[4,640,384]{2,1,0:T(8,128)(2,1)} %copy-done.2, bf16[4,640,384]{2,1,0:T(8,128)(2,1)} %collective-permute-done.25.refs_1_, ...), custom_call_target="tpu_custom_call" | custom-call | tf_op jit(solution)/shard_map/project_heads/pallas_call | solution.py:237
  316.4 11.6 %attend.2 = bf16[2,24,64,128]{3,2,1,0:T(8,128)(2,1)} custom-call(s32[2,24,8]{2,1,0:T(8,128)} %slice.83.slots_ref, s32[2,24]{1,0:T(2,128)} %slice.84.counts_ref, s32[24]{0:T(128)} %fusion.10.from_ref, s32[2,4]{1,0:T(2,128)} %slice.85.most_ref, bf16[2,12,64,128]{3,2,1,0:T(8,128)(2,1)} %bitcast.47, bf16[2,12,64,128]{3,2,1,0:T(8,128)(2,1)} %bitcast.50, ...), custom_call_target="tpu_custom_call" | custom-call | tf_op jit(solution)/shard_map/attend/pallas_call | solution.py:333
  329.4 6.9 %attend.3 = bf16[1,24,64,128]{3,2,1,0:T(8,128)(2,1)} custom-call(s32[1,24,8]{2,1,0:T(8,128)} %slice.96.slots_ref, s32[1,24]{1,0:T(1,128)} %slice.97.counts_ref, s32[24]{0:T(128)} %fusion.10.from_ref, s32[1,4]{1,0:T(1,128)} %slice.98.most_ref, bf16[1,12,64,128]{3,2,1,0:T(8,128)(2,1)} %bitcast.51, bf16[1,12,64,128]{3,2,1,0:T(8,128)(2,1)} %bitcast.52, ...), custom_call_target="tpu_custom_call" | custom-call | tf_op jit(solution)/shard_map/attend/pallas_call | solution.py:333
  340.8 10.0 %all-to-all-done.4.refs_1_ = bf16[4,1,384,128]{3,2,1,0:T(8,128)(2,1)S(1)} async-done(((bf16[4,1,384,128]{3,2,1,0:T(8,128)(2,1)}), bf16[4,1,384,128]{3,2,1,0:T(8,128)(2,1)S(1)}, u32[]{:S(2)}, u32[]{:S(2)}) %all-to-all-start.4) | async-done | bytes 393248 | tf_op jit(solution)/shard_map/all_to_all | solution.py:439
  354.8 17.6 %all-to-all-done.3.refs_0_ = bf16[4,2,384,128]{3,2,1,0:T(8,128)(2,1)S(1)} async-done(((bf16[4,2,384,128]{3,2,1,0:T(8,128)(2,1)}), bf16[4,2,384,128]{3,2,1,0:T(8,128)(2,1)S(1)}, u32[]{:S(2)}, u32[]{:S(2)}) %all-to-all-start.3) | async-done | bytes 786464 | tf_op jit(solution)/shard_map/all_to_all | solution.py:439
  373.3 8.0 %out_blocks.3 = (bf16[384,1280]{1,0:T(8,128)(2,1)}, bf16[384,1280]{1,0:T(8,128)(2,1)}) custom-call(s32[2]{0:T(128)} %get-tuple-element.127.which_ref, s32[1]{0:T(128)} %bitcast.2.sign_ref, bf16[4,2,384,128]{3,2,1,0:T(8,128)(2,1)} %copy-done.8, bf16[4,1,384,128]{3,2,1,0:T(8,128)(2,1)} %copy-done.9, bf16[1536,5120]{1,0:T(8,128)(2,1)} %bitcast.34), custom_call_target="tpu_custom_call" | custom-call | tf_op jit(solution)/shard_map/out_blocks/pallas_call | solution.py:373
  383.6 8.3 %out_blocks.2 = (bf16[384,1280]{1,0:T(8,128)(2,1)}, f32[384,1280]{1,0:T(8,128)}) custom-call(s32[2]{0:T(128)} %get-tuple-element.126.which_ref, s32[1]{0:T(128)} %bitcast.2.sign_ref, bf16[4,2,384,128]{3,2,1,0:T(8,128)(2,1)} %copy-done.8, bf16[4,1,384,128]{3,2,1,0:T(8,128)(2,1)} %copy-done.9, bf16[1536,5120]{1,0:T(8,128)(2,1)} %bitcast.35), custom_call_target="tpu_custom_call" | custom-call | tf_op jit(solution)/shard_map/out_blocks/pallas_call | solution.py:373
  393.1 32.0 %collective-permute-done.35 = bf16[384,1280]{1,0:T(8,128)(2,1)S(1)} collective-permute-done((bf16[384,1280]{1,0:T(8,128)(2,1)}, bf16[384,1280]{1,0:T(8,128)(2,1)S(1)}, u32[]{:S(2)}, u32[]{:S(2)}) %collective-permute-start.35) | collective-permute-done | bytes 983072 | tf_op jit(solution)/shard_map/ppermute | solution.py:584
  (172 shorter events, 118.1 us)
Async XLA Ops:
  3.8 62.2 %all-to-all-start = ((bf16[4,640,384]{2,1,0:T(8,128)(2,1)}), bf16[4,640,384]{2,1,0:T(8,128)(2,1)S(1)}, u32[]{:S(2)}, u32[]{:S(2)}) async-start(bf16[4,640,384]{2,1,0:T(8,128)(2,1)} %cut_columns.3), calls=%async_computation | async-start | bytes 3932160 | tf_op jit(solution)/shard_map/all_to_all | solution.py:439
  32.4 33.6 %collective-permute-start.5 = (bf16[384,1280]{1,0:T(8,128)(2,1)S(1)}, bf16[384,1280]{1,0:T(8,128)(2,1)}, u32[]{:S(2)}, u32[]{:S(2)}) collective-permute-start(bf16[384,1280]{1,0:T(8,128)(2,1)S(1)} %multiply_convert_fusion.refs_4_.refs_2_), channel_id=1, source_target_pairs={{4,0},{8,4},{12,8},{5,1},{9,5},{13,9},{6,2},{10,6},{14,10},{7,3},{... | collective-permute-start | bytes 2949128 | tf_op jit(solution)/shard_map/ppermute | solution.py:485
  33.7 32.3 %collective-permute-start.6 = (bf16[384,1280]{1,0:T(8,128)(2,1)S(1)}, bf16[384,1280]{1,0:T(8,128)(2,1)}, u32[]{:S(2)}, u32[]{:S(2)}) collective-permute-start(bf16[384,1280]{1,0:T(8,128)(2,1)S(1)} %multiply_convert_fusion.refs_4_.refs_2_), channel_id=1, source_target_pairs={{0,1},{1,0},{2,3},{3,2},{4,5},{5,4},{6,7},{7,6},{8,9},{9,8},{10,11... | collective-permute-start | bytes 2949128 | tf_op jit(solution)/shard_map/ppermute | solution.py:473
  35.4 30.6 %collective-permute-start.7 = (bf16[384,1280]{1,0:T(8,128)(2,1)S(1)}, bf16[384,1280]{1,0:T(8,128)(2,1)}, u32[]{:S(2)}, u32[]{:S(2)}) collective-permute-start(bf16[384,1280]{1,0:T(8,128)(2,1)S(1)} %multiply_convert_fusion.refs_4_.refs_2_), channel_id=1, source_target_pairs={{0,16},{16,0},{1,17},{17,1},{2,18},{18,2},{3,19},{19,3},{4,20},{20... | collective-permute-start | bytes 2949128 | tf_op jit(solution)/shard_map/ppermute | solution.py:472
  73.9 35.1 %collective-permute-start.9 = (bf16[384,1280]{1,0:T(8,128)(2,1)}, bf16[384,1280]{1,0:T(8,128)(2,1)}, u32[]{:S(2)}, u32[]{:S(2)}) collective-permute-start(bf16[384,1280]{1,0:T(8,128)(2,1)} %collective-permute-done.5), channel_id=1, source_target_pairs={{4,0},{8,4},{5,1},{9,5},{6,2},{10,6},{7,3},{11,7},{20,16},{24,20},... | collective-permute-start | bytes 2949128 | tf_op jit(solution)/shard_map/ppermute | solution.py:485
  109.0 56.3 %all-to-all-start.1 = ((bf16[4,640,384]{2,1,0:T(8,128)(2,1)}), bf16[4,640,384]{2,1,0:T(8,128)(2,1)S(1)}, u32[]{:S(2)}, u32[]{:S(2)}) async-start(bf16[4,640,384]{2,1,0:T(8,128)(2,1)} %cut_columns.4), calls=%async_computation.1 | async-start | bytes 3932160 | tf_op jit(solution)/shard_map/all_to_all | solution.py:439
  115.9 31.3 %collective-permute-start.16 = (bf16[384,1280]{1,0:T(8,128)(2,1)S(1)}, bf16[384,1280]{1,0:T(8,128)(2,1)}, u32[]{:S(2)}, u32[]{:S(2)}) collective-permute-start(bf16[384,1280]{1,0:T(8,128)(2,1)S(1)} %fusion.2.refs_4_.refs_2_), channel_id=1, source_target_pairs={{0,1},{1,0},{2,3},{3,2},{4,5},{5,4},{6,7},{7,6},{8,9},{9,8},{10,11... | collective-permute-start | bytes 2949128 | tf_op jit(solution)/shard_map/ppermute | solution.py:473
  116.5 30.7 %collective-permute-start.17 = (bf16[384,1280]{1,0:T(8,128)(2,1)S(1)}, bf16[384,1280]{1,0:T(8,128)(2,1)}, u32[]{:S(2)}, u32[]{:S(2)}) collective-permute-start(bf16[384,1280]{1,0:T(8,128)(2,1)S(1)} %fusion.2.refs_4_.refs_2_), channel_id=1, source_target_pairs={{0,16},{16,0},{1,17},{17,1},{2,18},{18,2},{3,19},{19,3},{4,20},{20... | collective-permute-start | bytes 2949128 | tf_op jit(solution)/shard_map/ppermute | solution.py:472
  118.0 47.3 %collective-permute-start.15 = (bf16[384,1280]{1,0:T(8,128)(2,1)}, bf16[384,1280]{1,0:T(8,128)(2,1)}, u32[]{:S(2)}, u32[]{:S(2)}) collective-permute-start(bf16[384,1280]{1,0:T(8,128)(2,1)} %collective-permute-done.9), channel_id=1, source_target_pairs={{4,0},{5,1},{6,2},{7,3},{20,16},{21,17},{22,18},{23,19}} | collective-permute-start | bytes 2949128 | tf_op jit(solution)/shard_map/ppermute | solution.py:485
  119.3 46.0 %collective-permute-start.18 = (bf16[384,1280]{1,0:T(8,128)(2,1)}, bf16[384,1280]{1,0:T(8,128)(2,1)}, u32[]{:S(2)}, u32[]{:S(2)}) collective-permute-start(bf16[384,1280]{1,0:T(8,128)(2,1)} %collective-permute-done.12), channel_id=1, source_target_pairs={{8,12},{9,13},{10,14},{11,15},{24,28},{25,29},{26,30},{27,31}} | collective-permute-start | bytes 2949128 | tf_op jit(solution)/shard_map/ppermute | solution.py:482
  166.6 52.2 %all-to-all-start.2 = ((bf16[4,640,384]{2,1,0:T(8,128)(2,1)}), bf16[4,640,384]{2,1,0:T(8,128)(2,1)S(1)}, u32[]{:S(2)}, u32[]{:S(2)}) async-start(bf16[4,640,384]{2,1,0:T(8,128)(2,1)} %cut_columns.5), calls=%async_computation.2 | async-start | bytes 3932160 | tf_op jit(solution)/shard_map/all_to_all | solution.py:439
  170.2 86.7 %collective-permute-start.13 = (bf16[4,640,384]{2,1,0:T(8,128)(2,1)}, bf16[4,640,384]{2,1,0:T(8,128)(2,1)}, u32[]{:S(2)}, u32[]{:S(2)}) collective-permute-start(bf16[4,640,384]{2,1,0:T(8,128)(2,1)} %copy-done.3), channel_id=1, source_target_pairs={{0,2},{2,0},{1,3},{3,1},{4,6},{6,4},{5,7},{7,5},{8,10},{10,8},{9,1... | collective-permute-start | bytes 5898248 | tf_op jit(solution)/shard_map/ppermute | solution.py:518
  170.3 87.9 %collective-permute-start.14 = (bf16[4,640,384]{2,1,0:T(8,128)(2,1)}, bf16[4,640,384]{2,1,0:T(8,128)(2,1)}, u32[]{:S(2)}, u32[]{:S(2)}) collective-permute-start(bf16[4,640,384]{2,1,0:T(8,128)(2,1)} %copy-done.4), channel_id=1, source_target_pairs={{0,2},{2,0},{1,3},{3,1},{4,6},{6,4},{5,7},{7,5},{8,10},{10,8},{9,1... | collective-permute-start | bytes 5898248 | tf_op jit(solution)/shard_map/ppermute | solution.py:518
  171.1 31.5 %collective-permute-start = (s32[12,6,9]{2,1,0:T(8,128)S(1)}, s32[12,6,9]{2,1,0:T(8,128)S(1)}, u32[]{:S(2)}, u32[]{:S(2)}) collective-permute-start(s32[12,6,9]{2,1,0:T(8,128)S(1)} %pad_add_fusion), channel_id=1, source_target_pairs={{0,12},{4,0},{8,4},{12,8},{1,13},{5,1},{9,5},{13,9},{2,14},{6,2},{... | collective-permute-start | bytes 7784 | tf_op jit(solution)/shard_map/ppermute | solution.py:491
  175.0 43.3 %collective-permute-start.1 = (s32[12,6,9]{2,1,0:T(8,128)S(1)}, s32[12,6,9]{2,1,0:T(8,128)S(1)}, u32[]{:S(2)}, u32[]{:S(2)}) collective-permute-start(s32[12,6,9]{2,1,0:T(8,128)S(1)} %pad_add_fusion), channel_id=1, source_target_pairs={{0,8},{4,12},{8,0},{12,4},{1,9},{5,13},{9,1},{13,5},{2,10},{6,14},... | collective-permute-start | bytes 7784 | tf_op jit(solution)/shard_map/ppermute | solution.py:491
  175.0 43.8 %collective-permute-start.2 = (s32[12,6,9]{2,1,0:T(8,128)S(1)}, s32[12,6,9]{2,1,0:T(8,128)S(1)}, u32[]{:S(2)}, u32[]{:S(2)}) collective-permute-start(s32[12,6,9]{2,1,0:T(8,128)S(1)} %pad_add_fusion), channel_id=1, source_target_pairs={{0,4},{4,8},{8,12},{12,0},{1,5},{5,9},{9,13},{13,1},{2,6},{6,10},{... | collective-permute-start | bytes 7784 | tf_op jit(solution)/shard_map/ppermute | solution.py:491
  219.4 58.4 %collective-permute-start.25 = (bf16[4,640,384]{2,1,0:T(8,128)(2,1)S(1)}, bf16[4,640,384]{2,1,0:T(8,128)(2,1)}, u32[]{:S(2)}, u32[]{:S(2)}) collective-permute-start(bf16[4,640,384]{2,1,0:T(8,128)(2,1)S(1)} %all-to-all-done.2.refs_0_), channel_id=1, source_target_pairs={{0,2},{2,0},{1,3},{3,1},{4,6},{6,4},{5,7},{7,5},{8,10},{10,8},{9,1... | collective-permute-start | bytes 5898248 | tf_op jit(solution)/shard_map/ppermute | solution.py:518
  221.6 30.3 %collective-permute-start.21 = (bf16[384,1280]{1,0:T(8,128)(2,1)S(1)}, bf16[384,1280]{1,0:T(8,128)(2,1)}, u32[]{:S(2)}, u32[]{:S(2)}) collective-permute-start(bf16[384,1280]{1,0:T(8,128)(2,1)S(1)} %select_select_fusion.2.refs_9_.refs_7_), channel_id=1, source_target_pairs={{0,1},{1,0},{2,3},{3,2},{4,5},{5,4},{6,7},{7,6},{8,9},{9,8},{10,11... | collective-permute-start | bytes 2949128 | tf_op jit(solution)/shard_map/ppermute | solution.py:473
  251.9 34.6 %collective-permute-start.26 = (bf16[192,1280]{1,0:T(8,128)(2,1)}, bf16[192,1280]{1,0:T(8,128)(2,1)}, u32[]{:S(2)}, u32[]{:S(2)}) collective-permute-start(bf16[192,1280]{1,0:T(8,128)(2,1)} %slice.92), channel_id=1, source_target_pairs={{0,16},{16,0},{1,17},{17,1},{2,18},{18,2},{3,19},{19,3},{4,20},{20... | collective-permute-start | bytes 1474568 | tf_op jit(solution)/shard_map/ppermute | solution.py:477
  252.7 33.8 %collective-permute-start.27 = (bf16[192,1280]{1,0:T(8,128)(2,1)}, bf16[192,1280]{1,0:T(8,128)(2,1)}, u32[]{:S(2)}, u32[]{:S(2)}) collective-permute-start(bf16[192,1280]{1,0:T(8,128)(2,1)} %slice.93), channel_id=1, source_target_pairs={{0,1},{1,0},{2,3},{3,2},{4,5},{5,4},{6,7},{7,6},{8,9},{9,8},{10,11... | collective-permute-start | bytes 1474568 | tf_op jit(solution)/shard_map/ppermute | solution.py:478
  277.9 37.3 %collective-permute-start.30 = (bf16[2,2,12,64,128]{4,3,2,1,0:T(8,128)(2,1)}, bf16[2,2,12,64,128]{4,3,2,1,0:T(8,128)(2,1)S(1)}, u32[]{:S(2)}, u32[]{:S(2)}) collective-permute-start(bf16[2,2,12,64,128]{4,3,2,1,0:T(8,128)(2,1)} %bitcast.41), channel_id=1, source_target_pairs={{0,2},{2,0},{1,3},{3,1},{4,6},{6,4},{5,7},{7,5},{8,10},{10,8},{9,1... | collective-permute-start | bytes 2359304 | tf_op jit(solution)/shard_map/ppermute | solution.py:561
  381.3 43.8 %collective-permute-start.35 = (bf16[384,1280]{1,0:T(8,128)(2,1)}, bf16[384,1280]{1,0:T(8,128)(2,1)S(1)}, u32[]{:S(2)}, u32[]{:S(2)}) collective-permute-start(bf16[384,1280]{1,0:T(8,128)(2,1)} %get-tuple-element.111), channel_id=1, source_target_pairs={{0,1},{1,0},{2,3},{3,2},{4,5},{5,4},{6,7},{7,6},{8,9},{9,8},{10,11... | collective-permute-start | bytes 2949128 | tf_op jit(solution)/shard_map/ppermute | solution.py:584
  381.8 43.4 %collective-permute-start.36 = (bf16[384,1280]{1,0:T(8,128)(2,1)}, bf16[384,1280]{1,0:T(8,128)(2,1)S(1)}, u32[]{:S(2)}, u32[]{:S(2)}) collective-permute-start(bf16[384,1280]{1,0:T(8,128)(2,1)} %get-tuple-element.112), channel_id=1, source_target_pairs={{0,17},{1,16},{16,1},{17,0},{2,19},{3,18},{18,3},{19,2},{4,21},{5,... | collective-permute-start | bytes 2949128 | tf_op jit(solution)/shard_map/ppermute | solution.py:583
  391.9 34.5 %collective-permute-start.34 = (bf16[384,1280]{1,0:T(8,128)(2,1)}, bf16[384,1280]{1,0:T(8,128)(2,1)S(1)}, u32[]{:S(2)}, u32[]{:S(2)}) collective-permute-start(bf16[384,1280]{1,0:T(8,128)(2,1)} %get-tuple-element.110), channel_id=1, source_target_pairs={{0,16},{16,0},{1,17},{17,1},{2,18},{18,2},{3,19},{19,3},{4,20},{20... | collective-permute-start | bytes 2949128 | tf_op jit(solution)/shard_map/ppermute | solution.py:585
  (45 other events, 890.3 us)

commit v6 on v5

--- a/solution.py
+++ b/solution.py
@@ -171,13 +171,14 @@
     turns = len(rounds)
     per_round = len(rounds[0])
     half = tokens // 2
+    joint = 2 if slabs % 2 == 0 else 1
     dtype = weights_own[0].dtype
 
     def body(places_ref, gains_ref, *refs):
         own_refs, other_refs = refs[:heads], refs[heads : 2 * heads]
         piece_refs = refs[2 * heads : 2 * heads + len(pieces)]
         query_ref, kv_ref = refs[2 * heads + len(pieces) : 2 * heads + len(pieces) + 2]
-        table, rows, total, weight_sems, row_sems = refs[2 * heads + len(pieces) + 2 :]
+        table, rows, weight_sems, row_sems = refs[2 * heads + len(pieces) + 2 :]
         core = places_ref[slabs]
         copies = []
         for slab in range(slabs):
@@ -188,7 +189,13 @@
                     here.append(
                         pltpu.make_async_copy(
                             ref.at[places_ref[slab]],
-                            table.at[slab, place, :, pl.ds(head * columns, columns)],
+                            table.at[
+                                slab // joint,
+                                slab % joint,
+                                place,
+                                :,
+                                pl.ds(head * columns, columns),
+                            ],
                             weight_sems.at[slab, head, side],
                         )
                     )
@@ -199,29 +206,30 @@
                     here.append(
                         pltpu.make_async_copy(
                             piece_refs[turn * per_round + which],
-                            rows.at[slab, pl.ds(first, count)],
+                            rows.at[
+                                slab // joint,
+                                pl.ds(first, count),
+                                pl.ds(slab % joint * features, features),
+                            ],
                             row_sems.at[which, turn],
                         )
                     )
             for copy in here:
                 copy.start()
             copies.append(here)
-        for slab in range(slabs):
-            for copy in copies[slab]:
-                copy.wait()
+        total = None
+        for group in range(slabs // joint):
+            for slab in range(group * joint, (group + 1) * joint):
+                for copy in copies[slab]:
+                    copy.wait()
             part = jnp.dot(
-                rows[slab],
-                table[slab].reshape(CORES * depth, heads * columns),
+                rows[group],
+                table[group].reshape(joint * CORES * depth, heads * columns),
                 preferred_element_type=jnp.float32,
             )
-            if slab == 0:
-                total[...] = part
-            elif slab < slabs - 1:
-                total[...] += part
-            else:
-                part = total[...] + part
+            total = part if total is None else total + part
         for turn in range(turns):
-            here = part[turn * tokens : (turn + 1) * tokens]
+            here = total[turn * tokens : (turn + 1) * tokens]
             for head in range(heads):
                 at = head * columns
                 for which in range(2):
@@ -243,9 +251,8 @@
             jax.ShapeDtypeStruct((heads, 2, turns, tokens, HEAD_DIM), dtype),
         ),
         scratch_shapes=[
-            pltpu.VMEM((slabs, CORES, depth, heads * columns), dtype),
-            pltpu.VMEM((slabs, turns * tokens, features), dtype),
-            pltpu.VMEM((turns * tokens, heads * columns), jnp.float32),
+            pltpu.VMEM((slabs // joint, joint, CORES, depth, heads * columns), dtype),
+            pltpu.VMEM((slabs // joint, turns * tokens, joint * features), dtype),
             pltpu.SemaphoreType.DMA((slabs, heads, 2)),
             pltpu.SemaphoreType.DMA((per_round, turns)),
         ],
@@ -254,30 +261,30 @@
     )(places, gains, *weights_own, *weights_other, *pieces)
 
 
-def attend(key_slots, counts, query_slots, group_most, queries, kv_own, kv_other):
-    heads, blocks, most = key_slots.shape
+def attend(first_head, heads, key_slots, counts, query_slots, group_most, parts):
+    _, blocks, most = key_slots.shape
     groups = group_most.shape[1]
     together = blocks // groups
-    parts = len(queries)
-    sizes = [one.shape[1] for one in queries]
-    starts = [sum(sizes[:at]) for at in range(parts)]
     scale = 1.0 / math.sqrt(HEAD_DIM)
-    dtype = queries[0].dtype
+    dtype = parts[0][4].dtype
+    arrays = [array for part in parts for array in part[4:]]
 
     def body(slots_ref, counts_ref, from_ref, most_ref, *refs):
-        query_refs = refs[:parts]
-        own_refs = refs[parts : 2 * parts]
-        other_refs = refs[2 * parts : 3 * parts]
-        out_ref, query_table, table, query_sems, sems = refs[3 * parts :]
+        out_ref, query_table, table, sems = refs[len(arrays) :]
         copies = []
-        for at in range(parts):
-            span = pl.ds(starts[at], sizes[at])
+        for at, (head, size, block, span, _, _, _) in enumerate(parts):
+            query_part, own_part, other_part = refs[3 * at : 3 * at + 3]
+            rows = pl.ds(head, size)
             copies.append(
-                pltpu.make_async_copy(query_refs[at], query_table.at[:, span], query_sems.at[at])
+                pltpu.make_async_copy(
+                    query_part, query_table.at[rows, pl.ds(block, span)], sems.at[at, 0]
+                )
             )
-            for side, ref in enumerate((own_refs[at], other_refs[at])):
-                span = pl.ds(side * blocks + starts[at], sizes[at])
-                copies.append(pltpu.make_async_copy(ref, table.at[:, :, span], sems.at[at, side]))
+            for side, ref in enumerate((own_part, other_part)):
+                place = pl.ds(side * blocks + block, span)
+                copies.append(
+                    pltpu.make_async_copy(ref, table.at[rows, :, place], sems.at[at, 1 + side])
+                )
         for copy in copies:
             copy.start()
         for copy in copies:
@@ -286,7 +293,7 @@
         def run(head, group, listed, batch):
             for first in range(0, together, batch):
                 spots = [group * together + at for at in range(first, min(first + batch, together))]
-                slots = [[slots_ref[head, at, entry] for entry in range(listed)] for at in spots]
+                slots = [[slots_ref[first_head + head, at, entry] for entry in range(listed)] for at in spots]
                 scores = []
                 for at, listing in zip(spots, slots):
                     keys = jnp.concatenate([table[head, 0, slot] for slot in listing], axis=0)
@@ -300,7 +307,7 @@
                     )
                 column = lax.broadcasted_iota(jnp.int32, (1, listed * BLOCK), 1)
                 scores = [
-                    jnp.where(column < counts_ref[head, at] * BLOCK, one * scale, -jnp.inf)
+                    jnp.where(column < counts_ref[first_head + head, at] * BLOCK, one * scale, -jnp.inf)
                     for at, one in zip(spots, scores)
                 ]
                 highest = [jnp.max(one, axis=1, keepdims=True) for one in scores]
@@ -311,12 +318,12 @@
                 for one, listing in zip(weights, slots):
                     values = jnp.concatenate([table[head, 1, slot] for slot in listing], axis=0)
                     mixed.append(jnp.dot(one, values, preferred_element_type=jnp.float32))
-                for at, one in zip(spots, mixed):
-                    out_ref[head, at] = one.astype(dtype)
+                for at, one in enumerate(mixed):
+                    out_ref[group, head, first + at] = one.astype(dtype)
 
         def step(at, carry):
             head, group = at // groups, at % groups
-            few = most_ref[head, group] <= most // 2
+            few = most_ref[first_head + head, group] <= most // 2
 
             @pl.when(few)
             def _():
@@ -332,57 +339,73 @@
 
     return pl.pallas_call(
         body,
-        in_specs=[in_smem()] * 4 + [in_hbm()] * (3 * parts),
+        in_specs=[in_smem()] * 4 + [in_hbm()] * len(arrays),
         out_specs=whole_in_vmem(),
-        out_shape=jax.ShapeDtypeStruct((heads, blocks, BLOCK, HEAD_DIM), dtype),
+        out_shape=jax.ShapeDtypeStruct((groups, heads, together, BLOCK, HEAD_DIM), dtype),
         scratch_shapes=[
             pltpu.VMEM((heads, blocks, BLOCK, HEAD_DIM), dtype),
             pltpu.VMEM((heads, 2, CORES * blocks, BLOCK, HEAD_DIM), dtype),
-            pltpu.SemaphoreType.DMA((parts,)),
-            pltpu.SemaphoreType.DMA((parts, 2)),
+            pltpu.SemaphoreType.DMA((len(parts), 3)),
         ],
         compiler_params=pltpu.CompilerParams(vmem_limit_bytes=VMEM_BYTES),
         name="attend",
-    )(key_slots, counts, query_slots, group_most, *queries, *kv_own, *kv_other)
-
-
-def out_blocks(which, sign, attended, out_weight, dtypes, blocks):
-    groups, _, tokens, _ = attended[0].shape
-    sizes = [one.shape[1] for one in attended]
-    count = len(attended)
+    )(key_slots, counts, query_slots, group_most, *arrays)
+
+
+def out_blocks(which, sign, attended, place, out_weight, blocks, dtypes, before=None, skip=0):
+    groups, heads, tokens, _ = attended.shape
     depth, features = out_weight.shape
     width = features // blocks
-    wanted = len(dtypes)
-
-    def body(which_ref, sign_ref, *refs):
-        parts, weight_ref, out_refs = refs[:count], refs[count], refs[count + 1 :]
-        columns = []
-        for group in range(groups):
-            for chunk in range(count):
-                for head in range(sizes[chunk]):
-                    columns.append(parts[chunk][group, head])
-        joined = jnp.concatenate(columns, axis=1)
-        total = jnp.dot(joined, weight_ref[...], preferred_element_type=jnp.float32)
+    wanted = which.shape[0]
+    rows = heads * HEAD_DIM
+    weight = out_weight.reshape(groups, depth // groups, features)
+    stacked = len(dtypes) == 1 and wanted > 1
+
+    def body(which_ref, sign_ref, mixed_ref, weight_ref, *refs):
+        out_refs = refs if before is None else refs[1:]
+        joined = jnp.concatenate(
+            [mixed_ref[group, head] for group in range(groups) for head in range(heads)], axis=1
+        )
+        total = jnp.dot(
+            joined,
+            weight_ref[...].reshape(groups * rows, width),
+            preferred_element_type=jnp.float32,
+        )
         total = total * sign_ref[0].astype(jnp.float32)
-        for at in range(wanted):
-
-            @pl.when(pl.program_id(0) == at)
-            def _(at=at):
-                out_refs[at][...] = total.astype(dtypes[at])
-
+        if before is not None:
+            total = total + refs[0][0]
+        if stacked:
+            out_refs[0][0] = total.astype(dtypes[0])
+        else:
+            for at in range(wanted):
+
+                @pl.when(pl.program_id(0) == at)
+                def _(at=at):
+                    out_refs[at][...] = total.astype(dtypes[at])
+
+    in_specs = [
+        pl.BlockSpec(attended.shape, lambda i, w, s: (0, 0, 0, 0)),
+        pl.BlockSpec((groups, rows, width), lambda i, w, s: (0, place, w[i])),
+    ]
+    operands = [attended, weight]
+    if before is not None:
+        in_specs.append(pl.BlockSpec((1, tokens, width), lambda i, w, s: (i + skip, 0, 0)))
+        operands.append(before)
+    if stacked:
+        out_specs = [pl.BlockSpec((1, tokens, width), lambda i, w, s: (i, 0, 0))]
+        out_shape = [jax.ShapeDtypeStruct((wanted, tokens, width), dtypes[0])]
+    else:
+        out_specs = [pl.BlockSpec((tokens, width), lambda i, w, s: (0, 0))] * wanted
+        out_shape = [jax.ShapeDtypeStruct((tokens, width), dtype) for dtype in dtypes]
     return pl.pallas_call(
         body,
         grid_spec=pltpu.PrefetchScalarGridSpec(
-            num_scalar_prefetch=2,
-            grid=(wanted,),
-            in_specs=[pl.BlockSpec(one.shape, lambda i, w, s: (0, 0, 0, 0)) for one in attended]
-            + [pl.BlockSpec((depth, width), lambda i, w, s: (0, w[i]))],
-            out_specs=[pl.BlockSpec((tokens, width), lambda i, w, s: (0, 0))] * wanted,
+            num_scalar_prefetch=2, grid=(wanted,), in_specs=in_specs, out_specs=out_specs
         ),
-        out_shape=[jax.ShapeDtypeStruct((tokens, width), dtype) for dtype in dtypes],
+        out_shape=out_shape,
         compiler_params=pltpu.CompilerParams(vmem_limit_bytes=VMEM_BYTES),
         name="out_blocks",
-    )(which, sign, *attended, out_weight)
+    )(which, sign, *operands)
 
 
 def nearest(chips):
@@ -398,7 +421,7 @@
 
 
 def chunk_sizes(heads):
-    last = max(1, heads // 3)
+    last = heads // 3 if heads % 3 == 0 else 1
     return [heads - last, last] if heads > last else [heads]
 
 
@@ -485,16 +508,16 @@
             sent["down"] = lax.ppermute(
                 down, "chip", [(at + 1, at) for at in range(chips - step)]
             )
-        if phase == chips - 1:
+        if phase == 0:
             for shift in range(1, chips):
                 pairs = [(at, (at + shift) % chips) for at in range(chips)]
-                gathered.append(lax.ppermute(lists, "chip", pairs))
-        if phase == 0:
+                sent["lists" + str(shift)] = lax.ppermute(lists, "chip", pairs)
             sent["weights"] = weights_own.pop()
         if phase < chips:
             sent, shard, late = lax.optimization_barrier((sent, shard, late))
         if phase == 0:
             weights_own.append(sent["weights"])
+            gathered += [sent["lists" + str(shift)] for shift in range(1, chips)]
         if late is not None:
             rounds.append(late)
         late = diagonal
@@ -509,9 +532,11 @@
                 source = order[here][step - 1]
                 options.append(ups[here - source] if source < here else downs[source - here])
             shard = pick(chip, options)
-        if 1 <= phase < chips - 1 and len(weights_own) < heads:
-            held, _ = lax.optimization_barrier((cuts[len(weights_own)], sent))
-            weights_own.append(exchange(held))
+        if phase == chips - 2 and len(weights_own) < heads:
+            cuts[1:], _ = lax.optimization_barrier((cuts[1:], sent))
+            for cut in cuts[1:]:
+                held, _ = lax.optimization_barrier((cut, weights_own[-1]))
+                weights_own.append(exchange(held))
     rounds.append(late)
     while len(weights_own) < heads:
         weights_own.append(exchange(cuts[len(weights_own)]))
@@ -546,40 +571,59 @@
     chunks = chunk_sizes(heads)
     spans = [slice(sum(chunks[:at]), sum(chunks[: at + 1])) for at in range(len(chunks))]
     middle = (chips + 1) // 2
-    projected = [([], [], []) for _ in chunks]
     tables = (key_slots, counts, query_slots, group_most)
     held_places, tables = lax.optimization_barrier((places, tables))
     key_slots, counts, query_slots, group_most = tables
-    for part in (rounds[:middle], rounds[middle:]):
-        for span, size, (queries, kv_own, kv_other) in zip(spans, chunks, projected):
-            query, kv = project_heads(
-                held_places, gains[:, span], part, weights_own[span], weights_other[span]
-            )
-            here = len(part) * local_blocks
-            queries.append(query.reshape(size, here, BLOCK, HEAD_DIM))
-            kv_own.append(kv.reshape(size, 2, here, BLOCK, HEAD_DIM))
-            kv_other.append(lax.ppermute(kv_own[-1], "core", swap))
-            held_places, _ = lax.optimization_barrier((places, kv))
+    parts = [[] for _ in chunks]
+
+    def project(chunk, first, size, begin, end, places):
+        at = spans[chunk].start + first
+        span = slice(at, at + size)
+        query, kv = project_heads(
+            places, gains[:, span], rounds[begin:end], weights_own[span], weights_other[span]
+        )
+        here = (end - begin) * local_blocks
+        kv = kv.reshape(size, 2, here, BLOCK, HEAD_DIM)
+        kv_other = lax.ppermute(kv, "core", swap)
+        query = query.reshape(size, here, BLOCK, HEAD_DIM)
+        parts[chunk].append((first, size, begin * local_blocks, here, query, kv, kv_other))
+        return lax.optimization_barrier((places, kv))[0]
+
     attended = []
-    held = counts
-    for span, size, (queries, kv_own, kv_other) in zip(spans, chunks, projected):
+    for chunk, size in enumerate(chunks):
+        if chunk == 0:
+            for at in range(size):
+                held_places = project(0, at, 1, 0, middle, held_places)
+            held_places = project(0, 0, size, middle, chips, held_places)
+        else:
+            held_places = project(chunk, 0, size, 0, chips, held_places)
         mixed = attend(
-            key_slots[span], held[span], query_slots, group_most[span], queries, kv_own, kv_other
+            spans[chunk].start, size, key_slots, counts, query_slots, group_most, parts[chunk]
         )
-        held, _ = lax.optimization_barrier((counts, mixed))
-        mixed = mixed.reshape(size, chips, tokens, HEAD_DIM).transpose(1, 0, 2, 3)
+        held_places, mixed = lax.optimization_barrier((held_places, mixed))
+        mixed = mixed.reshape(chips, size, tokens, HEAD_DIM)
+        if attended:
+            mixed, attended = lax.optimization_barrier((mixed, attended))
         attended.append(exchange(mixed))
 
     sign = (2 * role - 1).astype(jnp.int32)[None]
     blocks = sides * lax.axis_size("role")
-
-    def blocks_of(first, second, dtypes):
-        which = jnp.stack([peers[first], peers[second]])
-        return out_blocks(which, sign, attended, out_weight[0], dtypes, blocks)
-
+    which = jnp.stack([peers[3], peers[2], peers[1], peers[0]])
+    before = None
+    for chunk, size in enumerate(chunks[:-1]):
+        before = out_blocks(
+            which, sign, attended[chunk], spans[chunk].start // size, out_weight[0], blocks,
+            (jnp.float32,), before,
+        )[0]
+    place = spans[-1].start // chunks[-1]
+    (diagonal,) = out_blocks(
+        which[:1], sign, attended[-1], place, out_weight[0], blocks, (jnp.bfloat16,), before
+    )
+    over_head, over_role, own = out_blocks(
+        which[1:], sign, attended[-1], place, out_weight[0], blocks,
+        (jnp.bfloat16, jnp.bfloat16, jnp.float32), before, 1,
+    )
     far_swap = [(0, 3), (1, 2), (2, 1), (3, 0)]
-    diagonal, over_head = blocks_of(3, 2, (jnp.bfloat16, jnp.bfloat16))
-    over_role, own = blocks_of(1, 0, (jnp.bfloat16, jnp.float32))
     from_diagonal = lax.ppermute(diagonal, ("role", "head"), far_swap)
     from_head = lax.ppermute(over_head, "head", swap)
     from_role = lax.ppermute(over_role, "role", swap)

time: 433 us -> 407 us (0.940)
  waiting for transfers between devices: 213 us -> 133 us
  blocking collectives: 0 us -> 45 us
  Pallas kernels: 91.8 us -> 105 us
  local copies, waits for them, and re-layouts: 28.5 us -> 20.5 us
  starting transfers between devices: 62.9 us -> 69.1 us
    ppermute x3, waiting for transfers between devices: 58.7 us -> 13.3 us  [per_device_by_heads(): lax.ppermute(down, 'chip', [(at + 1, at) for at in range(chips - step)])]
    all_to_all x0 -> x1, blocking collectives: none -> 45 us  [exchange(): lax.all_to_all(array, 'chip', split_axis=0, concat_axis=0, tiled=True)]
    all_to_all x5 -> x4, waiting for transfers between devices: 27.6 us -> 3.9 us  [exchange(): lax.all_to_all(array, 'chip', split_axis=0, concat_axis=0, tiled=True)]
    ppermute x4, waiting for transfers between devices: 20 us -> 0.79 us  [per_device_by_heads(): sent['head'] = lax.ppermute(shard, 'head', swap)]
    ppermute x1, waiting for transfers between devices: 0.01 us -> 14.1 us  [per_device_by_heads(): from_diagonal = lax.ppermute(diagonal, ('role', 'head'), far_swap)]
    ppermute x1, waiting for transfers between devices: 32 us -> 18.9 us  [per_device_by_heads(): from_head = lax.ppermute(over_head, 'head', swap)]
    ppermute x7, starting transfers between devices: 6.17 us -> 13.1 us  [the longest x3 12.1 us: per_device_by_heads(): sent['lists' + str(shift)] = lax.ppermute(lists, 'chip', pairs)]
    pallas_call x2 -> x3, Pallas kernels: 16.3 us -> 22.7 us  [out_blocks(): pl.pallas_call(body, grid_spec=pltpu.PrefetchScalarGridSpec(num_scalar_pr...]
  transfers between devices with their start and end apart: 42 -> 41, of which waited for: 18 -> 18; matrix products, arithmetic and copies ran while one was open for 11% -> 11% of each run, Pallas kernels for 17% -> 24%
where the time goes in v6:
time: 407 us; the launch traced here: 406 us
  waiting for transfers between devices  133 us (33%)
  Pallas kernels  105 us (26%)
  starting transfers between devices  69.1 us (17%)
  blocking collectives  45 us (11%)
  local copies, waits for them, and re-layouts  20.5 us (5%)
  other arithmetic  20.5 us (5%)
  matrix products  12.7 us (3%)
    pallas_call x4, Pallas kernels, project_heads(): pl.pallas_call(body, in_specs=[in_smem(), in_smem()] + [in_hbm()] * (2 *...  51.5 us
    all_to_all x1, blocking collectives, exchange(): lax.all_to_all(array, 'chip', split_axis=0, concat_axis=0, tiled=True)  45 us
    ppermute x3, waiting for transfers between devices, per_device_by_heads(): sent['lists' + str(shift)] = lax.ppermute(lists, 'chip', pairs)  30.3 us
    ppermute x4, waiting for transfers between devices, per_device_by_heads(): lax.ppermute(straight[1][half:], 'head', swap)  27.9 us
    pallas_call x3, Pallas kernels, out_blocks(): pl.pallas_call(body, grid_spec=pltpu.PrefetchScalarGridSpec(num_scalar_pr...  22.7 us
    all_to_all x4, starting transfers between devices, exchange(): lax.all_to_all(array, 'chip', split_axis=0, concat_axis=0, tiled=True)  19.8 us
    pallas_call x2, Pallas kernels, attend(): pl.pallas_call(body, in_specs=[in_smem()] * 4 + [in_hbm()] * len(arrays),...  19.2 us
    ppermute x1, waiting for transfers between devices, per_device_by_heads(): from_head = lax.ppermute(over_head, 'head', swap)  18.9 us
  transfers between devices with their start and end apart: 41, of which 18 were waited for; matrix products, arithmetic and copies ran while one was open for 11% of the time, Pallas kernels for 24%

profile of v6, /device:TPU:0, one launch (start us, length us, event | category | flops | bytes accessed | tf_op | source)
XLA Modules:
  0.0 406.3 jit_solution(12314053276554339738)
XLA Ops:
  3.8 6.4 %all-to-all-start = ((bf16[4,640,384]{2,1,0:T(8,128)(2,1)}), bf16[4,640,384]{2,1,0:T(8,128)(2,1)S(1)}, u32[]{:S(2)}, u32[]{:S(2)}) async-start(bf16[4,640,384]{2,1,0:T(8,128)(2,1)} %cut_columns.3), calls=%async_computation | async-start | bytes 3932160 | tf_op jit(solution)/shard_map/all_to_all | solution.py:462
  10.6 12.7 %multiply_reduce_fusion = (f32[384]{0:T(512)S(1)}, f32[384,1280]{1,0:T(8,128)}) fusion(bf16[384,5120]{1,0:T(8,128)(2,1)} %param.12, s32[]{:T(128)S(6)} %select_n.207, f32[384]{0:T(512)S(1)} %mul.87, bf16[384,5120]{1,0:T(8,128)(2,1)} %param.10, bf16[5120,1280]{1,0:T(8,128)(2,1)} %param.11, f32[384]{0:T(512)S(1)} %mul.83), kind=kOutput, calls=%fused_computation.5 | convolution fusion | flops 5036604928 | bytes 19993092 | tf_op jit(solution)/shard_map/dot_general | solution.py:470
  36.8 5.5 %collective-permute-start.8 = (bf16[384,1280]{1,0:T(8,128)(2,1)S(1)}, bf16[384,1280]{1,0:T(8,128)(2,1)}, u32[]{:S(2)}, u32[]{:S(2)}) collective-permute-start(bf16[384,1280]{1,0:T(8,128)(2,1)S(1)} %multiply_convert_fusion.refs_2_), channel_id=1, source_target_pairs={{0,4},{4,8},{8,12},{1,5},{5,9},{9,13},{2,6},{6,10},{10,14},{3,7},{... | collective-permute-start | bytes 2949128 | tf_op jit(solution)/shard_map/ppermute | solution.py:505
  43.8 24.5 %collective-permute-done.4 = s32[12,6,9]{2,1,0:T(8,128)S(1)} collective-permute-done((s32[12,6,9]{2,1,0:T(8,128)S(1)}, s32[12,6,9]{2,1,0:T(8,128)S(1)}, u32[]{:S(2)}, u32[]{:S(2)}) %collective-permute-start.4) | collective-permute-done | bytes 2624 | tf_op jit(solution)/shard_map/ppermute | solution.py:514
  68.3 10.6 %collective-permute-start.5 = (s32[12,6,9]{2,1,0:T(8,128)S(1)}, s32[12,6,9]{2,1,0:T(8,128)S(1)}, u32[]{:S(2)}, u32[]{:S(2)}) collective-permute-start(s32[12,6,9]{2,1,0:T(8,128)S(1)} %pad_add_fusion), channel_id=1, source_target_pairs={{0,8},{4,12},{8,0},{12,4},{1,9},{5,13},{9,1},{13,5},{2,10},{6,14},... | collective-permute-start | bytes 7784 | tf_op jit(solution)/shard_map/ppermute | solution.py:514
  94.4 13.3 %collective-permute-done.10 = bf16[384,1280]{1,0:T(8,128)(2,1)} collective-permute-done((bf16[384,1280]{1,0:T(8,128)(2,1)}, bf16[384,1280]{1,0:T(8,128)(2,1)}, u32[]{:S(2)}, u32[]{:S(2)}) %collective-permute-start.10) | collective-permute-done | bytes 983072 | tf_op jit(solution)/shard_map/ppermute | solution.py:508
  108.5 5.8 %collective-permute-done.12.refs_8_ = bf16[384,1280]{1,0:T(8,128)(2,1)S(1)} collective-permute-done((bf16[384,1280]{1,0:T(8,128)(2,1)S(1)}, bf16[384,1280]{1,0:T(8,128)(2,1)S(1)}, u32[]{:S(2)}, u32[]{:S(2)}) %collective-permute-start.12) | collective-permute-done | bytes 983072 | tf_op jit(solution)/shard_map/ppermute | solution.py:495
  132.9 10.8 %collective-permute-done.19.refs_6_ = bf16[192,1280]{1,0:T(8,128)(2,1)} collective-permute-done((bf16[192,1280]{1,0:T(8,128)(2,1)}, bf16[192,1280]{1,0:T(8,128)(2,1)}, u32[]{:S(2)}, u32[]{:S(2)}) %collective-permute-start.19) | collective-permute-done | bytes 491552 | tf_op jit(solution)/shard_map/ppermute | solution.py:501
  143.7 45.0 %all_to_all.25.refs_0_.refs_1_ = bf16[4,640,384]{2,1,0:T(8,128)(2,1)} all-to-all(bf16[4,640,384]{2,1,0:T(8,128)(2,1)} %cut_columns.4), channel_id=1, replica_groups=mesh['role'=2,'chip'=4,'core'=2,'head'=2] {'chip'}, dimensions={0} | all-to-all | bytes 3932160 | tf_op jit(solution)/shard_map/all_to_all | solution.py:462
  188.7 4.8 %all-to-all-start.2 = ((bf16[4,640,384]{2,1,0:T(8,128)(2,1)}), bf16[4,640,384]{2,1,0:T(8,128)(2,1)}, u32[]{:S(2)}, u32[]{:S(2)}) async-start(bf16[4,640,384]{2,1,0:T(8,128)(2,1)} %cut_columns.5), calls=%async_computation.2 | async-start | bytes 3932160 | tf_op jit(solution)/shard_map/all_to_all | solution.py:462
  201.3 7.9 %collective-permute-done.22.refs_10_ = bf16[192,1280]{1,0:T(8,128)(2,1)S(1)} collective-permute-done((bf16[192,1280]{1,0:T(8,128)(2,1)}, bf16[192,1280]{1,0:T(8,128)(2,1)S(1)}, u32[]{:S(2)}, u32[]{:S(2)}) %collective-permute-start.22) | collective-permute-done | bytes 491552 | tf_op jit(solution)/shard_map/ppermute | solution.py:500
  214.7 17.2 %collective-permute-done.23.refs_11_ = bf16[192,1280]{1,0:T(8,128)(2,1)S(1)} collective-permute-done((bf16[192,1280]{1,0:T(8,128)(2,1)}, bf16[192,1280]{1,0:T(8,128)(2,1)S(1)}, u32[]{:S(2)}, u32[]{:S(2)}) %collective-permute-start.23) | collective-permute-done | bytes 491552 | tf_op jit(solution)/shard_map/ppermute | solution.py:501
  231.9 3.9 all-to-all-done.2.refs_0_
  253.1 10.3 %project_heads.4 = (bf16[1,2,384,128]{3,2,1,0:T(8,128)(2,1)}, bf16[1,2,2,384,128]{4,3,2,1,0:T(8,128)(2,1)}) custom-call(s32[5]{0:T(128)} %concatenate.10.places_ref, f32[2,1]{1,0:T(2,128)} %get-tuple-element.134.gains_ref, bf16[4,640,384]{2,1,0:T(8,128)(2,1)} %copy-done.2, bf16[4,640,384]{2,1,0:T(8,128)(2,1)} %collective-permute-done.9.refs_1_.refs_2_, ...), custom_call_target="tpu_custom_call" | custom-call | tf_op jit(solution)/shard_map/project_heads/pallas_call | solution.py:245
  263.4 10.3 %project_heads.5 = (bf16[1,2,384,128]{3,2,1,0:T(8,128)(2,1)}, bf16[1,2,2,384,128]{4,3,2,1,0:T(8,128)(2,1)}) custom-call(s32[5]{0:T(128)} %concatenate.10.places_ref, f32[2,1]{1,0:T(2,128)} %get-tuple-element.133.gains_ref, bf16[4,640,384]{2,1,0:T(8,128)(2,1)} %all_to_all.25.refs_0_.refs_1_, bf16[4,640,384]{2,1,0:T(8,128)(2,1)} %collective-permute-done.24.refs_1_.refs_3_, ...), custom_call_target="tpu_custom_call" | custom-call | tf_op jit(solution)/shard_map/project_heads/pallas_call | solution.py:245
  274.9 13.9 %project_heads.6 = (bf16[2,2,384,128]{3,2,1,0:T(8,128)(2,1)}, bf16[2,2,2,384,128]{4,3,2,1,0:T(8,128)(2,1)}) custom-call(s32[5]{0:T(128)} %concatenate.10.places_ref, f32[2,2]{1,0:T(2,128)} %bitcast.48, bf16[4,640,384]{2,1,0:T(8,128)(2,1)} %copy-done.2, bf16[4,640,384]{2,1,0:T(8,128)(2,1)} %all_to_all.25.refs_0_.refs_1_, ...), custom_call_target="tpu_custom_call" | custom-call | tf_op jit(solution)/shard_map/project_heads/pallas_call | solution.py:245
  293.3 11.9 %attend.2 = bf16[4,2,6,64,128]{4,3,2,1,0:T(8,128)(2,1)} custom-call(s32[3,24,8]{2,1,0:T(8,128)} %fusion.4.slots_ref, s32[3,24]{1,0:T(4,128)} %copy-done.24, s32[24]{0:T(128)} %fusion.10.from_ref, s32[3,4]{1,0:T(4,128)} %reduce_max.9.most_ref, bf16[1,12,64,128]{3,2,1,0:T(8,128)(2,1)} %bitcast.46, bf16[1,2,12,64,128]{4,3,2,1,0:T(8,128)(2,1)} %bitcast.40, ...), custom_call_target="tpu_custom_call" | custom-call | tf_op jit(solution)/shard_map/attend/pallas_call | solution.py:340
  308.7 17.0 %project_heads.7 = (bf16[1,4,384,128]{3,2,1,0:T(8,128)(2,1)}, bf16[1,2,4,384,128]{4,3,2,1,0:T(8,128)(2,1)}) custom-call(s32[5]{0:T(128)} %concatenate.10.places_ref, f32[2,1]{1,0:T(2,128)} %get-tuple-element.132.gains_ref, bf16[4,640,384]{2,1,0:T(8,128)(2,1)} %all-to-all-done.2.refs_0_, bf16[4,640,384]{2,1,0:T(8,128)(2,1)} %collective-permute-done.32.refs_1_, ...), custom_call_target="tpu_custom_call" | custom-call | tf_op jit(solution)/shard_map/project_heads/pallas_call | solution.py:245
  329.2 7.4 %attend.3 = bf16[4,1,6,64,128]{4,3,2,1,0:T(8,128)(2,1)} custom-call(s32[3,24,8]{2,1,0:T(8,128)} %fusion.4.slots_ref, s32[3,24]{1,0:T(4,128)} %copy-done.24, s32[24]{0:T(128)} %fusion.10.from_ref, s32[3,4]{1,0:T(4,128)} %reduce_max.9.most_ref, bf16[1,24,64,128]{3,2,1,0:T(8,128)(2,1)} %bitcast.45, bf16[1,2,24,64,128]{4,3,2,1,0:T(8,128)(2,1)} %bitcast.39, ...), custom_call_target="tpu_custom_call" | custom-call | tf_op jit(solution)/shard_map/attend/pallas_call | solution.py:340
  336.6 5.0 %all-to-all-start.4 = ((bf16[4,1,384,128]{3,2,1,0:T(8,128)(2,1)}), bf16[4,1,384,128]{3,2,1,0:T(8,128)(2,1)S(1)}, u32[]{:S(2)}, u32[]{:S(2)}) async-start(bf16[4,1,384,128]{3,2,1,0:T(8,128)(2,1)} %bitcast.35), calls=%async_computation.4 | async-start | bytes 786432 | tf_op jit(solution)/shard_map/all_to_all | solution.py:462
  342.9 10.7 %out_blocks.3.refs_0_ = f32[4,384,1280]{2,1,0:T(8,128)} custom-call(s32[4]{0:T(128)} %pad_add_fusion.3.which_ref, s32[1]{0:T(128)} %bitcast.3.sign_ref, bf16[4,2,384,128]{3,2,1,0:T(8,128)(2,1)} %copy-done.14, bf16[4,384,5120]{2,1,0:T(8,128)(2,1)} %bitcast.28), custom_call_target="tpu_custom_call" | custom-call | tf_op jit(solution)/shard_map/out_blocks/pallas_call | solution.py:400
  358.3 8.2 %out_blocks.4 = (bf16[384,1280]{1,0:T(8,128)(2,1)}, bf16[384,1280]{1,0:T(8,128)(2,1)}, f32[384,1280]{1,0:T(8,128)}) custom-call(s32[3]{0:T(128)} %pad_add_fusion.2.which_ref, s32[1]{0:T(128)} %bitcast.3.sign_ref, bf16[4,1,384,128]{3,2,1,0:T(8,128)(2,1)} %copy-done.13, bf16[4,384,5120]{2,1,0:T(8,128)(2,1)} %bitcast.30, f32[4,384,1280]{2,1,0:T(8,128)} %out_blocks.3.refs_0_), custom_call_target="tpu_custom_call" | custom-call | tf_op jit(solution)/shard_map/out_blocks/pallas_call | solution.py:400
  369.8 14.1 %collective-permute-done.36 = bf16[384,1280]{1,0:T(8,128)(2,1)S(1)} collective-permute-done((bf16[384,1280]{1,0:T(8,128)(2,1)}, bf16[384,1280]{1,0:T(8,128)(2,1)S(1)}, u32[]{:S(2)}, u32[]{:S(2)}) %collective-permute-start.36) | collective-permute-done | bytes 983072 | tf_op jit(solution)/shard_map/ppermute | solution.py:627
  384.0 18.9 %collective-permute-done.35 = bf16[384,1280]{1,0:T(8,128)(2,1)S(1)} collective-permute-done((bf16[384,1280]{1,0:T(8,128)(2,1)}, bf16[384,1280]{1,0:T(8,128)(2,1)S(1)}, u32[]{:S(2)}, u32[]{:S(2)}) %collective-permute-start.35) | collective-permute-done | bytes 983072 | tf_op jit(solution)/shard_map/ppermute | solution.py:628
  (176 shorter events, 109.6 us)
Async XLA Ops:
  3.8 81.3 %all-to-all-start = ((bf16[4,640,384]{2,1,0:T(8,128)(2,1)}), bf16[4,640,384]{2,1,0:T(8,128)(2,1)S(1)}, u32[]{:S(2)}, u32[]{:S(2)}) async-start(bf16[4,640,384]{2,1,0:T(8,128)(2,1)} %cut_columns.3), calls=%async_computation | async-start | bytes 3932160 | tf_op jit(solution)/shard_map/all_to_all | solution.py:462
  32.4 52.6 %collective-permute-start.2 = (bf16[384,1280]{1,0:T(8,128)(2,1)S(1)}, bf16[384,1280]{1,0:T(8,128)(2,1)}, u32[]{:S(2)}, u32[]{:S(2)}) collective-permute-start(bf16[384,1280]{1,0:T(8,128)(2,1)S(1)} %multiply_convert_fusion.refs_2_), channel_id=1, source_target_pairs={{4,0},{8,4},{12,8},{5,1},{9,5},{13,9},{6,2},{10,6},{14,10},{7,3},{... | collective-permute-start | bytes 2949128 | tf_op jit(solution)/shard_map/ppermute | solution.py:508
  33.7 51.3 %collective-permute-start.3 = (bf16[384,1280]{1,0:T(8,128)(2,1)S(1)}, bf16[384,1280]{1,0:T(8,128)(2,1)}, u32[]{:S(2)}, u32[]{:S(2)}) collective-permute-start(bf16[384,1280]{1,0:T(8,128)(2,1)S(1)} %multiply_convert_fusion.refs_2_), channel_id=1, source_target_pairs={{0,1},{1,0},{2,3},{3,2},{4,5},{5,4},{6,7},{7,6},{8,9},{9,8},{10,11... | collective-permute-start | bytes 2949128 | tf_op jit(solution)/shard_map/ppermute | solution.py:496
  35.5 49.6 %collective-permute-start.7 = (bf16[384,1280]{1,0:T(8,128)(2,1)S(1)}, bf16[384,1280]{1,0:T(8,128)(2,1)}, u32[]{:S(2)}, u32[]{:S(2)}) collective-permute-start(bf16[384,1280]{1,0:T(8,128)(2,1)S(1)} %multiply_convert_fusion.refs_2_), channel_id=1, source_target_pairs={{0,16},{16,0},{1,17},{17,1},{2,18},{18,2},{3,19},{19,3},{4,20},{20... | collective-permute-start | bytes 2949128 | tf_op jit(solution)/shard_map/ppermute | solution.py:495
  36.8 48.3 %collective-permute-start.8 = (bf16[384,1280]{1,0:T(8,128)(2,1)S(1)}, bf16[384,1280]{1,0:T(8,128)(2,1)}, u32[]{:S(2)}, u32[]{:S(2)}) collective-permute-start(bf16[384,1280]{1,0:T(8,128)(2,1)S(1)} %multiply_convert_fusion.refs_2_), channel_id=1, source_target_pairs={{0,4},{4,8},{8,12},{1,5},{5,9},{9,13},{2,6},{6,10},{10,14},{3,7},{... | collective-permute-start | bytes 2949128 | tf_op jit(solution)/shard_map/ppermute | solution.py:505
  42.7 25.6 %collective-permute-start.4 = (s32[12,6,9]{2,1,0:T(8,128)S(1)}, s32[12,6,9]{2,1,0:T(8,128)S(1)}, u32[]{:S(2)}, u32[]{:S(2)}) collective-permute-start(s32[12,6,9]{2,1,0:T(8,128)S(1)} %pad_add_fusion), channel_id=1, source_target_pairs={{0,4},{4,8},{8,12},{12,0},{1,5},{5,9},{9,13},{13,1},{2,6},{6,10},{... | collective-permute-start | bytes 7784 | tf_op jit(solution)/shard_map/ppermute | solution.py:514
  93.8 31.0 %collective-permute-start.18 = (bf16[192,1280]{1,0:T(8,128)(2,1)S(1)}, bf16[192,1280]{1,0:T(8,128)(2,1)S(1)}, u32[]{:S(2)}, u32[]{:S(2)}) collective-permute-start(bf16[192,1280]{1,0:T(8,128)(2,1)S(1)} %slice.72), channel_id=1, source_target_pairs={{0,16},{16,0},{1,17},{17,1},{2,18},{18,2},{3,19},{19,3},{4,20},{20... | collective-permute-start | bytes 1474568 | tf_op jit(solution)/shard_map/ppermute | solution.py:500
  115.3 28.4 %collective-permute-start.14 = (bf16[384,1280]{1,0:T(8,128)(2,1)}, bf16[384,1280]{1,0:T(8,128)(2,1)}, u32[]{:S(2)}, u32[]{:S(2)}) collective-permute-start(bf16[384,1280]{1,0:T(8,128)(2,1)} %collective-permute-done.10), channel_id=1, source_target_pairs={{4,0},{5,1},{6,2},{7,3},{20,16},{21,17},{22,18},{23,19}} | collective-permute-start | bytes 2949128 | tf_op jit(solution)/shard_map/ppermute | solution.py:508
  118.2 25.4 %collective-permute-start.15 = (bf16[384,1280]{1,0:T(8,128)(2,1)S(1)}, bf16[384,1280]{1,0:T(8,128)(2,1)}, u32[]{:S(2)}, u32[]{:S(2)}) collective-permute-start(bf16[384,1280]{1,0:T(8,128)(2,1)S(1)} %fusion.2.refs_4_.refs_12_), channel_id=1, source_target_pairs={{0,1},{1,0},{2,3},{3,2},{4,5},{5,4},{6,7},{7,6},{8,9},{9,8},{10,11... | collective-permute-start | bytes 2949128 | tf_op jit(solution)/shard_map/ppermute | solution.py:496
  118.8 24.9 %collective-permute-start.16 = (bf16[384,1280]{1,0:T(8,128)(2,1)S(1)}, bf16[384,1280]{1,0:T(8,128)(2,1)}, u32[]{:S(2)}, u32[]{:S(2)}) collective-permute-start(bf16[384,1280]{1,0:T(8,128)(2,1)S(1)} %fusion.2.refs_4_.refs_12_), channel_id=1, source_target_pairs={{0,16},{16,0},{1,17},{17,1},{2,18},{18,2},{3,19},{19,3},{4,20},{20... | collective-permute-start | bytes 2949128 | tf_op jit(solution)/shard_map/ppermute | solution.py:495
  188.7 47.1 %all-to-all-start.2 = ((bf16[4,640,384]{2,1,0:T(8,128)(2,1)}), bf16[4,640,384]{2,1,0:T(8,128)(2,1)}, u32[]{:S(2)}, u32[]{:S(2)}) async-start(bf16[4,640,384]{2,1,0:T(8,128)(2,1)} %cut_columns.5), calls=%async_computation.2 | async-start | bytes 3932160 | tf_op jit(solution)/shard_map/all_to_all | solution.py:462
  193.5 51.3 %collective-permute-start.9 = (bf16[4,640,384]{2,1,0:T(8,128)(2,1)S(1)}, bf16[4,640,384]{2,1,0:T(8,128)(2,1)}, u32[]{:S(2)}, u32[]{:S(2)}) collective-permute-start(bf16[4,640,384]{2,1,0:T(8,128)(2,1)S(1)} %all-to-all-done.refs_0_), channel_id=1, source_target_pairs={{0,2},{2,0},{1,3},{3,1},{4,6},{6,4},{5,7},{7,5},{8,10},{10,8},{9,1... | collective-permute-start | bytes 5898248 | tf_op jit(solution)/shard_map/ppermute | solution.py:543
  193.6 53.0 %collective-permute-start.24 = (bf16[4,640,384]{2,1,0:T(8,128)(2,1)}, bf16[4,640,384]{2,1,0:T(8,128)(2,1)}, u32[]{:S(2)}, u32[]{:S(2)}) collective-permute-start(bf16[4,640,384]{2,1,0:T(8,128)(2,1)} %all_to_all.25.refs_0_.refs_1_), channel_id=1, source_target_pairs={{0,2},{2,0},{1,3},{3,1},{4,6},{6,4},{5,7},{7,5},{8,10},{10,8},{9,1... | collective-permute-start | bytes 5898248 | tf_op jit(solution)/shard_map/ppermute | solution.py:543
  197.6 42.7 %collective-permute-start.20 = (bf16[384,1280]{1,0:T(8,128)(2,1)}, bf16[384,1280]{1,0:T(8,128)(2,1)}, u32[]{:S(2)}, u32[]{:S(2)}) collective-permute-start(bf16[384,1280]{1,0:T(8,128)(2,1)} %select_select_fusion.2.refs_9_.refs_17_), channel_id=1, source_target_pairs={{0,1},{1,0},{2,3},{3,2},{4,5},{5,4},{6,7},{7,6},{8,9},{9,8},{10,11... | collective-permute-start | bytes 2949128 | tf_op jit(solution)/shard_map/ppermute | solution.py:496
  198.1 42.5 %collective-permute-start.21 = (bf16[384,1280]{1,0:T(8,128)(2,1)}, bf16[384,1280]{1,0:T(8,128)(2,1)}, u32[]{:S(2)}, u32[]{:S(2)}) collective-permute-start(bf16[384,1280]{1,0:T(8,128)(2,1)} %select_select_fusion.2.refs_9_.refs_17_), channel_id=1, source_target_pairs={{0,16},{16,0},{1,17},{17,1},{2,18},{18,2},{3,19},{19,3},{4,20},{20... | collective-permute-start | bytes 2949128 | tf_op jit(solution)/shard_map/ppermute | solution.py:495
  235.8 73.0 %collective-permute-start.32 = (bf16[4,640,384]{2,1,0:T(8,128)(2,1)}, bf16[4,640,384]{2,1,0:T(8,128)(2,1)}, u32[]{:S(2)}, u32[]{:S(2)}) collective-permute-start(bf16[4,640,384]{2,1,0:T(8,128)(2,1)} %all-to-all-done.2.refs_0_), channel_id=1, source_target_pairs={{0,2},{2,0},{1,3},{3,1},{4,6},{6,4},{5,7},{7,5},{8,10},{10,8},{9,1... | collective-permute-start | bytes 5898248 | tf_op jit(solution)/shard_map/ppermute | solution.py:543
  240.3 33.4 %collective-permute-start.25 = (bf16[192,1280]{1,0:T(8,128)(2,1)}, bf16[192,1280]{1,0:T(8,128)(2,1)S(1)}, u32[]{:S(2)}, u32[]{:S(2)}) collective-permute-start(bf16[192,1280]{1,0:T(8,128)(2,1)} %slice.78), channel_id=1, source_target_pairs={{0,16},{16,0},{1,17},{17,1},{2,18},{18,2},{3,19},{19,3},{4,20},{20... | collective-permute-start | bytes 1474568 | tf_op jit(solution)/shard_map/ppermute | solution.py:500
  240.6 33.2 %collective-permute-start.26 = (bf16[192,1280]{1,0:T(8,128)(2,1)}, bf16[192,1280]{1,0:T(8,128)(2,1)}, u32[]{:S(2)}, u32[]{:S(2)}) collective-permute-start(bf16[192,1280]{1,0:T(8,128)(2,1)} %slice.79), channel_id=1, source_target_pairs={{0,1},{1,0},{2,3},{3,2},{4,5},{5,4},{6,7},{7,6},{8,9},{9,8},{10,11... | collective-permute-start | bytes 1474568 | tf_op jit(solution)/shard_map/ppermute | solution.py:501
  244.8 29.0 %collective-permute-start.27 = (bf16[192,1280]{1,0:T(8,128)(2,1)}, bf16[192,1280]{1,0:T(8,128)(2,1)S(1)}, u32[]{:S(2)}, u32[]{:S(2)}) collective-permute-start(bf16[192,1280]{1,0:T(8,128)(2,1)} %slice.80), channel_id=1, source_target_pairs={{0,16},{16,0},{1,17},{17,1},{2,18},{18,2},{3,19},{19,3},{4,20},{20... | collective-permute-start | bytes 1474568 | tf_op jit(solution)/shard_map/ppermute | solution.py:500
  246.6 27.2 %collective-permute-start.28 = (bf16[192,1280]{1,0:T(8,128)(2,1)}, bf16[192,1280]{1,0:T(8,128)(2,1)S(1)}, u32[]{:S(2)}, u32[]{:S(2)}) collective-permute-start(bf16[192,1280]{1,0:T(8,128)(2,1)} %slice.81), channel_id=1, source_target_pairs={{0,1},{1,0},{2,3},{3,2},{4,5},{5,4},{6,7},{7,6},{8,9},{9,8},{10,11... | collective-permute-start | bytes 1474568 | tf_op jit(solution)/shard_map/ppermute | solution.py:501
  305.2 31.4 %all-to-all-start.3 = ((bf16[4,2,384,128]{3,2,1,0:T(8,128)(2,1)}), bf16[4,2,384,128]{3,2,1,0:T(8,128)(2,1)S(1)}, u32[]{:S(2)}, u32[]{:S(2)}) async-start(bf16[4,2,384,128]{3,2,1,0:T(8,128)(2,1)} %bitcast.34), calls=%async_computation.3 | async-start | bytes 1572864 | tf_op jit(solution)/shard_map/all_to_all | solution.py:462
  358.1 25.8 %collective-permute-start.36 = (bf16[384,1280]{1,0:T(8,128)(2,1)}, bf16[384,1280]{1,0:T(8,128)(2,1)S(1)}, u32[]{:S(2)}, u32[]{:S(2)}) collective-permute-start(bf16[384,1280]{1,0:T(8,128)(2,1)} %out_blocks.5), channel_id=1, source_target_pairs={{0,17},{1,16},{16,1},{17,0},{2,19},{3,18},{18,3},{19,2},{4,21},{5,... | collective-permute-start | bytes 2949128 | tf_op jit(solution)/shard_map/ppermute | solution.py:627
  366.6 36.3 %collective-permute-start.35 = (bf16[384,1280]{1,0:T(8,128)(2,1)}, bf16[384,1280]{1,0:T(8,128)(2,1)S(1)}, u32[]{:S(2)}, u32[]{:S(2)}) collective-permute-start(bf16[384,1280]{1,0:T(8,128)(2,1)} %get-tuple-element.126), channel_id=1, source_target_pairs={{0,1},{1,0},{2,3},{3,2},{4,5},{5,4},{6,7},{7,6},{8,9},{9,8},{10,11... | collective-permute-start | bytes 2949128 | tf_op jit(solution)/shard_map/ppermute | solution.py:628
  368.1 34.8 %collective-permute-start.34 = (bf16[384,1280]{1,0:T(8,128)(2,1)}, bf16[384,1280]{1,0:T(8,128)(2,1)S(1)}, u32[]{:S(2)}, u32[]{:S(2)}) collective-permute-start(bf16[384,1280]{1,0:T(8,128)(2,1)} %get-tuple-element.125), channel_id=1, source_target_pairs={{0,16},{16,0},{1,17},{17,1},{2,18},{18,2},{3,19},{19,3},{4,20},{20... | collective-permute-start | bytes 2949128 | tf_op jit(solution)/shard_map/ppermute | solution.py:629
  (49 other events, 873.1 us)

commit v7 on v6

--- a/solution.py
+++ b/solution.py
@@ -145,32 +145,40 @@
     return pl.BlockSpec(memory_space=pltpu.SMEM)
 
 
-def cut_columns(weight, chips, head):
+def cut_columns(weight, chips, head, extra=None):
     rows, columns = weight.shape
     wide = 3 * HEAD_DIM
     chip_heads = columns // (chips * wide)
-
-    def body(weight_ref, out_ref):
-        out_ref[0] = weight_ref[...]
-
+    more = 0 if extra is None else extra.shape[1]
+
+    def body(weight_ref, *refs):
+        out_ref = refs[-1]
+        out_ref[0, :rows] = weight_ref[...]
+        if more:
+            out_ref[0, rows:] = refs[0][0]
+
+    in_specs = [pl.BlockSpec((rows, wide), lambda chip: (0, chip * chip_heads + head))]
+    operands = [weight]
+    if more:
+        in_specs.append(pl.BlockSpec((1, more, wide), lambda chip: (chip, 0, 0)))
+        operands.append(extra)
     return pl.pallas_call(
         body,
         grid=(chips,),
-        in_specs=[pl.BlockSpec((rows, wide), lambda chip: (0, chip * chip_heads + head))],
-        out_specs=pl.BlockSpec((1, rows, wide), lambda chip: (chip, 0, 0)),
-        out_shape=jax.ShapeDtypeStruct((chips, rows, wide), weight.dtype),
+        in_specs=in_specs,
+        out_specs=pl.BlockSpec((1, rows + more, wide), lambda chip: (chip, 0, 0)),
+        out_shape=jax.ShapeDtypeStruct((chips, rows + more, wide), weight.dtype),
         name="cut_columns",
-    )(weight)
-
-
-def project_heads(places, gains, rounds, weights_own, weights_other):
+    )(*operands)
+
+
+def project_heads(places, gains, rounds, depth, weights_own, weights_other):
     heads = len(weights_own)
-    slabs, depth, columns = weights_own[0].shape
+    slabs, _, columns = weights_own[0].shape
     tokens, features = rounds[0][0].shape
     pieces = [piece for one in rounds for piece in one]
     turns = len(rounds)
-    per_round = len(rounds[0])
-    half = tokens // 2
+    most = max(len(one) for one in rounds)
     joint = 2 if slabs % 2 == 0 else 1
     dtype = weights_own[0].dtype
 
@@ -188,7 +196,7 @@
                     place = core if side == 0 else 1 - core
                     here.append(
                         pltpu.make_async_copy(
-                            ref.at[places_ref[slab]],
+                            ref.at[places_ref[slab], pl.ds(0, depth)],
                             table.at[
                                 slab // joint,
                                 slab % joint,
@@ -199,21 +207,25 @@
                             weight_sems.at[slab, head, side],
                         )
                     )
+            at = 0
             for turn in range(turns):
-                for which in [slab] if slab < slabs - 1 else [slab, slab + 1]:
-                    first = turn * tokens + max(which - slabs + 1, 0) * half
-                    count = tokens if slab < slabs - 1 else half
-                    here.append(
-                        pltpu.make_async_copy(
-                            piece_refs[turn * per_round + which],
-                            rows.at[
-                                slab // joint,
-                                pl.ds(first, count),
-                                pl.ds(slab % joint * features, features),
-                            ],
-                            row_sems.at[which, turn],
+                first = turn * tokens
+                for which in range(len(rounds[turn])):
+                    if min(which, slabs - 1) == slab:
+                        count = rounds[turn][which].shape[0]
+                        here.append(
+                            pltpu.make_async_copy(
+                                piece_refs[at],
+                                rows.at[
+                                    slab // joint,
+                                    pl.ds(first, count),
+                                    pl.ds(slab % joint * features, features),
+                                ],
+                                row_sems.at[which, turn],
+                            )
                         )
-                    )
+                        first += count
+                    at += 1
             for copy in here:
                 copy.start()
             copies.append(here)
@@ -254,7 +266,7 @@
             pltpu.VMEM((slabs // joint, joint, CORES, depth, heads * columns), dtype),
             pltpu.VMEM((slabs // joint, turns * tokens, joint * features), dtype),
             pltpu.SemaphoreType.DMA((slabs, heads, 2)),
-            pltpu.SemaphoreType.DMA((per_round, turns)),
+            pltpu.SemaphoreType.DMA((most, turns)),
         ],
         compiler_params=pltpu.CompilerParams(vmem_limit_bytes=VMEM_BYTES),
         name="project_heads",
@@ -446,6 +458,7 @@
     features = gen_weight.shape[1]
     all_blocks = chips * local_blocks
     swap = [(0, 1), (1, 0)]
+    far_swap = [(0, 3), (1, 2), (2, 1), (3, 0)]
     order, turns = nearest(chips)
     turn_here = jnp.asarray(turns, dtype=jnp.int32)[chip]
 
@@ -462,9 +475,19 @@
         return lax.all_to_all(array, "chip", split_axis=0, concat_axis=0, tiled=True)
 
     weight_here = qkv_weight[0]
-    cuts = [cut_columns(weight_here, chips, at) for at in range(heads)]
+    depth = weight_here.shape[0]
+    wide = 3 * HEAD_DIM
+    lists = jnp.concatenate([block_keys, block_count[:, :, None]], axis=2)
+    lists = lists.reshape(chips, -1).astype(jnp.bfloat16)
+    listed = lists.shape[1]
+    spare = -(-listed // (16 * wide)) * 16
+    lists = jnp.pad(lists, ((0, 0), (0, spare * wide - listed))).reshape(chips, spare, wide)
+    cuts = [
+        cut_columns(weight_here, chips, at, lists if at == 0 else None) for at in range(heads)
+    ]
     hidden_rows, cuts[0] = lax.optimization_barrier((hidden_rows, cuts[0]))
     weights_own = [exchange(cuts[0])]
+    weights_other = []
 
     mine = role * lax.axis_size("head") + head
     generated = jnp.dot(hidden_rows, gen_weight, preferred_element_type=jnp.float32)
@@ -481,19 +504,61 @@
     normed = (noisy * lax.rsqrt(squares / width + 1e-06)[:, :, None]).astype(jnp.bfloat16)
     normed = normed.reshape(tokens, features)
 
-    lists = jnp.concatenate([block_keys, block_count[:, :, None]], axis=2)
+    def tables_of(lists):
+        lists = lists.reshape(chips, spare * wide)[:, :listed].astype(jnp.int32)
+        lists = lists.reshape(chips, heads, local_blocks, most + 1).transpose(1, 0, 2, 3)
+        lists = lists.reshape(heads, all_blocks, most + 1)
+        owner = lists[:, :, :most] // local_blocks
+        turn = turn_of(owner // CORES)
+        far = (owner % CORES != core).astype(jnp.int32)
+        key_slots = far * all_blocks + turn * local_blocks + lists[:, :, :most] % local_blocks
+        counts = lists[:, :, most]
+        group_most = jnp.max(counts.reshape(heads, chips, local_blocks), axis=2)
+        spot = jnp.arange(all_blocks, dtype=jnp.int32)
+        query_slots = turn_of(spot // local_blocks)
+        query_slots = query_slots * local_blocks + spot % local_blocks
+
+        return key_slots, counts, query_slots, group_most
+
+    sides = lax.axis_size("head")
+    peers = jnp.stack(
+        [
+            role * sides + head,
+            (1 - role) * sides + head,
+            role * sides + 1 - head,
+            (1 - role) * sides + 1 - head,
+        ]
+    ).astype(jnp.int32)
+    places = jnp.concatenate([peers, core[None].astype(jnp.int32)])
+    gains = lax.dynamic_slice_in_dim(qk_gain[0], chip * heads, heads, axis=1)
+
+    chunks = chunk_sizes(heads)
+    spans = [slice(sum(chunks[:at]), sum(chunks[: at + 1])) for at in range(len(chunks))]
+    parts = [[] for _ in chunks]
+
+    def project(chunk, first, size, begin, some, places):
+        at = spans[chunk].start + first
+        span = slice(at, at + size)
+        query, kv = project_heads(
+            places, gains[:, span], some, depth, weights_own[span], weights_other[span]
+        )
+        here = len(some) * local_blocks
+        kv = kv.reshape(size, 2, here, BLOCK, HEAD_DIM)
+        kv_other = lax.ppermute(kv, "core", swap)
+        query = query.reshape(size, here, BLOCK, HEAD_DIM)
+        parts[chunk].append((first, size, begin * local_blocks, here, query, kv, kv_other))
+        return lax.optimization_barrier((places, kv))[0]
+
     half = tokens // 2
     rounds = []
     straight = None
     shard, up, down = normed, normed, normed
     ups, downs = [None], [None]
-    gathered = [lists]
     late = None
-    for phase in range(chips + 1):
+    for phase in range(chips):
         sent = {}
-        if phase < chips:
-            sent["role"] = lax.ppermute(shard, "role", swap)
-            sent["head"] = lax.ppermute(shard, "head", swap)
+        sent["role"] = lax.ppermute(shard, "role", swap)
+        sent["head"] = lax.ppermute(shard, "head", swap)
         diagonal = None
         if straight is not None:
             diagonal = straight + (
@@ -508,21 +573,30 @@
             sent["down"] = lax.ppermute(
                 down, "chip", [(at + 1, at) for at in range(chips - step)]
             )
+        else:
+            sent["far"] = lax.ppermute(shard, ("role", "head"), far_swap)
         if phase == 0:
-            for shift in range(1, chips):
-                pairs = [(at, (at + shift) % chips) for at in range(chips)]
-                sent["lists" + str(shift)] = lax.ppermute(lists, "chip", pairs)
             sent["weights"] = weights_own.pop()
-        if phase < chips:
-            sent, shard, late = lax.optimization_barrier((sent, shard, late))
+        if phase == 1:
+            sent["weights"] = lax.ppermute(weights_own[0], "core", swap)
+        if step == chips:
+            early = rounds + [late]
+            tables = tables_of(weights_own[0][:, depth:])
+            held_places, tables = lax.optimization_barrier((places, tables))
+            held_places = project(0, 0, 1, 0, early, held_places)
+            sent["places"] = held_places
+            sent["diagonal"] = diagonal
+        sent, shard, late = lax.optimization_barrier((sent, shard, late))
         if phase == 0:
             weights_own.append(sent["weights"])
-            gathered += [sent["lists" + str(shift)] for shift in range(1, chips)]
+        if phase == 1:
+            weights_other.append(sent["weights"])
+        if step == chips:
+            held_places, diagonal = sent["places"], sent["diagonal"]
         if late is not None:
             rounds.append(late)
         late = diagonal
-        if phase < chips:
-            straight = (shard, sent["role"], sent["head"])
+        straight = (shard, sent["role"], sent["head"])
         if step < chips:
             up, down = sent["up"], sent["down"]
             ups.append(up)
@@ -532,74 +606,27 @@
                 source = order[here][step - 1]
                 options.append(ups[here - source] if source < here else downs[source - here])
             shard = pick(chip, options)
-        if phase == chips - 2 and len(weights_own) < heads:
-            cuts[1:], _ = lax.optimization_barrier((cuts[1:], sent))
-            for cut in cuts[1:]:
-                held, _ = lax.optimization_barrier((cut, weights_own[-1]))
-                weights_own.append(exchange(held))
+        if phase >= chips - 2 and len(weights_own) < heads:
+            held, _ = lax.optimization_barrier((cuts[len(weights_own)], sent))
+            weights_own.append(exchange(held))
+            if step == chips:
+                weights_other += [lax.ppermute(one, "core", swap) for one in weights_own[1:]]
     rounds.append(late)
+    rounds.append(straight + (sent["far"],))
     while len(weights_own) < heads:
         weights_own.append(exchange(cuts[len(weights_own)]))
-    weights_other = [lax.ppermute(one, "core", swap) for one in weights_own]
-
-    gathered = [lax.dynamic_slice_in_dim(one, chip * heads, heads, axis=0) for one in gathered]
-    lists = jnp.concatenate(
-        [pick((chip - at) % chips, gathered) for at in range(chips)], axis=1
-    )
-    owner = lists[:, :, :most] // local_blocks
-    turn = turn_of(owner // CORES)
-    far = (owner % CORES != core).astype(jnp.int32)
-    key_slots = far * all_blocks + turn * local_blocks + lists[:, :, :most] % local_blocks
-    counts = lists[:, :, most]
-    group_most = jnp.max(counts.reshape(heads, chips, local_blocks), axis=2)
-    spot = jnp.arange(all_blocks, dtype=jnp.int32)
-    query_slots = turn_of(spot // local_blocks)
-    query_slots = query_slots * local_blocks + spot % local_blocks
-
-    sides = lax.axis_size("head")
-    peers = jnp.stack(
-        [
-            role * sides + head,
-            (1 - role) * sides + head,
-            role * sides + 1 - head,
-            (1 - role) * sides + 1 - head,
-        ]
-    ).astype(jnp.int32)
-    places = jnp.concatenate([peers, core[None].astype(jnp.int32)])
-    gains = lax.dynamic_slice_in_dim(qk_gain[0], chip * heads, heads, axis=1)
-
-    chunks = chunk_sizes(heads)
-    spans = [slice(sum(chunks[:at]), sum(chunks[: at + 1])) for at in range(len(chunks))]
-    middle = (chips + 1) // 2
-    tables = (key_slots, counts, query_slots, group_most)
-    held_places, tables = lax.optimization_barrier((places, tables))
-    key_slots, counts, query_slots, group_most = tables
-    parts = [[] for _ in chunks]
-
-    def project(chunk, first, size, begin, end, places):
-        at = spans[chunk].start + first
-        span = slice(at, at + size)
-        query, kv = project_heads(
-            places, gains[:, span], rounds[begin:end], weights_own[span], weights_other[span]
-        )
-        here = (end - begin) * local_blocks
-        kv = kv.reshape(size, 2, here, BLOCK, HEAD_DIM)
-        kv_other = lax.ppermute(kv, "core", swap)
-        query = query.reshape(size, here, BLOCK, HEAD_DIM)
-        parts[chunk].append((first, size, begin * local_blocks, here, query, kv, kv_other))
-        return lax.optimization_barrier((places, kv))[0]
+    for at in range(len(weights_other), heads):
+        weights_other.append(lax.ppermute(weights_own[at], "core", swap))
 
     attended = []
     for chunk, size in enumerate(chunks):
         if chunk == 0:
-            for at in range(size):
-                held_places = project(0, at, 1, 0, middle, held_places)
-            held_places = project(0, 0, size, middle, chips, held_places)
+            for at in range(1, size):
+                held_places = project(0, at, 1, 0, early, held_places)
+            held_places = project(0, 0, size, len(early), rounds[len(early) :], held_places)
         else:
-            held_places = project(chunk, 0, size, 0, chips, held_places)
-        mixed = attend(
-            spans[chunk].start, size, key_slots, counts, query_slots, group_most, parts[chunk]
-        )
+            held_places = project(chunk, 0, size, 0, rounds, held_places)
+        mixed = attend(spans[chunk].start, size, *tables, parts[chunk])
         held_places, mixed = lax.optimization_barrier((held_places, mixed))
         mixed = mixed.reshape(chips, size, tokens, HEAD_DIM)
         if attended:
@@ -623,7 +650,6 @@
         which[1:], sign, attended[-1], place, out_weight[0], blocks,
         (jnp.bfloat16, jnp.bfloat16, jnp.float32), before, 1,
     )
-    far_swap = [(0, 3), (1, 2), (2, 1), (3, 0)]
     from_diagonal = lax.ppermute(diagonal, ("role", "head"), far_swap)
     from_head = lax.ppermute(over_head, "head", swap)
     from_role = lax.ppermute(over_role, "role", swap)
@@ -648,6 +674,7 @@
         and width % (role * head * 256) == 0
         and width % (seq * 16) == 0
         and tokens % (2 * BLOCK) == 0
+        and hidden_rows.shape[0] // BLOCK <= 256
     )
 
 

time: 407 us -> 419 us (1.029)
  waiting for transfers between devices: 133 us -> 196 us
  blocking collectives: 45 us -> 0 us
    all_to_all x1 -> x0, blocking collectives: 45 us -> none  [exchange(): lax.all_to_all(array, 'chip', split_axis=0, concat_axis=0, tiled=True)]
    ppermute x3, waiting for transfers between devices: 13.3 us -> 52.8 us  [per_device_by_heads(): lax.ppermute(down, 'chip', [(at + 1, at) for at in range(chips - step)])]
    all_to_all x4 -> x5, waiting for transfers between devices: 3.9 us -> 42.3 us  [exchange(): lax.all_to_all(array, 'chip', split_axis=0, concat_axis=0, tiled=True)]
    ppermute x6 -> x4, waiting for transfers between devices: 30.3 us -> 0.01 us  [the longest x2 0.01 us: per_device_by_heads(): lax.ppermute(one, 'core', swap)]
    ppermute x4 -> x3, waiting for transfers between devices: 27.9 us -> 43.6 us  [per_device_by_heads(): lax.ppermute(straight[1][half:], 'head', swap)]
    ppermute x6 -> x4, starting transfers between devices: 12.7 us -> 2.59 us  [the longest x1 2.51 us: per_device_by_heads(): sent['far'] = lax.ppermute(shard, ('role', 'head'), far_swap)]
    all_to_all x4 -> x5, starting transfers between devices: 19.8 us -> 27.9 us  [exchange(): lax.all_to_all(array, 'chip', split_axis=0, concat_axis=0, tiled=True)]
    ppermute x4 -> x3, waiting for transfers between devices: 9.01 us -> 15.6 us  [per_device_by_heads(): lax.ppermute(straight[2][:half], 'role', swap)]
  transfers between devices with their start and end apart: 41 -> 38, of which waited for: 18 -> 16; matrix products, arithmetic and copies ran while one was open for 11% -> 9% of each run, Pallas kernels for 24% -> 24%
where the time goes in v7:
time: 419 us; the launch traced here: 418 us
  waiting for transfers between devices  196 us (47%)
  Pallas kernels  106 us (25%)
  starting transfers between devices  65.7 us (16%)
  other arithmetic  18.9 us (5%)
  local copies, waits for them, and re-layouts  18.7 us (4%)
  matrix products  12.7 us (3%)
    ppermute x3, waiting for transfers between devices, per_device_by_heads(): lax.ppermute(down, 'chip', [(at + 1, at) for at in range(chips - step)])  52.8 us
    pallas_call x4, Pallas kernels, project_heads(): pl.pallas_call(body, in_specs=[in_smem(), in_smem()] + [in_hbm()] * (2 *...  51.6 us
    ppermute x3, waiting for transfers between devices, per_device_by_heads(): lax.ppermute(straight[1][half:], 'head', swap)  43.6 us
    all_to_all x5, waiting for transfers between devices, exchange(): lax.all_to_all(array, 'chip', split_axis=0, concat_axis=0, tiled=True)  42.3 us
    all_to_all x5, starting transfers between devices, exchange(): lax.all_to_all(array, 'chip', split_axis=0, concat_axis=0, tiled=True)  27.9 us
    pallas_call x3, Pallas kernels, out_blocks(): pl.pallas_call(body, grid_spec=pltpu.PrefetchScalarGridSpec(num_scalar_pr...  22.7 us
    pallas_call x2, Pallas kernels, attend(): pl.pallas_call(body, in_specs=[in_smem()] * 4 + [in_hbm()] * len(arrays),...  20.7 us
    ppermute x1, waiting for transfers between devices, per_device_by_heads(): from_head = lax.ppermute(over_head, 'head', swap)  18 us
  transfers between devices with their start and end apart: 38, of which 16 were waited for; matrix products, arithmetic and copies ran while one was open for 9% of the time, Pallas kernels for 24%

profile of v7, /device:TPU:0, one launch (start us, length us, event | category | flops | bytes accessed | tf_op | source)
XLA Modules:
  0.0 418.4 jit_solution(7807643349706991738)
XLA Ops:
  6.2 6.4 %all-to-all-start = ((bf16[4,656,384]{2,1,0:T(8,128)(2,1)}), bf16[4,656,384]{2,1,0:T(8,128)(2,1)S(1)}, u32[]{:S(2)}, u32[]{:S(2)}) async-start(bf16[4,656,384]{2,1,0:T(8,128)(2,1)} %cut_columns.3), calls=%async_computation | async-start | bytes 4030464 | tf_op jit(solution)/shard_map/all_to_all | solution.py:475
  13.0 12.7 %multiply_reduce_fusion = (f32[384]{0:T(512)S(1)}, f32[384,1280]{1,0:T(8,128)}) fusion(bf16[384,5120]{1,0:T(8,128)(2,1)} %param.12, s32[]{:T(128)S(6)} %select_n.109, f32[384]{0:T(512)S(1)} %mul.83, bf16[384,5120]{1,0:T(8,128)(2,1)} %param.10, bf16[5120,1280]{1,0:T(8,128)(2,1)} %param.11, f32[384]{0:T(512)S(1)} %mul.79), kind=kOutput, calls=%fused_computation.5 | convolution fusion | flops 5036604928 | bytes 19993092 | tf_op jit(solution)/shard_map/dot_general | solution.py:493
  39.2 5.5 %collective-permute-start.5 = (bf16[384,1280]{1,0:T(8,128)(2,1)S(1)}, bf16[384,1280]{1,0:T(8,128)(2,1)}, u32[]{:S(2)}, u32[]{:S(2)}) collective-permute-start(bf16[384,1280]{1,0:T(8,128)(2,1)S(1)} %multiply_convert_fusion.refs_2_), channel_id=1, source_target_pairs={{0,4},{4,8},{8,12},{1,5},{5,9},{9,13},{2,6},{6,10},{10,14},{3,7},{... | collective-permute-start | bytes 2949128 | tf_op jit(solution)/shard_map/ppermute | solution.py:570
  44.7 24.0 %collective-permute-done.2 = bf16[384,1280]{1,0:T(8,128)(2,1)S(1)} collective-permute-done((bf16[384,1280]{1,0:T(8,128)(2,1)S(1)}, bf16[384,1280]{1,0:T(8,128)(2,1)S(1)}, u32[]{:S(2)}, u32[]{:S(2)}) %collective-permute-start.2) | collective-permute-done | bytes 983072 | tf_op jit(solution)/shard_map/ppermute | solution.py:573
  79.0 28.8 %collective-permute-done.6 = bf16[384,1280]{1,0:T(8,128)(2,1)} collective-permute-done((bf16[384,1280]{1,0:T(8,128)(2,1)}, bf16[384,1280]{1,0:T(8,128)(2,1)}, u32[]{:S(2)}, u32[]{:S(2)}) %collective-permute-start.6) | collective-permute-done | bytes 983072 | tf_op jit(solution)/shard_map/ppermute | solution.py:573
  117.9 4.1 collective-permute-done.15.refs_5_
  127.3 20.0 %collective-permute-done.16.refs_6_ = bf16[192,1280]{1,0:T(8,128)(2,1)} collective-permute-done((bf16[192,1280]{1,0:T(8,128)(2,1)}, bf16[192,1280]{1,0:T(8,128)(2,1)}, u32[]{:S(2)}, u32[]{:S(2)}) %collective-permute-start.16) | collective-permute-done | bytes 491552 | tf_op jit(solution)/shard_map/ppermute | solution.py:566
  147.3 8.1 %all-to-all-start.1 = ((bf16[4,640,384]{2,1,0:T(8,128)(2,1)}), bf16[4,640,384]{2,1,0:T(8,128)(2,1)}, u32[]{:S(2)}, u32[]{:S(2)}) async-start(bf16[4,640,384]{2,1,0:T(8,128)(2,1)} %cut_columns.4), calls=%async_computation.1 | async-start | bytes 3932160 | tf_op jit(solution)/shard_map/all_to_all | solution.py:475
  155.4 3.8 cut_columns.5
  176.6 22.3 %collective-permute-done.22.refs_11_ = bf16[192,1280]{1,0:T(8,128)(2,1)} collective-permute-done((bf16[192,1280]{1,0:T(8,128)(2,1)S(1)}, bf16[192,1280]{1,0:T(8,128)(2,1)}, u32[]{:S(2)}, u32[]{:S(2)}) %collective-permute-start.22) | collective-permute-done | bytes 491552 | tf_op jit(solution)/shard_map/ppermute | solution.py:566
  205.6 10.3 %project_heads.4 = (bf16[1,2,384,128]{3,2,1,0:T(8,128)(2,1)}, bf16[1,2,2,384,128]{4,3,2,1,0:T(8,128)(2,1)}) custom-call(s32[5]{0:T(128)} %concatenate.8.places_ref, f32[2,1]{1,0:T(2,128)} %get-tuple-element.137.gains_ref, bf16[4,656,384]{2,1,0:T(8,128)(2,1)} %copy-done.2, bf16[4,656,384]{2,1,0:T(8,128)(2,1)} %collective-permute-done.10.refs_1_.refs_2_, ...), custom_call_target="tpu_custom_call" | custom-call | tf_op jit(solution)/shard_map/project_heads/pallas_call | solution.py:257
  216.0 9.5 %collective-permute-done.17.refs_7_.refs_15_ = bf16[192,1280]{1,0:T(8,128)(2,1)S(1)} collective-permute-done((bf16[192,1280]{1,0:T(8,128)(2,1)S(1)}, bf16[192,1280]{1,0:T(8,128)(2,1)S(1)}, u32[]{:S(2)}, u32[]{:S(2)}) %collective-permute-start.17) | collective-permute-done | bytes 491552 | tf_op jit(solution)/shard_map/ppermute | solution.py:565
  227.6 4.8 %all-to-all-start.2 = ((bf16[4,640,384]{2,1,0:T(8,128)(2,1)}), bf16[4,640,384]{2,1,0:T(8,128)(2,1)}, u32[]{:S(2)}, u32[]{:S(2)}) async-start(bf16[4,640,384]{2,1,0:T(8,128)(2,1)} %cut_columns.5), calls=%async_computation.2 | async-start | bytes 3932160 | tf_op jit(solution)/shard_map/all_to_all | solution.py:475
  232.4 42.3 %all-to-all-done.2.refs_0_ = bf16[4,640,384]{2,1,0:T(8,128)(2,1)} async-done(((bf16[4,640,384]{2,1,0:T(8,128)(2,1)}), bf16[4,640,384]{2,1,0:T(8,128)(2,1)}, u32[]{:S(2)}, u32[]{:S(2)}) %all-to-all-start.2) | async-done | bytes 1966112 | tf_op jit(solution)/shard_map/all_to_all | solution.py:475
  276.0 10.3 %project_heads.5 = (bf16[1,2,384,128]{3,2,1,0:T(8,128)(2,1)}, bf16[1,2,2,384,128]{4,3,2,1,0:T(8,128)(2,1)}) custom-call(s32[5]{0:T(128)} %concatenate.8.places_ref, f32[2,1]{1,0:T(2,128)} %get-tuple-element.136.gains_ref, bf16[4,640,384]{2,1,0:T(8,128)(2,1)} %all-to-all-done.1.refs_0_.refs_1_, bf16[4,640,384]{2,1,0:T(8,128)(2,1)} %copy-done.14, ...), custom_call_target="tpu_custom_call" | custom-call | tf_op jit(solution)/shard_map/project_heads/pallas_call | solution.py:257
  286.3 14.0 %project_heads.6 = (bf16[2,2,384,128]{3,2,1,0:T(8,128)(2,1)}, bf16[2,2,2,384,128]{4,3,2,1,0:T(8,128)(2,1)}) custom-call(s32[5]{0:T(128)} %concatenate.8.places_ref, f32[2,2]{1,0:T(2,128)} %bitcast.67, bf16[4,656,384]{2,1,0:T(8,128)(2,1)} %copy-done.2, bf16[4,640,384]{2,1,0:T(8,128)(2,1)} %all-to-all-done.1.refs_0_.refs_1_, ...), custom_call_target="tpu_custom_call" | custom-call | tf_op jit(solution)/shard_map/project_heads/pallas_call | solution.py:257
  304.9 12.9 %attend.2 = bf16[4,2,6,64,128]{4,3,2,1,0:T(8,128)(2,1)} custom-call(s32[3,24,8]{2,1,0:T(8,128)} %fusion.4.slots_ref, s32[3,24]{1,0:T(4,128)} %get-tuple-element.73.counts_ref, s32[24]{0:T(128)} %fusion.8.from_ref, s32[3,4]{1,0:T(4,128)} %reduce_max.9.most_ref, bf16[1,12,64,128]{3,2,1,0:T(8,128)(2,1)} %bitcast.62, bf16[1,2,12,64,128]{4,3,2,1,0:T(8,128)(2,1)} %bitcast.55, ...), custom_call_target="tpu_custom_call" | custom-call | tf_op jit(solution)/shard_map/attend/pallas_call | solution.py:352
  321.5 17.0 %project_heads.7 = (bf16[1,4,384,128]{3,2,1,0:T(8,128)(2,1)}, bf16[1,2,4,384,128]{4,3,2,1,0:T(8,128)(2,1)}) custom-call(s32[5]{0:T(128)} %concatenate.8.places_ref, f32[2,1]{1,0:T(2,128)} %get-tuple-element.135.gains_ref, bf16[4,640,384]{2,1,0:T(8,128)(2,1)} %all-to-all-done.2.refs_0_, bf16[4,640,384]{2,1,0:T(8,128)(2,1)} %collective-permute-done.28.refs_1_, ...), custom_call_target="tpu_custom_call" | custom-call | tf_op jit(solution)/shard_map/project_heads/pallas_call | solution.py:257
  342.0 7.8 %attend.3 = bf16[4,1,6,64,128]{4,3,2,1,0:T(8,128)(2,1)} custom-call(s32[3,24,8]{2,1,0:T(8,128)} %fusion.4.slots_ref, s32[3,24]{1,0:T(4,128)} %get-tuple-element.73.counts_ref, s32[24]{0:T(128)} %fusion.8.from_ref, s32[3,4]{1,0:T(4,128)} %reduce_max.9.most_ref, bf16[1,24,64,128]{3,2,1,0:T(8,128)(2,1)} %bitcast.60, bf16[1,2,24,64,128]{4,3,2,1,0:T(8,128)(2,1)} %bitcast.54, ...), custom_call_target="tpu_custom_call" | custom-call | tf_op jit(solution)/shard_map/attend/pallas_call | solution.py:352
  349.9 4.8 %all-to-all-start.4 = ((bf16[4,1,384,128]{3,2,1,0:T(8,128)(2,1)}), bf16[4,1,384,128]{3,2,1,0:T(8,128)(2,1)S(1)}, u32[]{:S(2)}, u32[]{:S(2)}) async-start(bf16[4,1,384,128]{3,2,1,0:T(8,128)(2,1)} %bitcast.50), calls=%async_computation.4 | async-start | bytes 786432 | tf_op jit(solution)/shard_map/all_to_all | solution.py:475
  356.0 10.7 %out_blocks.3.refs_0_ = f32[4,384,1280]{2,1,0:T(8,128)} custom-call(s32[4]{0:T(128)} %pad_add_fusion.1.which_ref, s32[1]{0:T(128)} %bitcast.3.sign_ref, bf16[4,2,384,128]{3,2,1,0:T(8,128)(2,1)} %copy-done.20, bf16[4,384,5120]{2,1,0:T(8,128)(2,1)} %bitcast.43), custom_call_target="tpu_custom_call" | custom-call | tf_op jit(solution)/shard_map/out_blocks/pallas_call | solution.py:412
  372.6 8.2 %out_blocks.4 = (bf16[384,1280]{1,0:T(8,128)(2,1)}, bf16[384,1280]{1,0:T(8,128)(2,1)}, f32[384,1280]{1,0:T(8,128)}) custom-call(s32[3]{0:T(128)} %pad_add_fusion.which_ref, s32[1]{0:T(128)} %bitcast.3.sign_ref, bf16[4,1,384,128]{3,2,1,0:T(8,128)(2,1)} %copy-done.19, bf16[4,384,5120]{2,1,0:T(8,128)(2,1)} %bitcast.45, f32[4,384,1280]{2,1,0:T(8,128)} %out_blocks.3.refs_0_), custom_call_target="tpu_custom_call" | custom-call | tf_op jit(solution)/shard_map/out_blocks/pallas_call | solution.py:412
  382.9 14.1 %collective-permute-done.32 = bf16[384,1280]{1,0:T(8,128)(2,1)S(1)} collective-permute-done((bf16[384,1280]{1,0:T(8,128)(2,1)}, bf16[384,1280]{1,0:T(8,128)(2,1)S(1)}, u32[]{:S(2)}, u32[]{:S(2)}) %collective-permute-start.32) | collective-permute-done | bytes 983072 | tf_op jit(solution)/shard_map/ppermute | solution.py:653
  397.0 18.0 %collective-permute-done.31 = bf16[384,1280]{1,0:T(8,128)(2,1)S(1)} collective-permute-done((bf16[384,1280]{1,0:T(8,128)(2,1)}, bf16[384,1280]{1,0:T(8,128)(2,1)S(1)}, u32[]{:S(2)}, u32[]{:S(2)}) %collective-permute-start.31) | collective-permute-done | bytes 983072 | tf_op jit(solution)/shard_map/ppermute | solution.py:654
  (177 shorter events, 97.3 us)
Async XLA Ops:
  6.2 64.8 %all-to-all-start = ((bf16[4,656,384]{2,1,0:T(8,128)(2,1)}), bf16[4,656,384]{2,1,0:T(8,128)(2,1)S(1)}, u32[]{:S(2)}, u32[]{:S(2)}) async-start(bf16[4,656,384]{2,1,0:T(8,128)(2,1)} %cut_columns.3), calls=%async_computation | async-start | bytes 4030464 | tf_op jit(solution)/shard_map/all_to_all | solution.py:475
  34.8 33.9 %collective-permute-start.2 = (bf16[384,1280]{1,0:T(8,128)(2,1)S(1)}, bf16[384,1280]{1,0:T(8,128)(2,1)S(1)}, u32[]{:S(2)}, u32[]{:S(2)}) collective-permute-start(bf16[384,1280]{1,0:T(8,128)(2,1)S(1)} %multiply_convert_fusion.refs_2_), channel_id=1, source_target_pairs={{4,0},{8,4},{12,8},{5,1},{9,5},{13,9},{6,2},{10,6},{14,10},{7,3},{... | collective-permute-start | bytes 2949128 | tf_op jit(solution)/shard_map/ppermute | solution.py:573
  36.1 32.6 %collective-permute-start.3 = (bf16[384,1280]{1,0:T(8,128)(2,1)S(1)}, bf16[384,1280]{1,0:T(8,128)(2,1)S(1)}, u32[]{:S(2)}, u32[]{:S(2)}) collective-permute-start(bf16[384,1280]{1,0:T(8,128)(2,1)S(1)} %multiply_convert_fusion.refs_2_), channel_id=1, source_target_pairs={{0,1},{1,0},{2,3},{3,2},{4,5},{5,4},{6,7},{7,6},{8,9},{9,8},{10,11... | collective-permute-start | bytes 2949128 | tf_op jit(solution)/shard_map/ppermute | solution.py:561
  71.0 38.4 %collective-permute-start.10 = (bf16[4,656,384]{2,1,0:T(8,128)(2,1)S(1)}, bf16[4,656,384]{2,1,0:T(8,128)(2,1)}, u32[]{:S(2)}, u32[]{:S(2)}) collective-permute-start(bf16[4,656,384]{2,1,0:T(8,128)(2,1)S(1)} %all-to-all-done.refs_0_), channel_id=1, source_target_pairs={{0,2},{2,0},{1,3},{3,1},{4,6},{6,4},{5,7},{7,5},{8,10},{10,8},{9,1... | collective-permute-start | bytes 6045704 | tf_op jit(solution)/shard_map/ppermute | solution.py:581
  71.1 36.8 %collective-permute-start.6 = (bf16[384,1280]{1,0:T(8,128)(2,1)}, bf16[384,1280]{1,0:T(8,128)(2,1)}, u32[]{:S(2)}, u32[]{:S(2)}) collective-permute-start(bf16[384,1280]{1,0:T(8,128)(2,1)} %copy-done.17), channel_id=1, source_target_pairs={{4,0},{8,4},{5,1},{9,5},{6,2},{10,6},{7,3},{11,7},{20,16},{24,20},... | collective-permute-start | bytes 2949128 | tf_op jit(solution)/shard_map/ppermute | solution.py:573
  74.3 35.1 %collective-permute-start.7 = (bf16[384,1280]{1,0:T(8,128)(2,1)S(1)}, bf16[384,1280]{1,0:T(8,128)(2,1)S(1)}, u32[]{:S(2)}, u32[]{:S(2)}) collective-permute-start(bf16[384,1280]{1,0:T(8,128)(2,1)S(1)} %select_select_fusion.1.refs_7_), channel_id=1, source_target_pairs={{0,1},{1,0},{2,3},{3,2},{4,5},{5,4},{6,7},{7,6},{8,9},{9,8},{10,11... | collective-permute-start | bytes 2949128 | tf_op jit(solution)/shard_map/ppermute | solution.py:561
  76.0 33.4 %collective-permute-start.8 = (bf16[384,1280]{1,0:T(8,128)(2,1)S(1)}, bf16[384,1280]{1,0:T(8,128)(2,1)S(1)}, u32[]{:S(2)}, u32[]{:S(2)}) collective-permute-start(bf16[384,1280]{1,0:T(8,128)(2,1)S(1)} %select_select_fusion.1.refs_7_), channel_id=1, source_target_pairs={{0,16},{16,0},{1,17},{17,1},{2,18},{18,2},{3,19},{19,3},{4,20},{20... | collective-permute-start | bytes 2949128 | tf_op jit(solution)/shard_map/ppermute | solution.py:560
  77.4 32.0 %collective-permute-start.9 = (bf16[384,1280]{1,0:T(8,128)(2,1)}, bf16[384,1280]{1,0:T(8,128)(2,1)}, u32[]{:S(2)}, u32[]{:S(2)}) collective-permute-start(bf16[384,1280]{1,0:T(8,128)(2,1)} %collective-permute-done.5), channel_id=1, source_target_pairs={{4,8},{8,12},{5,9},{9,13},{6,10},{10,14},{7,11},{11,15},{20,24},{2... | collective-permute-start | bytes 2949128 | tf_op jit(solution)/shard_map/ppermute | solution.py:570
  110.7 36.6 %collective-permute-start.11 = (bf16[384,1280]{1,0:T(8,128)(2,1)}, bf16[384,1280]{1,0:T(8,128)(2,1)}, u32[]{:S(2)}, u32[]{:S(2)}) collective-permute-start(bf16[384,1280]{1,0:T(8,128)(2,1)} %collective-permute-done.6), channel_id=1, source_target_pairs={{4,0},{5,1},{6,2},{7,3},{20,16},{21,17},{22,18},{23,19}} | collective-permute-start | bytes 2949128 | tf_op jit(solution)/shard_map/ppermute | solution.py:573
  113.4 33.9 %collective-permute-start.12 = (bf16[384,1280]{1,0:T(8,128)(2,1)S(1)}, bf16[384,1280]{1,0:T(8,128)(2,1)}, u32[]{:S(2)}, u32[]{:S(2)}) collective-permute-start(bf16[384,1280]{1,0:T(8,128)(2,1)S(1)} %fusion.2.refs_4_.refs_12_), channel_id=1, source_target_pairs={{0,1},{1,0},{2,3},{3,2},{4,5},{5,4},{6,7},{7,6},{8,9},{9,8},{10,11... | collective-permute-start | bytes 2949128 | tf_op jit(solution)/shard_map/ppermute | solution.py:561
  114.9 32.3 %collective-permute-start.13 = (bf16[384,1280]{1,0:T(8,128)(2,1)S(1)}, bf16[384,1280]{1,0:T(8,128)(2,1)}, u32[]{:S(2)}, u32[]{:S(2)}) collective-permute-start(bf16[384,1280]{1,0:T(8,128)(2,1)S(1)} %fusion.2.refs_4_.refs_12_), channel_id=1, source_target_pairs={{0,16},{16,0},{1,17},{17,1},{2,18},{18,2},{3,19},{19,3},{4,20},{20... | collective-permute-start | bytes 2949128 | tf_op jit(solution)/shard_map/ppermute | solution.py:560
  115.5 31.8 %collective-permute-start.14 = (bf16[384,1280]{1,0:T(8,128)(2,1)}, bf16[384,1280]{1,0:T(8,128)(2,1)}, u32[]{:S(2)}, u32[]{:S(2)}) collective-permute-start(bf16[384,1280]{1,0:T(8,128)(2,1)} %collective-permute-done.9), channel_id=1, source_target_pairs={{8,12},{9,13},{10,14},{11,15},{24,28},{25,29},{26,30},{27,31}} | collective-permute-start | bytes 2949128 | tf_op jit(solution)/shard_map/ppermute | solution.py:570
  147.3 79.5 %all-to-all-start.1 = ((bf16[4,640,384]{2,1,0:T(8,128)(2,1)}), bf16[4,640,384]{2,1,0:T(8,128)(2,1)}, u32[]{:S(2)}, u32[]{:S(2)}) async-start(bf16[4,640,384]{2,1,0:T(8,128)(2,1)} %cut_columns.4), calls=%async_computation.1 | async-start | bytes 3932160 | tf_op jit(solution)/shard_map/all_to_all | solution.py:475
  163.5 35.4 %collective-permute-start.22 = (bf16[192,1280]{1,0:T(8,128)(2,1)S(1)}, bf16[192,1280]{1,0:T(8,128)(2,1)}, u32[]{:S(2)}, u32[]{:S(2)}) collective-permute-start(bf16[192,1280]{1,0:T(8,128)(2,1)S(1)} %slice.79), channel_id=1, source_target_pairs={{0,1},{1,0},{2,3},{3,2},{4,5},{5,4},{6,7},{7,6},{8,9},{9,8},{10,11... | collective-permute-start | bytes 1474568 | tf_op jit(solution)/shard_map/ppermute | solution.py:566
  165.5 61.3 %collective-permute-start.19 = (bf16[384,1280]{1,0:T(8,128)(2,1)S(1)}, bf16[384,1280]{1,0:T(8,128)(2,1)}, u32[]{:S(2)}, u32[]{:S(2)}) collective-permute-start(bf16[384,1280]{1,0:T(8,128)(2,1)S(1)} %select_select_fusion.2.refs_9_.refs_17_), channel_id=1, source_target_pairs={{0,17},{1,16},{16,1},{17,0},{2,19},{3,18},{18,3},{19,2},{4,21},{5,... | collective-permute-start | bytes 2949128 | tf_op jit(solution)/shard_map/ppermute | solution.py:577
  168.0 58.8 %collective-permute-start.20 = (bf16[384,1280]{1,0:T(8,128)(2,1)S(1)}, bf16[384,1280]{1,0:T(8,128)(2,1)}, u32[]{:S(2)}, u32[]{:S(2)}) collective-permute-start(bf16[384,1280]{1,0:T(8,128)(2,1)S(1)} %select_select_fusion.2.refs_9_.refs_17_), channel_id=1, source_target_pairs={{0,1},{1,0},{2,3},{3,2},{4,5},{5,4},{6,7},{7,6},{8,9},{9,8},{10,11... | collective-permute-start | bytes 2949128 | tf_op jit(solution)/shard_map/ppermute | solution.py:561
  168.5 58.3 %collective-permute-start.23 = (bf16[384,1280]{1,0:T(8,128)(2,1)S(1)}, bf16[384,1280]{1,0:T(8,128)(2,1)}, u32[]{:S(2)}, u32[]{:S(2)}) collective-permute-start(bf16[384,1280]{1,0:T(8,128)(2,1)S(1)} %select_select_fusion.2.refs_9_.refs_17_), channel_id=1, source_target_pairs={{0,16},{16,0},{1,17},{17,1},{2,18},{18,2},{3,19},{19,3},{4,20},{20... | collective-permute-start | bytes 2949128 | tf_op jit(solution)/shard_map/ppermute | solution.py:560
  176.1 49.4 %collective-permute-start.17 = (bf16[192,1280]{1,0:T(8,128)(2,1)S(1)}, bf16[192,1280]{1,0:T(8,128)(2,1)S(1)}, u32[]{:S(2)}, u32[]{:S(2)}) collective-permute-start(bf16[192,1280]{1,0:T(8,128)(2,1)S(1)} %slice.75), channel_id=1, source_target_pairs={{0,16},{16,0},{1,17},{17,1},{2,18},{18,2},{3,19},{19,3},{4,20},{20... | collective-permute-start | bytes 1474568 | tf_op jit(solution)/shard_map/ppermute | solution.py:565
  227.6 47.1 %all-to-all-start.2 = ((bf16[4,640,384]{2,1,0:T(8,128)(2,1)}), bf16[4,640,384]{2,1,0:T(8,128)(2,1)}, u32[]{:S(2)}, u32[]{:S(2)}) async-start(bf16[4,640,384]{2,1,0:T(8,128)(2,1)} %cut_columns.5), calls=%async_computation.2 | async-start | bytes 3932160 | tf_op jit(solution)/shard_map/all_to_all | solution.py:475
  232.4 42.3 %collective-permute-start.24 = (bf16[4,640,384]{2,1,0:T(8,128)(2,1)}, bf16[4,640,384]{2,1,0:T(8,128)(2,1)S(1)}, u32[]{:S(2)}, u32[]{:S(2)}) collective-permute-start(bf16[4,640,384]{2,1,0:T(8,128)(2,1)} %all-to-all-done.1.refs_0_.refs_1_), channel_id=1, source_target_pairs={{0,2},{2,0},{1,3},{3,1},{4,6},{6,4},{5,7},{7,5},{8,10},{10,8},{9,1... | collective-permute-start | bytes 5898248 | tf_op jit(solution)/shard_map/ppermute | solution.py:613
  274.7 46.8 %collective-permute-start.28 = (bf16[4,640,384]{2,1,0:T(8,128)(2,1)}, bf16[4,640,384]{2,1,0:T(8,128)(2,1)}, u32[]{:S(2)}, u32[]{:S(2)}) collective-permute-start(bf16[4,640,384]{2,1,0:T(8,128)(2,1)} %all-to-all-done.2.refs_0_), channel_id=1, source_target_pairs={{0,2},{2,0},{1,3},{3,1},{4,6},{6,4},{5,7},{7,5},{8,10},{10,8},{9,1... | collective-permute-start | bytes 5898248 | tf_op jit(solution)/shard_map/ppermute | solution.py:613
  317.8 32.1 %all-to-all-start.3 = ((bf16[4,2,384,128]{3,2,1,0:T(8,128)(2,1)}), bf16[4,2,384,128]{3,2,1,0:T(8,128)(2,1)S(1)}, u32[]{:S(2)}, u32[]{:S(2)}) async-start(bf16[4,2,384,128]{3,2,1,0:T(8,128)(2,1)} %bitcast.49), calls=%async_computation.3 | async-start | bytes 1572864 | tf_op jit(solution)/shard_map/all_to_all | solution.py:475
  380.8 34.2 %collective-permute-start.31 = (bf16[384,1280]{1,0:T(8,128)(2,1)}, bf16[384,1280]{1,0:T(8,128)(2,1)S(1)}, u32[]{:S(2)}, u32[]{:S(2)}) collective-permute-start(bf16[384,1280]{1,0:T(8,128)(2,1)} %get-tuple-element.132), channel_id=1, source_target_pairs={{0,1},{1,0},{2,3},{3,2},{4,5},{5,4},{6,7},{7,6},{8,9},{9,8},{10,11... | collective-permute-start | bytes 2949128 | tf_op jit(solution)/shard_map/ppermute | solution.py:654
  382.4 32.7 %collective-permute-start.30 = (bf16[384,1280]{1,0:T(8,128)(2,1)}, bf16[384,1280]{1,0:T(8,128)(2,1)S(1)}, u32[]{:S(2)}, u32[]{:S(2)}) collective-permute-start(bf16[384,1280]{1,0:T(8,128)(2,1)} %get-tuple-element.131), channel_id=1, source_target_pairs={{0,16},{16,0},{1,17},{17,1},{2,18},{18,2},{3,19},{19,3},{4,20},{20... | collective-permute-start | bytes 2949128 | tf_op jit(solution)/shard_map/ppermute | solution.py:655
  (46 other events, 802.7 us)

commit v8 on v7

--- a/solution.py
+++ b/solution.py
@@ -554,18 +554,14 @@
     straight = None
     shard, up, down = normed, normed, normed
     ups, downs = [None], [None]
-    late = None
     for phase in range(chips):
+        step = phase + 1
         sent = {}
         sent["role"] = lax.ppermute(shard, "role", swap)
         sent["head"] = lax.ppermute(shard, "head", swap)
-        diagonal = None
         if straight is not None:
-            diagonal = straight + (
-                lax.ppermute(straight[2][:half], "role", swap),
-                lax.ppermute(straight[1][half:], "head", swap),
-            )
-        step = phase + 1
+            sent["first"] = lax.ppermute(straight[2][:half], "role", swap)
+            sent["second"] = lax.ppermute(straight[1][half:], "head", swap)
         if step < chips:
             sent["up"] = lax.ppermute(
                 up, "chip", [(at, at + 1) for at in range(step - 1, chips - 1)]
@@ -577,25 +573,36 @@
             sent["far"] = lax.ppermute(shard, ("role", "head"), far_swap)
         if phase == 0:
             sent["weights"] = weights_own.pop()
+            sent["cuts"] = cuts[1:]
         if phase == 1:
             sent["weights"] = lax.ppermute(weights_own[0], "core", swap)
+            sent["places"] = places
+            sent["gains"] = gains
         if step == chips:
-            early = rounds + [late]
+            early = list(rounds)
             tables = tables_of(weights_own[0][:, depth:])
             held_places, tables = lax.optimization_barrier((places, tables))
-            held_places = project(0, 0, 1, 0, early, held_places)
-            sent["places"] = held_places
-            sent["diagonal"] = diagonal
-        sent, shard, late = lax.optimization_barrier((sent, shard, late))
+            sent["places"] = project(0, 0, 1, 0, early, held_places)
+            if len(weights_own) < heads:
+                held, _ = lax.optimization_barrier(
+                    (cuts[len(weights_own)], (sent["role"], sent["head"]))
+                )
+                weights_own.append(exchange(held))
+        if step == chips - 1 and len(weights_own) < heads - 1:
+            for cut in cuts[len(weights_own) : heads - 1]:
+                held, _ = lax.optimization_barrier((cut, (sent["up"], sent["down"])))
+                weights_own.append(exchange(held))
+        sent, shard = lax.optimization_barrier((sent, shard))
         if phase == 0:
             weights_own.append(sent["weights"])
+            cuts[1:] = sent["cuts"]
         if phase == 1:
             weights_other.append(sent["weights"])
+            places, gains = sent["places"], sent["gains"]
+        if straight is not None:
+            rounds.append(straight + (sent["first"], sent["second"]))
         if step == chips:
-            held_places, diagonal = sent["places"], sent["diagonal"]
-        if late is not None:
-            rounds.append(late)
-        late = diagonal
+            held_places = sent["places"]
         straight = (shard, sent["role"], sent["head"])
         if step < chips:
             up, down = sent["up"], sent["down"]
@@ -606,16 +613,8 @@
                 source = order[here][step - 1]
                 options.append(ups[here - source] if source < here else downs[source - here])
             shard = pick(chip, options)
-        if phase >= chips - 2 and len(weights_own) < heads:
-            held, _ = lax.optimization_barrier((cuts[len(weights_own)], sent))
-            weights_own.append(exchange(held))
-            if step == chips:
-                weights_other += [lax.ppermute(one, "core", swap) for one in weights_own[1:]]
-    rounds.append(late)
     rounds.append(straight + (sent["far"],))
-    while len(weights_own) < heads:
-        weights_own.append(exchange(cuts[len(weights_own)]))
-    for at in range(len(weights_other), heads):
+    for at in range(len(weights_other), heads - 1):
         weights_other.append(lax.ppermute(weights_own[at], "core", swap))
 
     attended = []
@@ -624,6 +623,11 @@
             for at in range(1, size):
                 held_places = project(0, at, 1, 0, early, held_places)
             held_places = project(0, 0, size, len(early), rounds[len(early) :], held_places)
+            for at in range(len(weights_other), heads):
+                weights_own[at], held_places = lax.optimization_barrier(
+                    (weights_own[at], held_places)
+                )
+                weights_other.append(lax.ppermute(weights_own[at], "core", swap))
         else:
             held_places = project(chunk, 0, size, 0, rounds, held_places)
         mixed = attend(spans[chunk].start, size, *tables, parts[chunk])

time: 419 us -> 400 us (0.955)
  waiting for transfers between devices: 196 us -> 181 us
    all_to_all x5, waiting for transfers between devices: 42.3 us -> 0.01 us  [exchange(): lax.all_to_all(array, 'chip', split_axis=0, concat_axis=0, tiled=True)]
    ppermute x4, waiting for transfers between devices: 0.01 us -> 19.6 us  [per_device_by_heads(): sent['role'] = lax.ppermute(shard, 'role', swap)]
    ppermute x1, waiting for transfers between devices: 0.01 us -> 19.1 us  [per_device_by_heads(): from_role = lax.ppermute(over_role, 'role', swap)]
    ppermute x1, waiting for transfers between devices: 18 us -> 0.81 us  [per_device_by_heads(): from_head = lax.ppermute(over_head, 'head', swap)]
    ppermute x4, waiting for transfers between devices: 0.01 us -> 15.8 us  [per_device_by_heads(): sent['head'] = lax.ppermute(shard, 'head', swap)]
    ppermute x8, waiting for transfers between devices: 59.2 us -> 47.4 us  [the longest x3 39.4 us: per_device_by_heads(): sent['first'] = lax.ppermute(straight[2][:half], 'role', swap)]
    unnamed x68 -> x54, local copies, waits for them, and re-layouts: 9.62 us -> 6.24 us
  transfers between devices with their start and end apart: 38 -> 38, of which waited for: 16 -> 20; matrix products, arithmetic and copies ran while one was open for 9% -> 10% of each run, Pallas kernels for 24% -> 24%
where the time goes in v8:
time: 400 us; the launch traced here: 397 us
  waiting for transfers between devices  181 us (45%)
  Pallas kernels  102 us (26%)
  starting transfers between devices  63.9 us (16%)
  other arithmetic  19.5 us (5%)
  local copies, waits for them, and re-layouts  18.2 us (5%)
  matrix products  12.7 us (3%)
    ppermute x3, waiting for transfers between devices, per_device_by_heads(): lax.ppermute(down, 'chip', [(at + 1, at) for at in range(chips - step)])  52.1 us
    pallas_call x4, Pallas kernels, project_heads(): pl.pallas_call(body, in_specs=[in_smem(), in_smem()] + [in_hbm()] * (2 *...  51.6 us
    ppermute x3, waiting for transfers between devices, per_device_by_heads(): sent['first'] = lax.ppermute(straight[2][:half], 'role', swap)  39.4 us
    all_to_all x5, starting transfers between devices, exchange(): lax.all_to_all(array, 'chip', split_axis=0, concat_axis=0, tiled=True)  26.1 us
    pallas_call x3, Pallas kernels, out_blocks(): pl.pallas_call(body, grid_spec=pltpu.PrefetchScalarGridSpec(num_scalar_pr...  22.7 us
    ppermute x4, waiting for transfers between devices, per_device_by_heads(): sent['role'] = lax.ppermute(shard, 'role', swap)  19.6 us
    ppermute x1, waiting for transfers between devices, per_device_by_heads(): from_role = lax.ppermute(over_role, 'role', swap)  19.1 us
    pallas_call x2, Pallas kernels, attend(): pl.pallas_call(body, in_specs=[in_smem()] * 4 + [in_hbm()] * len(arrays),...  16.5 us
  transfers between devices with their start and end apart: 38, of which 20 were waited for; matrix products, arithmetic and copies ran while one was open for 10% of the time, Pallas kernels for 24%

profile of v8, /device:TPU:0, one launch (start us, length us, event | category | flops | bytes accessed | tf_op | source)
XLA Modules:
  0.0 397.4 jit_solution(6096303722343505735)
XLA Ops:
  6.2 6.4 %all-to-all-start = ((bf16[4,656,384]{2,1,0:T(8,128)(2,1)}), bf16[4,656,384]{2,1,0:T(8,128)(2,1)S(1)}, u32[]{:S(2)}, u32[]{:S(2)}) async-start(bf16[4,656,384]{2,1,0:T(8,128)(2,1)} %cut_columns.5), calls=%async_computation | async-start | bytes 4030464 | tf_op jit(solution)/shard_map/all_to_all | solution.py:475
  13.0 12.7 %multiply_reduce_fusion = (f32[384]{0:T(512)S(1)}, f32[384,1280]{1,0:T(8,128)}) fusion(bf16[384,5120]{1,0:T(8,128)(2,1)} %param.12, s32[]{:T(128)S(6)} %select_n.109, f32[384]{0:T(512)S(1)} %mul.83, bf16[384,5120]{1,0:T(8,128)(2,1)} %param.10, bf16[5120,1280]{1,0:T(8,128)(2,1)} %param.11, f32[384]{0:T(512)S(1)} %mul.79), kind=kOutput, calls=%fused_computation.5 | convolution fusion | flops 5036604928 | bytes 19993092 | tf_op jit(solution)/shard_map/dot_general | solution.py:493
  39.2 5.5 %collective-permute-start.5 = (bf16[384,1280]{1,0:T(8,128)(2,1)S(1)}, bf16[384,1280]{1,0:T(8,128)(2,1)}, u32[]{:S(2)}, u32[]{:S(2)}) collective-permute-start(bf16[384,1280]{1,0:T(8,128)(2,1)S(1)} %multiply_convert_fusion.refs_2_), channel_id=1, source_target_pairs={{0,4},{4,8},{8,12},{1,5},{5,9},{9,13},{2,6},{6,10},{10,14},{3,7},{... | collective-permute-start | bytes 2949128 | tf_op jit(solution)/shard_map/ppermute | solution.py:566
  52.2 16.6 %collective-permute-done.2 = bf16[384,1280]{1,0:T(8,128)(2,1)} collective-permute-done((bf16[384,1280]{1,0:T(8,128)(2,1)S(1)}, bf16[384,1280]{1,0:T(8,128)(2,1)}, u32[]{:S(2)}, u32[]{:S(2)}) %collective-permute-start.2) | collective-permute-done | bytes 983072 | tf_op jit(solution)/shard_map/ppermute | solution.py:569
  77.3 7.2 %collective-permute-done.10.refs_6_ = bf16[192,1280]{1,0:T(8,128)(2,1)S(1)} collective-permute-done((bf16[192,1280]{1,0:T(8,128)(2,1)S(1)}, bf16[192,1280]{1,0:T(8,128)(2,1)S(1)}, u32[]{:S(2)}, u32[]{:S(2)}) %collective-permute-start.10) | collective-permute-done | bytes 491552 | tf_op jit(solution)/shard_map/ppermute | solution.py:564
  89.5 15.4 %collective-permute-done.8.refs_9_ = bf16[384,1280]{1,0:T(8,128)(2,1)} collective-permute-done((bf16[384,1280]{1,0:T(8,128)(2,1)S(1)}, bf16[384,1280]{1,0:T(8,128)(2,1)}, u32[]{:S(2)}, u32[]{:S(2)}) %collective-permute-start.8) | collective-permute-done | bytes 983072 | tf_op jit(solution)/shard_map/ppermute | solution.py:561
  107.3 15.0 %collective-permute-done.6 = bf16[384,1280]{1,0:T(8,128)(2,1)} collective-permute-done((bf16[384,1280]{1,0:T(8,128)(2,1)}, bf16[384,1280]{1,0:T(8,128)(2,1)}, u32[]{:S(2)}, u32[]{:S(2)}) %collective-permute-start.6) | collective-permute-done | bytes 983072 | tf_op jit(solution)/shard_map/ppermute | solution.py:569
  125.2 20.6 %collective-permute-done.13 = bf16[384,1280]{1,0:T(8,128)(2,1)} collective-permute-done((bf16[384,1280]{1,0:T(8,128)(2,1)}, bf16[384,1280]{1,0:T(8,128)(2,1)}, u32[]{:S(2)}, u32[]{:S(2)}) %collective-permute-start.13) | collective-permute-done | bytes 983072 | tf_op jit(solution)/shard_map/ppermute | solution.py:569
  158.3 25.8 %collective-permute-done.14.refs_10_ = bf16[192,1280]{1,0:T(8,128)(2,1)S(1)} collective-permute-done((bf16[192,1280]{1,0:T(8,128)(2,1)S(1)}, bf16[192,1280]{1,0:T(8,128)(2,1)S(1)}, u32[]{:S(2)}, u32[]{:S(2)}) %collective-permute-start.14) | collective-permute-done | bytes 491552 | tf_op jit(solution)/shard_map/ppermute | solution.py:563
  189.4 17.2 %collective-permute-done.19.refs_10_.refs_18_ = bf16[384,1280]{1,0:T(8,128)(2,1)S(1)} collective-permute-done((bf16[384,1280]{1,0:T(8,128)(2,1)S(1)}, bf16[384,1280]{1,0:T(8,128)(2,1)S(1)}, u32[]{:S(2)}, u32[]{:S(2)}) %collective-permute-start.19) | collective-permute-done | bytes 983072 | tf_op jit(solution)/shard_map/ppermute | solution.py:560
  207.9 5.0 %all-to-all-start.1 = ((bf16[4,640,384]{2,1,0:T(8,128)(2,1)}), bf16[4,640,384]{2,1,0:T(8,128)(2,1)}, u32[]{:S(2)}, u32[]{:S(2)}) async-start(bf16[4,640,384]{2,1,0:T(8,128)(2,1)} %cut_columns.4), calls=%async_computation.1 | async-start | bytes 3932160 | tf_op jit(solution)/shard_map/all_to_all | solution.py:475
  229.6 10.3 %project_heads.4 = (bf16[1,2,384,128]{3,2,1,0:T(8,128)(2,1)}, bf16[1,2,2,384,128]{4,3,2,1,0:T(8,128)(2,1)}) custom-call(s32[5]{0:T(128)} %concatenate.9.places_ref, f32[2,1]{1,0:T(2,128)} %get-tuple-element.131.gains_ref, bf16[4,656,384]{2,1,0:T(8,128)(2,1)} %copy-done.2, bf16[4,656,384]{2,1,0:T(8,128)(2,1)} %collective-permute-done.12.refs_1_.refs_2_, ...), custom_call_target="tpu_custom_call" | custom-call | tf_op jit(solution)/shard_map/project_heads/pallas_call | solution.py:257
  239.9 12.3 %collective-permute-done.22.refs_7_.refs_15_ = bf16[192,1280]{1,0:T(8,128)(2,1)S(1)} collective-permute-done((bf16[192,1280]{1,0:T(8,128)(2,1)S(1)}, bf16[192,1280]{1,0:T(8,128)(2,1)S(1)}, u32[]{:S(2)}, u32[]{:S(2)}) %collective-permute-start.22) | collective-permute-done | bytes 491552 | tf_op jit(solution)/shard_map/ppermute | solution.py:563
  253.0 10.3 %project_heads.5 = (bf16[1,2,384,128]{3,2,1,0:T(8,128)(2,1)}, bf16[1,2,2,384,128]{4,3,2,1,0:T(8,128)(2,1)}) custom-call(s32[5]{0:T(128)} %concatenate.9.places_ref, f32[2,1]{1,0:T(2,128)} %get-tuple-element.130.gains_ref, bf16[4,640,384]{2,1,0:T(8,128)(2,1)} %all-to-all-done.2.refs_0_.refs_1_, bf16[4,640,384]{2,1,0:T(8,128)(2,1)} %collective-permute-done.24.refs_1_.refs_3_, ...), custom_call_target="tpu_custom_call" | custom-call | tf_op jit(solution)/shard_map/project_heads/pallas_call | solution.py:257
  263.4 13.9 %project_heads.6 = (bf16[2,2,384,128]{3,2,1,0:T(8,128)(2,1)}, bf16[2,2,2,384,128]{4,3,2,1,0:T(8,128)(2,1)}) custom-call(s32[5]{0:T(128)} %concatenate.9.places_ref, f32[2,2]{1,0:T(2,128)} %bitcast.67, bf16[4,656,384]{2,1,0:T(8,128)(2,1)} %copy-done.2, bf16[4,640,384]{2,1,0:T(8,128)(2,1)} %all-to-all-done.2.refs_0_.refs_1_, ...), custom_call_target="tpu_custom_call" | custom-call | tf_op jit(solution)/shard_map/project_heads/pallas_call | solution.py:257
  284.6 10.1 %attend.2 = bf16[4,2,6,64,128]{4,3,2,1,0:T(8,128)(2,1)} custom-call(s32[3,24,8]{2,1,0:T(8,128)} %fusion.4.slots_ref, s32[3,24]{1,0:T(4,128)} %get-tuple-element.75.counts_ref, s32[24]{0:T(128)} %fusion.8.from_ref, s32[3,4]{1,0:T(4,128)} %reduce_max.9.most_ref, bf16[1,12,64,128]{3,2,1,0:T(8,128)(2,1)} %bitcast.62, bf16[1,2,12,64,128]{4,3,2,1,0:T(8,128)(2,1)} %bitcast.55, ...), custom_call_target="tpu_custom_call" | custom-call | tf_op jit(solution)/shard_map/attend/pallas_call | solution.py:352
  294.7 5.1 %all-to-all-start.3 = ((bf16[4,2,384,128]{3,2,1,0:T(8,128)(2,1)}), bf16[4,2,384,128]{3,2,1,0:T(8,128)(2,1)S(1)}, u32[]{:S(2)}, u32[]{:S(2)}) async-start(bf16[4,2,384,128]{3,2,1,0:T(8,128)(2,1)} %bitcast.49), calls=%async_computation.3 | async-start | bytes 1572864 | tf_op jit(solution)/shard_map/all_to_all | solution.py:475
  299.8 17.0 %project_heads.7 = (bf16[1,4,384,128]{3,2,1,0:T(8,128)(2,1)}, bf16[1,2,4,384,128]{4,3,2,1,0:T(8,128)(2,1)}) custom-call(s32[5]{0:T(128)} %concatenate.9.places_ref, f32[2,1]{1,0:T(2,128)} %get-tuple-element.129.gains_ref, bf16[4,640,384]{2,1,0:T(8,128)(2,1)} %all-to-all-done.1.refs_0_, bf16[4,640,384]{2,1,0:T(8,128)(2,1)} %collective-permute-done.28.refs_1_, ...), custom_call_target="tpu_custom_call" | custom-call | tf_op jit(solution)/shard_map/project_heads/pallas_call | solution.py:257
  320.3 6.5 %attend.3 = bf16[4,1,6,64,128]{4,3,2,1,0:T(8,128)(2,1)} custom-call(s32[3,24,8]{2,1,0:T(8,128)} %fusion.4.slots_ref, s32[3,24]{1,0:T(4,128)} %get-tuple-element.75.counts_ref, s32[24]{0:T(128)} %fusion.8.from_ref, s32[3,4]{1,0:T(4,128)} %reduce_max.9.most_ref, bf16[1,24,64,128]{3,2,1,0:T(8,128)(2,1)} %bitcast.60, bf16[1,2,24,64,128]{4,3,2,1,0:T(8,128)(2,1)} %bitcast.54, ...), custom_call_target="tpu_custom_call" | custom-call | tf_op jit(solution)/shard_map/attend/pallas_call | solution.py:352
  326.8 5.1 %all-to-all-start.4 = ((bf16[4,1,384,128]{3,2,1,0:T(8,128)(2,1)}), bf16[4,1,384,128]{3,2,1,0:T(8,128)(2,1)S(1)}, u32[]{:S(2)}, u32[]{:S(2)}) async-start(bf16[4,1,384,128]{3,2,1,0:T(8,128)(2,1)} %bitcast.50), calls=%async_computation.4 | async-start | bytes 786432 | tf_op jit(solution)/shard_map/all_to_all | solution.py:475
  333.2 10.7 %out_blocks.3.refs_0_ = f32[4,384,1280]{2,1,0:T(8,128)} custom-call(s32[4]{0:T(128)} %pad_add_fusion.1.which_ref, s32[1]{0:T(128)} %bitcast.3.sign_ref, bf16[4,2,384,128]{3,2,1,0:T(8,128)(2,1)} %copy-done.14, bf16[4,384,5120]{2,1,0:T(8,128)(2,1)} %bitcast.43), custom_call_target="tpu_custom_call" | custom-call | tf_op jit(solution)/shard_map/out_blocks/pallas_call | solution.py:412
  349.6 8.2 %out_blocks.4 = (bf16[384,1280]{1,0:T(8,128)(2,1)}, bf16[384,1280]{1,0:T(8,128)(2,1)}, f32[384,1280]{1,0:T(8,128)}) custom-call(s32[3]{0:T(128)} %pad_add_fusion.which_ref, s32[1]{0:T(128)} %bitcast.3.sign_ref, bf16[4,1,384,128]{3,2,1,0:T(8,128)(2,1)} %copy-done.13, bf16[4,384,5120]{2,1,0:T(8,128)(2,1)} %bitcast.45, f32[4,384,1280]{2,1,0:T(8,128)} %out_blocks.3.refs_0_), custom_call_target="tpu_custom_call" | custom-call | tf_op jit(solution)/shard_map/out_blocks/pallas_call | solution.py:412
  360.1 14.1 %collective-permute-done.32 = bf16[384,1280]{1,0:T(8,128)(2,1)S(1)} collective-permute-done((bf16[384,1280]{1,0:T(8,128)(2,1)}, bf16[384,1280]{1,0:T(8,128)(2,1)S(1)}, u32[]{:S(2)}, u32[]{:S(2)}) %collective-permute-start.32) | collective-permute-done | bytes 983072 | tf_op jit(solution)/shard_map/ppermute | solution.py:657
  374.2 19.1 %collective-permute-done.30 = bf16[384,1280]{1,0:T(8,128)(2,1)S(1)} collective-permute-done((bf16[384,1280]{1,0:T(8,128)(2,1)}, bf16[384,1280]{1,0:T(8,128)(2,1)S(1)}, u32[]{:S(2)}, u32[]{:S(2)}) %collective-permute-start.30) | collective-permute-done | bytes 983072 | tf_op jit(solution)/shard_map/ppermute | solution.py:659
  (163 shorter events, 106.9 us)
Async XLA Ops:
  6.2 62.6 %all-to-all-start = ((bf16[4,656,384]{2,1,0:T(8,128)(2,1)}), bf16[4,656,384]{2,1,0:T(8,128)(2,1)S(1)}, u32[]{:S(2)}, u32[]{:S(2)}) async-start(bf16[4,656,384]{2,1,0:T(8,128)(2,1)} %cut_columns.5), calls=%async_computation | async-start | bytes 4030464 | tf_op jit(solution)/shard_map/all_to_all | solution.py:475
  34.8 34.0 %collective-permute-start.2 = (bf16[384,1280]{1,0:T(8,128)(2,1)S(1)}, bf16[384,1280]{1,0:T(8,128)(2,1)}, u32[]{:S(2)}, u32[]{:S(2)}) collective-permute-start(bf16[384,1280]{1,0:T(8,128)(2,1)S(1)} %multiply_convert_fusion.refs_2_), channel_id=1, source_target_pairs={{4,0},{8,4},{12,8},{5,1},{9,5},{13,9},{6,2},{10,6},{14,10},{7,3},{... | collective-permute-start | bytes 2949128 | tf_op jit(solution)/shard_map/ppermute | solution.py:569
  36.1 32.7 %collective-permute-start.3 = (bf16[384,1280]{1,0:T(8,128)(2,1)S(1)}, bf16[384,1280]{1,0:T(8,128)(2,1)}, u32[]{:S(2)}, u32[]{:S(2)}) collective-permute-start(bf16[384,1280]{1,0:T(8,128)(2,1)S(1)} %multiply_convert_fusion.refs_2_), channel_id=1, source_target_pairs={{0,1},{1,0},{2,3},{3,2},{4,5},{5,4},{6,7},{7,6},{8,9},{9,8},{10,11... | collective-permute-start | bytes 2949128 | tf_op jit(solution)/shard_map/ppermute | solution.py:561
  37.8 31.0 %collective-permute-start.4 = (bf16[384,1280]{1,0:T(8,128)(2,1)S(1)}, bf16[384,1280]{1,0:T(8,128)(2,1)}, u32[]{:S(2)}, u32[]{:S(2)}) collective-permute-start(bf16[384,1280]{1,0:T(8,128)(2,1)S(1)} %multiply_convert_fusion.refs_2_), channel_id=1, source_target_pairs={{0,16},{16,0},{1,17},{17,1},{2,18},{18,2},{3,19},{19,3},{4,20},{20... | collective-permute-start | bytes 2949128 | tf_op jit(solution)/shard_map/ppermute | solution.py:560
  39.2 29.6 %collective-permute-start.5 = (bf16[384,1280]{1,0:T(8,128)(2,1)S(1)}, bf16[384,1280]{1,0:T(8,128)(2,1)}, u32[]{:S(2)}, u32[]{:S(2)}) collective-permute-start(bf16[384,1280]{1,0:T(8,128)(2,1)S(1)} %multiply_convert_fusion.refs_2_), channel_id=1, source_target_pairs={{0,4},{4,8},{8,12},{1,5},{5,9},{9,13},{2,6},{6,10},{10,14},{3,7},{... | collective-permute-start | bytes 2949128 | tf_op jit(solution)/shard_map/ppermute | solution.py:566
  68.8 53.5 %collective-permute-start.12 = (bf16[4,656,384]{2,1,0:T(8,128)(2,1)S(1)}, bf16[4,656,384]{2,1,0:T(8,128)(2,1)}, u32[]{:S(2)}, u32[]{:S(2)}) collective-permute-start(bf16[4,656,384]{2,1,0:T(8,128)(2,1)S(1)} %all-to-all-done.refs_0_), channel_id=1, source_target_pairs={{0,2},{2,0},{1,3},{3,1},{4,6},{6,4},{5,7},{7,5},{8,10},{10,8},{9,1... | collective-permute-start | bytes 6045704 | tf_op jit(solution)/shard_map/ppermute | solution.py:578
  76.2 28.7 %collective-permute-start.8 = (bf16[384,1280]{1,0:T(8,128)(2,1)S(1)}, bf16[384,1280]{1,0:T(8,128)(2,1)}, u32[]{:S(2)}, u32[]{:S(2)}) collective-permute-start(bf16[384,1280]{1,0:T(8,128)(2,1)S(1)} %select_select_fusion.1.refs_7_), channel_id=1, source_target_pairs={{0,1},{1,0},{2,3},{3,2},{4,5},{5,4},{6,7},{7,6},{8,9},{9,8},{10,11... | collective-permute-start | bytes 2949128 | tf_op jit(solution)/shard_map/ppermute | solution.py:561
  76.8 30.5 %collective-permute-start.9 = (bf16[384,1280]{1,0:T(8,128)(2,1)S(1)}, bf16[384,1280]{1,0:T(8,128)(2,1)}, u32[]{:S(2)}, u32[]{:S(2)}) collective-permute-start(bf16[384,1280]{1,0:T(8,128)(2,1)S(1)} %select_select_fusion.1.refs_7_), channel_id=1, source_target_pairs={{0,16},{16,0},{1,17},{17,1},{2,18},{18,2},{3,19},{19,3},{4,20},{20... | collective-permute-start | bytes 2949128 | tf_op jit(solution)/shard_map/ppermute | solution.py:560
  87.4 34.9 %collective-permute-start.6 = (bf16[384,1280]{1,0:T(8,128)(2,1)}, bf16[384,1280]{1,0:T(8,128)(2,1)}, u32[]{:S(2)}, u32[]{:S(2)}) collective-permute-start(bf16[384,1280]{1,0:T(8,128)(2,1)} %collective-permute-done.2), channel_id=1, source_target_pairs={{4,0},{8,4},{5,1},{9,5},{6,2},{10,6},{7,3},{11,7},{20,16},{24,20},... | collective-permute-start | bytes 2949128 | tf_op jit(solution)/shard_map/ppermute | solution.py:569
  122.3 23.5 %collective-permute-start.13 = (bf16[384,1280]{1,0:T(8,128)(2,1)}, bf16[384,1280]{1,0:T(8,128)(2,1)}, u32[]{:S(2)}, u32[]{:S(2)}) collective-permute-start(bf16[384,1280]{1,0:T(8,128)(2,1)} %collective-permute-done.6), channel_id=1, source_target_pairs={{4,0},{5,1},{6,2},{7,3},{20,16},{21,17},{22,18},{23,19}} | collective-permute-start | bytes 2949128 | tf_op jit(solution)/shard_map/ppermute | solution.py:569
  145.8 62.1 %all-to-all-start.2 = ((bf16[4,640,384]{2,1,0:T(8,128)(2,1)}), bf16[4,640,384]{2,1,0:T(8,128)(2,1)}, u32[]{:S(2)}, u32[]{:S(2)}) async-start(bf16[4,640,384]{2,1,0:T(8,128)(2,1)} %cut_columns.3), calls=%async_computation.2 | async-start | bytes 3932160 | tf_op jit(solution)/shard_map/all_to_all | solution.py:475
  151.9 32.2 %collective-permute-start.15 = (bf16[384,1280]{1,0:T(8,128)(2,1)S(1)}, bf16[384,1280]{1,0:T(8,128)(2,1)S(1)}, u32[]{:S(2)}, u32[]{:S(2)}) collective-permute-start(bf16[384,1280]{1,0:T(8,128)(2,1)S(1)} %fusion.2.refs_4_.refs_12_), channel_id=1, source_target_pairs={{0,1},{1,0},{2,3},{3,2},{4,5},{5,4},{6,7},{7,6},{8,9},{9,8},{10,11... | collective-permute-start | bytes 2949128 | tf_op jit(solution)/shard_map/ppermute | solution.py:561
  153.5 32.5 %collective-permute-start.16 = (bf16[384,1280]{1,0:T(8,128)(2,1)S(1)}, bf16[384,1280]{1,0:T(8,128)(2,1)}, u32[]{:S(2)}, u32[]{:S(2)}) collective-permute-start(bf16[384,1280]{1,0:T(8,128)(2,1)S(1)} %fusion.2.refs_4_.refs_12_), channel_id=1, source_target_pairs={{0,16},{16,0},{1,17},{17,1},{2,18},{18,2},{3,19},{19,3},{4,20},{20... | collective-permute-start | bytes 2949128 | tf_op jit(solution)/shard_map/ppermute | solution.py:560
  156.0 28.1 %collective-permute-start.14 = (bf16[192,1280]{1,0:T(8,128)(2,1)S(1)}, bf16[192,1280]{1,0:T(8,128)(2,1)S(1)}, u32[]{:S(2)}, u32[]{:S(2)}) collective-permute-start(bf16[192,1280]{1,0:T(8,128)(2,1)S(1)} %slice.75), channel_id=1, source_target_pairs={{0,16},{16,0},{1,17},{17,1},{2,18},{18,2},{3,19},{19,3},{4,20},{20... | collective-permute-start | bytes 1474568 | tf_op jit(solution)/shard_map/ppermute | solution.py:563
  157.7 26.4 %collective-permute-start.17 = (bf16[192,1280]{1,0:T(8,128)(2,1)S(1)}, bf16[192,1280]{1,0:T(8,128)(2,1)S(1)}, u32[]{:S(2)}, u32[]{:S(2)}) collective-permute-start(bf16[192,1280]{1,0:T(8,128)(2,1)S(1)} %slice.76), channel_id=1, source_target_pairs={{0,1},{1,0},{2,3},{3,2},{4,5},{5,4},{6,7},{7,6},{8,9},{9,8},{10,11... | collective-permute-start | bytes 1474568 | tf_op jit(solution)/shard_map/ppermute | solution.py:564
  207.9 69.4 %all-to-all-start.1 = ((bf16[4,640,384]{2,1,0:T(8,128)(2,1)}), bf16[4,640,384]{2,1,0:T(8,128)(2,1)}, u32[]{:S(2)}, u32[]{:S(2)}) async-start(bf16[4,640,384]{2,1,0:T(8,128)(2,1)} %cut_columns.4), calls=%async_computation.1 | async-start | bytes 3932160 | tf_op jit(solution)/shard_map/all_to_all | solution.py:475
  213.0 40.1 %collective-permute-start.24 = (bf16[4,640,384]{2,1,0:T(8,128)(2,1)}, bf16[4,640,384]{2,1,0:T(8,128)(2,1)}, u32[]{:S(2)}, u32[]{:S(2)}) collective-permute-start(bf16[4,640,384]{2,1,0:T(8,128)(2,1)} %all-to-all-done.2.refs_0_.refs_1_), channel_id=1, source_target_pairs={{0,2},{2,0},{1,3},{3,1},{4,6},{6,4},{5,7},{7,5},{8,10},{10,8},{9,1... | collective-permute-start | bytes 5898248 | tf_op jit(solution)/shard_map/ppermute | solution.py:618
  217.4 35.6 %collective-permute-start.21 = (bf16[384,1280]{1,0:T(8,128)(2,1)S(1)}, bf16[384,1280]{1,0:T(8,128)(2,1)}, u32[]{:S(2)}, u32[]{:S(2)}) collective-permute-start(bf16[384,1280]{1,0:T(8,128)(2,1)S(1)} %copy-done.7), channel_id=1, source_target_pairs={{0,17},{1,16},{16,1},{17,0},{2,19},{3,18},{18,3},{19,2},{4,21},{5,... | collective-permute-start | bytes 2949128 | tf_op jit(solution)/shard_map/ppermute | solution.py:573
  220.1 32.1 %collective-permute-start.22 = (bf16[192,1280]{1,0:T(8,128)(2,1)S(1)}, bf16[192,1280]{1,0:T(8,128)(2,1)S(1)}, u32[]{:S(2)}, u32[]{:S(2)}) collective-permute-start(bf16[192,1280]{1,0:T(8,128)(2,1)S(1)} %slice.77), channel_id=1, source_target_pairs={{0,16},{16,0},{1,17},{17,1},{2,18},{18,2},{3,19},{19,3},{4,20},{20... | collective-permute-start | bytes 1474568 | tf_op jit(solution)/shard_map/ppermute | solution.py:563
  222.9 30.2 %collective-permute-start.23 = (bf16[192,1280]{1,0:T(8,128)(2,1)}, bf16[192,1280]{1,0:T(8,128)(2,1)S(1)}, u32[]{:S(2)}, u32[]{:S(2)}) collective-permute-start(bf16[192,1280]{1,0:T(8,128)(2,1)} %slice.79), channel_id=1, source_target_pairs={{0,1},{1,0},{2,3},{3,2},{4,5},{5,4},{6,7},{7,6},{8,9},{9,8},{10,11... | collective-permute-start | bytes 1474568 | tf_op jit(solution)/shard_map/ppermute | solution.py:564
  294.7 32.1 %all-to-all-start.3 = ((bf16[4,2,384,128]{3,2,1,0:T(8,128)(2,1)}), bf16[4,2,384,128]{3,2,1,0:T(8,128)(2,1)S(1)}, u32[]{:S(2)}, u32[]{:S(2)}) async-start(bf16[4,2,384,128]{3,2,1,0:T(8,128)(2,1)} %bitcast.49), calls=%async_computation.3 | async-start | bytes 1572864 | tf_op jit(solution)/shard_map/all_to_all | solution.py:475
  348.4 25.8 %collective-permute-start.32 = (bf16[384,1280]{1,0:T(8,128)(2,1)}, bf16[384,1280]{1,0:T(8,128)(2,1)S(1)}, u32[]{:S(2)}, u32[]{:S(2)}) collective-permute-start(bf16[384,1280]{1,0:T(8,128)(2,1)} %out_blocks.5), channel_id=1, source_target_pairs={{0,17},{1,16},{16,1},{17,0},{2,19},{3,18},{18,3},{19,2},{4,21},{5,... | collective-permute-start | bytes 2949128 | tf_op jit(solution)/shard_map/ppermute | solution.py:657
  357.9 35.4 %collective-permute-start.30 = (bf16[384,1280]{1,0:T(8,128)(2,1)}, bf16[384,1280]{1,0:T(8,128)(2,1)S(1)}, u32[]{:S(2)}, u32[]{:S(2)}) collective-permute-start(bf16[384,1280]{1,0:T(8,128)(2,1)} %get-tuple-element.125), channel_id=1, source_target_pairs={{0,16},{16,0},{1,17},{17,1},{2,18},{18,2},{3,19},{19,3},{4,20},{20... | collective-permute-start | bytes 2949128 | tf_op jit(solution)/shard_map/ppermute | solution.py:659
  358.7 35.4 %collective-permute-start.31 = (bf16[384,1280]{1,0:T(8,128)(2,1)}, bf16[384,1280]{1,0:T(8,128)(2,1)S(1)}, u32[]{:S(2)}, u32[]{:S(2)}) collective-permute-start(bf16[384,1280]{1,0:T(8,128)(2,1)} %get-tuple-element.126), channel_id=1, source_target_pairs={{0,1},{1,0},{2,3},{3,2},{4,5},{5,4},{6,7},{7,6},{8,9},{9,8},{10,11... | collective-permute-start | bytes 2949128 | tf_op jit(solution)/shard_map/ppermute | solution.py:658
  (39 other events, 885.3 us)

commit v9 on v8

--- a/solution.py
+++ b/solution.py
@@ -420,18 +420,6 @@
     )(which, sign, *operands)
 
 
-def nearest(chips):
-    order = [
-        sorted((at for at in range(chips) if at != here), key=lambda at: (abs(at - here), at))
-        for here in range(chips)
-    ]
-    turns = [
-        [0 if at == here else order[here].index(at) + 1 for at in range(chips)]
-        for here in range(chips)
-    ]
-    return order, turns
-
-
 def chunk_sizes(heads):
     last = heads // 3 if heads % 3 == 0 else 1
     return [heads - last, last] if heads > last else [heads]
@@ -459,17 +447,10 @@
     all_blocks = chips * local_blocks
     swap = [(0, 1), (1, 0)]
     far_swap = [(0, 3), (1, 2), (2, 1), (3, 0)]
-    order, turns = nearest(chips)
-    turn_here = jnp.asarray(turns, dtype=jnp.int32)[chip]
-
-    def pick(index, options):
-        picked = options[0]
-        for at in range(1, len(options)):
-            picked = jnp.where(index == at, options[at], picked)
-        return picked
+    ring = [(at, (at + 1) % chips) for at in range(chips)]
 
     def turn_of(other):
-        return pick(other, [turn_here[at] for at in range(chips)])
+        return (chip - other) % chips
 
     def exchange(array):
         return lax.all_to_all(array, "chip", split_axis=0, concat_axis=0, tiled=True)
@@ -552,68 +533,47 @@
     half = tokens // 2
     rounds = []
     straight = None
-    shard, up, down = normed, normed, normed
-    ups, downs = [None], [None]
-    for phase in range(chips):
+    shard = normed
+    for phase in range(chips + 1):
         step = phase + 1
         sent = {}
-        sent["role"] = lax.ppermute(shard, "role", swap)
-        sent["head"] = lax.ppermute(shard, "head", swap)
+        if phase < chips:
+            sent["role"] = lax.ppermute(shard, "role", swap)
+            sent["head"] = lax.ppermute(shard, "head", swap)
         if straight is not None:
             sent["first"] = lax.ppermute(straight[2][:half], "role", swap)
             sent["second"] = lax.ppermute(straight[1][half:], "head", swap)
         if step < chips:
-            sent["up"] = lax.ppermute(
-                up, "chip", [(at, at + 1) for at in range(step - 1, chips - 1)]
-            )
-            sent["down"] = lax.ppermute(
-                down, "chip", [(at + 1, at) for at in range(chips - step)]
-            )
-        else:
-            sent["far"] = lax.ppermute(shard, ("role", "head"), far_swap)
+            sent["next"] = lax.ppermute(shard, "chip", ring)
         if phase == 0:
             sent["weights"] = weights_own.pop()
             sent["cuts"] = cuts[1:]
         if phase == 1:
-            sent["weights"] = lax.ppermute(weights_own[0], "core", swap)
             sent["places"] = places
             sent["gains"] = gains
         if step == chips:
+            weights_other.append(lax.ppermute(weights_own[0], "core", swap))
             early = list(rounds)
             tables = tables_of(weights_own[0][:, depth:])
             held_places, tables = lax.optimization_barrier((places, tables))
             sent["places"] = project(0, 0, 1, 0, early, held_places)
-            if len(weights_own) < heads:
-                held, _ = lax.optimization_barrier(
-                    (cuts[len(weights_own)], (sent["role"], sent["head"]))
-                )
-                weights_own.append(exchange(held))
-        if step == chips - 1 and len(weights_own) < heads - 1:
-            for cut in cuts[len(weights_own) : heads - 1]:
-                held, _ = lax.optimization_barrier((cut, (sent["up"], sent["down"])))
-                weights_own.append(exchange(held))
         sent, shard = lax.optimization_barrier((sent, shard))
         if phase == 0:
             weights_own.append(sent["weights"])
             cuts[1:] = sent["cuts"]
         if phase == 1:
-            weights_other.append(sent["weights"])
             places, gains = sent["places"], sent["gains"]
         if straight is not None:
             rounds.append(straight + (sent["first"], sent["second"]))
         if step == chips:
             held_places = sent["places"]
-        straight = (shard, sent["role"], sent["head"])
+        if phase < chips:
+            straight = (shard, sent["role"], sent["head"])
         if step < chips:
-            up, down = sent["up"], sent["down"]
-            ups.append(up)
-            downs.append(down)
-            options = []
-            for here in range(chips):
-                source = order[here][step - 1]
-                options.append(ups[here - source] if source < here else downs[source - here])
-            shard = pick(chip, options)
-    rounds.append(straight + (sent["far"],))
+            shard = sent["next"]
+        if chips - 2 <= phase and len(weights_own) < heads:
+            held, _ = lax.optimization_barrier((cuts[len(weights_own)], sent))
+            weights_own.append(exchange(held))
     for at in range(len(weights_other), heads - 1):
         weights_other.append(lax.ppermute(weights_own[at], "core", swap))
 

time: 400 us -> 365 us (0.912)
  waiting for transfers between devices: 181 us -> 166 us
  starting transfers between devices: 63.9 us -> 52.5 us
  other arithmetic: 19.5 us -> 9.87 us
    ppermute x3 -> x4, waiting for transfers between devices: 39.4 us -> 78.5 us  [per_device_by_heads(): sent['first'] = lax.ppermute(straight[2][:half], 'role', swap)]
    ppermute x8 -> x4, waiting for transfers between devices: 52.1 us -> 14.1 us  [the longest x3 14.1 us: per_device_by_heads(): sent['next'] = lax.ppermute(shard, 'chip', ring)]
    ppermute x4, waiting for transfers between devices: 19.6 us -> 0.01 us  [per_device_by_heads(): sent['role'] = lax.ppermute(shard, 'role', swap)]
    all_to_all x5, waiting for transfers between devices: 0.01 us -> 18.6 us  [exchange(): lax.all_to_all(array, 'chip', split_axis=0, concat_axis=0, tiled=True)]
    ppermute x8 -> x4, starting transfers between devices: 13.9 us -> 2.68 us  [the longest x3 2.68 us: per_device_by_heads(): sent['next'] = lax.ppermute(shard, 'chip', ring)]
    ppermute x3 -> x4, waiting for transfers between devices: 8.03 us -> 1.22 us  [per_device_by_heads(): sent['second'] = lax.ppermute(straight[1][half:], 'head', swap)]
    ppermute x4, waiting for transfers between devices: 15.8 us -> 9.05 us  [per_device_by_heads(): sent['head'] = lax.ppermute(shard, 'head', swap)]
    select_n x3 -> x0, other arithmetic: 4.64 us -> none  [pick(): picked = jnp.where(index == at, options[at], picked)]
  transfers between devices with their start and end apart: 38 -> 36, of which waited for: 20 -> 18; matrix products, arithmetic and copies ran while one was open for 10% -> 8% of each run, Pallas kernels for 24% -> 27%
where the time goes in v9:
time: 365 us; the launch traced here: 363 us
  waiting for transfers between devices  166 us (45%)
  Pallas kernels  105 us (29%)
  starting transfers between devices  52.5 us (14%)
  local copies, waits for them, and re-layouts  17.3 us (5%)
  matrix products  12.6 us (3%)
  other arithmetic  9.87 us (3%)
    ppermute x4, waiting for transfers between devices, per_device_by_heads(): sent['first'] = lax.ppermute(straight[2][:half], 'role', swap)  78.5 us
    pallas_call x4, Pallas kernels, project_heads(): pl.pallas_call(body, in_specs=[in_smem(), in_smem()] + [in_hbm()] * (2 *...  51.5 us
    all_to_all x5, starting transfers between devices, exchange(): lax.all_to_all(array, 'chip', split_axis=0, concat_axis=0, tiled=True)  23.6 us
    pallas_call x3, Pallas kernels, out_blocks(): pl.pallas_call(body, grid_spec=pltpu.PrefetchScalarGridSpec(num_scalar_pr...  22.7 us
    pallas_call x2, Pallas kernels, attend(): pl.pallas_call(body, in_specs=[in_smem()] * 4 + [in_hbm()] * len(arrays),...  19.2 us
    ppermute x1, waiting for transfers between devices, per_device_by_heads(): from_role = lax.ppermute(over_role, 'role', swap)  18.8 us
    all_to_all x5, waiting for transfers between devices, exchange(): lax.all_to_all(array, 'chip', split_axis=0, concat_axis=0, tiled=True)  18.6 us
    ppermute x1, waiting for transfers between devices, per_device_by_heads(): from_diagonal = lax.ppermute(diagonal, ('role', 'head'), far_swap)  14.1 us
  transfers between devices with their start and end apart: 36, of which 18 were waited for; matrix products, arithmetic and copies ran while one was open for 8% of the time, Pallas kernels for 27%

profile of v9, /device:TPU:0, one launch (start us, length us, event | category | flops | bytes accessed | tf_op | source)
XLA Modules:
  0.0 363.5 jit_solution(16422447732794218440)
XLA Ops:
  2.4 3.8 %cut_columns.5 = bf16[4,656,384]{2,1,0:T(8,128)(2,1)} custom-call(bf16[640,4608]{1,0:T(8,128)(2,1)} %bitcast.42, bf16[4,16,384]{2,1,0:T(8,128)(2,1)} %bitcast.57), custom_call_target="tpu_custom_call" | custom-call | tf_op jit(solution)/shard_map/cut_columns/pallas_call | solution.py:165
  6.2 6.4 %all-to-all-start = ((bf16[4,656,384]{2,1,0:T(8,128)(2,1)}), bf16[4,656,384]{2,1,0:T(8,128)(2,1)S(1)}, u32[]{:S(2)}, u32[]{:S(2)}) async-start(bf16[4,656,384]{2,1,0:T(8,128)(2,1)} %cut_columns.5), calls=%async_computation | async-start | bytes 4030464 | tf_op jit(solution)/shard_map/all_to_all | solution.py:456
  13.0 12.6 %multiply_reduce_fusion = (f32[384]{0:T(512)S(1)}, f32[384,1280]{1,0:T(8,128)}) fusion(bf16[384,5120]{1,0:T(8,128)(2,1)} %param.11, s32[]{:T(128)S(6)} %select_n.44, f32[384]{0:T(512)S(1)} %mul.83, bf16[384,5120]{1,0:T(8,128)(2,1)} %param.9, bf16[5120,1280]{1,0:T(8,128)(2,1)} %param.10, f32[384]{0:T(512)S(1)} %mul.79), kind=kOutput, calls=%fused_computation.5 | convolution fusion | flops 5036604928 | bytes 19993092 | tf_op jit(solution)/shard_map/dot_general | solution.py:474
  47.4 9.0 %collective-permute-done.2.refs_4_ = bf16[384,1280]{1,0:T(8,128)(2,1)} collective-permute-done((bf16[384,1280]{1,0:T(8,128)(2,1)S(1)}, bf16[384,1280]{1,0:T(8,128)(2,1)}, u32[]{:S(2)}, u32[]{:S(2)}) %collective-permute-start.2) | collective-permute-done | bytes 983072 | tf_op jit(solution)/shard_map/ppermute | solution.py:542
  56.4 14.1 %collective-permute-done.3.refs_7_ = bf16[384,1280]{1,0:T(8,128)(2,1)} collective-permute-done((bf16[384,1280]{1,0:T(8,128)(2,1)S(1)}, bf16[384,1280]{1,0:T(8,128)(2,1)}, u32[]{:S(2)}, u32[]{:S(2)}) %collective-permute-start.3) | collective-permute-done | bytes 983072 | tf_op jit(solution)/shard_map/ppermute | solution.py:547
  70.5 9.6 %all-to-all-done.refs_0_ = bf16[4,656,384]{2,1,0:T(8,128)(2,1)S(1)} async-done(((bf16[4,656,384]{2,1,0:T(8,128)(2,1)}), bf16[4,656,384]{2,1,0:T(8,128)(2,1)S(1)}, u32[]{:S(2)}, u32[]{:S(2)}) %all-to-all-start) | async-done | bytes 2015264 | tf_op jit(solution)/shard_map/all_to_all | solution.py:456
  88.6 26.3 %collective-permute-done.5.refs_5_ = bf16[192,1280]{1,0:T(8,128)(2,1)S(1)} collective-permute-done((bf16[192,1280]{1,0:T(8,128)(2,1)}, bf16[192,1280]{1,0:T(8,128)(2,1)S(1)}, u32[]{:S(2)}, u32[]{:S(2)}) %collective-permute-start.5) | collective-permute-done | bytes 491552 | tf_op jit(solution)/shard_map/ppermute | solution.py:544
  120.9 26.8 %collective-permute-done.10.refs_10_ = bf16[192,1280]{1,0:T(8,128)(2,1)} collective-permute-done((bf16[192,1280]{1,0:T(8,128)(2,1)S(1)}, bf16[192,1280]{1,0:T(8,128)(2,1)}, u32[]{:S(2)}, u32[]{:S(2)}) %collective-permute-start.10) | collective-permute-done | bytes 491552 | tf_op jit(solution)/shard_map/ppermute | solution.py:544
  147.7 4.8 %all-to-all-start.2 = ((bf16[4,640,384]{2,1,0:T(8,128)(2,1)}), bf16[4,640,384]{2,1,0:T(8,128)(2,1)}, u32[]{:S(2)}, u32[]{:S(2)}) async-start(bf16[4,640,384]{2,1,0:T(8,128)(2,1)} %cut_columns.3), calls=%async_computation.2 | async-start | bytes 3932160 | tf_op jit(solution)/shard_map/all_to_all | solution.py:456
  164.1 10.3 %project_heads.4 = (bf16[1,2,384,128]{3,2,1,0:T(8,128)(2,1)}, bf16[1,2,2,384,128]{4,3,2,1,0:T(8,128)(2,1)}) custom-call(s32[5]{0:T(128)} %concatenate.9.places_ref, f32[2,1]{1,0:T(2,128)} %get-tuple-element.125.gains_ref, bf16[4,656,384]{2,1,0:T(8,128)(2,1)} %copy-done.2, bf16[4,656,384]{2,1,0:T(8,128)(2,1)} %collective-permute-done.17.refs_1_.refs_2_, ...), custom_call_target="tpu_custom_call" | custom-call | tf_op jit(solution)/shard_map/project_heads/pallas_call | solution.py:257
  174.4 14.8 %collective-permute-done.15.refs_7_.refs_15_ = bf16[192,1280]{1,0:T(8,128)(2,1)S(1)} collective-permute-done((bf16[192,1280]{1,0:T(8,128)(2,1)}, bf16[192,1280]{1,0:T(8,128)(2,1)S(1)}, u32[]{:S(2)}, u32[]{:S(2)}) %collective-permute-start.15) | collective-permute-done | bytes 491552 | tf_op jit(solution)/shard_map/ppermute | solution.py:544
  189.2 5.8 %all-to-all-done.2.refs_0_.refs_1_ = bf16[4,640,384]{2,1,0:T(8,128)(2,1)} async-done(((bf16[4,640,384]{2,1,0:T(8,128)(2,1)}), bf16[4,640,384]{2,1,0:T(8,128)(2,1)}, u32[]{:S(2)}, u32[]{:S(2)}) %all-to-all-start.2) | async-done | bytes 1966112 | tf_op jit(solution)/shard_map/all_to_all | solution.py:456
  195.0 3.8 %all-to-all-start.1 = ((bf16[4,640,384]{2,1,0:T(8,128)(2,1)}), bf16[4,640,384]{2,1,0:T(8,128)(2,1)S(1)}, u32[]{:S(2)}, u32[]{:S(2)}) async-start(bf16[4,640,384]{2,1,0:T(8,128)(2,1)} %cut_columns.4), calls=%async_computation.1 | async-start | bytes 3932160 | tf_op jit(solution)/shard_map/all_to_all | solution.py:456
  203.1 10.6 %collective-permute-done.21.refs_12_.refs_20_ = bf16[192,1280]{1,0:T(8,128)(2,1)S(1)} collective-permute-done((bf16[192,1280]{1,0:T(8,128)(2,1)S(1)}, bf16[192,1280]{1,0:T(8,128)(2,1)S(1)}, u32[]{:S(2)}, u32[]{:S(2)}) %collective-permute-start.21) | collective-permute-done | bytes 491552 | tf_op jit(solution)/shard_map/ppermute | solution.py:544
  216.2 10.3 %project_heads.5 = (bf16[1,2,384,128]{3,2,1,0:T(8,128)(2,1)}, bf16[1,2,2,384,128]{4,3,2,1,0:T(8,128)(2,1)}) custom-call(s32[5]{0:T(128)} %concatenate.9.places_ref, f32[2,1]{1,0:T(2,128)} %get-tuple-element.124.gains_ref, bf16[4,640,384]{2,1,0:T(8,128)(2,1)} %all-to-all-done.2.refs_0_.refs_1_, bf16[4,640,384]{2,1,0:T(8,128)(2,1)} %copy-done.5, ...), custom_call_target="tpu_custom_call" | custom-call | tf_op jit(solution)/shard_map/project_heads/pallas_call | solution.py:257
  226.6 13.9 %project_heads.6 = (bf16[2,2,384,128]{3,2,1,0:T(8,128)(2,1)}, bf16[2,2,2,384,128]{4,3,2,1,0:T(8,128)(2,1)}) custom-call(s32[5]{0:T(128)} %concatenate.9.places_ref, f32[2,2]{1,0:T(2,128)} %bitcast.63, bf16[4,656,384]{2,1,0:T(8,128)(2,1)} %copy-done.2, bf16[4,640,384]{2,1,0:T(8,128)(2,1)} %all-to-all-done.2.refs_0_.refs_1_, ...), custom_call_target="tpu_custom_call" | custom-call | tf_op jit(solution)/shard_map/project_heads/pallas_call | solution.py:257
  250.6 11.9 %attend.2 = bf16[4,2,6,64,128]{4,3,2,1,0:T(8,128)(2,1)} custom-call(s32[3,24,8]{2,1,0:T(8,128)} %fusion.7.slots_ref, s32[3,24]{1,0:T(4,128)} %get-tuple-element.71.counts_ref, s32[24]{0:T(128)} %fusion.11.from_ref, s32[3,4]{1,0:T(4,128)} %reduce_max.9.most_ref, bf16[1,12,64,128]{3,2,1,0:T(8,128)(2,1)} %bitcast.58, bf16[1,2,12,64,128]{4,3,2,1,0:T(8,128)(2,1)} %bitcast.51, ...), custom_call_target="tpu_custom_call" | custom-call | tf_op jit(solution)/shard_map/attend/pallas_call | solution.py:352
  266.2 17.0 %project_heads.7 = (bf16[1,4,384,128]{3,2,1,0:T(8,128)(2,1)}, bf16[1,2,4,384,128]{4,3,2,1,0:T(8,128)(2,1)}) custom-call(s32[5]{0:T(128)} %concatenate.9.places_ref, f32[2,1]{1,0:T(2,128)} %get-tuple-element.123.gains_ref, bf16[4,640,384]{2,1,0:T(8,128)(2,1)} %copy-done.6, bf16[4,640,384]{2,1,0:T(8,128)(2,1)} %collective-permute-done.26.refs_1_, ...), custom_call_target="tpu_custom_call" | custom-call | tf_op jit(solution)/shard_map/project_heads/pallas_call | solution.py:257
  286.7 7.3 %attend.3 = bf16[4,1,6,64,128]{4,3,2,1,0:T(8,128)(2,1)} custom-call(s32[3,24,8]{2,1,0:T(8,128)} %fusion.7.slots_ref, s32[3,24]{1,0:T(4,128)} %get-tuple-element.71.counts_ref, s32[24]{0:T(128)} %fusion.11.from_ref, s32[3,4]{1,0:T(4,128)} %reduce_max.9.most_ref, bf16[1,24,64,128]{3,2,1,0:T(8,128)(2,1)} %bitcast.56, bf16[1,2,24,64,128]{4,3,2,1,0:T(8,128)(2,1)} %bitcast.50, ...), custom_call_target="tpu_custom_call" | custom-call | tf_op jit(solution)/shard_map/attend/pallas_call | solution.py:352
  294.0 4.8 %all-to-all-start.4 = ((bf16[4,1,384,128]{3,2,1,0:T(8,128)(2,1)}), bf16[4,1,384,128]{3,2,1,0:T(8,128)(2,1)S(1)}, u32[]{:S(2)}, u32[]{:S(2)}) async-start(bf16[4,1,384,128]{3,2,1,0:T(8,128)(2,1)} %bitcast.46), calls=%async_computation.4 | async-start | bytes 786432 | tf_op jit(solution)/shard_map/all_to_all | solution.py:456
  300.2 10.7 %out_blocks.3.refs_0_ = f32[4,384,1280]{2,1,0:T(8,128)} custom-call(s32[4]{0:T(128)} %pad_add_fusion.1.which_ref, s32[1]{0:T(128)} %bitcast.3.sign_ref, bf16[4,2,384,128]{3,2,1,0:T(8,128)(2,1)} %copy-done.10, bf16[4,384,5120]{2,1,0:T(8,128)(2,1)} %bitcast.39), custom_call_target="tpu_custom_call" | custom-call | tf_op jit(solution)/shard_map/out_blocks/pallas_call | solution.py:412
  318.1 8.2 %out_blocks.4 = (bf16[384,1280]{1,0:T(8,128)(2,1)}, bf16[384,1280]{1,0:T(8,128)(2,1)}, f32[384,1280]{1,0:T(8,128)}) custom-call(s32[3]{0:T(128)} %pad_add_fusion.which_ref, s32[1]{0:T(128)} %bitcast.3.sign_ref, bf16[4,1,384,128]{3,2,1,0:T(8,128)(2,1)} %copy-done.9, bf16[4,384,5120]{2,1,0:T(8,128)(2,1)} %bitcast.41, f32[4,384,1280]{2,1,0:T(8,128)} %out_blocks.3.refs_0_), custom_call_target="tpu_custom_call" | custom-call | tf_op jit(solution)/shard_map/out_blocks/pallas_call | solution.py:412
  327.2 14.1 %collective-permute-done.30 = bf16[384,1280]{1,0:T(8,128)(2,1)S(1)} collective-permute-done((bf16[384,1280]{1,0:T(8,128)(2,1)}, bf16[384,1280]{1,0:T(8,128)(2,1)S(1)}, u32[]{:S(2)}, u32[]{:S(2)}) %collective-permute-start.30) | collective-permute-done | bytes 983072 | tf_op jit(solution)/shard_map/ppermute | solution.py:617
  341.3 18.8 %collective-permute-done.28 = bf16[384,1280]{1,0:T(8,128)(2,1)S(1)} collective-permute-done((bf16[384,1280]{1,0:T(8,128)(2,1)}, bf16[384,1280]{1,0:T(8,128)(2,1)S(1)}, u32[]{:S(2)}, u32[]{:S(2)}) %collective-permute-start.28) | collective-permute-done | bytes 983072 | tf_op jit(solution)/shard_map/ppermute | solution.py:619
  (150 shorter events, 87.2 us)
Async XLA Ops:
  6.2 74.0 %all-to-all-start = ((bf16[4,656,384]{2,1,0:T(8,128)(2,1)}), bf16[4,656,384]{2,1,0:T(8,128)(2,1)S(1)}, u32[]{:S(2)}, u32[]{:S(2)}) async-start(bf16[4,656,384]{2,1,0:T(8,128)(2,1)} %cut_columns.5), calls=%async_computation | async-start | bytes 4030464 | tf_op jit(solution)/shard_map/all_to_all | solution.py:456
  36.3 34.2 %collective-permute-start.3 = (bf16[384,1280]{1,0:T(8,128)(2,1)S(1)}, bf16[384,1280]{1,0:T(8,128)(2,1)}, u32[]{:S(2)}, u32[]{:S(2)}) collective-permute-start(bf16[384,1280]{1,0:T(8,128)(2,1)S(1)} %multiply_convert_fusion.refs_2_), channel_id=1, source_target_pairs={{0,4},{4,8},{8,12},{12,0},{1,5},{5,9},{9,13},{13,1},{2,6},{6,10},{... | collective-permute-start | bytes 2949128 | tf_op jit(solution)/shard_map/ppermute | solution.py:547
  38.3 32.2 %collective-permute-start.4 = (bf16[384,1280]{1,0:T(8,128)(2,1)S(1)}, bf16[384,1280]{1,0:T(8,128)(2,1)}, u32[]{:S(2)}, u32[]{:S(2)}) collective-permute-start(bf16[384,1280]{1,0:T(8,128)(2,1)S(1)} %multiply_convert_fusion.refs_2_), channel_id=1, source_target_pairs={{0,16},{16,0},{1,17},{17,1},{2,18},{18,2},{3,19},{19,3},{4,20},{20... | collective-permute-start | bytes 2949128 | tf_op jit(solution)/shard_map/ppermute | solution.py:541
  80.1 34.7 %collective-permute-start.6 = (bf16[384,1280]{1,0:T(8,128)(2,1)}, bf16[384,1280]{1,0:T(8,128)(2,1)S(1)}, u32[]{:S(2)}, u32[]{:S(2)}) collective-permute-start(bf16[384,1280]{1,0:T(8,128)(2,1)} %collective-permute-done.3.refs_7_), channel_id=1, source_target_pairs={{0,1},{1,0},{2,3},{3,2},{4,5},{5,4},{6,7},{7,6},{8,9},{9,8},{10,11... | collective-permute-start | bytes 2949128 | tf_op jit(solution)/shard_map/ppermute | solution.py:542
  81.7 33.2 %collective-permute-start.7 = (bf16[384,1280]{1,0:T(8,128)(2,1)}, bf16[384,1280]{1,0:T(8,128)(2,1)}, u32[]{:S(2)}, u32[]{:S(2)}) collective-permute-start(bf16[384,1280]{1,0:T(8,128)(2,1)} %collective-permute-done.3.refs_7_), channel_id=1, source_target_pairs={{0,4},{4,8},{8,12},{12,0},{1,5},{5,9},{9,13},{13,1},{2,6},{6,10},{... | collective-permute-start | bytes 2949128 | tf_op jit(solution)/shard_map/ppermute | solution.py:547
  81.7 33.2 %collective-permute-start.8 = (bf16[384,1280]{1,0:T(8,128)(2,1)}, bf16[384,1280]{1,0:T(8,128)(2,1)}, u32[]{:S(2)}, u32[]{:S(2)}) collective-permute-start(bf16[384,1280]{1,0:T(8,128)(2,1)} %collective-permute-done.3.refs_7_), channel_id=1, source_target_pairs={{0,16},{16,0},{1,17},{17,1},{2,18},{18,2},{3,19},{19,3},{4,20},{20... | collective-permute-start | bytes 2949128 | tf_op jit(solution)/shard_map/ppermute | solution.py:541
  85.0 29.8 %collective-permute-start.5 = (bf16[192,1280]{1,0:T(8,128)(2,1)}, bf16[192,1280]{1,0:T(8,128)(2,1)S(1)}, u32[]{:S(2)}, u32[]{:S(2)}) collective-permute-start(bf16[192,1280]{1,0:T(8,128)(2,1)} %slice.51), channel_id=1, source_target_pairs={{0,16},{16,0},{1,17},{17,1},{2,18},{18,2},{3,19},{19,3},{4,20},{20... | collective-permute-start | bytes 1474568 | tf_op jit(solution)/shard_map/ppermute | solution.py:544
  87.4 27.5 %collective-permute-start.9 = (bf16[192,1280]{1,0:T(8,128)(2,1)}, bf16[192,1280]{1,0:T(8,128)(2,1)}, u32[]{:S(2)}, u32[]{:S(2)}) collective-permute-start(bf16[192,1280]{1,0:T(8,128)(2,1)} %slice.52), channel_id=1, source_target_pairs={{0,1},{1,0},{2,3},{3,2},{4,5},{5,4},{6,7},{7,6},{8,9},{9,8},{10,11... | collective-permute-start | bytes 1474568 | tf_op jit(solution)/shard_map/ppermute | solution.py:545
  114.9 32.8 %collective-permute-start.11 = (bf16[384,1280]{1,0:T(8,128)(2,1)}, bf16[384,1280]{1,0:T(8,128)(2,1)}, u32[]{:S(2)}, u32[]{:S(2)}) collective-permute-start(bf16[384,1280]{1,0:T(8,128)(2,1)} %collective-permute-done.7.refs_4_.refs_12_), channel_id=1, source_target_pairs={{0,1},{1,0},{2,3},{3,2},{4,5},{5,4},{6,7},{7,6},{8,9},{9,8},{10,11... | collective-permute-start | bytes 2949128 | tf_op jit(solution)/shard_map/ppermute | solution.py:542
  115.5 32.2 %collective-permute-start.12 = (bf16[384,1280]{1,0:T(8,128)(2,1)}, bf16[384,1280]{1,0:T(8,128)(2,1)}, u32[]{:S(2)}, u32[]{:S(2)}) collective-permute-start(bf16[384,1280]{1,0:T(8,128)(2,1)} %collective-permute-done.7.refs_4_.refs_12_), channel_id=1, source_target_pairs={{0,4},{4,8},{8,12},{12,0},{1,5},{5,9},{9,13},{13,1},{2,6},{6,10},{... | collective-permute-start | bytes 2949128 | tf_op jit(solution)/shard_map/ppermute | solution.py:547
  116.1 31.6 %collective-permute-start.13 = (bf16[384,1280]{1,0:T(8,128)(2,1)}, bf16[384,1280]{1,0:T(8,128)(2,1)}, u32[]{:S(2)}, u32[]{:S(2)}) collective-permute-start(bf16[384,1280]{1,0:T(8,128)(2,1)} %collective-permute-done.7.refs_4_.refs_12_), channel_id=1, source_target_pairs={{0,16},{16,0},{1,17},{17,1},{2,18},{18,2},{3,19},{19,3},{4,20},{20... | collective-permute-start | bytes 2949128 | tf_op jit(solution)/shard_map/ppermute | solution.py:541
  117.6 30.0 %collective-permute-start.10 = (bf16[192,1280]{1,0:T(8,128)(2,1)S(1)}, bf16[192,1280]{1,0:T(8,128)(2,1)}, u32[]{:S(2)}, u32[]{:S(2)}) collective-permute-start(bf16[192,1280]{1,0:T(8,128)(2,1)S(1)} %slice.57), channel_id=1, source_target_pairs={{0,16},{16,0},{1,17},{17,1},{2,18},{18,2},{3,19},{19,3},{4,20},{20... | collective-permute-start | bytes 1474568 | tf_op jit(solution)/shard_map/ppermute | solution.py:544
  119.3 28.4 %collective-permute-start.14 = (bf16[192,1280]{1,0:T(8,128)(2,1)S(1)}, bf16[192,1280]{1,0:T(8,128)(2,1)}, u32[]{:S(2)}, u32[]{:S(2)}) collective-permute-start(bf16[192,1280]{1,0:T(8,128)(2,1)S(1)} %slice.58), channel_id=1, source_target_pairs={{0,1},{1,0},{2,3},{3,2},{4,5},{5,4},{6,7},{7,6},{8,9},{9,8},{10,11... | collective-permute-start | bytes 1474568 | tf_op jit(solution)/shard_map/ppermute | solution.py:545
  147.7 47.3 %all-to-all-start.2 = ((bf16[4,640,384]{2,1,0:T(8,128)(2,1)}), bf16[4,640,384]{2,1,0:T(8,128)(2,1)}, u32[]{:S(2)}, u32[]{:S(2)}) async-start(bf16[4,640,384]{2,1,0:T(8,128)(2,1)} %cut_columns.3), calls=%async_computation.2 | async-start | bytes 3932160 | tf_op jit(solution)/shard_map/all_to_all | solution.py:456
  153.1 36.1 %collective-permute-start.16 = (bf16[384,1280]{1,0:T(8,128)(2,1)}, bf16[384,1280]{1,0:T(8,128)(2,1)S(1)}, u32[]{:S(2)}, u32[]{:S(2)}) collective-permute-start(bf16[384,1280]{1,0:T(8,128)(2,1)} %collective-permute-done.12.refs_9_.refs_17_), channel_id=1, source_target_pairs={{0,1},{1,0},{2,3},{3,2},{4,5},{5,4},{6,7},{7,6},{8,9},{9,8},{10,11... | collective-permute-start | bytes 2949128 | tf_op jit(solution)/shard_map/ppermute | solution.py:542
  154.6 34.7 %collective-permute-start.18 = (bf16[384,1280]{1,0:T(8,128)(2,1)}, bf16[384,1280]{1,0:T(8,128)(2,1)}, u32[]{:S(2)}, u32[]{:S(2)}) collective-permute-start(bf16[384,1280]{1,0:T(8,128)(2,1)} %collective-permute-done.12.refs_9_.refs_17_), channel_id=1, source_target_pairs={{0,16},{16,0},{1,17},{17,1},{2,18},{18,2},{3,19},{19,3},{4,20},{20... | collective-permute-start | bytes 2949128 | tf_op jit(solution)/shard_map/ppermute | solution.py:541
  160.2 29.0 %collective-permute-start.15 = (bf16[192,1280]{1,0:T(8,128)(2,1)}, bf16[192,1280]{1,0:T(8,128)(2,1)S(1)}, u32[]{:S(2)}, u32[]{:S(2)}) collective-permute-start(bf16[192,1280]{1,0:T(8,128)(2,1)} %slice.59), channel_id=1, source_target_pairs={{0,16},{16,0},{1,17},{17,1},{2,18},{18,2},{3,19},{19,3},{4,20},{20... | collective-permute-start | bytes 1474568 | tf_op jit(solution)/shard_map/ppermute | solution.py:544
  160.7 28.5 %collective-permute-start.19 = (bf16[192,1280]{1,0:T(8,128)(2,1)}, bf16[192,1280]{1,0:T(8,128)(2,1)}, u32[]{:S(2)}, u32[]{:S(2)}) collective-permute-start(bf16[192,1280]{1,0:T(8,128)(2,1)} %slice.61), channel_id=1, source_target_pairs={{0,1},{1,0},{2,3},{3,2},{4,5},{5,4},{6,7},{7,6},{8,9},{9,8},{10,11... | collective-permute-start | bytes 1474568 | tf_op jit(solution)/shard_map/ppermute | solution.py:545
  195.0 48.6 %all-to-all-start.1 = ((bf16[4,640,384]{2,1,0:T(8,128)(2,1)}), bf16[4,640,384]{2,1,0:T(8,128)(2,1)S(1)}, u32[]{:S(2)}, u32[]{:S(2)}) async-start(bf16[4,640,384]{2,1,0:T(8,128)(2,1)} %cut_columns.4), calls=%async_computation.1 | async-start | bytes 3932160 | tf_op jit(solution)/shard_map/all_to_all | solution.py:456
  243.6 22.6 %collective-permute-start.26 = (bf16[4,640,384]{2,1,0:T(8,128)(2,1)S(1)}, bf16[4,640,384]{2,1,0:T(8,128)(2,1)}, u32[]{:S(2)}, u32[]{:S(2)}) collective-permute-start(bf16[4,640,384]{2,1,0:T(8,128)(2,1)S(1)} %all-to-all-done.1.refs_0_), channel_id=1, source_target_pairs={{0,2},{2,0},{1,3},{3,1},{4,6},{6,4},{5,7},{7,5},{8,10},{10,8},{9,1... | collective-permute-start | bytes 5898248 | tf_op jit(solution)/shard_map/ppermute | solution.py:590
  262.5 31.5 %all-to-all-start.3 = ((bf16[4,2,384,128]{3,2,1,0:T(8,128)(2,1)}), bf16[4,2,384,128]{3,2,1,0:T(8,128)(2,1)S(1)}, u32[]{:S(2)}, u32[]{:S(2)}) async-start(bf16[4,2,384,128]{3,2,1,0:T(8,128)(2,1)} %bitcast.45), calls=%async_computation.3 | async-start | bytes 1572864 | tf_op jit(solution)/shard_map/all_to_all | solution.py:456
  315.4 25.8 %collective-permute-start.30 = (bf16[384,1280]{1,0:T(8,128)(2,1)}, bf16[384,1280]{1,0:T(8,128)(2,1)S(1)}, u32[]{:S(2)}, u32[]{:S(2)}) collective-permute-start(bf16[384,1280]{1,0:T(8,128)(2,1)} %out_blocks.5), channel_id=1, source_target_pairs={{0,17},{1,16},{16,1},{17,0},{2,19},{3,18},{18,3},{19,2},{4,21},{5,... | collective-permute-start | bytes 2949128 | tf_op jit(solution)/shard_map/ppermute | solution.py:617
  326.3 33.8 %collective-permute-start.28 = (bf16[384,1280]{1,0:T(8,128)(2,1)}, bf16[384,1280]{1,0:T(8,128)(2,1)S(1)}, u32[]{:S(2)}, u32[]{:S(2)}) collective-permute-start(bf16[384,1280]{1,0:T(8,128)(2,1)} %get-tuple-element.119), channel_id=1, source_target_pairs={{0,16},{16,0},{1,17},{17,1},{2,18},{18,2},{3,19},{19,3},{4,20},{20... | collective-permute-start | bytes 2949128 | tf_op jit(solution)/shard_map/ppermute | solution.py:619
  326.8 33.2 %collective-permute-start.29 = (bf16[384,1280]{1,0:T(8,128)(2,1)}, bf16[384,1280]{1,0:T(8,128)(2,1)S(1)}, u32[]{:S(2)}, u32[]{:S(2)}) collective-permute-start(bf16[384,1280]{1,0:T(8,128)(2,1)} %get-tuple-element.120), channel_id=1, source_target_pairs={{0,1},{1,0},{2,3},{3,2},{4,5},{5,4},{6,7},{7,6},{8,9},{9,8},{10,11... | collective-permute-start | bytes 2949128 | tf_op jit(solution)/shard_map/ppermute | solution.py:618
  (34 other events, 548.4 us)

commit v10 on v9

--- a/solution.py
+++ b/solution.py
@@ -420,6 +420,53 @@
     )(which, sign, *operands)
 
 
+def finish(own, sign, attended, place, out_weight, blocks, before, far_attended, far_weight, received):
+    groups, heads, tokens, _ = attended.shape
+    depth, features = out_weight.shape
+    width = features // blocks
+    rows = heads * HEAD_DIM
+    weight = out_weight.reshape(groups, depth // groups, features)
+    tile = 2 * HEAD_DIM
+    steps = width // tile
+    last = before.shape[0] - 1
+
+    def body(own_ref, sign_ref, mixed_ref, weight_ref, far_ref, far_weight_ref, before_ref, *refs):
+        def product(rows_ref, columns_ref):
+            joined = jnp.concatenate(
+                [rows_ref[group, head] for group in range(groups) for head in range(heads)], axis=1
+            )
+            columns = columns_ref[...].reshape(groups * rows, tile)
+            return jnp.dot(joined, columns, preferred_element_type=jnp.float32)
+
+        total = product(mixed_ref, weight_ref) - product(far_ref, far_weight_ref)
+        total = total * sign_ref[0].astype(jnp.float32) + before_ref[0]
+        for ref in refs[:-1]:
+            total = total + ref[...].astype(jnp.float32)
+        refs[-1][...] = total
+
+    whole = pl.BlockSpec(attended.shape, lambda i, w, s: (0, 0, 0, 0))
+    part = pl.BlockSpec((tokens, tile), lambda i, w, s: (0, i))
+    return pl.pallas_call(
+        body,
+        grid_spec=pltpu.PrefetchScalarGridSpec(
+            num_scalar_prefetch=2,
+            grid=(steps,),
+            in_specs=[
+                whole,
+                pl.BlockSpec((groups, rows, tile), lambda i, w, s: (0, place, w[0] * steps + i)),
+                whole,
+                pl.BlockSpec((groups, rows, tile), lambda i, w, s: (0, 0, i)),
+                pl.BlockSpec((1, tokens, tile), lambda i, w, s: (last, 0, i)),
+            ]
+            + [part] * len(received),
+            out_specs=part,
+        ),
+        out_shape=jax.ShapeDtypeStruct((tokens, width), jnp.float32),
+        compiler_params=pltpu.CompilerParams(vmem_limit_bytes=VMEM_BYTES),
+        name="finish",
+    )(own, sign, attended, weight, far_attended, far_weight, before, *received)
+
+
 def chunk_sizes(heads):
     last = heads // 3 if heads % 3 == 0 else 1
     return [heads - last, last] if heads > last else [heads]
@@ -533,6 +580,7 @@
     half = tokens // 2
     rounds = []
     straight = None
+    held_places = places
     shard = normed
     for phase in range(chips + 1):
         step = phase + 1
@@ -555,18 +603,20 @@
             weights_other.append(lax.ppermute(weights_own[0], "core", swap))
             early = list(rounds)
             tables = tables_of(weights_own[0][:, depth:])
-            held_places, tables = lax.optimization_barrier((places, tables))
+            held_places, tables = lax.optimization_barrier((held_places, tables))
             sent["places"] = project(0, 0, 1, 0, early, held_places)
+        if step > chips and chunks[0] > 1:
+            weights_other.append(lax.ppermute(weights_own[1], "core", swap))
+            sent["places"] = project(0, 1, 1, 0, early, held_places)
         sent, shard = lax.optimization_barrier((sent, shard))
         if phase == 0:
             weights_own.append(sent["weights"])
             cuts[1:] = sent["cuts"]
         if phase == 1:
-            places, gains = sent["places"], sent["gains"]
+            gains = sent["gains"]
         if straight is not None:
             rounds.append(straight + (sent["first"], sent["second"]))
-        if step == chips:
-            held_places = sent["places"]
+        held_places = sent.get("places", held_places)
         if phase < chips:
             straight = (shard, sent["role"], sent["head"])
         if step < chips:
@@ -574,13 +624,24 @@
         if chips - 2 <= phase and len(weights_own) < heads:
             held, _ = lax.optimization_barrier((cuts[len(weights_own)], sent))
             weights_own.append(exchange(held))
+    while len(weights_own) < heads:
+        weights_own.append(exchange(cuts[len(weights_own)]))
     for at in range(len(weights_other), heads - 1):
         weights_other.append(lax.ppermute(weights_own[at], "core", swap))
 
+    sign = (2 * role - 1).astype(jnp.int32)[None]
+    blocks = sides * lax.axis_size("role")
+    which = jnp.stack([peers[3], peers[2], peers[1], peers[0]])
+    out_here = out_weight[0]
+    out_width = out_here.shape[1] // blocks
+    place = spans[-1].start // chunks[-1]
+
     attended = []
+    received = []
     for chunk, size in enumerate(chunks):
+        last = chunk == len(chunks) - 1
         if chunk == 0:
-            for at in range(1, size):
+            for at in range(min(size, 2), size):
                 held_places = project(0, at, 1, 0, early, held_places)
             held_places = project(0, 0, size, len(early), rounds[len(early) :], held_places)
             for at in range(len(weights_other), heads):
@@ -588,8 +649,25 @@
                     (weights_own[at], held_places)
                 )
                 weights_other.append(lax.ppermute(weights_own[at], "core", swap))
+            corner, held_places = lax.optimization_barrier((which[0] * out_width, held_places))
+            far_weight = lax.dynamic_slice(
+                out_here.reshape(chips, heads * HEAD_DIM, -1),
+                (0, spans[-1].start * HEAD_DIM, corner),
+                (chips, chunks[-1] * HEAD_DIM, out_width),
+            )
+            far_weight = lax.ppermute(far_weight, ("role", "head"), far_swap)
         else:
             held_places = project(chunk, 0, size, 0, rounds, held_places)
+        if last:
+            for earlier in range(len(attended)):
+                (diagonal,) = out_blocks(
+                    which[:1], sign, attended[earlier], spans[earlier].start // chunks[earlier],
+                    out_here, blocks, (jnp.bfloat16,),
+                )
+                tables, diagonal, far_weight = lax.optimization_barrier(
+                    (tables, diagonal, far_weight)
+                )
+                received.append(lax.ppermute(diagonal, ("role", "head"), far_swap))
         mixed = attend(spans[chunk].start, size, *tables, parts[chunk])
         held_places, mixed = lax.optimization_barrier((held_places, mixed))
         mixed = mixed.reshape(chips, size, tokens, HEAD_DIM)
@@ -597,30 +675,21 @@
             mixed, attended = lax.optimization_barrier((mixed, attended))
         attended.append(exchange(mixed))
 
-    sign = (2 * role - 1).astype(jnp.int32)[None]
-    blocks = sides * lax.axis_size("role")
-    which = jnp.stack([peers[3], peers[2], peers[1], peers[0]])
     before = None
     for chunk, size in enumerate(chunks[:-1]):
         before = out_blocks(
-            which, sign, attended[chunk], spans[chunk].start // size, out_weight[0], blocks,
+            which[1:], sign, attended[chunk], spans[chunk].start // size, out_here, blocks,
             (jnp.float32,), before,
         )[0]
-    place = spans[-1].start // chunks[-1]
-    (diagonal,) = out_blocks(
-        which[:1], sign, attended[-1], place, out_weight[0], blocks, (jnp.bfloat16,), before
-    )
-    over_head, over_role, own = out_blocks(
-        which[1:], sign, attended[-1], place, out_weight[0], blocks,
-        (jnp.bfloat16, jnp.bfloat16, jnp.float32), before, 1,
-    )
-    from_diagonal = lax.ppermute(diagonal, ("role", "head"), far_swap)
-    from_head = lax.ppermute(over_head, "head", swap)
-    from_role = lax.ppermute(over_role, "role", swap)
-    return own + (
-        from_role.astype(jnp.float32)
-        + from_head.astype(jnp.float32)
-        + from_diagonal.astype(jnp.float32)
+    far_attended = lax.ppermute(attended[-1], ("role", "head"), far_swap)
+    over_head, over_role = out_blocks(
+        which[1:3], sign, attended[-1], place, out_here, blocks, (jnp.bfloat16, jnp.bfloat16), before
+    )
+    received.append(lax.ppermute(over_head, "head", swap))
+    received.append(lax.ppermute(over_role, "role", swap))
+    return finish(
+        which[3:], sign, attended[-1], place, out_here, blocks, before, far_attended, far_weight,
+        received,
     )
 
 
@@ -634,6 +703,7 @@
     tokens = hidden_rows.shape[0] // seq
     return (
         heads % chips == 0
+        and heads // chips > 1
         and chips == role * head
         and width % (role * head * 256) == 0
         and width % (seq * 16) == 0

time: 365 us -> 368 us (level)
  waiting for transfers between devices: 166 us -> 157 us
  local copies, waits for them, and re-layouts: 17.3 us -> 24.6 us
  starting transfers between devices: 52.5 us -> 56.5 us
    all_to_all x5, waiting for transfers between devices: 18.6 us -> 29.6 us  [exchange(): lax.all_to_all(array, 'chip', split_axis=0, concat_axis=0, tiled=True)]
    ppermute x4, waiting for transfers between devices: 78.5 us -> 67.8 us  [per_device_by_heads(): sent['first'] = lax.ppermute(straight[2][:half], 'role', swap)]
    ppermute x4, waiting for transfers between devices: 7.51 us -> 0.01 us  [project(): kv_other = lax.ppermute(kv, 'core', swap)]
    pallas_call x0 -> x1, Pallas kernels: none -> 6.85 us  [finish(): pl.pallas_call(body, grid_spec=pltpu.PrefetchScalarGridSpec(num_scalar_pr...]
    ppermute x3 -> x6, starting transfers between devices: 3.49 us -> 7.85 us  [the longest x1 2.66 us: per_device_by_heads(): far_weight = lax.ppermute(far_weight, ('role', 'head'), far_swap)]
    unnamed x48 -> x54, local copies, waits for them, and re-layouts: 4.66 us -> 8.68 us
    ppermute x3 -> x6, waiting for transfers between devices: 32.9 us -> 31.8 us  [the longest x1 27.3 us: per_device_by_heads(): far_attended = lax.ppermute(attended[-1], ('role', 'head'), far_swap)]
  transfers between devices with their start and end apart: 36 -> 38, of which waited for: 18 -> 14; matrix products, arithmetic and copies ran while one was open for 8% -> 9% of each run, Pallas kernels for 27% -> 25%
where the time goes in v10:
time: 368 us; the launch traced here: 366 us
  waiting for transfers between devices  157 us (43%)
  Pallas kernels  108 us (29%)
  starting transfers between devices  56.5 us (15%)
  local copies, waits for them, and re-layouts  24.6 us (7%)
  matrix products  12.6 us (3%)
  other arithmetic  6.53 us (2%)
    ppermute x4, waiting for transfers between devices, per_device_by_heads(): sent['first'] = lax.ppermute(straight[2][:half], 'role', swap)  67.8 us
    pallas_call x4, Pallas kernels, project_heads(): pl.pallas_call(body, in_specs=[in_smem(), in_smem()] + [in_hbm()] * (2 *...  51.4 us
    all_to_all x5, waiting for transfers between devices, exchange(): lax.all_to_all(array, 'chip', split_axis=0, concat_axis=0, tiled=True)  29.6 us
    ppermute x1, waiting for transfers between devices, per_device_by_heads(): far_attended = lax.ppermute(attended[-1], ('role', 'head'), far_swap)  27.3 us
    all_to_all x5, starting transfers between devices, exchange(): lax.all_to_all(array, 'chip', split_axis=0, concat_axis=0, tiled=True)  23.4 us
    pallas_call x3, Pallas kernels, out_blocks(): pl.pallas_call(body, grid_spec=pltpu.PrefetchScalarGridSpec(num_scalar_pr...  19.4 us
    pallas_call x2, Pallas kernels, attend(): pl.pallas_call(body, in_specs=[in_smem()] * 4 + [in_hbm()] * len(arrays),...  19.3 us
    ppermute x3, waiting for transfers between devices, per_device_by_heads(): sent['next'] = lax.ppermute(shard, 'chip', ring)  14.1 us
  transfers between devices with their start and end apart: 38, of which 14 were waited for; matrix products, arithmetic and copies ran while one was open for 9% of the time, Pallas kernels for 25%

profile of v10, /device:TPU:0, one launch (start us, length us, event | category | flops | bytes accessed | tf_op | source)
XLA Modules:
  0.0 365.8 jit_solution(12116315565955688826)
XLA Ops:
  6.2 6.4 %all-to-all-start = ((bf16[4,656,384]{2,1,0:T(8,128)(2,1)}), bf16[4,656,384]{2,1,0:T(8,128)(2,1)S(1)}, u32[]{:S(2)}, u32[]{:S(2)}) async-start(bf16[4,656,384]{2,1,0:T(8,128)(2,1)} %cut_columns.5), calls=%async_computation | async-start | bytes 4030464 | tf_op jit(solution)/shard_map/all_to_all | solution.py:503
  13.0 12.6 %multiply_reduce_fusion = (f32[384]{0:T(512)S(1)}, f32[384,1280]{1,0:T(8,128)}) fusion(bf16[384,5120]{1,0:T(8,128)(2,1)} %param.11, s32[]{:T(128)S(6)} %select_n.47, f32[384]{0:T(512)S(1)} %mul.85, bf16[384,5120]{1,0:T(8,128)(2,1)} %param.9, bf16[5120,1280]{1,0:T(8,128)(2,1)} %param.10, f32[384]{0:T(512)S(1)} %mul.81), kind=kOutput, calls=%fused_computation.4 | convolution fusion | flops 5036604928 | bytes 19993092 | tf_op jit(solution)/shard_map/dot_general | solution.py:521
  47.3 9.0 %collective-permute-done.2.refs_4_ = bf16[384,1280]{1,0:T(8,128)(2,1)} collective-permute-done((bf16[384,1280]{1,0:T(8,128)(2,1)S(1)}, bf16[384,1280]{1,0:T(8,128)(2,1)}, u32[]{:S(2)}, u32[]{:S(2)}) %collective-permute-start.2) | collective-permute-done | bytes 983072 | tf_op jit(solution)/shard_map/ppermute | solution.py:590
  56.4 14.1 %collective-permute-done.3.refs_7_ = bf16[384,1280]{1,0:T(8,128)(2,1)} collective-permute-done((bf16[384,1280]{1,0:T(8,128)(2,1)S(1)}, bf16[384,1280]{1,0:T(8,128)(2,1)}, u32[]{:S(2)}, u32[]{:S(2)}) %collective-permute-start.3) | collective-permute-done | bytes 983072 | tf_op jit(solution)/shard_map/ppermute | solution.py:595
  70.5 9.6 %all-to-all-done.refs_0_ = bf16[4,656,384]{2,1,0:T(8,128)(2,1)S(1)} async-done(((bf16[4,656,384]{2,1,0:T(8,128)(2,1)}), bf16[4,656,384]{2,1,0:T(8,128)(2,1)S(1)}, u32[]{:S(2)}, u32[]{:S(2)}) %all-to-all-start) | async-done | bytes 2015264 | tf_op jit(solution)/shard_map/all_to_all | solution.py:503
  88.5 26.3 %collective-permute-done.5.refs_5_ = bf16[192,1280]{1,0:T(8,128)(2,1)S(1)} collective-permute-done((bf16[192,1280]{1,0:T(8,128)(2,1)}, bf16[192,1280]{1,0:T(8,128)(2,1)S(1)}, u32[]{:S(2)}, u32[]{:S(2)}) %collective-permute-start.5) | collective-permute-done | bytes 491552 | tf_op jit(solution)/shard_map/ppermute | solution.py:592
  120.9 26.8 %collective-permute-done.10.refs_10_ = bf16[192,1280]{1,0:T(8,128)(2,1)} collective-permute-done((bf16[192,1280]{1,0:T(8,128)(2,1)S(1)}, bf16[192,1280]{1,0:T(8,128)(2,1)}, u32[]{:S(2)}, u32[]{:S(2)}) %collective-permute-start.10) | collective-permute-done | bytes 491552 | tf_op jit(solution)/shard_map/ppermute | solution.py:592
  147.7 4.8 %all-to-all-start.2 = ((bf16[4,640,384]{2,1,0:T(8,128)(2,1)}), bf16[4,640,384]{2,1,0:T(8,128)(2,1)}, u32[]{:S(2)}, u32[]{:S(2)}) async-start(bf16[4,640,384]{2,1,0:T(8,128)(2,1)} %cut_columns.3), calls=%async_computation.2 | async-start | bytes 3932160 | tf_op jit(solution)/shard_map/all_to_all | solution.py:503
  164.2 10.4 %project_heads.4 = (bf16[1,2,384,128]{3,2,1,0:T(8,128)(2,1)}, bf16[1,2,2,384,128]{4,3,2,1,0:T(8,128)(2,1)}) custom-call(s32[5]{0:T(128)} %concatenate.10.places_ref, f32[2,1]{1,0:T(2,128)} %get-tuple-element.141.gains_ref, bf16[4,656,384]{2,1,0:T(8,128)(2,1)} %copy-done.2, bf16[4,656,384]{2,1,0:T(8,128)(2,1)} %collective-permute-done.17.refs_1_.refs_2_, ...), custom_call_target="tpu_custom_call" | custom-call | tf_op jit(solution)/shard_map/project_heads/pallas_call | solution.py:257
  174.5 14.7 %collective-permute-done.15.refs_7_.refs_15_ = bf16[192,1280]{1,0:T(8,128)(2,1)S(1)} collective-permute-done((bf16[192,1280]{1,0:T(8,128)(2,1)}, bf16[192,1280]{1,0:T(8,128)(2,1)S(1)}, u32[]{:S(2)}, u32[]{:S(2)}) %collective-permute-start.15) | collective-permute-done | bytes 491552 | tf_op jit(solution)/shard_map/ppermute | solution.py:592
  189.3 5.7 %all-to-all-done.2.refs_0_.refs_1_ = bf16[4,640,384]{2,1,0:T(8,128)(2,1)} async-done(((bf16[4,640,384]{2,1,0:T(8,128)(2,1)}), bf16[4,640,384]{2,1,0:T(8,128)(2,1)}, u32[]{:S(2)}, u32[]{:S(2)}) %all-to-all-start.2) | async-done | bytes 1966112 | tf_op jit(solution)/shard_map/all_to_all | solution.py:503
  204.4 10.3 %project_heads.5 = (bf16[1,2,384,128]{3,2,1,0:T(8,128)(2,1)}, bf16[1,2,2,384,128]{4,3,2,1,0:T(8,128)(2,1)}) custom-call(s32[5]{0:T(128)} %concatenate.10.places_ref, f32[2,1]{1,0:T(2,128)} %get-tuple-element.140.gains_ref, bf16[4,640,384]{2,1,0:T(8,128)(2,1)} %all-to-all-done.2.refs_0_.refs_1_, bf16[4,640,384]{2,1,0:T(8,128)(2,1)} %copy-done.5, ...), custom_call_target="tpu_custom_call" | custom-call | tf_op jit(solution)/shard_map/project_heads/pallas_call | solution.py:257
  215.8 13.7 %project_heads.6 = (bf16[2,2,384,128]{3,2,1,0:T(8,128)(2,1)}, bf16[2,2,2,384,128]{4,3,2,1,0:T(8,128)(2,1)}) custom-call(s32[5]{0:T(128)} %concatenate.10.places_ref, f32[2,2]{1,0:T(2,128)} %bitcast.65, bf16[4,656,384]{2,1,0:T(8,128)(2,1)} %copy-done.2, bf16[4,640,384]{2,1,0:T(8,128)(2,1)} %all-to-all-done.2.refs_0_.refs_1_, ...), custom_call_target="tpu_custom_call" | custom-call | tf_op jit(solution)/shard_map/project_heads/pallas_call | solution.py:257
  229.5 14.1 %all-to-all-done.1.refs_0_ = bf16[4,640,384]{2,1,0:T(8,128)(2,1)S(1)} async-done(((bf16[4,640,384]{2,1,0:T(8,128)(2,1)}), bf16[4,640,384]{2,1,0:T(8,128)(2,1)S(1)}, u32[]{:S(2)}, u32[]{:S(2)}) %all-to-all-start.1) | async-done | bytes 1966112 | tf_op jit(solution)/shard_map/all_to_all | solution.py:503
  251.7 11.9 %attend.2 = bf16[4,2,6,64,128]{4,3,2,1,0:T(8,128)(2,1)} custom-call(s32[3,24,8]{2,1,0:T(8,128)} %fusion.7.slots_ref, s32[3,24]{1,0:T(4,128)} %get-tuple-element.124.counts_ref, s32[24]{0:T(128)} %fusion.11.from_ref, s32[3,4]{1,0:T(4,128)} %reduce_max.9.most_ref, bf16[1,12,64,128]{3,2,1,0:T(8,128)(2,1)} %bitcast.60, bf16[1,2,12,64,128]{4,3,2,1,0:T(8,128)(2,1)} %bitcast.54, ...), custom_call_target="tpu_custom_call" | custom-call | tf_op jit(solution)/shard_map/attend/pallas_call | solution.py:352
  267.3 17.0 %project_heads.7 = (bf16[1,4,384,128]{3,2,1,0:T(8,128)(2,1)}, bf16[1,2,4,384,128]{4,3,2,1,0:T(8,128)(2,1)}) custom-call(s32[5]{0:T(128)} %concatenate.10.places_ref, f32[2,1]{1,0:T(2,128)} %get-tuple-element.139.gains_ref, bf16[4,640,384]{2,1,0:T(8,128)(2,1)} %copy-done.6, bf16[4,640,384]{2,1,0:T(8,128)(2,1)} %collective-permute-done.27.refs_1_, ...), custom_call_target="tpu_custom_call" | custom-call | tf_op jit(solution)/shard_map/project_heads/pallas_call | solution.py:257
  285.6 4.1 %out_blocks.3 = bf16[384,1280]{1,0:T(8,128)(2,1)} custom-call(s32[1]{0:T(128)} %bitcast.7.which_ref, s32[1]{0:T(128)} %bitcast.1.sign_ref, bf16[4,2,384,128]{3,2,1,0:T(8,128)(2,1)} %copy-done.7, bf16[4,384,5120]{2,1,0:T(8,128)(2,1)} %bitcast.40), custom_call_target="tpu_custom_call" | custom-call | tf_op jit(solution)/shard_map/out_blocks/pallas_call | solution.py:412
  290.6 7.3 %attend.3 = bf16[4,1,6,64,128]{4,3,2,1,0:T(8,128)(2,1)} custom-call(s32[3,24,8]{2,1,0:T(8,128)} %fusion.7.slots_ref, s32[3,24]{1,0:T(4,128)} %get-tuple-element.124.counts_ref, s32[24]{0:T(128)} %fusion.11.from_ref, s32[3,4]{1,0:T(4,128)} %reduce_max.9.most_ref, bf16[1,24,64,128]{3,2,1,0:T(8,128)(2,1)} %bitcast.58, bf16[1,2,24,64,128]{4,3,2,1,0:T(8,128)(2,1)} %bitcast.52, ...), custom_call_target="tpu_custom_call" | custom-call | tf_op jit(solution)/shard_map/attend/pallas_call | solution.py:352
  298.0 4.6 %all-to-all-start.4 = ((bf16[4,1,384,128]{3,2,1,0:T(8,128)(2,1)}), bf16[4,1,384,128]{3,2,1,0:T(8,128)(2,1)S(1)}, u32[]{:S(2)}, u32[]{:S(2)}) async-start(bf16[4,1,384,128]{3,2,1,0:T(8,128)(2,1)} %bitcast.48), calls=%async_computation.4 | async-start | bytes 786432 | tf_op jit(solution)/shard_map/all_to_all | solution.py:503
  305.5 9.5 %out_blocks.4.refs_0_.before_ref = f32[3,384,1280]{2,1,0:T(8,128)} custom-call(s32[3]{0:T(128)} %pad_add_fusion.which_ref, s32[1]{0:T(128)} %bitcast.1.sign_ref, bf16[4,2,384,128]{3,2,1,0:T(8,128)(2,1)} %copy-done.7, bf16[4,384,5120]{2,1,0:T(8,128)(2,1)} %bitcast.41), custom_call_target="tpu_custom_call" | custom-call | tf_op jit(solution)/shard_map/out_blocks/pallas_call | solution.py:412
  315.7 5.8 %out_blocks.5 = (bf16[384,1280]{1,0:T(8,128)(2,1)}, bf16[384,1280]{1,0:T(8,128)(2,1)}) custom-call(s32[2]{0:T(128)} %pad_add_fusion.1.which_ref, s32[1]{0:T(128)} %bitcast.1.sign_ref, bf16[4,1,384,128]{3,2,1,0:T(8,128)(2,1)} %copy-done.10, bf16[4,384,5120]{2,1,0:T(8,128)(2,1)} %bitcast.42, f32[3,384,1280]{2,1,0:T(8,128)} %out_blocks.4.refs_0_.before_ref), custom_call_target="tpu_custom_call" | custom-call | tf_op jit(solution)/shard_map/out_blocks/pallas_call | solution.py:412
  325.0 4.5 %collective-permute-done.30.refs_0_ = bf16[384,1280]{1,0:T(8,128)(2,1)S(1)} collective-permute-done((bf16[384,1280]{1,0:T(8,128)(2,1)S(1)}, bf16[384,1280]{1,0:T(8,128)(2,1)S(1)}, u32[]{:S(2)}, u32[]{:S(2)}) %collective-permute-start.30) | collective-permute-done | bytes 983072 | tf_op jit(solution)/shard_map/ppermute | solution.py:670
  329.5 27.3 %collective-permute-done.29.far_ref = bf16[4,1,384,128]{3,2,1,0:T(8,128)(2,1)S(1)} collective-permute-done((bf16[4,1,384,128]{3,2,1,0:T(8,128)(2,1)}, bf16[4,1,384,128]{3,2,1,0:T(8,128)(2,1)S(1)}, u32[]{:S(2)}, u32[]{:S(2)}) %collective-permute-start.29) | collective-permute-done | bytes 393248 | tf_op jit(solution)/shard_map/ppermute | solution.py:684
  358.8 6.8 %finish.1 = f32[384,1280]{1,0:T(8,128)} custom-call(s32[1]{0:T(128)} %bitcast.own_ref, s32[1]{0:T(128)} %bitcast.1.sign_ref, bf16[4,1,384,128]{3,2,1,0:T(8,128)(2,1)} %copy-done.10, bf16[4,384,5120]{2,1,0:T(8,128)(2,1)} %bitcast.43, bf16[4,1,384,128]{3,2,1,0:T(8,128)(2,1)} %copy-done.20, bf16[4,128,1280]{2,1,0:T(8,128)(2,1)} %collective-permute-done.26.far_weight_ref, ...), custom_call_target="tpu_custom_call" | custom-call | tf_op jit(solution)/shard_map/finish/pallas_call | solution.py:449
  (161 shorter events, 87.7 us)
Async XLA Ops:
  6.2 74.0 %all-to-all-start = ((bf16[4,656,384]{2,1,0:T(8,128)(2,1)}), bf16[4,656,384]{2,1,0:T(8,128)(2,1)S(1)}, u32[]{:S(2)}, u32[]{:S(2)}) async-start(bf16[4,656,384]{2,1,0:T(8,128)(2,1)} %cut_columns.5), calls=%async_computation | async-start | bytes 4030464 | tf_op jit(solution)/shard_map/all_to_all | solution.py:503
  36.3 34.2 %collective-permute-start.3 = (bf16[384,1280]{1,0:T(8,128)(2,1)S(1)}, bf16[384,1280]{1,0:T(8,128)(2,1)}, u32[]{:S(2)}, u32[]{:S(2)}) collective-permute-start(bf16[384,1280]{1,0:T(8,128)(2,1)S(1)} %multiply_convert_fusion.refs_2_), channel_id=1, source_target_pairs={{0,4},{4,8},{8,12},{12,0},{1,5},{5,9},{9,13},{13,1},{2,6},{6,10},{... | collective-permute-start | bytes 2949128 | tf_op jit(solution)/shard_map/ppermute | solution.py:595
  38.3 32.2 %collective-permute-start.4 = (bf16[384,1280]{1,0:T(8,128)(2,1)S(1)}, bf16[384,1280]{1,0:T(8,128)(2,1)}, u32[]{:S(2)}, u32[]{:S(2)}) collective-permute-start(bf16[384,1280]{1,0:T(8,128)(2,1)S(1)} %multiply_convert_fusion.refs_2_), channel_id=1, source_target_pairs={{0,16},{16,0},{1,17},{17,1},{2,18},{18,2},{3,19},{19,3},{4,20},{20... | collective-permute-start | bytes 2949128 | tf_op jit(solution)/shard_map/ppermute | solution.py:589
  80.1 34.7 %collective-permute-start.6 = (bf16[384,1280]{1,0:T(8,128)(2,1)}, bf16[384,1280]{1,0:T(8,128)(2,1)S(1)}, u32[]{:S(2)}, u32[]{:S(2)}) collective-permute-start(bf16[384,1280]{1,0:T(8,128)(2,1)} %collective-permute-done.3.refs_7_), channel_id=1, source_target_pairs={{0,1},{1,0},{2,3},{3,2},{4,5},{5,4},{6,7},{7,6},{8,9},{9,8},{10,11... | collective-permute-start | bytes 2949128 | tf_op jit(solution)/shard_map/ppermute | solution.py:590
  81.6 33.2 %collective-permute-start.7 = (bf16[384,1280]{1,0:T(8,128)(2,1)}, bf16[384,1280]{1,0:T(8,128)(2,1)}, u32[]{:S(2)}, u32[]{:S(2)}) collective-permute-start(bf16[384,1280]{1,0:T(8,128)(2,1)} %collective-permute-done.3.refs_7_), channel_id=1, source_target_pairs={{0,4},{4,8},{8,12},{12,0},{1,5},{5,9},{9,13},{13,1},{2,6},{6,10},{... | collective-permute-start | bytes 2949128 | tf_op jit(solution)/shard_map/ppermute | solution.py:595
  81.6 33.2 %collective-permute-start.8 = (bf16[384,1280]{1,0:T(8,128)(2,1)}, bf16[384,1280]{1,0:T(8,128)(2,1)}, u32[]{:S(2)}, u32[]{:S(2)}) collective-permute-start(bf16[384,1280]{1,0:T(8,128)(2,1)} %collective-permute-done.3.refs_7_), channel_id=1, source_target_pairs={{0,16},{16,0},{1,17},{17,1},{2,18},{18,2},{3,19},{19,3},{4,20},{20... | collective-permute-start | bytes 2949128 | tf_op jit(solution)/shard_map/ppermute | solution.py:589
  85.0 29.9 %collective-permute-start.5 = (bf16[192,1280]{1,0:T(8,128)(2,1)}, bf16[192,1280]{1,0:T(8,128)(2,1)S(1)}, u32[]{:S(2)}, u32[]{:S(2)}) collective-permute-start(bf16[192,1280]{1,0:T(8,128)(2,1)} %slice.53), channel_id=1, source_target_pairs={{0,16},{16,0},{1,17},{17,1},{2,18},{18,2},{3,19},{19,3},{4,20},{20... | collective-permute-start | bytes 1474568 | tf_op jit(solution)/shard_map/ppermute | solution.py:592
  87.3 27.5 %collective-permute-start.9 = (bf16[192,1280]{1,0:T(8,128)(2,1)}, bf16[192,1280]{1,0:T(8,128)(2,1)}, u32[]{:S(2)}, u32[]{:S(2)}) collective-permute-start(bf16[192,1280]{1,0:T(8,128)(2,1)} %slice.54), channel_id=1, source_target_pairs={{0,1},{1,0},{2,3},{3,2},{4,5},{5,4},{6,7},{7,6},{8,9},{9,8},{10,11... | collective-permute-start | bytes 1474568 | tf_op jit(solution)/shard_map/ppermute | solution.py:593
  114.9 32.8 %collective-permute-start.11 = (bf16[384,1280]{1,0:T(8,128)(2,1)}, bf16[384,1280]{1,0:T(8,128)(2,1)}, u32[]{:S(2)}, u32[]{:S(2)}) collective-permute-start(bf16[384,1280]{1,0:T(8,128)(2,1)} %collective-permute-done.7.refs_4_.refs_12_), channel_id=1, source_target_pairs={{0,1},{1,0},{2,3},{3,2},{4,5},{5,4},{6,7},{7,6},{8,9},{9,8},{10,11... | collective-permute-start | bytes 2949128 | tf_op jit(solution)/shard_map/ppermute | solution.py:590
  115.4 32.2 %collective-permute-start.12 = (bf16[384,1280]{1,0:T(8,128)(2,1)}, bf16[384,1280]{1,0:T(8,128)(2,1)}, u32[]{:S(2)}, u32[]{:S(2)}) collective-permute-start(bf16[384,1280]{1,0:T(8,128)(2,1)} %collective-permute-done.7.refs_4_.refs_12_), channel_id=1, source_target_pairs={{0,4},{4,8},{8,12},{12,0},{1,5},{5,9},{9,13},{13,1},{2,6},{6,10},{... | collective-permute-start | bytes 2949128 | tf_op jit(solution)/shard_map/ppermute | solution.py:595
  116.1 31.6 %collective-permute-start.13 = (bf16[384,1280]{1,0:T(8,128)(2,1)}, bf16[384,1280]{1,0:T(8,128)(2,1)}, u32[]{:S(2)}, u32[]{:S(2)}) collective-permute-start(bf16[384,1280]{1,0:T(8,128)(2,1)} %collective-permute-done.7.refs_4_.refs_12_), channel_id=1, source_target_pairs={{0,16},{16,0},{1,17},{17,1},{2,18},{18,2},{3,19},{19,3},{4,20},{20... | collective-permute-start | bytes 2949128 | tf_op jit(solution)/shard_map/ppermute | solution.py:589
  117.6 30.0 %collective-permute-start.10 = (bf16[192,1280]{1,0:T(8,128)(2,1)S(1)}, bf16[192,1280]{1,0:T(8,128)(2,1)}, u32[]{:S(2)}, u32[]{:S(2)}) collective-permute-start(bf16[192,1280]{1,0:T(8,128)(2,1)S(1)} %slice.59), channel_id=1, source_target_pairs={{0,16},{16,0},{1,17},{17,1},{2,18},{18,2},{3,19},{19,3},{4,20},{20... | collective-permute-start | bytes 1474568 | tf_op jit(solution)/shard_map/ppermute | solution.py:592
  119.3 28.4 %collective-permute-start.14 = (bf16[192,1280]{1,0:T(8,128)(2,1)S(1)}, bf16[192,1280]{1,0:T(8,128)(2,1)}, u32[]{:S(2)}, u32[]{:S(2)}) collective-permute-start(bf16[192,1280]{1,0:T(8,128)(2,1)S(1)} %slice.60), channel_id=1, source_target_pairs={{0,1},{1,0},{2,3},{3,2},{4,5},{5,4},{6,7},{7,6},{8,9},{9,8},{10,11... | collective-permute-start | bytes 1474568 | tf_op jit(solution)/shard_map/ppermute | solution.py:593
  147.7 47.3 %all-to-all-start.2 = ((bf16[4,640,384]{2,1,0:T(8,128)(2,1)}), bf16[4,640,384]{2,1,0:T(8,128)(2,1)}, u32[]{:S(2)}, u32[]{:S(2)}) async-start(bf16[4,640,384]{2,1,0:T(8,128)(2,1)} %cut_columns.3), calls=%async_computation.2 | async-start | bytes 3932160 | tf_op jit(solution)/shard_map/all_to_all | solution.py:503
  153.1 36.1 %collective-permute-start.16 = (bf16[384,1280]{1,0:T(8,128)(2,1)}, bf16[384,1280]{1,0:T(8,128)(2,1)S(1)}, u32[]{:S(2)}, u32[]{:S(2)}) collective-permute-start(bf16[384,1280]{1,0:T(8,128)(2,1)} %collective-permute-done.12.refs_9_.refs_17_), channel_id=1, source_target_pairs={{0,1},{1,0},{2,3},{3,2},{4,5},{5,4},{6,7},{7,6},{8,9},{9,8},{10,11... | collective-permute-start | bytes 2949128 | tf_op jit(solution)/shard_map/ppermute | solution.py:590
  154.6 34.7 %collective-permute-start.18 = (bf16[384,1280]{1,0:T(8,128)(2,1)}, bf16[384,1280]{1,0:T(8,128)(2,1)}, u32[]{:S(2)}, u32[]{:S(2)}) collective-permute-start(bf16[384,1280]{1,0:T(8,128)(2,1)} %collective-permute-done.12.refs_9_.refs_17_), channel_id=1, source_target_pairs={{0,16},{16,0},{1,17},{17,1},{2,18},{18,2},{3,19},{19,3},{4,20},{20... | collective-permute-start | bytes 2949128 | tf_op jit(solution)/shard_map/ppermute | solution.py:589
  160.2 29.0 %collective-permute-start.15 = (bf16[192,1280]{1,0:T(8,128)(2,1)}, bf16[192,1280]{1,0:T(8,128)(2,1)S(1)}, u32[]{:S(2)}, u32[]{:S(2)}) collective-permute-start(bf16[192,1280]{1,0:T(8,128)(2,1)} %slice.61), channel_id=1, source_target_pairs={{0,16},{16,0},{1,17},{17,1},{2,18},{18,2},{3,19},{19,3},{4,20},{20... | collective-permute-start | bytes 1474568 | tf_op jit(solution)/shard_map/ppermute | solution.py:592
  160.8 28.5 %collective-permute-start.19 = (bf16[192,1280]{1,0:T(8,128)(2,1)}, bf16[192,1280]{1,0:T(8,128)(2,1)}, u32[]{:S(2)}, u32[]{:S(2)}) collective-permute-start(bf16[192,1280]{1,0:T(8,128)(2,1)} %slice.63), channel_id=1, source_target_pairs={{0,1},{1,0},{2,3},{3,2},{4,5},{5,4},{6,7},{7,6},{8,9},{9,8},{10,11... | collective-permute-start | bytes 1474568 | tf_op jit(solution)/shard_map/ppermute | solution.py:593
  195.0 48.6 %all-to-all-start.1 = ((bf16[4,640,384]{2,1,0:T(8,128)(2,1)}), bf16[4,640,384]{2,1,0:T(8,128)(2,1)S(1)}, u32[]{:S(2)}, u32[]{:S(2)}) async-start(bf16[4,640,384]{2,1,0:T(8,128)(2,1)} %cut_columns.4), calls=%async_computation.1 | async-start | bytes 3932160 | tf_op jit(solution)/shard_map/all_to_all | solution.py:503
  247.9 41.9 %collective-permute-start.26 = (bf16[4,128,1280]{2,1,0:T(8,128)(2,1)}, bf16[4,128,1280]{2,1,0:T(8,128)(2,1)}, u32[]{:S(2)}, u32[]{:S(2)}) collective-permute-start(bf16[4,128,1280]{2,1,0:T(8,128)(2,1)} %constant_dynamic-slice_fusion), channel_id=1, source_target_pairs={{0,17},{1,16},{16,1},{17,0},{2,19},{3,18},{18,3},{19,2},{4,21},{5,... | collective-permute-start | bytes 3932168 | tf_op jit(solution)/shard_map/ppermute | solution.py:658
  303.8 25.6 %collective-permute-start.30 = (bf16[384,1280]{1,0:T(8,128)(2,1)S(1)}, bf16[384,1280]{1,0:T(8,128)(2,1)S(1)}, u32[]{:S(2)}, u32[]{:S(2)}) collective-permute-start(bf16[384,1280]{1,0:T(8,128)(2,1)S(1)} %copy-done.14), channel_id=1, source_target_pairs={{0,17},{1,16},{16,1},{17,0},{2,19},{3,18},{18,3},{19,2},{4,21},{5,... | collective-permute-start | bytes 2949128 | tf_op jit(solution)/shard_map/ppermute | solution.py:670
  321.5 35.3 %collective-permute-start.31 = (bf16[384,1280]{1,0:T(8,128)(2,1)}, bf16[384,1280]{1,0:T(8,128)(2,1)S(1)}, u32[]{:S(2)}, u32[]{:S(2)}) collective-permute-start(bf16[384,1280]{1,0:T(8,128)(2,1)} %get-tuple-element.135), channel_id=1, source_target_pairs={{0,1},{1,0},{2,3},{3,2},{4,5},{5,4},{6,7},{7,6},{8,9},{9,8},{10,11... | collective-permute-start | bytes 2949128 | tf_op jit(solution)/shard_map/ppermute | solution.py:688
  321.9 34.9 %collective-permute-start.32 = (bf16[384,1280]{1,0:T(8,128)(2,1)}, bf16[384,1280]{1,0:T(8,128)(2,1)S(1)}, u32[]{:S(2)}, u32[]{:S(2)}) collective-permute-start(bf16[384,1280]{1,0:T(8,128)(2,1)} %get-tuple-element.136), channel_id=1, source_target_pairs={{0,16},{16,0},{1,17},{17,1},{2,18},{18,2},{3,19},{19,3},{4,20},{20... | collective-permute-start | bytes 2949128 | tf_op jit(solution)/shard_map/ppermute | solution.py:689
  323.4 33.4 %collective-permute-start.29 = (bf16[4,1,384,128]{3,2,1,0:T(8,128)(2,1)}, bf16[4,1,384,128]{3,2,1,0:T(8,128)(2,1)S(1)}, u32[]{:S(2)}, u32[]{:S(2)}) collective-permute-start(bf16[4,1,384,128]{3,2,1,0:T(8,128)(2,1)} %copy-done.10), channel_id=1, source_target_pairs={{0,17},{1,16},{16,1},{17,0},{2,19},{3,18},{18,3},{19,2},{4,21},{5,... | collective-permute-start | bytes 1179656 | tf_op jit(solution)/shard_map/ppermute | solution.py:684
  (39 other events, 575.1 us)

commit v11 on v9

--- a/solution.py
+++ b/solution.py
@@ -385,7 +385,7 @@
         )
         total = total * sign_ref[0].astype(jnp.float32)
         if before is not None:
-            total = total + refs[0][0]
+            total = total + refs[0][0].astype(jnp.float32)
         if stacked:
             out_refs[0][0] = total.astype(dtypes[0])
         else:
@@ -533,6 +533,7 @@
     half = tokens // 2
     rounds = []
     straight = None
+    held_places = places
     shard = normed
     for phase in range(chips + 1):
         step = phase + 1
@@ -555,18 +556,20 @@
             weights_other.append(lax.ppermute(weights_own[0], "core", swap))
             early = list(rounds)
             tables = tables_of(weights_own[0][:, depth:])
-            held_places, tables = lax.optimization_barrier((places, tables))
+            held_places, tables = lax.optimization_barrier((held_places, tables))
             sent["places"] = project(0, 0, 1, 0, early, held_places)
+        if step > chips and chunks[0] > 1:
+            weights_other.append(lax.ppermute(weights_own[1], "core", swap))
+            sent["places"] = project(0, 1, 1, 0, early, held_places)
         sent, shard = lax.optimization_barrier((sent, shard))
         if phase == 0:
             weights_own.append(sent["weights"])
             cuts[1:] = sent["cuts"]
         if phase == 1:
-            places, gains = sent["places"], sent["gains"]
+            gains = sent["gains"]
         if straight is not None:
             rounds.append(straight + (sent["first"], sent["second"]))
-        if step == chips:
-            held_places = sent["places"]
+        held_places = sent.get("places", held_places)
         if phase < chips:
             straight = (shard, sent["role"], sent["head"])
         if step < chips:
@@ -574,54 +577,81 @@
         if chips - 2 <= phase and len(weights_own) < heads:
             held, _ = lax.optimization_barrier((cuts[len(weights_own)], sent))
             weights_own.append(exchange(held))
+    while len(weights_own) < heads:
+        weights_own.append(exchange(cuts[len(weights_own)]))
     for at in range(len(weights_other), heads - 1):
         weights_other.append(lax.ppermute(weights_own[at], "core", swap))
 
+    sign = (2 * role - 1).astype(jnp.int32)[None]
+    blocks = sides * lax.axis_size("role")
+    which = jnp.stack([peers[3], peers[2], peers[1], peers[0]])
+    out_here = out_weight[0]
+    out_width = out_here.shape[1] // blocks
+    place = spans[-1].start // chunks[-1]
+
     attended = []
+    received = []
     for chunk, size in enumerate(chunks):
+        last = chunk == len(chunks) - 1
         if chunk == 0:
-            for at in range(1, size):
+            for at in range(min(size, 2), size):
                 held_places = project(0, at, 1, 0, early, held_places)
             held_places = project(0, 0, size, len(early), rounds[len(early) :], held_places)
+        else:
+            held_places = project(chunk, 0, size, 0, rounds, held_places)
+        if last:
+            for earlier in range(len(attended)):
+                (diagonal,) = out_blocks(
+                    which[:1], sign, attended[earlier], spans[earlier].start // chunks[earlier],
+                    out_here, blocks, (jnp.bfloat16,),
+                )
+                tables, diagonal, far_weight = lax.optimization_barrier(
+                    (tables, diagonal, far_weight)
+                )
+                received.append(lax.ppermute(diagonal, ("role", "head"), far_swap))
+        mixed = attend(spans[chunk].start, size, *tables, parts[chunk])
+        held_places, mixed = lax.optimization_barrier((held_places, mixed))
+        if chunk == 0:
             for at in range(len(weights_other), heads):
                 weights_own[at], held_places = lax.optimization_barrier(
                     (weights_own[at], held_places)
                 )
                 weights_other.append(lax.ppermute(weights_own[at], "core", swap))
-        else:
-            held_places = project(chunk, 0, size, 0, rounds, held_places)
-        mixed = attend(spans[chunk].start, size, *tables, parts[chunk])
-        held_places, mixed = lax.optimization_barrier((held_places, mixed))
+            corner, held_places = lax.optimization_barrier((which[0] * out_width, held_places))
+            far_weight = lax.dynamic_slice(
+                out_here.reshape(chips, heads * HEAD_DIM, -1),
+                (0, spans[-1].start * HEAD_DIM, corner),
+                (chips, chunks[-1] * HEAD_DIM, out_width),
+            )
+            far_weight = lax.ppermute(far_weight, ("role", "head"), far_swap)
         mixed = mixed.reshape(chips, size, tokens, HEAD_DIM)
         if attended:
             mixed, attended = lax.optimization_barrier((mixed, attended))
         attended.append(exchange(mixed))
 
-    sign = (2 * role - 1).astype(jnp.int32)[None]
-    blocks = sides * lax.axis_size("role")
-    which = jnp.stack([peers[3], peers[2], peers[1], peers[0]])
-    before = None
-    for chunk, size in enumerate(chunks[:-1]):
-        before = out_blocks(
-            which, sign, attended[chunk], spans[chunk].start // size, out_weight[0], blocks,
-            (jnp.float32,), before,
-        )[0]
-    place = spans[-1].start // chunks[-1]
-    (diagonal,) = out_blocks(
-        which[:1], sign, attended[-1], place, out_weight[0], blocks, (jnp.bfloat16,), before
-    )
-    over_head, over_role, own = out_blocks(
-        which[1:], sign, attended[-1], place, out_weight[0], blocks,
-        (jnp.bfloat16, jnp.bfloat16, jnp.float32), before, 1,
-    )
-    from_diagonal = lax.ppermute(diagonal, ("role", "head"), far_swap)
-    from_head = lax.ppermute(over_head, "head", swap)
-    from_role = lax.ppermute(over_role, "role", swap)
-    return own + (
-        from_role.astype(jnp.float32)
-        + from_head.astype(jnp.float32)
-        + from_diagonal.astype(jnp.float32)
-    )
+    def contributions(wanted, dtypes, before=None):
+        for chunk, size in enumerate(chunks[:-1]):
+            before = jnp.stack(
+                out_blocks(
+                    wanted, sign, attended[chunk], spans[chunk].start // size, out_here, blocks,
+                    (jnp.float32,), before,
+                )
+            ).reshape(-1, tokens, out_width)
+        return out_blocks(wanted, sign, attended[-1], place, out_here, blocks, dtypes, before)
+
+    far_attended = lax.ppermute(attended[-1], ("role", "head"), far_swap)
+    over_head, over_role = contributions(which[1:3], (jnp.bfloat16, jnp.bfloat16))
+    received.append(lax.ppermute(over_head, "head", swap))
+    received.append(lax.ppermute(over_role, "role", swap))
+    (far,) = out_blocks(
+        jnp.zeros_like(which[:1]), -sign, far_attended, 0, far_weight.reshape(-1, out_width), 1,
+        (jnp.float32,), received[0][None],
+    )
+    (own,) = contributions(which[3:], (jnp.float32,), far[None])
+    total = received[1].astype(jnp.float32)
+    for one in received[2:]:
+        total = total + one.astype(jnp.float32)
+    return own + total
 
 
 def splits_heads(mesh, qkv_weight, hidden_rows):
@@ -634,6 +664,7 @@
     tokens = hidden_rows.shape[0] // seq
     return (
         heads % chips == 0
+        and heads // chips > 1
         and chips == role * head
         and width % (role * head * 256) == 0
         and width % (seq * 16) == 0

time: 365 us -> 364 us (level)
  waiting for transfers between devices: 166 us -> 150 us
  local copies, waits for them, and re-layouts: 17.3 us -> 23.7 us
  starting transfers between devices: 52.5 us -> 58.1 us
    ppermute x4, waiting for transfers between devices: 78.5 us -> 67.8 us  [per_device_by_heads(): sent['first'] = lax.ppermute(straight[2][:half], 'role', swap)]
    pallas_call x3 -> x6, Pallas kernels: 22.7 us -> 29.1 us  [out_blocks(): pl.pallas_call(body, grid_spec=pltpu.PrefetchScalarGridSpec(num_scalar_pr...]
    ppermute x3 -> x6, starting transfers between devices: 3.49 us -> 8.54 us  [the longest x1 2.5 us: per_device_by_heads(): received.append(lax.ppermute(diagonal, ('role', 'head'), far_swap))]
    ppermute x4, waiting for transfers between devices: 7.51 us -> 2.78 us  [project(): kv_other = lax.ppermute(kv, 'core', swap)]
    dynamic_slice x0 -> x1, local copies, waits for them, and re-layouts: none -> 3.74 us  [per_device_by_heads(): lax.dynamic_slice(out_here.reshape(chips, heads * HEAD_DIM, -1), (0, span...]
    unnamed x48 -> x54, local copies, waits for them, and re-layouts: 4.66 us -> 7.36 us
    ppermute x3 -> x6, waiting for transfers between devices: 32.9 us -> 31.9 us  [the longest x1 27.4 us: per_device_by_heads(): far_attended = lax.ppermute(attended[-1], ('role', 'head'), far_swap)]
  transfers between devices with their start and end apart: 36 -> 38, of which waited for: 18 -> 16; matrix products, arithmetic and copies ran while one was open for 8% -> 9% of each run, Pallas kernels for 27% -> 27%
where the time goes in v11:
time: 364 us; the launch traced here: 362 us
  waiting for transfers between devices  150 us (41%)
  Pallas kernels  108 us (30%)
  starting transfers between devices  58.1 us (16%)
  local copies, waits for them, and re-layouts  23.7 us (7%)
  matrix products  12.7 us (3%)
  other arithmetic  9.02 us (2%)
    ppermute x4, waiting for transfers between devices, per_device_by_heads(): sent['first'] = lax.ppermute(straight[2][:half], 'role', swap)  67.8 us
    pallas_call x4, Pallas kernels, project_heads(): pl.pallas_call(body, in_specs=[in_smem(), in_smem()] + [in_hbm()] * (2 *...  51.5 us
    pallas_call x6, Pallas kernels, out_blocks(): pl.pallas_call(body, grid_spec=pltpu.PrefetchScalarGridSpec(num_scalar_pr...  29.1 us
    ppermute x1, waiting for transfers between devices, per_device_by_heads(): far_attended = lax.ppermute(attended[-1], ('role', 'head'), far_swap)  27.4 us
    all_to_all x5, starting transfers between devices, exchange(): lax.all_to_all(array, 'chip', split_axis=0, concat_axis=0, tiled=True)  24.2 us
    all_to_all x5, waiting for transfers between devices, exchange(): lax.all_to_all(array, 'chip', split_axis=0, concat_axis=0, tiled=True)  20.1 us
    pallas_call x2, Pallas kernels, attend(): pl.pallas_call(body, in_specs=[in_smem()] * 4 + [in_hbm()] * len(arrays),...  16.5 us
    ppermute x3, waiting for transfers between devices, per_device_by_heads(): sent['next'] = lax.ppermute(shard, 'chip', ring)  14 us
  transfers between devices with their start and end apart: 38, of which 16 were waited for; matrix products, arithmetic and copies ran while one was open for 9% of the time, Pallas kernels for 27%

profile of v11, /device:TPU:0, one launch (start us, length us, event | category | flops | bytes accessed | tf_op | source)
XLA Modules:
  0.0 362.1 jit_solution(10618367791125353188)
XLA Ops:
  6.2 6.4 %all-to-all-start = ((bf16[4,656,384]{2,1,0:T(8,128)(2,1)}), bf16[4,656,384]{2,1,0:T(8,128)(2,1)S(1)}, u32[]{:S(2)}, u32[]{:S(2)}) async-start(bf16[4,656,384]{2,1,0:T(8,128)(2,1)} %cut_columns.5), calls=%async_computation | async-start | bytes 4030464 | tf_op jit(solution)/shard_map/all_to_all | solution.py:456
  13.0 12.7 %multiply_reduce_fusion = (f32[384]{0:T(512)S(1)}, f32[384,1280]{1,0:T(8,128)}) fusion(bf16[384,5120]{1,0:T(8,128)(2,1)} %param.11, s32[]{:T(128)S(6)} %select_n.47, f32[384]{0:T(512)S(1)} %mul.85, bf16[384,5120]{1,0:T(8,128)(2,1)} %param.9, bf16[5120,1280]{1,0:T(8,128)(2,1)} %param.10, f32[384]{0:T(512)S(1)} %mul.81), kind=kOutput, calls=%fused_computation.5 | convolution fusion | flops 5036604928 | bytes 19993092 | tf_op jit(solution)/shard_map/dot_general | solution.py:474
  47.4 9.1 %collective-permute-done.2.refs_4_ = bf16[384,1280]{1,0:T(8,128)(2,1)} collective-permute-done((bf16[384,1280]{1,0:T(8,128)(2,1)S(1)}, bf16[384,1280]{1,0:T(8,128)(2,1)}, u32[]{:S(2)}, u32[]{:S(2)}) %collective-permute-start.2) | collective-permute-done | bytes 983072 | tf_op jit(solution)/shard_map/ppermute | solution.py:543
  56.5 14.0 %collective-permute-done.3.refs_7_ = bf16[384,1280]{1,0:T(8,128)(2,1)} collective-permute-done((bf16[384,1280]{1,0:T(8,128)(2,1)S(1)}, bf16[384,1280]{1,0:T(8,128)(2,1)}, u32[]{:S(2)}, u32[]{:S(2)}) %collective-permute-start.3) | collective-permute-done | bytes 983072 | tf_op jit(solution)/shard_map/ppermute | solution.py:548
  70.5 9.6 %all-to-all-done.refs_0_ = bf16[4,656,384]{2,1,0:T(8,128)(2,1)S(1)} async-done(((bf16[4,656,384]{2,1,0:T(8,128)(2,1)}), bf16[4,656,384]{2,1,0:T(8,128)(2,1)S(1)}, u32[]{:S(2)}, u32[]{:S(2)}) %all-to-all-start) | async-done | bytes 2015264 | tf_op jit(solution)/shard_map/all_to_all | solution.py:456
  88.5 26.3 %collective-permute-done.5.refs_5_ = bf16[192,1280]{1,0:T(8,128)(2,1)S(1)} collective-permute-done((bf16[192,1280]{1,0:T(8,128)(2,1)}, bf16[192,1280]{1,0:T(8,128)(2,1)S(1)}, u32[]{:S(2)}, u32[]{:S(2)}) %collective-permute-start.5) | collective-permute-done | bytes 491552 | tf_op jit(solution)/shard_map/ppermute | solution.py:545
  120.9 26.8 %collective-permute-done.10.refs_10_ = bf16[192,1280]{1,0:T(8,128)(2,1)} collective-permute-done((bf16[192,1280]{1,0:T(8,128)(2,1)S(1)}, bf16[192,1280]{1,0:T(8,128)(2,1)}, u32[]{:S(2)}, u32[]{:S(2)}) %collective-permute-start.10) | collective-permute-done | bytes 491552 | tf_op jit(solution)/shard_map/ppermute | solution.py:545
  147.7 4.8 %all-to-all-start.1 = ((bf16[4,640,384]{2,1,0:T(8,128)(2,1)}), bf16[4,640,384]{2,1,0:T(8,128)(2,1)}, u32[]{:S(2)}, u32[]{:S(2)}) async-start(bf16[4,640,384]{2,1,0:T(8,128)(2,1)} %cut_columns.3), calls=%async_computation.1 | async-start | bytes 3932160 | tf_op jit(solution)/shard_map/all_to_all | solution.py:456
  164.2 10.4 %project_heads.4 = (bf16[1,2,384,128]{3,2,1,0:T(8,128)(2,1)}, bf16[1,2,2,384,128]{4,3,2,1,0:T(8,128)(2,1)}) custom-call(s32[5]{0:T(128)} %concatenate.8.places_ref, f32[2,1]{1,0:T(2,128)} %get-tuple-element.141.gains_ref, bf16[4,656,384]{2,1,0:T(8,128)(2,1)} %copy-done.2, bf16[4,656,384]{2,1,0:T(8,128)(2,1)} %collective-permute-done.17.refs_1_.refs_2_, ...), custom_call_target="tpu_custom_call" | custom-call | tf_op jit(solution)/shard_map/project_heads/pallas_call | solution.py:257
  174.5 14.7 %collective-permute-done.15.refs_7_.refs_15_ = bf16[192,1280]{1,0:T(8,128)(2,1)S(1)} collective-permute-done((bf16[192,1280]{1,0:T(8,128)(2,1)}, bf16[192,1280]{1,0:T(8,128)(2,1)S(1)}, u32[]{:S(2)}, u32[]{:S(2)}) %collective-permute-start.15) | collective-permute-done | bytes 491552 | tf_op jit(solution)/shard_map/ppermute | solution.py:545
  189.3 5.7 %all-to-all-done.1.refs_0_.refs_1_ = bf16[4,640,384]{2,1,0:T(8,128)(2,1)} async-done(((bf16[4,640,384]{2,1,0:T(8,128)(2,1)}), bf16[4,640,384]{2,1,0:T(8,128)(2,1)}, u32[]{:S(2)}, u32[]{:S(2)}) %all-to-all-start.1) | async-done | bytes 1966112 | tf_op jit(solution)/shard_map/all_to_all | solution.py:456
  204.4 10.3 %project_heads.5 = (bf16[1,2,384,128]{3,2,1,0:T(8,128)(2,1)}, bf16[1,2,2,384,128]{4,3,2,1,0:T(8,128)(2,1)}) custom-call(s32[5]{0:T(128)} %concatenate.8.places_ref, f32[2,1]{1,0:T(2,128)} %get-tuple-element.140.gains_ref, bf16[4,640,384]{2,1,0:T(8,128)(2,1)} %all-to-all-done.1.refs_0_.refs_1_, bf16[4,640,384]{2,1,0:T(8,128)(2,1)} %copy-done.6, ...), custom_call_target="tpu_custom_call" | custom-call | tf_op jit(solution)/shard_map/project_heads/pallas_call | solution.py:257
  215.8 13.9 %project_heads.6 = (bf16[2,2,384,128]{3,2,1,0:T(8,128)(2,1)}, bf16[2,2,2,384,128]{4,3,2,1,0:T(8,128)(2,1)}) custom-call(s32[5]{0:T(128)} %concatenate.8.places_ref, f32[2,2]{1,0:T(2,128)} %bitcast.71, bf16[4,656,384]{2,1,0:T(8,128)(2,1)} %copy-done.2, bf16[4,640,384]{2,1,0:T(8,128)(2,1)} %all-to-all-done.1.refs_0_.refs_1_, ...), custom_call_target="tpu_custom_call" | custom-call | tf_op jit(solution)/shard_map/project_heads/pallas_call | solution.py:257
  234.1 10.1 %attend.2 = bf16[4,2,6,64,128]{4,3,2,1,0:T(8,128)(2,1)} custom-call(s32[3,24,8]{2,1,0:T(8,128)} %fusion.7.slots_ref, s32[3,24]{1,0:T(4,128)} %get-tuple-element.124.counts_ref, s32[24]{0:T(128)} %fusion.11.from_ref, s32[3,4]{1,0:T(4,128)} %reduce_max.9.most_ref, bf16[1,12,64,128]{3,2,1,0:T(8,128)(2,1)} %bitcast.66, bf16[1,2,12,64,128]{4,3,2,1,0:T(8,128)(2,1)} %bitcast.59, ...), custom_call_target="tpu_custom_call" | custom-call | tf_op jit(solution)/shard_map/attend/pallas_call | solution.py:352
  250.6 4.8 %all-to-all-start.2 = ((bf16[4,2,384,128]{3,2,1,0:T(8,128)(2,1)}), bf16[4,2,384,128]{3,2,1,0:T(8,128)(2,1)S(1)}, u32[]{:S(2)}, u32[]{:S(2)}) async-start(bf16[4,2,384,128]{3,2,1,0:T(8,128)(2,1)} %bitcast.17), calls=%async_computation.2 | async-start | bytes 1572864 | tf_op jit(solution)/shard_map/all_to_all | solution.py:456
  255.4 17.0 %project_heads.7 = (bf16[1,4,384,128]{3,2,1,0:T(8,128)(2,1)}, bf16[1,2,4,384,128]{4,3,2,1,0:T(8,128)(2,1)}) custom-call(s32[5]{0:T(128)} %concatenate.8.places_ref, f32[2,1]{1,0:T(2,128)} %get-tuple-element.139.gains_ref, bf16[4,640,384]{2,1,0:T(8,128)(2,1)} %copy-done.7, bf16[4,640,384]{2,1,0:T(8,128)(2,1)} %collective-permute-done.27.refs_1_, ...), custom_call_target="tpu_custom_call" | custom-call | tf_op jit(solution)/shard_map/project_heads/pallas_call | solution.py:257
  276.5 4.1 %out_blocks.6 = bf16[384,1280]{1,0:T(8,128)(2,1)} custom-call(s32[1]{0:T(128)} %bitcast.7.which_ref, s32[1]{0:T(128)} %bitcast.1.sign_ref, bf16[4,2,384,128]{3,2,1,0:T(8,128)(2,1)} %copy-done.4, bf16[4,384,5120]{2,1,0:T(8,128)(2,1)} %bitcast.43), custom_call_target="tpu_custom_call" | custom-call | tf_op jit(solution)/shard_map/out_blocks/pallas_call | solution.py:412
  281.5 6.4 %attend.3 = bf16[4,1,6,64,128]{4,3,2,1,0:T(8,128)(2,1)} custom-call(s32[3,24,8]{2,1,0:T(8,128)} %fusion.7.slots_ref, s32[3,24]{1,0:T(4,128)} %get-tuple-element.124.counts_ref, s32[24]{0:T(128)} %fusion.11.from_ref, s32[3,4]{1,0:T(4,128)} %reduce_max.9.most_ref, bf16[1,24,64,128]{3,2,1,0:T(8,128)(2,1)} %bitcast.64, bf16[1,2,24,64,128]{4,3,2,1,0:T(8,128)(2,1)} %bitcast.58, ...), custom_call_target="tpu_custom_call" | custom-call | tf_op jit(solution)/shard_map/attend/pallas_call | solution.py:352
  288.0 4.3 %all-to-all-start.4 = ((bf16[4,1,384,128]{3,2,1,0:T(8,128)(2,1)}), bf16[4,1,384,128]{3,2,1,0:T(8,128)(2,1)S(1)}, u32[]{:S(2)}, u32[]{:S(2)}) async-start(bf16[4,1,384,128]{3,2,1,0:T(8,128)(2,1)} %bitcast.53), calls=%async_computation.4 | async-start | bytes 786432 | tf_op jit(solution)/shard_map/all_to_all | solution.py:456
  295.4 6.3 %out_blocks.10.refs_0_ = f32[2,384,1280]{2,1,0:T(8,128)} custom-call(s32[2]{0:T(128)} %pad_add_fusion.which_ref, s32[1]{0:T(128)} %bitcast.1.sign_ref, bf16[4,2,384,128]{3,2,1,0:T(8,128)(2,1)} %copy-done.4, bf16[4,384,5120]{2,1,0:T(8,128)(2,1)} %bitcast.44), custom_call_target="tpu_custom_call" | custom-call | tf_op jit(solution)/shard_map/out_blocks/pallas_call | solution.py:412
  304.2 5.8 %out_blocks.11 = (bf16[384,1280]{1,0:T(8,128)(2,1)}, bf16[384,1280]{1,0:T(8,128)(2,1)}) custom-call(s32[2]{0:T(128)} %pad_add_fusion.which_ref, s32[1]{0:T(128)} %bitcast.1.sign_ref, bf16[4,1,384,128]{3,2,1,0:T(8,128)(2,1)} %copy-done.10, bf16[4,384,5120]{2,1,0:T(8,128)(2,1)} %bitcast.45, f32[2,384,1280]{2,1,0:T(8,128)} %out_blocks.10.refs_0_), custom_call_target="tpu_custom_call" | custom-call | tf_op jit(solution)/shard_map/out_blocks/pallas_call | solution.py:412
  313.5 4.4 %collective-permute-done.30 = bf16[384,1280]{1,0:T(8,128)(2,1)S(1)} collective-permute-done((bf16[384,1280]{1,0:T(8,128)(2,1)S(1)}, bf16[384,1280]{1,0:T(8,128)(2,1)S(1)}, u32[]{:S(2)}, u32[]{:S(2)}) %collective-permute-start.30) | collective-permute-done | bytes 983072 | tf_op jit(solution)/shard_map/ppermute | solution.py:611
  318.0 27.4 %collective-permute-done.29.mixed_ref = bf16[4,1,384,128]{3,2,1,0:T(8,128)(2,1)S(1)} collective-permute-done((bf16[4,1,384,128]{3,2,1,0:T(8,128)(2,1)}, bf16[4,1,384,128]{3,2,1,0:T(8,128)(2,1)S(1)}, u32[]{:S(2)}, u32[]{:S(2)}) %collective-permute-start.29) | collective-permute-done | bytes 393248 | tf_op jit(solution)/shard_map/ppermute | solution.py:642
  349.8 5.1 %out_blocks.8 = f32[384,1280]{1,0:T(8,128)} custom-call(s32[1]{0:T(128)} %bitcast.which_ref, s32[1]{0:T(128)} %bitcast.1.sign_ref, bf16[4,2,384,128]{3,2,1,0:T(8,128)(2,1)} %copy-done.4, bf16[4,384,5120]{2,1,0:T(8,128)(2,1)} %bitcast.46, f32[1,384,1280]{2,1,0:T(8,128)} %bitcast.51), custom_call_target="tpu_custom_call" | custom-call | tf_op jit(solution)/shard_map/out_blocks/pallas_call | solution.py:412
  (163 shorter events, 101.1 us)
Async XLA Ops:
  6.2 74.0 %all-to-all-start = ((bf16[4,656,384]{2,1,0:T(8,128)(2,1)}), bf16[4,656,384]{2,1,0:T(8,128)(2,1)S(1)}, u32[]{:S(2)}, u32[]{:S(2)}) async-start(bf16[4,656,384]{2,1,0:T(8,128)(2,1)} %cut_columns.5), calls=%async_computation | async-start | bytes 4030464 | tf_op jit(solution)/shard_map/all_to_all | solution.py:456
  36.5 33.9 %collective-permute-start.3 = (bf16[384,1280]{1,0:T(8,128)(2,1)S(1)}, bf16[384,1280]{1,0:T(8,128)(2,1)}, u32[]{:S(2)}, u32[]{:S(2)}) collective-permute-start(bf16[384,1280]{1,0:T(8,128)(2,1)S(1)} %multiply_convert_fusion.refs_2_), channel_id=1, source_target_pairs={{0,4},{4,8},{8,12},{12,0},{1,5},{5,9},{9,13},{13,1},{2,6},{6,10},{... | collective-permute-start | bytes 2949128 | tf_op jit(solution)/shard_map/ppermute | solution.py:548
  38.5 31.9 %collective-permute-start.4 = (bf16[384,1280]{1,0:T(8,128)(2,1)S(1)}, bf16[384,1280]{1,0:T(8,128)(2,1)}, u32[]{:S(2)}, u32[]{:S(2)}) collective-permute-start(bf16[384,1280]{1,0:T(8,128)(2,1)S(1)} %multiply_convert_fusion.refs_2_), channel_id=1, source_target_pairs={{0,16},{16,0},{1,17},{17,1},{2,18},{18,2},{3,19},{19,3},{4,20},{20... | collective-permute-start | bytes 2949128 | tf_op jit(solution)/shard_map/ppermute | solution.py:542
  80.1 34.7 %collective-permute-start.6 = (bf16[384,1280]{1,0:T(8,128)(2,1)}, bf16[384,1280]{1,0:T(8,128)(2,1)S(1)}, u32[]{:S(2)}, u32[]{:S(2)}) collective-permute-start(bf16[384,1280]{1,0:T(8,128)(2,1)} %collective-permute-done.3.refs_7_), channel_id=1, source_target_pairs={{0,1},{1,0},{2,3},{3,2},{4,5},{5,4},{6,7},{7,6},{8,9},{9,8},{10,11... | collective-permute-start | bytes 2949128 | tf_op jit(solution)/shard_map/ppermute | solution.py:543
  81.6 33.2 %collective-permute-start.7 = (bf16[384,1280]{1,0:T(8,128)(2,1)}, bf16[384,1280]{1,0:T(8,128)(2,1)}, u32[]{:S(2)}, u32[]{:S(2)}) collective-permute-start(bf16[384,1280]{1,0:T(8,128)(2,1)} %collective-permute-done.3.refs_7_), channel_id=1, source_target_pairs={{0,4},{4,8},{8,12},{12,0},{1,5},{5,9},{9,13},{13,1},{2,6},{6,10},{... | collective-permute-start | bytes 2949128 | tf_op jit(solution)/shard_map/ppermute | solution.py:548
  81.6 33.2 %collective-permute-start.8 = (bf16[384,1280]{1,0:T(8,128)(2,1)}, bf16[384,1280]{1,0:T(8,128)(2,1)}, u32[]{:S(2)}, u32[]{:S(2)}) collective-permute-start(bf16[384,1280]{1,0:T(8,128)(2,1)} %collective-permute-done.3.refs_7_), channel_id=1, source_target_pairs={{0,16},{16,0},{1,17},{17,1},{2,18},{18,2},{3,19},{19,3},{4,20},{20... | collective-permute-start | bytes 2949128 | tf_op jit(solution)/shard_map/ppermute | solution.py:542
  85.0 29.9 %collective-permute-start.5 = (bf16[192,1280]{1,0:T(8,128)(2,1)}, bf16[192,1280]{1,0:T(8,128)(2,1)S(1)}, u32[]{:S(2)}, u32[]{:S(2)}) collective-permute-start(bf16[192,1280]{1,0:T(8,128)(2,1)} %slice.49), channel_id=1, source_target_pairs={{0,16},{16,0},{1,17},{17,1},{2,18},{18,2},{3,19},{19,3},{4,20},{20... | collective-permute-start | bytes 1474568 | tf_op jit(solution)/shard_map/ppermute | solution.py:545
  87.3 27.5 %collective-permute-start.9 = (bf16[192,1280]{1,0:T(8,128)(2,1)}, bf16[192,1280]{1,0:T(8,128)(2,1)}, u32[]{:S(2)}, u32[]{:S(2)}) collective-permute-start(bf16[192,1280]{1,0:T(8,128)(2,1)} %slice.50), channel_id=1, source_target_pairs={{0,1},{1,0},{2,3},{3,2},{4,5},{5,4},{6,7},{7,6},{8,9},{9,8},{10,11... | collective-permute-start | bytes 1474568 | tf_op jit(solution)/shard_map/ppermute | solution.py:546
  114.9 32.8 %collective-permute-start.11 = (bf16[384,1280]{1,0:T(8,128)(2,1)}, bf16[384,1280]{1,0:T(8,128)(2,1)}, u32[]{:S(2)}, u32[]{:S(2)}) collective-permute-start(bf16[384,1280]{1,0:T(8,128)(2,1)} %collective-permute-done.7.refs_4_.refs_12_), channel_id=1, source_target_pairs={{0,1},{1,0},{2,3},{3,2},{4,5},{5,4},{6,7},{7,6},{8,9},{9,8},{10,11... | collective-permute-start | bytes 2949128 | tf_op jit(solution)/shard_map/ppermute | solution.py:543
  115.4 32.2 %collective-permute-start.12 = (bf16[384,1280]{1,0:T(8,128)(2,1)}, bf16[384,1280]{1,0:T(8,128)(2,1)}, u32[]{:S(2)}, u32[]{:S(2)}) collective-permute-start(bf16[384,1280]{1,0:T(8,128)(2,1)} %collective-permute-done.7.refs_4_.refs_12_), channel_id=1, source_target_pairs={{0,4},{4,8},{8,12},{12,0},{1,5},{5,9},{9,13},{13,1},{2,6},{6,10},{... | collective-permute-start | bytes 2949128 | tf_op jit(solution)/shard_map/ppermute | solution.py:548
  116.1 31.6 %collective-permute-start.13 = (bf16[384,1280]{1,0:T(8,128)(2,1)}, bf16[384,1280]{1,0:T(8,128)(2,1)}, u32[]{:S(2)}, u32[]{:S(2)}) collective-permute-start(bf16[384,1280]{1,0:T(8,128)(2,1)} %collective-permute-done.7.refs_4_.refs_12_), channel_id=1, source_target_pairs={{0,16},{16,0},{1,17},{17,1},{2,18},{18,2},{3,19},{19,3},{4,20},{20... | collective-permute-start | bytes 2949128 | tf_op jit(solution)/shard_map/ppermute | solution.py:542
  117.6 30.0 %collective-permute-start.10 = (bf16[192,1280]{1,0:T(8,128)(2,1)S(1)}, bf16[192,1280]{1,0:T(8,128)(2,1)}, u32[]{:S(2)}, u32[]{:S(2)}) collective-permute-start(bf16[192,1280]{1,0:T(8,128)(2,1)S(1)} %slice.55), channel_id=1, source_target_pairs={{0,16},{16,0},{1,17},{17,1},{2,18},{18,2},{3,19},{19,3},{4,20},{20... | collective-permute-start | bytes 1474568 | tf_op jit(solution)/shard_map/ppermute | solution.py:545
  119.3 28.4 %collective-permute-start.14 = (bf16[192,1280]{1,0:T(8,128)(2,1)S(1)}, bf16[192,1280]{1,0:T(8,128)(2,1)}, u32[]{:S(2)}, u32[]{:S(2)}) collective-permute-start(bf16[192,1280]{1,0:T(8,128)(2,1)S(1)} %slice.56), channel_id=1, source_target_pairs={{0,1},{1,0},{2,3},{3,2},{4,5},{5,4},{6,7},{7,6},{8,9},{9,8},{10,11... | collective-permute-start | bytes 1474568 | tf_op jit(solution)/shard_map/ppermute | solution.py:546
  147.7 47.3 %all-to-all-start.1 = ((bf16[4,640,384]{2,1,0:T(8,128)(2,1)}), bf16[4,640,384]{2,1,0:T(8,128)(2,1)}, u32[]{:S(2)}, u32[]{:S(2)}) async-start(bf16[4,640,384]{2,1,0:T(8,128)(2,1)} %cut_columns.3), calls=%async_computation.1 | async-start | bytes 3932160 | tf_op jit(solution)/shard_map/all_to_all | solution.py:456
  153.1 36.1 %collective-permute-start.16 = (bf16[384,1280]{1,0:T(8,128)(2,1)}, bf16[384,1280]{1,0:T(8,128)(2,1)S(1)}, u32[]{:S(2)}, u32[]{:S(2)}) collective-permute-start(bf16[384,1280]{1,0:T(8,128)(2,1)} %collective-permute-done.12.refs_9_.refs_17_), channel_id=1, source_target_pairs={{0,1},{1,0},{2,3},{3,2},{4,5},{5,4},{6,7},{7,6},{8,9},{9,8},{10,11... | collective-permute-start | bytes 2949128 | tf_op jit(solution)/shard_map/ppermute | solution.py:543
  154.6 34.7 %collective-permute-start.18 = (bf16[384,1280]{1,0:T(8,128)(2,1)}, bf16[384,1280]{1,0:T(8,128)(2,1)}, u32[]{:S(2)}, u32[]{:S(2)}) collective-permute-start(bf16[384,1280]{1,0:T(8,128)(2,1)} %collective-permute-done.12.refs_9_.refs_17_), channel_id=1, source_target_pairs={{0,16},{16,0},{1,17},{17,1},{2,18},{18,2},{3,19},{19,3},{4,20},{20... | collective-permute-start | bytes 2949128 | tf_op jit(solution)/shard_map/ppermute | solution.py:542
  160.2 29.0 %collective-permute-start.15 = (bf16[192,1280]{1,0:T(8,128)(2,1)}, bf16[192,1280]{1,0:T(8,128)(2,1)S(1)}, u32[]{:S(2)}, u32[]{:S(2)}) collective-permute-start(bf16[192,1280]{1,0:T(8,128)(2,1)} %slice.57), channel_id=1, source_target_pairs={{0,16},{16,0},{1,17},{17,1},{2,18},{18,2},{3,19},{19,3},{4,20},{20... | collective-permute-start | bytes 1474568 | tf_op jit(solution)/shard_map/ppermute | solution.py:545
  160.8 28.5 %collective-permute-start.19 = (bf16[192,1280]{1,0:T(8,128)(2,1)}, bf16[192,1280]{1,0:T(8,128)(2,1)}, u32[]{:S(2)}, u32[]{:S(2)}) collective-permute-start(bf16[192,1280]{1,0:T(8,128)(2,1)} %slice.59), channel_id=1, source_target_pairs={{0,1},{1,0},{2,3},{3,2},{4,5},{5,4},{6,7},{7,6},{8,9},{9,8},{10,11... | collective-permute-start | bytes 1474568 | tf_op jit(solution)/shard_map/ppermute | solution.py:546
  195.0 49.2 %all-to-all-start.3 = ((bf16[4,640,384]{2,1,0:T(8,128)(2,1)}), bf16[4,640,384]{2,1,0:T(8,128)(2,1)S(1)}, u32[]{:S(2)}, u32[]{:S(2)}) async-start(bf16[4,640,384]{2,1,0:T(8,128)(2,1)} %cut_columns.4), calls=%async_computation.3 | async-start | bytes 3932160 | tf_op jit(solution)/shard_map/all_to_all | solution.py:456
  248.2 32.5 %collective-permute-start.26 = (bf16[4,128,1280]{2,1,0:T(8,128)(2,1)}, bf16[4,128,1280]{2,1,0:T(8,128)(2,1)}, u32[]{:S(2)}, u32[]{:S(2)}) collective-permute-start(bf16[4,128,1280]{2,1,0:T(8,128)(2,1)} %constant_dynamic-slice_fusion), channel_id=1, source_target_pairs={{0,17},{1,16},{16,1},{17,0},{2,19},{3,18},{18,3},{19,2},{4,21},{5,... | collective-permute-start | bytes 3932168 | tf_op jit(solution)/shard_map/ppermute | solution.py:626
  292.3 25.6 %collective-permute-start.30 = (bf16[384,1280]{1,0:T(8,128)(2,1)S(1)}, bf16[384,1280]{1,0:T(8,128)(2,1)S(1)}, u32[]{:S(2)}, u32[]{:S(2)}) collective-permute-start(bf16[384,1280]{1,0:T(8,128)(2,1)S(1)} %copy-done.15), channel_id=1, source_target_pairs={{0,17},{1,16},{16,1},{17,0},{2,19},{3,18},{18,3},{19,2},{4,21},{5,... | collective-permute-start | bytes 2949128 | tf_op jit(solution)/shard_map/ppermute | solution.py:611
  310.0 48.9 %collective-permute-start.31 = (bf16[384,1280]{1,0:T(8,128)(2,1)}, bf16[384,1280]{1,0:T(8,128)(2,1)S(1)}, u32[]{:S(2)}, u32[]{:S(2)}) collective-permute-start(bf16[384,1280]{1,0:T(8,128)(2,1)} %get-tuple-element.135), channel_id=1, source_target_pairs={{0,1},{1,0},{2,3},{3,2},{4,5},{5,4},{6,7},{7,6},{8,9},{9,8},{10,11... | collective-permute-start | bytes 2949128 | tf_op jit(solution)/shard_map/ppermute | solution.py:644
  311.6 47.3 %collective-permute-start.32 = (bf16[384,1280]{1,0:T(8,128)(2,1)}, bf16[384,1280]{1,0:T(8,128)(2,1)S(1)}, u32[]{:S(2)}, u32[]{:S(2)}) collective-permute-start(bf16[384,1280]{1,0:T(8,128)(2,1)} %get-tuple-element.136), channel_id=1, source_target_pairs={{0,16},{16,0},{1,17},{17,1},{2,18},{18,2},{3,19},{19,3},{4,20},{20... | collective-permute-start | bytes 2949128 | tf_op jit(solution)/shard_map/ppermute | solution.py:645
  313.1 32.3 %collective-permute-start.29 = (bf16[4,1,384,128]{3,2,1,0:T(8,128)(2,1)}, bf16[4,1,384,128]{3,2,1,0:T(8,128)(2,1)S(1)}, u32[]{:S(2)}, u32[]{:S(2)}) collective-permute-start(bf16[4,1,384,128]{3,2,1,0:T(8,128)(2,1)} %copy-done.10), channel_id=1, source_target_pairs={{0,17},{1,16},{16,1},{17,0},{2,19},{3,18},{18,3},{19,2},{4,21},{5,... | collective-permute-start | bytes 1179656 | tf_op jit(solution)/shard_map/ppermute | solution.py:642
  (39 other events, 567.7 us)

commit v12 on v11

--- a/solution.py
+++ b/solution.py
@@ -530,6 +530,13 @@
         parts[chunk].append((first, size, begin * local_blocks, here, query, kv, kv_other))
         return lax.optimization_barrier((places, kv))[0]
 
+    sign = (2 * role - 1).astype(jnp.int32)[None]
+    blocks = sides * lax.axis_size("role")
+    which = jnp.stack([peers[3], peers[2], peers[1], peers[0]])
+    out_here = out_weight[0]
+    out_width = out_here.shape[1] // blocks
+    place = spans[-1].start // chunks[-1]
+
     half = tokens // 2
     rounds = []
     straight = None
@@ -552,6 +559,11 @@
         if phase == 1:
             sent["places"] = places
             sent["gains"] = gains
+            sent["corner"] = lax.dynamic_slice(
+                out_here.reshape(chips, heads * HEAD_DIM, -1),
+                (0, spans[-1].start * HEAD_DIM, which[0] * out_width),
+                (chips, chunks[-1] * HEAD_DIM, out_width),
+            )
         if step == chips:
             weights_other.append(lax.ppermute(weights_own[0], "core", swap))
             early = list(rounds)
@@ -566,7 +578,7 @@
             weights_own.append(sent["weights"])
             cuts[1:] = sent["cuts"]
         if phase == 1:
-            gains = sent["gains"]
+            gains, corner = sent["gains"], sent["corner"]
         if straight is not None:
             rounds.append(straight + (sent["first"], sent["second"]))
         held_places = sent.get("places", held_places)
@@ -582,13 +594,8 @@
     for at in range(len(weights_other), heads - 1):
         weights_other.append(lax.ppermute(weights_own[at], "core", swap))
 
-    sign = (2 * role - 1).astype(jnp.int32)[None]
-    blocks = sides * lax.axis_size("role")
-    which = jnp.stack([peers[3], peers[2], peers[1], peers[0]])
-    out_here = out_weight[0]
-    out_width = out_here.shape[1] // blocks
-    place = spans[-1].start // chunks[-1]
-
+    corner, held_places = lax.optimization_barrier((corner, held_places))
+    far_weight = lax.ppermute(corner, ("role", "head"), far_swap)
     attended = []
     received = []
     for chunk, size in enumerate(chunks):
@@ -617,13 +624,6 @@
                     (weights_own[at], held_places)
                 )
                 weights_other.append(lax.ppermute(weights_own[at], "core", swap))
-            corner, held_places = lax.optimization_barrier((which[0] * out_width, held_places))
-            far_weight = lax.dynamic_slice(
-                out_here.reshape(chips, heads * HEAD_DIM, -1),
-                (0, spans[-1].start * HEAD_DIM, corner),
-                (chips, chunks[-1] * HEAD_DIM, out_width),
-            )
-            far_weight = lax.ppermute(far_weight, ("role", "head"), far_swap)
         mixed = mixed.reshape(chips, size, tokens, HEAD_DIM)
         if attended:
             mixed, attended = lax.optimization_barrier((mixed, attended))
@@ -637,10 +637,14 @@
                     (jnp.float32,), before,
                 )
             ).reshape(-1, tokens, out_width)
+        wanted, _ = lax.optimization_barrier((wanted, received[0]))
         return out_blocks(wanted, sign, attended[-1], place, out_here, blocks, dtypes, before)
 
     far_attended = lax.ppermute(attended[-1], ("role", "head"), far_swap)
     over_head, over_role = contributions(which[1:3], (jnp.bfloat16, jnp.bfloat16))
+    (over_head, over_role), far_attended = lax.optimization_barrier(
+        ((over_head, over_role), far_attended)
+    )
     received.append(lax.ppermute(over_head, "head", swap))
     received.append(lax.ppermute(over_role, "role", swap))
     (far,) = out_blocks(

time: 364 us -> 346 us (0.951)
  waiting for transfers between devices: 150 us -> 122 us
  blocking collectives: 0 us -> 15.6 us
  starting transfers between devices: 58.1 us -> 53.2 us
    ppermute x1, waiting for transfers between devices: 27.4 us -> 0.01 us  [per_device_by_heads(): far_attended = lax.ppermute(attended[-1], ('role', 'head'), far_swap)]
    all_to_all x0 -> x1, blocking collectives: none -> 15.6 us  [exchange(): lax.all_to_all(array, 'chip', split_axis=0, concat_axis=0, tiled=True)]
    ppermute x1, waiting for transfers between devices: 0.01 us -> 6.22 us  [per_device_by_heads(): received.append(lax.ppermute(over_head, 'head', swap))]
    ppermute x1, waiting for transfers between devices: 4.42 us -> 0.01 us  [per_device_by_heads(): received.append(lax.ppermute(diagonal, ('role', 'head'), far_swap))]
    all_to_all x5 -> x4, starting transfers between devices: 24.2 us -> 19.9 us  [exchange(): lax.all_to_all(array, 'chip', split_axis=0, concat_axis=0, tiled=True)]
    unnamed x54 -> x52, local copies, waits for them, and re-layouts: 7.36 us -> 5.81 us
    all_to_all x5 -> x4, waiting for transfers between devices: 20.1 us -> 18.7 us  [exchange(): lax.all_to_all(array, 'chip', split_axis=0, concat_axis=0, tiled=True)]
  transfers between devices with their start and end apart: 38 -> 37, of which waited for: 16 -> 15; matrix products, arithmetic and copies ran while one was open for 9% -> 9% of each run, Pallas kernels for 27% -> 31%
where the time goes in v12:
time: 346 us; the launch traced here: 343 us
  waiting for transfers between devices  122 us (35%)
  Pallas kernels  110 us (32%)
  starting transfers between devices  53.2 us (15%)
  local copies, waits for them, and re-layouts  21 us (6%)
  blocking collectives  15.6 us (5%)
  matrix products  12.7 us (4%)
  other arithmetic  9.01 us (3%)
    ppermute x4, waiting for transfers between devices, per_device_by_heads(): sent['first'] = lax.ppermute(straight[2][:half], 'role', swap)  65.4 us
    pallas_call x4, Pallas kernels, project_heads(): pl.pallas_call(body, in_specs=[in_smem(), in_smem()] + [in_hbm()] * (2 *...  51.7 us
    pallas_call x6, Pallas kernels, out_blocks(): pl.pallas_call(body, grid_spec=pltpu.PrefetchScalarGridSpec(num_scalar_pr...  29.1 us
    all_to_all x4, starting transfers between devices, exchange(): lax.all_to_all(array, 'chip', split_axis=0, concat_axis=0, tiled=True)  19.9 us
    all_to_all x4, waiting for transfers between devices, exchange(): lax.all_to_all(array, 'chip', split_axis=0, concat_axis=0, tiled=True)  18.7 us
    pallas_call x2, Pallas kernels, attend(): pl.pallas_call(body, in_specs=[in_smem()] * 4 + [in_hbm()] * len(arrays),...  17.9 us
    all_to_all x1, blocking collectives, exchange(): lax.all_to_all(array, 'chip', split_axis=0, concat_axis=0, tiled=True)  15.6 us
    ppermute x3, waiting for transfers between devices, per_device_by_heads(): sent['next'] = lax.ppermute(shard, 'chip', ring)  14 us
  transfers between devices with their start and end apart: 37, of which 15 were waited for; matrix products, arithmetic and copies ran while one was open for 9% of the time, Pallas kernels for 31%

profile of v12, /device:TPU:0, one launch (start us, length us, event | category | flops | bytes accessed | tf_op | source)
XLA Modules:
  0.0 343.4 jit_solution(16241543603990658093)
XLA Ops:
  6.2 6.4 %all-to-all-start = ((bf16[4,656,384]{2,1,0:T(8,128)(2,1)}), bf16[4,656,384]{2,1,0:T(8,128)(2,1)S(1)}, u32[]{:S(2)}, u32[]{:S(2)}) async-start(bf16[4,656,384]{2,1,0:T(8,128)(2,1)} %cut_columns.5), calls=%async_computation | async-start | bytes 4030464 | tf_op jit(solution)/shard_map/all_to_all | solution.py:456
  13.0 12.7 %multiply_reduce_fusion = (f32[384]{0:T(512)S(1)}, f32[384,1280]{1,0:T(8,128)}) fusion(bf16[384,5120]{1,0:T(8,128)(2,1)} %param.11, s32[]{:T(128)S(6)} %select_n.48, f32[384]{0:T(512)S(1)} %mul.87, bf16[384,5120]{1,0:T(8,128)(2,1)} %param.9, bf16[5120,1280]{1,0:T(8,128)(2,1)} %param.10, f32[384]{0:T(512)S(1)} %mul.83), kind=kOutput, calls=%fused_computation.5 | convolution fusion | flops 5036604928 | bytes 19993092 | tf_op jit(solution)/shard_map/dot_general | solution.py:474
  47.4 9.1 %collective-permute-done.2.refs_4_ = bf16[384,1280]{1,0:T(8,128)(2,1)} collective-permute-done((bf16[384,1280]{1,0:T(8,128)(2,1)S(1)}, bf16[384,1280]{1,0:T(8,128)(2,1)}, u32[]{:S(2)}, u32[]{:S(2)}) %collective-permute-start.2) | collective-permute-done | bytes 983072 | tf_op jit(solution)/shard_map/ppermute | solution.py:550
  56.5 14.0 %collective-permute-done.3.refs_7_ = bf16[384,1280]{1,0:T(8,128)(2,1)} collective-permute-done((bf16[384,1280]{1,0:T(8,128)(2,1)S(1)}, bf16[384,1280]{1,0:T(8,128)(2,1)}, u32[]{:S(2)}, u32[]{:S(2)}) %collective-permute-start.3) | collective-permute-done | bytes 983072 | tf_op jit(solution)/shard_map/ppermute | solution.py:555
  70.5 9.6 %all-to-all-done.refs_0_ = bf16[4,656,384]{2,1,0:T(8,128)(2,1)S(1)} async-done(((bf16[4,656,384]{2,1,0:T(8,128)(2,1)}), bf16[4,656,384]{2,1,0:T(8,128)(2,1)S(1)}, u32[]{:S(2)}, u32[]{:S(2)}) %all-to-all-start) | async-done | bytes 2015264 | tf_op jit(solution)/shard_map/all_to_all | solution.py:456
  91.1 23.8 %collective-permute-done.5.refs_5_ = bf16[192,1280]{1,0:T(8,128)(2,1)S(1)} collective-permute-done((bf16[192,1280]{1,0:T(8,128)(2,1)}, bf16[192,1280]{1,0:T(8,128)(2,1)S(1)}, u32[]{:S(2)}, u32[]{:S(2)}) %collective-permute-start.5) | collective-permute-done | bytes 491552 | tf_op jit(solution)/shard_map/ppermute | solution.py:552
  120.9 26.8 %collective-permute-done.10.refs_10_ = bf16[192,1280]{1,0:T(8,128)(2,1)} collective-permute-done((bf16[192,1280]{1,0:T(8,128)(2,1)S(1)}, bf16[192,1280]{1,0:T(8,128)(2,1)}, u32[]{:S(2)}, u32[]{:S(2)}) %collective-permute-start.10) | collective-permute-done | bytes 491552 | tf_op jit(solution)/shard_map/ppermute | solution.py:552
  147.7 4.8 %all-to-all-start.1 = ((bf16[4,640,384]{2,1,0:T(8,128)(2,1)}), bf16[4,640,384]{2,1,0:T(8,128)(2,1)}, u32[]{:S(2)}, u32[]{:S(2)}) async-start(bf16[4,640,384]{2,1,0:T(8,128)(2,1)} %cut_columns.3), calls=%async_computation.1 | async-start | bytes 3932160 | tf_op jit(solution)/shard_map/all_to_all | solution.py:456
  164.1 10.3 %project_heads.4 = (bf16[1,2,384,128]{3,2,1,0:T(8,128)(2,1)}, bf16[1,2,2,384,128]{4,3,2,1,0:T(8,128)(2,1)}) custom-call(s32[5]{0:T(128)} %concatenate.8.places_ref, f32[2,1]{1,0:T(2,128)} %get-tuple-element.153.gains_ref, bf16[4,656,384]{2,1,0:T(8,128)(2,1)} %copy-done.2, bf16[4,656,384]{2,1,0:T(8,128)(2,1)} %collective-permute-done.17.refs_1_.refs_2_, ...), custom_call_target="tpu_custom_call" | custom-call | tf_op jit(solution)/shard_map/project_heads/pallas_call | solution.py:257
  174.4 14.8 %collective-permute-done.15.refs_7_.refs_15_ = bf16[192,1280]{1,0:T(8,128)(2,1)S(1)} collective-permute-done((bf16[192,1280]{1,0:T(8,128)(2,1)}, bf16[192,1280]{1,0:T(8,128)(2,1)S(1)}, u32[]{:S(2)}, u32[]{:S(2)}) %collective-permute-start.15) | collective-permute-done | bytes 491552 | tf_op jit(solution)/shard_map/ppermute | solution.py:552
  189.2 5.7 %all-to-all-done.1.refs_0_.refs_1_ = bf16[4,640,384]{2,1,0:T(8,128)(2,1)} async-done(((bf16[4,640,384]{2,1,0:T(8,128)(2,1)}), bf16[4,640,384]{2,1,0:T(8,128)(2,1)}, u32[]{:S(2)}, u32[]{:S(2)}) %all-to-all-start.1) | async-done | bytes 1966112 | tf_op jit(solution)/shard_map/all_to_all | solution.py:456
  204.3 10.3 %project_heads.5 = (bf16[1,2,384,128]{3,2,1,0:T(8,128)(2,1)}, bf16[1,2,2,384,128]{4,3,2,1,0:T(8,128)(2,1)}) custom-call(s32[5]{0:T(128)} %concatenate.8.places_ref, f32[2,1]{1,0:T(2,128)} %get-tuple-element.152.gains_ref, bf16[4,640,384]{2,1,0:T(8,128)(2,1)} %all-to-all-done.1.refs_0_.refs_1_, bf16[4,640,384]{2,1,0:T(8,128)(2,1)} %copy-done.6, ...), custom_call_target="tpu_custom_call" | custom-call | tf_op jit(solution)/shard_map/project_heads/pallas_call | solution.py:257
  215.7 14.1 %project_heads.6 = (bf16[2,2,384,128]{3,2,1,0:T(8,128)(2,1)}, bf16[2,2,2,384,128]{4,3,2,1,0:T(8,128)(2,1)}) custom-call(s32[5]{0:T(128)} %concatenate.8.places_ref, f32[2,2]{1,0:T(2,128)} %bitcast.72, bf16[4,656,384]{2,1,0:T(8,128)(2,1)} %copy-done.2, bf16[4,640,384]{2,1,0:T(8,128)(2,1)} %all-to-all-done.1.refs_0_.refs_1_, ...), custom_call_target="tpu_custom_call" | custom-call | tf_op jit(solution)/shard_map/project_heads/pallas_call | solution.py:257
  234.3 11.0 %attend.2 = bf16[4,2,6,64,128]{4,3,2,1,0:T(8,128)(2,1)} custom-call(s32[3,24,8]{2,1,0:T(8,128)} %fusion.7.slots_ref, s32[3,24]{1,0:T(4,128)} %get-tuple-element.130.counts_ref, s32[24]{0:T(128)} %fusion.11.from_ref, s32[3,4]{1,0:T(4,128)} %reduce_max.9.most_ref, bf16[1,12,64,128]{3,2,1,0:T(8,128)(2,1)} %bitcast.67, bf16[1,2,12,64,128]{4,3,2,1,0:T(8,128)(2,1)} %bitcast.60, ...), custom_call_target="tpu_custom_call" | custom-call | tf_op jit(solution)/shard_map/attend/pallas_call | solution.py:352
  247.9 4.8 %all-to-all-start.2 = ((bf16[4,2,384,128]{3,2,1,0:T(8,128)(2,1)}), bf16[4,2,384,128]{3,2,1,0:T(8,128)(2,1)S(1)}, u32[]{:S(2)}, u32[]{:S(2)}) async-start(bf16[4,2,384,128]{3,2,1,0:T(8,128)(2,1)} %bitcast.53), calls=%async_computation.2 | async-start | bytes 1572864 | tf_op jit(solution)/shard_map/all_to_all | solution.py:456
  252.7 17.0 %project_heads.7 = (bf16[1,4,384,128]{3,2,1,0:T(8,128)(2,1)}, bf16[1,2,4,384,128]{4,3,2,1,0:T(8,128)(2,1)}) custom-call(s32[5]{0:T(128)} %concatenate.8.places_ref, f32[2,1]{1,0:T(2,128)} %get-tuple-element.151.gains_ref, bf16[4,640,384]{2,1,0:T(8,128)(2,1)} %copy-done.7, bf16[4,640,384]{2,1,0:T(8,128)(2,1)} %collective-permute-done.28.refs_1_, ...), custom_call_target="tpu_custom_call" | custom-call | tf_op jit(solution)/shard_map/project_heads/pallas_call | solution.py:257
  274.0 4.1 %out_blocks.6 = bf16[384,1280]{1,0:T(8,128)(2,1)} custom-call(s32[1]{0:T(128)} %bitcast.7.which_ref, s32[1]{0:T(128)} %bitcast.11.sign_ref, bf16[4,2,384,128]{3,2,1,0:T(8,128)(2,1)} %copy-done.4, bf16[4,384,5120]{2,1,0:T(8,128)(2,1)} %bitcast.43), custom_call_target="tpu_custom_call" | custom-call | tf_op jit(solution)/shard_map/out_blocks/pallas_call | solution.py:412
  281.1 6.9 %attend.3 = bf16[4,1,6,64,128]{4,3,2,1,0:T(8,128)(2,1)} custom-call(s32[3,24,8]{2,1,0:T(8,128)} %fusion.7.slots_ref, s32[3,24]{1,0:T(4,128)} %get-tuple-element.130.counts_ref, s32[24]{0:T(128)} %fusion.11.from_ref, s32[3,4]{1,0:T(4,128)} %reduce_max.9.most_ref, bf16[1,24,64,128]{3,2,1,0:T(8,128)(2,1)} %bitcast.65, bf16[1,2,24,64,128]{4,3,2,1,0:T(8,128)(2,1)} %bitcast.59, ...), custom_call_target="tpu_custom_call" | custom-call | tf_op jit(solution)/shard_map/attend/pallas_call | solution.py:352
  288.0 15.6 %all_to_all.25.mixed_ref = bf16[4,1,384,128]{3,2,1,0:T(8,128)(2,1)S(1)} all-to-all(bf16[4,1,384,128]{3,2,1,0:T(8,128)(2,1)} %bitcast.54), channel_id=1, replica_groups=mesh['role'=2,'chip'=4,'core'=2,'head'=2] {'chip'}, dimensions={0} | all-to-all | bytes 786432 | tf_op jit(solution)/shard_map/all_to_all | solution.py:456
  304.8 6.3 %out_blocks.7.refs_0_ = f32[2,384,1280]{2,1,0:T(8,128)} custom-call(s32[2]{0:T(128)} %pad_add_fusion.which_ref, s32[1]{0:T(128)} %bitcast.11.sign_ref, bf16[4,2,384,128]{3,2,1,0:T(8,128)(2,1)} %copy-done.4, bf16[4,384,5120]{2,1,0:T(8,128)(2,1)} %bitcast.44), custom_call_target="tpu_custom_call" | custom-call | tf_op jit(solution)/shard_map/out_blocks/pallas_call | solution.py:412
  311.1 5.8 %out_blocks.8 = (bf16[384,1280]{1,0:T(8,128)(2,1)}, bf16[384,1280]{1,0:T(8,128)(2,1)}) custom-call(s32[2]{0:T(128)} %pad_add_fusion.which_ref, s32[1]{0:T(128)} %bitcast.11.sign_ref, bf16[4,1,384,128]{3,2,1,0:T(8,128)(2,1)} %copy-done.10, bf16[4,384,5120]{2,1,0:T(8,128)(2,1)} %bitcast.45, f32[2,384,1280]{2,1,0:T(8,128)} %out_blocks.7.refs_0_), custom_call_target="tpu_custom_call" | custom-call | tf_op jit(solution)/shard_map/out_blocks/pallas_call | solution.py:412
  323.7 5.1 %out_blocks.10 = f32[384,1280]{1,0:T(8,128)} custom-call(s32[1]{0:T(128)} %bitcast.which_ref, s32[1]{0:T(128)} %bitcast.11.sign_ref, bf16[4,2,384,128]{3,2,1,0:T(8,128)(2,1)} %copy-done.4, bf16[4,384,5120]{2,1,0:T(8,128)(2,1)} %bitcast.46, f32[1,384,1280]{2,1,0:T(8,128)} %bitcast.51), custom_call_target="tpu_custom_call" | custom-call | tf_op jit(solution)/shard_map/out_blocks/pallas_call | solution.py:412
  328.8 4.0 %out_blocks.11 = f32[384,1280]{1,0:T(8,128)} custom-call(s32[1]{0:T(128)} %bitcast.which_ref, s32[1]{0:T(128)} %bitcast.11.sign_ref, bf16[4,1,384,128]{3,2,1,0:T(8,128)(2,1)} %copy-done.10, bf16[4,384,5120]{2,1,0:T(8,128)(2,1)} %bitcast.47, f32[1,384,1280]{2,1,0:T(8,128)} %bitcast.52), custom_call_target="tpu_custom_call" | custom-call | tf_op jit(solution)/shard_map/out_blocks/pallas_call | solution.py:412
  332.8 6.2 %collective-permute-done.31 = bf16[384,1280]{1,0:T(8,128)(2,1)S(1)} collective-permute-done((bf16[384,1280]{1,0:T(8,128)(2,1)}, bf16[384,1280]{1,0:T(8,128)(2,1)S(1)}, u32[]{:S(2)}, u32[]{:S(2)}) %collective-permute-start.31) | collective-permute-done | bytes 983072 | tf_op jit(solution)/shard_map/ppermute | solution.py:648
  (160 shorter events, 93.6 us)
Async XLA Ops:
  6.2 74.0 %all-to-all-start = ((bf16[4,656,384]{2,1,0:T(8,128)(2,1)}), bf16[4,656,384]{2,1,0:T(8,128)(2,1)S(1)}, u32[]{:S(2)}, u32[]{:S(2)}) async-start(bf16[4,656,384]{2,1,0:T(8,128)(2,1)} %cut_columns.5), calls=%async_computation | async-start | bytes 4030464 | tf_op jit(solution)/shard_map/all_to_all | solution.py:456
  36.5 33.9 %collective-permute-start.3 = (bf16[384,1280]{1,0:T(8,128)(2,1)S(1)}, bf16[384,1280]{1,0:T(8,128)(2,1)}, u32[]{:S(2)}, u32[]{:S(2)}) collective-permute-start(bf16[384,1280]{1,0:T(8,128)(2,1)S(1)} %multiply_convert_fusion.refs_2_), channel_id=1, source_target_pairs={{0,4},{4,8},{8,12},{12,0},{1,5},{5,9},{9,13},{13,1},{2,6},{6,10},{... | collective-permute-start | bytes 2949128 | tf_op jit(solution)/shard_map/ppermute | solution.py:555
  38.5 31.9 %collective-permute-start.4 = (bf16[384,1280]{1,0:T(8,128)(2,1)S(1)}, bf16[384,1280]{1,0:T(8,128)(2,1)}, u32[]{:S(2)}, u32[]{:S(2)}) collective-permute-start(bf16[384,1280]{1,0:T(8,128)(2,1)S(1)} %multiply_convert_fusion.refs_2_), channel_id=1, source_target_pairs={{0,16},{16,0},{1,17},{17,1},{2,18},{18,2},{3,19},{19,3},{4,20},{20... | collective-permute-start | bytes 2949128 | tf_op jit(solution)/shard_map/ppermute | solution.py:549
  80.1 34.7 %collective-permute-start.6 = (bf16[384,1280]{1,0:T(8,128)(2,1)}, bf16[384,1280]{1,0:T(8,128)(2,1)S(1)}, u32[]{:S(2)}, u32[]{:S(2)}) collective-permute-start(bf16[384,1280]{1,0:T(8,128)(2,1)} %collective-permute-done.3.refs_7_), channel_id=1, source_target_pairs={{0,1},{1,0},{2,3},{3,2},{4,5},{5,4},{6,7},{7,6},{8,9},{9,8},{10,11... | collective-permute-start | bytes 2949128 | tf_op jit(solution)/shard_map/ppermute | solution.py:550
  81.6 33.2 %collective-permute-start.7 = (bf16[384,1280]{1,0:T(8,128)(2,1)}, bf16[384,1280]{1,0:T(8,128)(2,1)}, u32[]{:S(2)}, u32[]{:S(2)}) collective-permute-start(bf16[384,1280]{1,0:T(8,128)(2,1)} %collective-permute-done.3.refs_7_), channel_id=1, source_target_pairs={{0,4},{4,8},{8,12},{12,0},{1,5},{5,9},{9,13},{13,1},{2,6},{6,10},{... | collective-permute-start | bytes 2949128 | tf_op jit(solution)/shard_map/ppermute | solution.py:555
  81.6 33.2 %collective-permute-start.8 = (bf16[384,1280]{1,0:T(8,128)(2,1)}, bf16[384,1280]{1,0:T(8,128)(2,1)}, u32[]{:S(2)}, u32[]{:S(2)}) collective-permute-start(bf16[384,1280]{1,0:T(8,128)(2,1)} %collective-permute-done.3.refs_7_), channel_id=1, source_target_pairs={{0,16},{16,0},{1,17},{17,1},{2,18},{18,2},{3,19},{19,3},{4,20},{20... | collective-permute-start | bytes 2949128 | tf_op jit(solution)/shard_map/ppermute | solution.py:549
  85.0 29.8 %collective-permute-start.5 = (bf16[192,1280]{1,0:T(8,128)(2,1)}, bf16[192,1280]{1,0:T(8,128)(2,1)S(1)}, u32[]{:S(2)}, u32[]{:S(2)}) collective-permute-start(bf16[192,1280]{1,0:T(8,128)(2,1)} %slice.49), channel_id=1, source_target_pairs={{0,16},{16,0},{1,17},{17,1},{2,18},{18,2},{3,19},{19,3},{4,20},{20... | collective-permute-start | bytes 1474568 | tf_op jit(solution)/shard_map/ppermute | solution.py:552
  87.4 27.5 %collective-permute-start.9 = (bf16[192,1280]{1,0:T(8,128)(2,1)}, bf16[192,1280]{1,0:T(8,128)(2,1)}, u32[]{:S(2)}, u32[]{:S(2)}) collective-permute-start(bf16[192,1280]{1,0:T(8,128)(2,1)} %slice.50), channel_id=1, source_target_pairs={{0,1},{1,0},{2,3},{3,2},{4,5},{5,4},{6,7},{7,6},{8,9},{9,8},{10,11... | collective-permute-start | bytes 1474568 | tf_op jit(solution)/shard_map/ppermute | solution.py:553
  114.9 32.8 %collective-permute-start.11 = (bf16[384,1280]{1,0:T(8,128)(2,1)}, bf16[384,1280]{1,0:T(8,128)(2,1)}, u32[]{:S(2)}, u32[]{:S(2)}) collective-permute-start(bf16[384,1280]{1,0:T(8,128)(2,1)} %collective-permute-done.7.refs_4_.refs_12_), channel_id=1, source_target_pairs={{0,1},{1,0},{2,3},{3,2},{4,5},{5,4},{6,7},{7,6},{8,9},{9,8},{10,11... | collective-permute-start | bytes 2949128 | tf_op jit(solution)/shard_map/ppermute | solution.py:550
  115.4 32.2 %collective-permute-start.12 = (bf16[384,1280]{1,0:T(8,128)(2,1)}, bf16[384,1280]{1,0:T(8,128)(2,1)}, u32[]{:S(2)}, u32[]{:S(2)}) collective-permute-start(bf16[384,1280]{1,0:T(8,128)(2,1)} %collective-permute-done.7.refs_4_.refs_12_), channel_id=1, source_target_pairs={{0,4},{4,8},{8,12},{12,0},{1,5},{5,9},{9,13},{13,1},{2,6},{6,10},{... | collective-permute-start | bytes 2949128 | tf_op jit(solution)/shard_map/ppermute | solution.py:555
  116.1 31.6 %collective-permute-start.13 = (bf16[384,1280]{1,0:T(8,128)(2,1)}, bf16[384,1280]{1,0:T(8,128)(2,1)}, u32[]{:S(2)}, u32[]{:S(2)}) collective-permute-start(bf16[384,1280]{1,0:T(8,128)(2,1)} %collective-permute-done.7.refs_4_.refs_12_), channel_id=1, source_target_pairs={{0,16},{16,0},{1,17},{17,1},{2,18},{18,2},{3,19},{19,3},{4,20},{20... | collective-permute-start | bytes 2949128 | tf_op jit(solution)/shard_map/ppermute | solution.py:549
  117.6 30.0 %collective-permute-start.10 = (bf16[192,1280]{1,0:T(8,128)(2,1)S(1)}, bf16[192,1280]{1,0:T(8,128)(2,1)}, u32[]{:S(2)}, u32[]{:S(2)}) collective-permute-start(bf16[192,1280]{1,0:T(8,128)(2,1)S(1)} %slice.55), channel_id=1, source_target_pairs={{0,16},{16,0},{1,17},{17,1},{2,18},{18,2},{3,19},{19,3},{4,20},{20... | collective-permute-start | bytes 1474568 | tf_op jit(solution)/shard_map/ppermute | solution.py:552
  119.3 28.4 %collective-permute-start.14 = (bf16[192,1280]{1,0:T(8,128)(2,1)S(1)}, bf16[192,1280]{1,0:T(8,128)(2,1)}, u32[]{:S(2)}, u32[]{:S(2)}) collective-permute-start(bf16[192,1280]{1,0:T(8,128)(2,1)S(1)} %slice.56), channel_id=1, source_target_pairs={{0,1},{1,0},{2,3},{3,2},{4,5},{5,4},{6,7},{7,6},{8,9},{9,8},{10,11... | collective-permute-start | bytes 1474568 | tf_op jit(solution)/shard_map/ppermute | solution.py:553
  147.7 47.3 %all-to-all-start.1 = ((bf16[4,640,384]{2,1,0:T(8,128)(2,1)}), bf16[4,640,384]{2,1,0:T(8,128)(2,1)}, u32[]{:S(2)}, u32[]{:S(2)}) async-start(bf16[4,640,384]{2,1,0:T(8,128)(2,1)} %cut_columns.3), calls=%async_computation.1 | async-start | bytes 3932160 | tf_op jit(solution)/shard_map/all_to_all | solution.py:456
  153.1 36.1 %collective-permute-start.16 = (bf16[384,1280]{1,0:T(8,128)(2,1)}, bf16[384,1280]{1,0:T(8,128)(2,1)S(1)}, u32[]{:S(2)}, u32[]{:S(2)}) collective-permute-start(bf16[384,1280]{1,0:T(8,128)(2,1)} %collective-permute-done.12.refs_9_.refs_17_), channel_id=1, source_target_pairs={{0,1},{1,0},{2,3},{3,2},{4,5},{5,4},{6,7},{7,6},{8,9},{9,8},{10,11... | collective-permute-start | bytes 2949128 | tf_op jit(solution)/shard_map/ppermute | solution.py:550
  154.6 34.7 %collective-permute-start.18 = (bf16[384,1280]{1,0:T(8,128)(2,1)}, bf16[384,1280]{1,0:T(8,128)(2,1)}, u32[]{:S(2)}, u32[]{:S(2)}) collective-permute-start(bf16[384,1280]{1,0:T(8,128)(2,1)} %collective-permute-done.12.refs_9_.refs_17_), channel_id=1, source_target_pairs={{0,16},{16,0},{1,17},{17,1},{2,18},{18,2},{3,19},{19,3},{4,20},{20... | collective-permute-start | bytes 2949128 | tf_op jit(solution)/shard_map/ppermute | solution.py:549
  160.2 29.0 %collective-permute-start.15 = (bf16[192,1280]{1,0:T(8,128)(2,1)}, bf16[192,1280]{1,0:T(8,128)(2,1)S(1)}, u32[]{:S(2)}, u32[]{:S(2)}) collective-permute-start(bf16[192,1280]{1,0:T(8,128)(2,1)} %slice.57), channel_id=1, source_target_pairs={{0,16},{16,0},{1,17},{17,1},{2,18},{18,2},{3,19},{19,3},{4,20},{20... | collective-permute-start | bytes 1474568 | tf_op jit(solution)/shard_map/ppermute | solution.py:552
  160.7 28.5 %collective-permute-start.19 = (bf16[192,1280]{1,0:T(8,128)(2,1)}, bf16[192,1280]{1,0:T(8,128)(2,1)}, u32[]{:S(2)}, u32[]{:S(2)}) collective-permute-start(bf16[192,1280]{1,0:T(8,128)(2,1)} %slice.59), channel_id=1, source_target_pairs={{0,1},{1,0},{2,3},{3,2},{4,5},{5,4},{6,7},{7,6},{8,9},{9,8},{10,11... | collective-permute-start | bytes 1474568 | tf_op jit(solution)/shard_map/ppermute | solution.py:553
  195.0 50.3 %all-to-all-start.3 = ((bf16[4,640,384]{2,1,0:T(8,128)(2,1)}), bf16[4,640,384]{2,1,0:T(8,128)(2,1)S(1)}, u32[]{:S(2)}, u32[]{:S(2)}) async-start(bf16[4,640,384]{2,1,0:T(8,128)(2,1)} %cut_columns.4), calls=%async_computation.3 | async-start | bytes 3932160 | tf_op jit(solution)/shard_map/all_to_all | solution.py:456
  245.4 32.8 %collective-permute-start.26 = (bf16[4,128,1280]{2,1,0:T(8,128)(2,1)}, bf16[4,128,1280]{2,1,0:T(8,128)(2,1)}, u32[]{:S(2)}, u32[]{:S(2)}) collective-permute-start(bf16[4,128,1280]{2,1,0:T(8,128)(2,1)} %constant_dynamic-slice_fusion), channel_id=1, source_target_pairs={{0,17},{1,16},{16,1},{17,0},{2,19},{3,18},{18,3},{19,2},{4,21},{5,... | collective-permute-start | bytes 3932168 | tf_op jit(solution)/shard_map/ppermute | solution.py:598
  247.9 25.3 %all-to-all-start.2 = ((bf16[4,2,384,128]{3,2,1,0:T(8,128)(2,1)}), bf16[4,2,384,128]{3,2,1,0:T(8,128)(2,1)S(1)}, u32[]{:S(2)}, u32[]{:S(2)}) async-start(bf16[4,2,384,128]{3,2,1,0:T(8,128)(2,1)} %bitcast.53), calls=%async_computation.2 | async-start | bytes 1572864 | tf_op jit(solution)/shard_map/all_to_all | solution.py:456
  278.2 26.6 %collective-permute-start.27 = (bf16[384,1280]{1,0:T(8,128)(2,1)}, bf16[384,1280]{1,0:T(8,128)(2,1)S(1)}, u32[]{:S(2)}, u32[]{:S(2)}) collective-permute-start(bf16[384,1280]{1,0:T(8,128)(2,1)} %out_blocks.6), channel_id=1, source_target_pairs={{0,17},{1,16},{16,1},{17,0},{2,19},{3,18},{18,3},{19,2},{4,21},{5,... | collective-permute-start | bytes 2949128 | tf_op jit(solution)/shard_map/ppermute | solution.py:618
  316.9 22.1 %collective-permute-start.31 = (bf16[384,1280]{1,0:T(8,128)(2,1)}, bf16[384,1280]{1,0:T(8,128)(2,1)S(1)}, u32[]{:S(2)}, u32[]{:S(2)}) collective-permute-start(bf16[384,1280]{1,0:T(8,128)(2,1)} %get-tuple-element.147), channel_id=1, source_target_pairs={{0,1},{1,0},{2,3},{3,2},{4,5},{5,4},{6,7},{7,6},{8,9},{9,8},{10,11... | collective-permute-start | bytes 2949128 | tf_op jit(solution)/shard_map/ppermute | solution.py:648
  318.5 21.7 %collective-permute-start.32 = (bf16[384,1280]{1,0:T(8,128)(2,1)}, bf16[384,1280]{1,0:T(8,128)(2,1)S(1)}, u32[]{:S(2)}, u32[]{:S(2)}) collective-permute-start(bf16[384,1280]{1,0:T(8,128)(2,1)} %get-tuple-element.148), channel_id=1, source_target_pairs={{0,16},{16,0},{1,17},{17,1},{2,18},{18,2},{3,19},{19,3},{4,20},{20... | collective-permute-start | bytes 2949128 | tf_op jit(solution)/shard_map/ppermute | solution.py:649
  (37 other events, 524.1 us)

commit v13 on v12

--- a/solution.py
+++ b/solution.py
@@ -629,7 +629,7 @@
             mixed, attended = lax.optimization_barrier((mixed, attended))
         attended.append(exchange(mixed))
 
-    def contributions(wanted, dtypes, before=None):
+    def earlier_share(wanted, before=None):
         for chunk, size in enumerate(chunks[:-1]):
             before = jnp.stack(
                 out_blocks(
@@ -637,11 +637,15 @@
                     (jnp.float32,), before,
                 )
             ).reshape(-1, tokens, out_width)
-        wanted, _ = lax.optimization_barrier((wanted, received[0]))
-        return out_blocks(wanted, sign, attended[-1], place, out_here, blocks, dtypes, before)
-
+        return before
+
+    leaving = earlier_share(which[1:3])
+    attended[-1], leaving = lax.optimization_barrier((attended[-1], leaving))
     far_attended = lax.ppermute(attended[-1], ("role", "head"), far_swap)
-    over_head, over_role = contributions(which[1:3], (jnp.bfloat16, jnp.bfloat16))
+    wanted, _ = lax.optimization_barrier((which[1:3], received[0]))
+    over_head, over_role = out_blocks(
+        wanted, sign, attended[-1], place, out_here, blocks, (jnp.bfloat16, jnp.bfloat16), leaving
+    )
     (over_head, over_role), far_attended = lax.optimization_barrier(
         ((over_head, over_role), far_attended)
     )
@@ -651,7 +655,10 @@
         jnp.zeros_like(which[:1]), -sign, far_attended, 0, far_weight.reshape(-1, out_width), 1,
         (jnp.float32,), received[0][None],
     )
-    (own,) = contributions(which[3:], (jnp.float32,), far[None])
+    (own,) = out_blocks(
+        which[3:], sign, attended[-1], place, out_here, blocks, (jnp.float32,),
+        earlier_share(which[3:], far[None]),
+    )
     total = received[1].astype(jnp.float32)
     for one in received[2:]:
         total = total + one.astype(jnp.float32)

time: 346 us -> 339 us (0.980)
  blocking collectives: 15.6 us -> 0 us
  waiting for transfers between devices: 122 us -> 129 us
    all_to_all x1 -> x0, blocking collectives: 15.6 us -> none  [exchange(): lax.all_to_all(array, 'chip', split_axis=0, concat_axis=0, tiled=True)]
    all_to_all x4 -> x5, starting transfers between devices: 19.9 us -> 24.7 us  [exchange(): lax.all_to_all(array, 'chip', split_axis=0, concat_axis=0, tiled=True)]
    all_to_all x4 -> x5, waiting for transfers between devices: 18.7 us -> 22.8 us  [exchange(): lax.all_to_all(array, 'chip', split_axis=0, concat_axis=0, tiled=True)]
  transfers between devices with their start and end apart: 37 -> 38, of which waited for: 15 -> 17; matrix products, arithmetic and copies ran while one was open for 9% -> 9% of each run, Pallas kernels for 31% -> 31%
where the time goes in v13:
time: 339 us; the launch traced here: 338 us
  waiting for transfers between devices  129 us (38%)
  Pallas kernels  110 us (32%)
  starting transfers between devices  56.1 us (17%)
  local copies, waits for them, and re-layouts  21.2 us (6%)
  matrix products  12.7 us (4%)
  other arithmetic  8.98 us (3%)
    ppermute x4, waiting for transfers between devices, per_device_by_heads(): sent['first'] = lax.ppermute(straight[2][:half], 'role', swap)  65.4 us
    pallas_call x4, Pallas kernels, project_heads(): pl.pallas_call(body, in_specs=[in_smem(), in_smem()] + [in_hbm()] * (2 *...  51.7 us
    pallas_call x6, Pallas kernels, out_blocks(): pl.pallas_call(body, grid_spec=pltpu.PrefetchScalarGridSpec(num_scalar_pr...  29.1 us
    all_to_all x5, starting transfers between devices, exchange(): lax.all_to_all(array, 'chip', split_axis=0, concat_axis=0, tiled=True)  24.7 us
    all_to_all x5, waiting for transfers between devices, exchange(): lax.all_to_all(array, 'chip', split_axis=0, concat_axis=0, tiled=True)  22.8 us
    pallas_call x2, Pallas kernels, attend(): pl.pallas_call(body, in_specs=[in_smem()] * 4 + [in_hbm()] * len(arrays),...  17.8 us
    ppermute x3, waiting for transfers between devices, per_device_by_heads(): sent['next'] = lax.ppermute(shard, 'chip', ring)  14 us
    dot_general x1, matrix products, per_device_by_heads(): jnp.dot(hidden_rows, gen_weight, preferred_element_type=jnp.float32)  12.7 us
  transfers between devices with their start and end apart: 38, of which 17 were waited for; matrix products, arithmetic and copies ran while one was open for 9% of the time, Pallas kernels for 31%

profile of v13, /device:TPU:0, one launch (start us, length us, event | category | flops | bytes accessed | tf_op | source)
XLA Modules:
  0.0 338.1 jit_solution(9747346327612568364)
XLA Ops:
  6.2 6.4 %all-to-all-start = ((bf16[4,656,384]{2,1,0:T(8,128)(2,1)}), bf16[4,656,384]{2,1,0:T(8,128)(2,1)S(1)}, u32[]{:S(2)}, u32[]{:S(2)}) async-start(bf16[4,656,384]{2,1,0:T(8,128)(2,1)} %cut_columns.5), calls=%async_computation | async-start | bytes 4030464 | tf_op jit(solution)/shard_map/all_to_all | solution.py:456
  13.0 12.7 %multiply_reduce_fusion = (f32[384]{0:T(512)S(1)}, f32[384,1280]{1,0:T(8,128)}) fusion(bf16[384,5120]{1,0:T(8,128)(2,1)} %param.11, s32[]{:T(128)S(6)} %select_n.48, f32[384]{0:T(512)S(1)} %mul.87, bf16[384,5120]{1,0:T(8,128)(2,1)} %param.9, bf16[5120,1280]{1,0:T(8,128)(2,1)} %param.10, f32[384]{0:T(512)S(1)} %mul.83), kind=kOutput, calls=%fused_computation.5 | convolution fusion | flops 5036604928 | bytes 19993092 | tf_op jit(solution)/shard_map/dot_general | solution.py:474
  47.4 9.1 %collective-permute-done.2.refs_4_ = bf16[384,1280]{1,0:T(8,128)(2,1)} collective-permute-done((bf16[384,1280]{1,0:T(8,128)(2,1)S(1)}, bf16[384,1280]{1,0:T(8,128)(2,1)}, u32[]{:S(2)}, u32[]{:S(2)}) %collective-permute-start.2) | collective-permute-done | bytes 983072 | tf_op jit(solution)/shard_map/ppermute | solution.py:550
  56.5 14.0 %collective-permute-done.3.refs_7_ = bf16[384,1280]{1,0:T(8,128)(2,1)} collective-permute-done((bf16[384,1280]{1,0:T(8,128)(2,1)S(1)}, bf16[384,1280]{1,0:T(8,128)(2,1)}, u32[]{:S(2)}, u32[]{:S(2)}) %collective-permute-start.3) | collective-permute-done | bytes 983072 | tf_op jit(solution)/shard_map/ppermute | solution.py:555
  70.5 9.6 %all-to-all-done.refs_0_ = bf16[4,656,384]{2,1,0:T(8,128)(2,1)S(1)} async-done(((bf16[4,656,384]{2,1,0:T(8,128)(2,1)}), bf16[4,656,384]{2,1,0:T(8,128)(2,1)S(1)}, u32[]{:S(2)}, u32[]{:S(2)}) %all-to-all-start) | async-done | bytes 2015264 | tf_op jit(solution)/shard_map/all_to_all | solution.py:456
  91.1 23.8 %collective-permute-done.5.refs_5_ = bf16[192,1280]{1,0:T(8,128)(2,1)S(1)} collective-permute-done((bf16[192,1280]{1,0:T(8,128)(2,1)}, bf16[192,1280]{1,0:T(8,128)(2,1)S(1)}, u32[]{:S(2)}, u32[]{:S(2)}) %collective-permute-start.5) | collective-permute-done | bytes 491552 | tf_op jit(solution)/shard_map/ppermute | solution.py:552
  120.9 26.8 %collective-permute-done.10.refs_10_ = bf16[192,1280]{1,0:T(8,128)(2,1)} collective-permute-done((bf16[192,1280]{1,0:T(8,128)(2,1)S(1)}, bf16[192,1280]{1,0:T(8,128)(2,1)}, u32[]{:S(2)}, u32[]{:S(2)}) %collective-permute-start.10) | collective-permute-done | bytes 491552 | tf_op jit(solution)/shard_map/ppermute | solution.py:552
  147.7 4.8 %all-to-all-start.1 = ((bf16[4,640,384]{2,1,0:T(8,128)(2,1)}), bf16[4,640,384]{2,1,0:T(8,128)(2,1)}, u32[]{:S(2)}, u32[]{:S(2)}) async-start(bf16[4,640,384]{2,1,0:T(8,128)(2,1)} %cut_columns.3), calls=%async_computation.1 | async-start | bytes 3932160 | tf_op jit(solution)/shard_map/all_to_all | solution.py:456
  164.1 10.3 %project_heads.4 = (bf16[1,2,384,128]{3,2,1,0:T(8,128)(2,1)}, bf16[1,2,2,384,128]{4,3,2,1,0:T(8,128)(2,1)}) custom-call(s32[5]{0:T(128)} %concatenate.9.places_ref, f32[2,1]{1,0:T(2,128)} %get-tuple-element.155.gains_ref, bf16[4,656,384]{2,1,0:T(8,128)(2,1)} %copy-done.2, bf16[4,656,384]{2,1,0:T(8,128)(2,1)} %collective-permute-done.17.refs_1_.refs_2_, ...), custom_call_target="tpu_custom_call" | custom-call | tf_op jit(solution)/shard_map/project_heads/pallas_call | solution.py:257
  174.4 14.8 %collective-permute-done.15.refs_7_.refs_15_ = bf16[192,1280]{1,0:T(8,128)(2,1)S(1)} collective-permute-done((bf16[192,1280]{1,0:T(8,128)(2,1)}, bf16[192,1280]{1,0:T(8,128)(2,1)S(1)}, u32[]{:S(2)}, u32[]{:S(2)}) %collective-permute-start.15) | collective-permute-done | bytes 491552 | tf_op jit(solution)/shard_map/ppermute | solution.py:552
  189.3 5.7 %all-to-all-done.1.refs_0_.refs_1_ = bf16[4,640,384]{2,1,0:T(8,128)(2,1)} async-done(((bf16[4,640,384]{2,1,0:T(8,128)(2,1)}), bf16[4,640,384]{2,1,0:T(8,128)(2,1)}, u32[]{:S(2)}, u32[]{:S(2)}) %all-to-all-start.1) | async-done | bytes 1966112 | tf_op jit(solution)/shard_map/all_to_all | solution.py:456
  204.4 10.3 %project_heads.5 = (bf16[1,2,384,128]{3,2,1,0:T(8,128)(2,1)}, bf16[1,2,2,384,128]{4,3,2,1,0:T(8,128)(2,1)}) custom-call(s32[5]{0:T(128)} %concatenate.9.places_ref, f32[2,1]{1,0:T(2,128)} %get-tuple-element.154.gains_ref, bf16[4,640,384]{2,1,0:T(8,128)(2,1)} %all-to-all-done.1.refs_0_.refs_1_, bf16[4,640,384]{2,1,0:T(8,128)(2,1)} %copy-done.6, ...), custom_call_target="tpu_custom_call" | custom-call | tf_op jit(solution)/shard_map/project_heads/pallas_call | solution.py:257
  215.7 14.1 %project_heads.6 = (bf16[2,2,384,128]{3,2,1,0:T(8,128)(2,1)}, bf16[2,2,2,384,128]{4,3,2,1,0:T(8,128)(2,1)}) custom-call(s32[5]{0:T(128)} %concatenate.9.places_ref, f32[2,2]{1,0:T(2,128)} %bitcast.72, bf16[4,656,384]{2,1,0:T(8,128)(2,1)} %copy-done.2, bf16[4,640,384]{2,1,0:T(8,128)(2,1)} %all-to-all-done.1.refs_0_.refs_1_, ...), custom_call_target="tpu_custom_call" | custom-call | tf_op jit(solution)/shard_map/project_heads/pallas_call | solution.py:257
  234.3 11.0 %attend.2 = bf16[4,2,6,64,128]{4,3,2,1,0:T(8,128)(2,1)} custom-call(s32[3,24,8]{2,1,0:T(8,128)} %fusion.7.slots_ref, s32[3,24]{1,0:T(4,128)} %get-tuple-element.129.counts_ref, s32[24]{0:T(128)} %fusion.11.from_ref, s32[3,4]{1,0:T(4,128)} %reduce_max.9.most_ref, bf16[1,12,64,128]{3,2,1,0:T(8,128)(2,1)} %bitcast.67, bf16[1,2,12,64,128]{4,3,2,1,0:T(8,128)(2,1)} %bitcast.60, ...), custom_call_target="tpu_custom_call" | custom-call | tf_op jit(solution)/shard_map/attend/pallas_call | solution.py:352
  247.9 4.8 %all-to-all-start.2 = ((bf16[4,2,384,128]{3,2,1,0:T(8,128)(2,1)}), bf16[4,2,384,128]{3,2,1,0:T(8,128)(2,1)S(1)}, u32[]{:S(2)}, u32[]{:S(2)}) async-start(bf16[4,2,384,128]{3,2,1,0:T(8,128)(2,1)} %bitcast.53), calls=%async_computation.2 | async-start | bytes 1572864 | tf_op jit(solution)/shard_map/all_to_all | solution.py:456
  252.7 17.0 %project_heads.7 = (bf16[1,4,384,128]{3,2,1,0:T(8,128)(2,1)}, bf16[1,2,4,384,128]{4,3,2,1,0:T(8,128)(2,1)}) custom-call(s32[5]{0:T(128)} %concatenate.9.places_ref, f32[2,1]{1,0:T(2,128)} %get-tuple-element.153.gains_ref, bf16[4,640,384]{2,1,0:T(8,128)(2,1)} %copy-done.7, bf16[4,640,384]{2,1,0:T(8,128)(2,1)} %collective-permute-done.27.refs_1_, ...), custom_call_target="tpu_custom_call" | custom-call | tf_op jit(solution)/shard_map/project_heads/pallas_call | solution.py:257
  274.0 4.1 %out_blocks.6 = bf16[384,1280]{1,0:T(8,128)(2,1)} custom-call(s32[1]{0:T(128)} %bitcast.8.which_ref, s32[1]{0:T(128)} %bitcast.1.sign_ref, bf16[4,2,384,128]{3,2,1,0:T(8,128)(2,1)} %copy-done.4, bf16[4,384,5120]{2,1,0:T(8,128)(2,1)} %bitcast.43), custom_call_target="tpu_custom_call" | custom-call | tf_op jit(solution)/shard_map/out_blocks/pallas_call | solution.py:412
  281.1 6.9 %attend.3 = bf16[4,1,6,64,128]{4,3,2,1,0:T(8,128)(2,1)} custom-call(s32[3,24,8]{2,1,0:T(8,128)} %fusion.7.slots_ref, s32[3,24]{1,0:T(4,128)} %get-tuple-element.129.counts_ref, s32[24]{0:T(128)} %fusion.11.from_ref, s32[3,4]{1,0:T(4,128)} %reduce_max.9.most_ref, bf16[1,24,64,128]{3,2,1,0:T(8,128)(2,1)} %bitcast.65, bf16[1,2,24,64,128]{4,3,2,1,0:T(8,128)(2,1)} %bitcast.59, ...), custom_call_target="tpu_custom_call" | custom-call | tf_op jit(solution)/shard_map/attend/pallas_call | solution.py:352
  287.9 4.8 %all-to-all-start.4 = ((bf16[4,1,384,128]{3,2,1,0:T(8,128)(2,1)}), bf16[4,1,384,128]{3,2,1,0:T(8,128)(2,1)S(1)}, u32[]{:S(2)}, u32[]{:S(2)}) async-start(bf16[4,1,384,128]{3,2,1,0:T(8,128)(2,1)} %bitcast.54), calls=%async_computation.4 | async-start | bytes 786432 | tf_op jit(solution)/shard_map/all_to_all | solution.py:456
  293.4 6.3 %out_blocks.7.refs_0_ = f32[2,384,1280]{2,1,0:T(8,128)} custom-call(s32[2]{0:T(128)} %pad_add_fusion.which_ref, s32[1]{0:T(128)} %bitcast.1.sign_ref, bf16[4,2,384,128]{3,2,1,0:T(8,128)(2,1)} %copy-done.4, bf16[4,384,5120]{2,1,0:T(8,128)(2,1)} %bitcast.44), custom_call_target="tpu_custom_call" | custom-call | tf_op jit(solution)/shard_map/out_blocks/pallas_call | solution.py:412
  299.7 4.2 %all-to-all-done.4.mixed_ref = bf16[4,1,384,128]{3,2,1,0:T(8,128)(2,1)S(1)} async-done(((bf16[4,1,384,128]{3,2,1,0:T(8,128)(2,1)}), bf16[4,1,384,128]{3,2,1,0:T(8,128)(2,1)S(1)}, u32[]{:S(2)}, u32[]{:S(2)}) %all-to-all-start.4) | async-done | bytes 393248 | tf_op jit(solution)/shard_map/all_to_all | solution.py:456
  304.6 5.8 %out_blocks.8 = (bf16[384,1280]{1,0:T(8,128)(2,1)}, bf16[384,1280]{1,0:T(8,128)(2,1)}) custom-call(s32[2]{0:T(128)} %pad_add_fusion.which_ref, s32[1]{0:T(128)} %bitcast.1.sign_ref, bf16[4,1,384,128]{3,2,1,0:T(8,128)(2,1)} %copy-done.10, bf16[4,384,5120]{2,1,0:T(8,128)(2,1)} %bitcast.45, f32[2,384,1280]{2,1,0:T(8,128)} %out_blocks.7.refs_0_), custom_call_target="tpu_custom_call" | custom-call | tf_op jit(solution)/shard_map/out_blocks/pallas_call | solution.py:412
  318.5 5.1 %out_blocks.10 = f32[384,1280]{1,0:T(8,128)} custom-call(s32[1]{0:T(128)} %bitcast.which_ref, s32[1]{0:T(128)} %bitcast.1.sign_ref, bf16[4,2,384,128]{3,2,1,0:T(8,128)(2,1)} %copy-done.4, bf16[4,384,5120]{2,1,0:T(8,128)(2,1)} %bitcast.46, f32[1,384,1280]{2,1,0:T(8,128)} %bitcast.51), custom_call_target="tpu_custom_call" | custom-call | tf_op jit(solution)/shard_map/out_blocks/pallas_call | solution.py:412
  327.7 7.2 %collective-permute-done.31 = bf16[384,1280]{1,0:T(8,128)(2,1)S(1)} collective-permute-done((bf16[384,1280]{1,0:T(8,128)(2,1)}, bf16[384,1280]{1,0:T(8,128)(2,1)S(1)}, u32[]{:S(2)}, u32[]{:S(2)}) %collective-permute-start.31) | collective-permute-done | bytes 983072 | tf_op jit(solution)/shard_map/ppermute | solution.py:652
  (161 shorter events, 98.1 us)
Async XLA Ops:
  6.2 74.0 %all-to-all-start = ((bf16[4,656,384]{2,1,0:T(8,128)(2,1)}), bf16[4,656,384]{2,1,0:T(8,128)(2,1)S(1)}, u32[]{:S(2)}, u32[]{:S(2)}) async-start(bf16[4,656,384]{2,1,0:T(8,128)(2,1)} %cut_columns.5), calls=%async_computation | async-start | bytes 4030464 | tf_op jit(solution)/shard_map/all_to_all | solution.py:456
  34.8 21.7 %collective-permute-start.2 = (bf16[384,1280]{1,0:T(8,128)(2,1)S(1)}, bf16[384,1280]{1,0:T(8,128)(2,1)}, u32[]{:S(2)}, u32[]{:S(2)}) collective-permute-start(bf16[384,1280]{1,0:T(8,128)(2,1)S(1)} %multiply_convert_fusion.refs_2_), channel_id=1, source_target_pairs={{0,1},{1,0},{2,3},{3,2},{4,5},{5,4},{6,7},{7,6},{8,9},{9,8},{10,11... | collective-permute-start | bytes 2949128 | tf_op jit(solution)/shard_map/ppermute | solution.py:550
  36.5 33.9 %collective-permute-start.3 = (bf16[384,1280]{1,0:T(8,128)(2,1)S(1)}, bf16[384,1280]{1,0:T(8,128)(2,1)}, u32[]{:S(2)}, u32[]{:S(2)}) collective-permute-start(bf16[384,1280]{1,0:T(8,128)(2,1)S(1)} %multiply_convert_fusion.refs_2_), channel_id=1, source_target_pairs={{0,4},{4,8},{8,12},{12,0},{1,5},{5,9},{9,13},{13,1},{2,6},{6,10},{... | collective-permute-start | bytes 2949128 | tf_op jit(solution)/shard_map/ppermute | solution.py:555
  38.6 31.9 %collective-permute-start.4 = (bf16[384,1280]{1,0:T(8,128)(2,1)S(1)}, bf16[384,1280]{1,0:T(8,128)(2,1)}, u32[]{:S(2)}, u32[]{:S(2)}) collective-permute-start(bf16[384,1280]{1,0:T(8,128)(2,1)S(1)} %multiply_convert_fusion.refs_2_), channel_id=1, source_target_pairs={{0,16},{16,0},{1,17},{17,1},{2,18},{18,2},{3,19},{19,3},{4,20},{20... | collective-permute-start | bytes 2949128 | tf_op jit(solution)/shard_map/ppermute | solution.py:549
  80.1 34.7 %collective-permute-start.6 = (bf16[384,1280]{1,0:T(8,128)(2,1)}, bf16[384,1280]{1,0:T(8,128)(2,1)S(1)}, u32[]{:S(2)}, u32[]{:S(2)}) collective-permute-start(bf16[384,1280]{1,0:T(8,128)(2,1)} %collective-permute-done.3.refs_7_), channel_id=1, source_target_pairs={{0,1},{1,0},{2,3},{3,2},{4,5},{5,4},{6,7},{7,6},{8,9},{9,8},{10,11... | collective-permute-start | bytes 2949128 | tf_op jit(solution)/shard_map/ppermute | solution.py:550
  81.6 33.2 %collective-permute-start.7 = (bf16[384,1280]{1,0:T(8,128)(2,1)}, bf16[384,1280]{1,0:T(8,128)(2,1)}, u32[]{:S(2)}, u32[]{:S(2)}) collective-permute-start(bf16[384,1280]{1,0:T(8,128)(2,1)} %collective-permute-done.3.refs_7_), channel_id=1, source_target_pairs={{0,4},{4,8},{8,12},{12,0},{1,5},{5,9},{9,13},{13,1},{2,6},{6,10},{... | collective-permute-start | bytes 2949128 | tf_op jit(solution)/shard_map/ppermute | solution.py:555
  81.7 33.2 %collective-permute-start.8 = (bf16[384,1280]{1,0:T(8,128)(2,1)}, bf16[384,1280]{1,0:T(8,128)(2,1)}, u32[]{:S(2)}, u32[]{:S(2)}) collective-permute-start(bf16[384,1280]{1,0:T(8,128)(2,1)} %collective-permute-done.3.refs_7_), channel_id=1, source_target_pairs={{0,16},{16,0},{1,17},{17,1},{2,18},{18,2},{3,19},{19,3},{4,20},{20... | collective-permute-start | bytes 2949128 | tf_op jit(solution)/shard_map/ppermute | solution.py:549
  85.0 29.8 %collective-permute-start.5 = (bf16[192,1280]{1,0:T(8,128)(2,1)}, bf16[192,1280]{1,0:T(8,128)(2,1)S(1)}, u32[]{:S(2)}, u32[]{:S(2)}) collective-permute-start(bf16[192,1280]{1,0:T(8,128)(2,1)} %slice.52), channel_id=1, source_target_pairs={{0,16},{16,0},{1,17},{17,1},{2,18},{18,2},{3,19},{19,3},{4,20},{20... | collective-permute-start | bytes 1474568 | tf_op jit(solution)/shard_map/ppermute | solution.py:552
  87.4 27.5 %collective-permute-start.9 = (bf16[192,1280]{1,0:T(8,128)(2,1)}, bf16[192,1280]{1,0:T(8,128)(2,1)}, u32[]{:S(2)}, u32[]{:S(2)}) collective-permute-start(bf16[192,1280]{1,0:T(8,128)(2,1)} %slice.53), channel_id=1, source_target_pairs={{0,1},{1,0},{2,3},{3,2},{4,5},{5,4},{6,7},{7,6},{8,9},{9,8},{10,11... | collective-permute-start | bytes 1474568 | tf_op jit(solution)/shard_map/ppermute | solution.py:553
  114.9 32.8 %collective-permute-start.11 = (bf16[384,1280]{1,0:T(8,128)(2,1)}, bf16[384,1280]{1,0:T(8,128)(2,1)}, u32[]{:S(2)}, u32[]{:S(2)}) collective-permute-start(bf16[384,1280]{1,0:T(8,128)(2,1)} %collective-permute-done.7.refs_4_.refs_12_), channel_id=1, source_target_pairs={{0,1},{1,0},{2,3},{3,2},{4,5},{5,4},{6,7},{7,6},{8,9},{9,8},{10,11... | collective-permute-start | bytes 2949128 | tf_op jit(solution)/shard_map/ppermute | solution.py:550
  115.5 32.2 %collective-permute-start.12 = (bf16[384,1280]{1,0:T(8,128)(2,1)}, bf16[384,1280]{1,0:T(8,128)(2,1)}, u32[]{:S(2)}, u32[]{:S(2)}) collective-permute-start(bf16[384,1280]{1,0:T(8,128)(2,1)} %collective-permute-done.7.refs_4_.refs_12_), channel_id=1, source_target_pairs={{0,4},{4,8},{8,12},{12,0},{1,5},{5,9},{9,13},{13,1},{2,6},{6,10},{... | collective-permute-start | bytes 2949128 | tf_op jit(solution)/shard_map/ppermute | solution.py:555
  116.1 31.6 %collective-permute-start.13 = (bf16[384,1280]{1,0:T(8,128)(2,1)}, bf16[384,1280]{1,0:T(8,128)(2,1)}, u32[]{:S(2)}, u32[]{:S(2)}) collective-permute-start(bf16[384,1280]{1,0:T(8,128)(2,1)} %collective-permute-done.7.refs_4_.refs_12_), channel_id=1, source_target_pairs={{0,16},{16,0},{1,17},{17,1},{2,18},{18,2},{3,19},{19,3},{4,20},{20... | collective-permute-start | bytes 2949128 | tf_op jit(solution)/shard_map/ppermute | solution.py:549
  117.6 30.0 %collective-permute-start.10 = (bf16[192,1280]{1,0:T(8,128)(2,1)S(1)}, bf16[192,1280]{1,0:T(8,128)(2,1)}, u32[]{:S(2)}, u32[]{:S(2)}) collective-permute-start(bf16[192,1280]{1,0:T(8,128)(2,1)S(1)} %slice.58), channel_id=1, source_target_pairs={{0,16},{16,0},{1,17},{17,1},{2,18},{18,2},{3,19},{19,3},{4,20},{20... | collective-permute-start | bytes 1474568 | tf_op jit(solution)/shard_map/ppermute | solution.py:552
  119.3 28.4 %collective-permute-start.14 = (bf16[192,1280]{1,0:T(8,128)(2,1)S(1)}, bf16[192,1280]{1,0:T(8,128)(2,1)}, u32[]{:S(2)}, u32[]{:S(2)}) collective-permute-start(bf16[192,1280]{1,0:T(8,128)(2,1)S(1)} %slice.59), channel_id=1, source_target_pairs={{0,1},{1,0},{2,3},{3,2},{4,5},{5,4},{6,7},{7,6},{8,9},{9,8},{10,11... | collective-permute-start | bytes 1474568 | tf_op jit(solution)/shard_map/ppermute | solution.py:553
  147.7 47.2 %all-to-all-start.1 = ((bf16[4,640,384]{2,1,0:T(8,128)(2,1)}), bf16[4,640,384]{2,1,0:T(8,128)(2,1)}, u32[]{:S(2)}, u32[]{:S(2)}) async-start(bf16[4,640,384]{2,1,0:T(8,128)(2,1)} %cut_columns.3), calls=%async_computation.1 | async-start | bytes 3932160 | tf_op jit(solution)/shard_map/all_to_all | solution.py:456
  153.1 36.1 %collective-permute-start.16 = (bf16[384,1280]{1,0:T(8,128)(2,1)}, bf16[384,1280]{1,0:T(8,128)(2,1)S(1)}, u32[]{:S(2)}, u32[]{:S(2)}) collective-permute-start(bf16[384,1280]{1,0:T(8,128)(2,1)} %collective-permute-done.12.refs_9_.refs_17_), channel_id=1, source_target_pairs={{0,1},{1,0},{2,3},{3,2},{4,5},{5,4},{6,7},{7,6},{8,9},{9,8},{10,11... | collective-permute-start | bytes 2949128 | tf_op jit(solution)/shard_map/ppermute | solution.py:550
  154.6 34.7 %collective-permute-start.18 = (bf16[384,1280]{1,0:T(8,128)(2,1)}, bf16[384,1280]{1,0:T(8,128)(2,1)}, u32[]{:S(2)}, u32[]{:S(2)}) collective-permute-start(bf16[384,1280]{1,0:T(8,128)(2,1)} %collective-permute-done.12.refs_9_.refs_17_), channel_id=1, source_target_pairs={{0,16},{16,0},{1,17},{17,1},{2,18},{18,2},{3,19},{19,3},{4,20},{20... | collective-permute-start | bytes 2949128 | tf_op jit(solution)/shard_map/ppermute | solution.py:549
  160.2 29.0 %collective-permute-start.15 = (bf16[192,1280]{1,0:T(8,128)(2,1)}, bf16[192,1280]{1,0:T(8,128)(2,1)S(1)}, u32[]{:S(2)}, u32[]{:S(2)}) collective-permute-start(bf16[192,1280]{1,0:T(8,128)(2,1)} %slice.60), channel_id=1, source_target_pairs={{0,16},{16,0},{1,17},{17,1},{2,18},{18,2},{3,19},{19,3},{4,20},{20... | collective-permute-start | bytes 1474568 | tf_op jit(solution)/shard_map/ppermute | solution.py:552
  160.7 28.5 %collective-permute-start.19 = (bf16[192,1280]{1,0:T(8,128)(2,1)}, bf16[192,1280]{1,0:T(8,128)(2,1)}, u32[]{:S(2)}, u32[]{:S(2)}) collective-permute-start(bf16[192,1280]{1,0:T(8,128)(2,1)} %slice.62), channel_id=1, source_target_pairs={{0,1},{1,0},{2,3},{3,2},{4,5},{5,4},{6,7},{7,6},{8,9},{9,8},{10,11... | collective-permute-start | bytes 1474568 | tf_op jit(solution)/shard_map/ppermute | solution.py:553
  195.0 50.3 %all-to-all-start.3 = ((bf16[4,640,384]{2,1,0:T(8,128)(2,1)}), bf16[4,640,384]{2,1,0:T(8,128)(2,1)S(1)}, u32[]{:S(2)}, u32[]{:S(2)}) async-start(bf16[4,640,384]{2,1,0:T(8,128)(2,1)} %cut_columns.4), calls=%async_computation.3 | async-start | bytes 3932160 | tf_op jit(solution)/shard_map/all_to_all | solution.py:456
  245.5 32.6 %collective-permute-start.26 = (bf16[4,128,1280]{2,1,0:T(8,128)(2,1)}, bf16[4,128,1280]{2,1,0:T(8,128)(2,1)}, u32[]{:S(2)}, u32[]{:S(2)}) collective-permute-start(bf16[4,128,1280]{2,1,0:T(8,128)(2,1)} %constant_dynamic-slice_fusion), channel_id=1, source_target_pairs={{0,17},{1,16},{16,1},{17,0},{2,19},{3,18},{18,3},{19,2},{4,21},{5,... | collective-permute-start | bytes 3932168 | tf_op jit(solution)/shard_map/ppermute | solution.py:598
  247.9 25.1 %all-to-all-start.2 = ((bf16[4,2,384,128]{3,2,1,0:T(8,128)(2,1)}), bf16[4,2,384,128]{3,2,1,0:T(8,128)(2,1)S(1)}, u32[]{:S(2)}, u32[]{:S(2)}) async-start(bf16[4,2,384,128]{3,2,1,0:T(8,128)(2,1)} %bitcast.53), calls=%async_computation.2 | async-start | bytes 1572864 | tf_op jit(solution)/shard_map/all_to_all | solution.py:456
  278.1 26.3 %collective-permute-start.29 = (bf16[384,1280]{1,0:T(8,128)(2,1)}, bf16[384,1280]{1,0:T(8,128)(2,1)S(1)}, u32[]{:S(2)}, u32[]{:S(2)}) collective-permute-start(bf16[384,1280]{1,0:T(8,128)(2,1)} %out_blocks.6), channel_id=1, source_target_pairs={{0,17},{1,16},{16,1},{17,0},{2,19},{3,18},{18,3},{19,2},{4,21},{5,... | collective-permute-start | bytes 2949128 | tf_op jit(solution)/shard_map/ppermute | solution.py:618
  313.8 21.1 %collective-permute-start.31 = (bf16[384,1280]{1,0:T(8,128)(2,1)}, bf16[384,1280]{1,0:T(8,128)(2,1)S(1)}, u32[]{:S(2)}, u32[]{:S(2)}) collective-permute-start(bf16[384,1280]{1,0:T(8,128)(2,1)} %get-tuple-element.149), channel_id=1, source_target_pairs={{0,1},{1,0},{2,3},{3,2},{4,5},{5,4},{6,7},{7,6},{8,9},{9,8},{10,11... | collective-permute-start | bytes 2949128 | tf_op jit(solution)/shard_map/ppermute | solution.py:652
  (38 other events, 526.3 us)

commit v14 on v13

--- a/solution.py
+++ b/solution.py
@@ -343,7 +343,7 @@
 
             @pl.when(jnp.logical_not(few))
             def _():
-                run(head, group, most, 3)
+                run(head, group, most, 6)
 
             return carry
 
@@ -605,6 +605,7 @@
                 held_places = project(0, at, 1, 0, early, held_places)
             held_places = project(0, 0, size, len(early), rounds[len(early) :], held_places)
         else:
+            held_places, far_weight = lax.optimization_barrier((held_places, far_weight))
             held_places = project(chunk, 0, size, 0, rounds, held_places)
         if last:
             for earlier in range(len(attended)):

time: 339 us -> 363 us (1.071)
  waiting for transfers between devices: 129 us -> 154 us
    ppermute x1, waiting for transfers between devices: 0.01 us -> 25 us  [per_device_by_heads(): far_weight = lax.ppermute(corner, ('role', 'head'), far_swap)]
  transfers between devices with their start and end apart: 38 -> 38, of which waited for: 17 -> 17; matrix products, arithmetic and copies ran while one was open for 9% -> 9% of each run, Pallas kernels for 31% -> 29%
where the time goes in v14:
time: 363 us; the launch traced here: 361 us
  waiting for transfers between devices  154 us (42%)
  Pallas kernels  108 us (30%)
  starting transfers between devices  56.5 us (16%)
  local copies, waits for them, and re-layouts  21.2 us (6%)
  matrix products  12.7 us (3%)
  other arithmetic  8.98 us (2%)
    ppermute x4, waiting for transfers between devices, per_device_by_heads(): sent['first'] = lax.ppermute(straight[2][:half], 'role', swap)  65.4 us
    pallas_call x4, Pallas kernels, project_heads(): pl.pallas_call(body, in_specs=[in_smem(), in_smem()] + [in_hbm()] * (2 *...  51.6 us
    pallas_call x6, Pallas kernels, out_blocks(): pl.pallas_call(body, grid_spec=pltpu.PrefetchScalarGridSpec(num_scalar_pr...  29.1 us
    ppermute x1, waiting for transfers between devices, per_device_by_heads(): far_weight = lax.ppermute(corner, ('role', 'head'), far_swap)  25 us
    all_to_all x5, starting transfers between devices, exchange(): lax.all_to_all(array, 'chip', split_axis=0, concat_axis=0, tiled=True)  24.7 us
    all_to_all x5, waiting for transfers between devices, exchange(): lax.all_to_all(array, 'chip', split_axis=0, concat_axis=0, tiled=True)  20.5 us
    pallas_call x2, Pallas kernels, attend(): pl.pallas_call(body, in_specs=[in_smem()] * 4 + [in_hbm()] * len(arrays),...  15.7 us
    ppermute x3, waiting for transfers between devices, per_device_by_heads(): sent['next'] = lax.ppermute(shard, 'chip', ring)  14 us
  transfers between devices with their start and end apart: 38, of which 17 were waited for; matrix products, arithmetic and copies ran while one was open for 9% of the time, Pallas kernels for 29%

profile of v14, /device:TPU:0, one launch (start us, length us, event | category | flops | bytes accessed | tf_op | source)
XLA Modules:
  0.0 361.3 jit_solution(14070511022418154220)
XLA Ops:
  6.2 6.4 %all-to-all-start = ((bf16[4,656,384]{2,1,0:T(8,128)(2,1)}), bf16[4,656,384]{2,1,0:T(8,128)(2,1)S(1)}, u32[]{:S(2)}, u32[]{:S(2)}) async-start(bf16[4,656,384]{2,1,0:T(8,128)(2,1)} %cut_columns.5), calls=%async_computation | async-start | bytes 4030464 | tf_op jit(solution)/shard_map/all_to_all | solution.py:456
  13.0 12.7 %multiply_reduce_fusion = (f32[384]{0:T(512)S(1)}, f32[384,1280]{1,0:T(8,128)}) fusion(bf16[384,5120]{1,0:T(8,128)(2,1)} %param.11, s32[]{:T(128)S(6)} %select_n.48, f32[384]{0:T(512)S(1)} %mul.87, bf16[384,5120]{1,0:T(8,128)(2,1)} %param.9, bf16[5120,1280]{1,0:T(8,128)(2,1)} %param.10, f32[384]{0:T(512)S(1)} %mul.83), kind=kOutput, calls=%fused_computation.5 | convolution fusion | flops 5036604928 | bytes 19993092 | tf_op jit(solution)/shard_map/dot_general | solution.py:474
  47.4 9.1 %collective-permute-done.2.refs_4_ = bf16[384,1280]{1,0:T(8,128)(2,1)} collective-permute-done((bf16[384,1280]{1,0:T(8,128)(2,1)S(1)}, bf16[384,1280]{1,0:T(8,128)(2,1)}, u32[]{:S(2)}, u32[]{:S(2)}) %collective-permute-start.2) | collective-permute-done | bytes 983072 | tf_op jit(solution)/shard_map/ppermute | solution.py:550
  56.5 14.0 %collective-permute-done.3.refs_7_ = bf16[384,1280]{1,0:T(8,128)(2,1)} collective-permute-done((bf16[384,1280]{1,0:T(8,128)(2,1)S(1)}, bf16[384,1280]{1,0:T(8,128)(2,1)}, u32[]{:S(2)}, u32[]{:S(2)}) %collective-permute-start.3) | collective-permute-done | bytes 983072 | tf_op jit(solution)/shard_map/ppermute | solution.py:555
  70.5 9.6 %all-to-all-done.refs_0_ = bf16[4,656,384]{2,1,0:T(8,128)(2,1)S(1)} async-done(((bf16[4,656,384]{2,1,0:T(8,128)(2,1)}), bf16[4,656,384]{2,1,0:T(8,128)(2,1)S(1)}, u32[]{:S(2)}, u32[]{:S(2)}) %all-to-all-start) | async-done | bytes 2015264 | tf_op jit(solution)/shard_map/all_to_all | solution.py:456
  91.1 23.8 %collective-permute-done.5.refs_5_ = bf16[192,1280]{1,0:T(8,128)(2,1)S(1)} collective-permute-done((bf16[192,1280]{1,0:T(8,128)(2,1)}, bf16[192,1280]{1,0:T(8,128)(2,1)S(1)}, u32[]{:S(2)}, u32[]{:S(2)}) %collective-permute-start.5) | collective-permute-done | bytes 491552 | tf_op jit(solution)/shard_map/ppermute | solution.py:552
  120.9 26.8 %collective-permute-done.10.refs_10_ = bf16[192,1280]{1,0:T(8,128)(2,1)} collective-permute-done((bf16[192,1280]{1,0:T(8,128)(2,1)S(1)}, bf16[192,1280]{1,0:T(8,128)(2,1)}, u32[]{:S(2)}, u32[]{:S(2)}) %collective-permute-start.10) | collective-permute-done | bytes 491552 | tf_op jit(solution)/shard_map/ppermute | solution.py:552
  147.7 4.8 %all-to-all-start.1 = ((bf16[4,640,384]{2,1,0:T(8,128)(2,1)}), bf16[4,640,384]{2,1,0:T(8,128)(2,1)}, u32[]{:S(2)}, u32[]{:S(2)}) async-start(bf16[4,640,384]{2,1,0:T(8,128)(2,1)} %cut_columns.3), calls=%async_computation.1 | async-start | bytes 3932160 | tf_op jit(solution)/shard_map/all_to_all | solution.py:456
  164.1 10.3 %project_heads.4 = (bf16[1,2,384,128]{3,2,1,0:T(8,128)(2,1)}, bf16[1,2,2,384,128]{4,3,2,1,0:T(8,128)(2,1)}) custom-call(s32[5]{0:T(128)} %concatenate.9.places_ref, f32[2,1]{1,0:T(2,128)} %get-tuple-element.159.gains_ref, bf16[4,656,384]{2,1,0:T(8,128)(2,1)} %copy-done.2, bf16[4,656,384]{2,1,0:T(8,128)(2,1)} %collective-permute-done.17.refs_1_.refs_2_, ...), custom_call_target="tpu_custom_call" | custom-call | tf_op jit(solution)/shard_map/project_heads/pallas_call | solution.py:257
  174.4 14.8 %collective-permute-done.15.refs_7_.refs_15_ = bf16[192,1280]{1,0:T(8,128)(2,1)S(1)} collective-permute-done((bf16[192,1280]{1,0:T(8,128)(2,1)}, bf16[192,1280]{1,0:T(8,128)(2,1)S(1)}, u32[]{:S(2)}, u32[]{:S(2)}) %collective-permute-start.15) | collective-permute-done | bytes 491552 | tf_op jit(solution)/shard_map/ppermute | solution.py:552
  189.3 5.7 %all-to-all-done.1.refs_0_.refs_1_ = bf16[4,640,384]{2,1,0:T(8,128)(2,1)} async-done(((bf16[4,640,384]{2,1,0:T(8,128)(2,1)}), bf16[4,640,384]{2,1,0:T(8,128)(2,1)}, u32[]{:S(2)}, u32[]{:S(2)}) %all-to-all-start.1) | async-done | bytes 1966112 | tf_op jit(solution)/shard_map/all_to_all | solution.py:456
  204.4 10.3 %project_heads.5 = (bf16[1,2,384,128]{3,2,1,0:T(8,128)(2,1)}, bf16[1,2,2,384,128]{4,3,2,1,0:T(8,128)(2,1)}) custom-call(s32[5]{0:T(128)} %concatenate.9.places_ref, f32[2,1]{1,0:T(2,128)} %get-tuple-element.158.gains_ref, bf16[4,640,384]{2,1,0:T(8,128)(2,1)} %all-to-all-done.1.refs_0_.refs_1_, bf16[4,640,384]{2,1,0:T(8,128)(2,1)} %copy-done.6, ...), custom_call_target="tpu_custom_call" | custom-call | tf_op jit(solution)/shard_map/project_heads/pallas_call | solution.py:257
  215.7 14.1 %project_heads.6 = (bf16[2,2,384,128]{3,2,1,0:T(8,128)(2,1)}, bf16[2,2,2,384,128]{4,3,2,1,0:T(8,128)(2,1)}) custom-call(s32[5]{0:T(128)} %concatenate.9.places_ref, f32[2,2]{1,0:T(2,128)} %bitcast.72, bf16[4,656,384]{2,1,0:T(8,128)(2,1)} %copy-done.2, bf16[4,640,384]{2,1,0:T(8,128)(2,1)} %all-to-all-done.1.refs_0_.refs_1_, ...), custom_call_target="tpu_custom_call" | custom-call | tf_op jit(solution)/shard_map/project_heads/pallas_call | solution.py:257
  234.3 9.5 %attend.2 = bf16[4,2,6,64,128]{4,3,2,1,0:T(8,128)(2,1)} custom-call(s32[3,24,8]{2,1,0:T(8,128)} %fusion.7.slots_ref, s32[3,24]{1,0:T(4,128)} %get-tuple-element.136.counts_ref, s32[24]{0:T(128)} %fusion.11.from_ref, s32[3,4]{1,0:T(4,128)} %reduce_max.9.most_ref, bf16[1,12,64,128]{3,2,1,0:T(8,128)(2,1)} %bitcast.67, bf16[1,2,12,64,128]{4,3,2,1,0:T(8,128)(2,1)} %bitcast.60, ...), custom_call_target="tpu_custom_call" | custom-call | tf_op jit(solution)/shard_map/attend/pallas_call | solution.py:352
  246.5 4.8 %all-to-all-start.2 = ((bf16[4,2,384,128]{3,2,1,0:T(8,128)(2,1)}), bf16[4,2,384,128]{3,2,1,0:T(8,128)(2,1)S(1)}, u32[]{:S(2)}, u32[]{:S(2)}) async-start(bf16[4,2,384,128]{3,2,1,0:T(8,128)(2,1)} %bitcast.53), calls=%async_computation.2 | async-start | bytes 1572864 | tf_op jit(solution)/shard_map/all_to_all | solution.py:456
  251.3 25.0 %collective-permute-done.26.weight_ref = bf16[4,128,1280]{2,1,0:T(8,128)(2,1)} collective-permute-done((bf16[4,128,1280]{2,1,0:T(8,128)(2,1)}, bf16[4,128,1280]{2,1,0:T(8,128)(2,1)}, u32[]{:S(2)}, u32[]{:S(2)}) %collective-permute-start.26) | collective-permute-done | bytes 1310752 | tf_op jit(solution)/shard_map/ppermute | solution.py:598
  276.3 17.0 %project_heads.7 = (bf16[1,4,384,128]{3,2,1,0:T(8,128)(2,1)}, bf16[1,2,4,384,128]{4,3,2,1,0:T(8,128)(2,1)}) custom-call(s32[5]{0:T(128)} %concatenate.9.places_ref, f32[2,1]{1,0:T(2,128)} %get-tuple-element.157.gains_ref, bf16[4,640,384]{2,1,0:T(8,128)(2,1)} %copy-done.7, bf16[4,640,384]{2,1,0:T(8,128)(2,1)} %collective-permute-done.27.refs_1_, ...), custom_call_target="tpu_custom_call" | custom-call | tf_op jit(solution)/shard_map/project_heads/pallas_call | solution.py:257
  301.8 6.1 %attend.3 = bf16[4,1,6,64,128]{4,3,2,1,0:T(8,128)(2,1)} custom-call(s32[3,24,8]{2,1,0:T(8,128)} %fusion.7.slots_ref, s32[3,24]{1,0:T(4,128)} %get-tuple-element.136.counts_ref, s32[24]{0:T(128)} %fusion.11.from_ref, s32[3,4]{1,0:T(4,128)} %reduce_max.9.most_ref, bf16[1,24,64,128]{3,2,1,0:T(8,128)(2,1)} %bitcast.65, bf16[1,2,24,64,128]{4,3,2,1,0:T(8,128)(2,1)} %bitcast.59, ...), custom_call_target="tpu_custom_call" | custom-call | tf_op jit(solution)/shard_map/attend/pallas_call | solution.py:352
  307.9 4.8 %all-to-all-start.4 = ((bf16[4,1,384,128]{3,2,1,0:T(8,128)(2,1)}), bf16[4,1,384,128]{3,2,1,0:T(8,128)(2,1)S(1)}, u32[]{:S(2)}, u32[]{:S(2)}) async-start(bf16[4,1,384,128]{3,2,1,0:T(8,128)(2,1)} %bitcast.54), calls=%async_computation.4 | async-start | bytes 786432 | tf_op jit(solution)/shard_map/all_to_all | solution.py:456
  313.3 6.3 %out_blocks.7.refs_0_ = f32[2,384,1280]{2,1,0:T(8,128)} custom-call(s32[2]{0:T(128)} %pad_add_fusion.which_ref, s32[1]{0:T(128)} %bitcast.1.sign_ref, bf16[4,2,384,128]{3,2,1,0:T(8,128)(2,1)} %copy-done.4, bf16[4,384,5120]{2,1,0:T(8,128)(2,1)} %bitcast.44), custom_call_target="tpu_custom_call" | custom-call | tf_op jit(solution)/shard_map/out_blocks/pallas_call | solution.py:412
  319.7 5.1 %all-to-all-done.4.mixed_ref = bf16[4,1,384,128]{3,2,1,0:T(8,128)(2,1)S(1)} async-done(((bf16[4,1,384,128]{3,2,1,0:T(8,128)(2,1)}), bf16[4,1,384,128]{3,2,1,0:T(8,128)(2,1)S(1)}, u32[]{:S(2)}, u32[]{:S(2)}) %all-to-all-start.4) | async-done | bytes 393248 | tf_op jit(solution)/shard_map/all_to_all | solution.py:456
  325.5 5.8 %out_blocks.8 = (bf16[384,1280]{1,0:T(8,128)(2,1)}, bf16[384,1280]{1,0:T(8,128)(2,1)}) custom-call(s32[2]{0:T(128)} %pad_add_fusion.which_ref, s32[1]{0:T(128)} %bitcast.1.sign_ref, bf16[4,1,384,128]{3,2,1,0:T(8,128)(2,1)} %copy-done.10, bf16[4,384,5120]{2,1,0:T(8,128)(2,1)} %bitcast.45, f32[2,384,1280]{2,1,0:T(8,128)} %out_blocks.7.refs_0_), custom_call_target="tpu_custom_call" | custom-call | tf_op jit(solution)/shard_map/out_blocks/pallas_call | solution.py:412
  340.5 5.1 %out_blocks.10 = f32[384,1280]{1,0:T(8,128)} custom-call(s32[1]{0:T(128)} %bitcast.which_ref, s32[1]{0:T(128)} %bitcast.1.sign_ref, bf16[4,2,384,128]{3,2,1,0:T(8,128)(2,1)} %copy-done.4, bf16[4,384,5120]{2,1,0:T(8,128)(2,1)} %bitcast.46, f32[1,384,1280]{2,1,0:T(8,128)} %bitcast.51), custom_call_target="tpu_custom_call" | custom-call | tf_op jit(solution)/shard_map/out_blocks/pallas_call | solution.py:412
  349.7 8.2 %collective-permute-done.31 = bf16[384,1280]{1,0:T(8,128)(2,1)S(1)} collective-permute-done((bf16[384,1280]{1,0:T(8,128)(2,1)}, bf16[384,1280]{1,0:T(8,128)(2,1)S(1)}, u32[]{:S(2)}, u32[]{:S(2)}) %collective-permute-start.31) | collective-permute-done | bytes 983072 | tf_op jit(solution)/shard_map/ppermute | solution.py:653
  (161 shorter events, 100.5 us)
Async XLA Ops:
  6.2 74.0 %all-to-all-start = ((bf16[4,656,384]{2,1,0:T(8,128)(2,1)}), bf16[4,656,384]{2,1,0:T(8,128)(2,1)S(1)}, u32[]{:S(2)}, u32[]{:S(2)}) async-start(bf16[4,656,384]{2,1,0:T(8,128)(2,1)} %cut_columns.5), calls=%async_computation | async-start | bytes 4030464 | tf_op jit(solution)/shard_map/all_to_all | solution.py:456
  36.5 33.9 %collective-permute-start.3 = (bf16[384,1280]{1,0:T(8,128)(2,1)S(1)}, bf16[384,1280]{1,0:T(8,128)(2,1)}, u32[]{:S(2)}, u32[]{:S(2)}) collective-permute-start(bf16[384,1280]{1,0:T(8,128)(2,1)S(1)} %multiply_convert_fusion.refs_2_), channel_id=1, source_target_pairs={{0,4},{4,8},{8,12},{12,0},{1,5},{5,9},{9,13},{13,1},{2,6},{6,10},{... | collective-permute-start | bytes 2949128 | tf_op jit(solution)/shard_map/ppermute | solution.py:555
  38.6 31.9 %collective-permute-start.4 = (bf16[384,1280]{1,0:T(8,128)(2,1)S(1)}, bf16[384,1280]{1,0:T(8,128)(2,1)}, u32[]{:S(2)}, u32[]{:S(2)}) collective-permute-start(bf16[384,1280]{1,0:T(8,128)(2,1)S(1)} %multiply_convert_fusion.refs_2_), channel_id=1, source_target_pairs={{0,16},{16,0},{1,17},{17,1},{2,18},{18,2},{3,19},{19,3},{4,20},{20... | collective-permute-start | bytes 2949128 | tf_op jit(solution)/shard_map/ppermute | solution.py:549
  80.1 34.7 %collective-permute-start.6 = (bf16[384,1280]{1,0:T(8,128)(2,1)}, bf16[384,1280]{1,0:T(8,128)(2,1)S(1)}, u32[]{:S(2)}, u32[]{:S(2)}) collective-permute-start(bf16[384,1280]{1,0:T(8,128)(2,1)} %collective-permute-done.3.refs_7_), channel_id=1, source_target_pairs={{0,1},{1,0},{2,3},{3,2},{4,5},{5,4},{6,7},{7,6},{8,9},{9,8},{10,11... | collective-permute-start | bytes 2949128 | tf_op jit(solution)/shard_map/ppermute | solution.py:550
  81.6 33.2 %collective-permute-start.7 = (bf16[384,1280]{1,0:T(8,128)(2,1)}, bf16[384,1280]{1,0:T(8,128)(2,1)}, u32[]{:S(2)}, u32[]{:S(2)}) collective-permute-start(bf16[384,1280]{1,0:T(8,128)(2,1)} %collective-permute-done.3.refs_7_), channel_id=1, source_target_pairs={{0,4},{4,8},{8,12},{12,0},{1,5},{5,9},{9,13},{13,1},{2,6},{6,10},{... | collective-permute-start | bytes 2949128 | tf_op jit(solution)/shard_map/ppermute | solution.py:555
  81.7 33.2 %collective-permute-start.8 = (bf16[384,1280]{1,0:T(8,128)(2,1)}, bf16[384,1280]{1,0:T(8,128)(2,1)}, u32[]{:S(2)}, u32[]{:S(2)}) collective-permute-start(bf16[384,1280]{1,0:T(8,128)(2,1)} %collective-permute-done.3.refs_7_), channel_id=1, source_target_pairs={{0,16},{16,0},{1,17},{17,1},{2,18},{18,2},{3,19},{19,3},{4,20},{20... | collective-permute-start | bytes 2949128 | tf_op jit(solution)/shard_map/ppermute | solution.py:549
  85.0 29.8 %collective-permute-start.5 = (bf16[192,1280]{1,0:T(8,128)(2,1)}, bf16[192,1280]{1,0:T(8,128)(2,1)S(1)}, u32[]{:S(2)}, u32[]{:S(2)}) collective-permute-start(bf16[192,1280]{1,0:T(8,128)(2,1)} %slice.52), channel_id=1, source_target_pairs={{0,16},{16,0},{1,17},{17,1},{2,18},{18,2},{3,19},{19,3},{4,20},{20... | collective-permute-start | bytes 1474568 | tf_op jit(solution)/shard_map/ppermute | solution.py:552
  87.4 27.5 %collective-permute-start.9 = (bf16[192,1280]{1,0:T(8,128)(2,1)}, bf16[192,1280]{1,0:T(8,128)(2,1)}, u32[]{:S(2)}, u32[]{:S(2)}) collective-permute-start(bf16[192,1280]{1,0:T(8,128)(2,1)} %slice.53), channel_id=1, source_target_pairs={{0,1},{1,0},{2,3},{3,2},{4,5},{5,4},{6,7},{7,6},{8,9},{9,8},{10,11... | collective-permute-start | bytes 1474568 | tf_op jit(solution)/shard_map/ppermute | solution.py:553
  114.9 32.8 %collective-permute-start.11 = (bf16[384,1280]{1,0:T(8,128)(2,1)}, bf16[384,1280]{1,0:T(8,128)(2,1)}, u32[]{:S(2)}, u32[]{:S(2)}) collective-permute-start(bf16[384,1280]{1,0:T(8,128)(2,1)} %collective-permute-done.7.refs_4_.refs_12_), channel_id=1, source_target_pairs={{0,1},{1,0},{2,3},{3,2},{4,5},{5,4},{6,7},{7,6},{8,9},{9,8},{10,11... | collective-permute-start | bytes 2949128 | tf_op jit(solution)/shard_map/ppermute | solution.py:550
  115.5 32.2 %collective-permute-start.12 = (bf16[384,1280]{1,0:T(8,128)(2,1)}, bf16[384,1280]{1,0:T(8,128)(2,1)}, u32[]{:S(2)}, u32[]{:S(2)}) collective-permute-start(bf16[384,1280]{1,0:T(8,128)(2,1)} %collective-permute-done.7.refs_4_.refs_12_), channel_id=1, source_target_pairs={{0,4},{4,8},{8,12},{12,0},{1,5},{5,9},{9,13},{13,1},{2,6},{6,10},{... | collective-permute-start | bytes 2949128 | tf_op jit(solution)/shard_map/ppermute | solution.py:555
  116.1 31.6 %collective-permute-start.13 = (bf16[384,1280]{1,0:T(8,128)(2,1)}, bf16[384,1280]{1,0:T(8,128)(2,1)}, u32[]{:S(2)}, u32[]{:S(2)}) collective-permute-start(bf16[384,1280]{1,0:T(8,128)(2,1)} %collective-permute-done.7.refs_4_.refs_12_), channel_id=1, source_target_pairs={{0,16},{16,0},{1,17},{17,1},{2,18},{18,2},{3,19},{19,3},{4,20},{20... | collective-permute-start | bytes 2949128 | tf_op jit(solution)/shard_map/ppermute | solution.py:549
  117.6 30.0 %collective-permute-start.10 = (bf16[192,1280]{1,0:T(8,128)(2,1)S(1)}, bf16[192,1280]{1,0:T(8,128)(2,1)}, u32[]{:S(2)}, u32[]{:S(2)}) collective-permute-start(bf16[192,1280]{1,0:T(8,128)(2,1)S(1)} %slice.58), channel_id=1, source_target_pairs={{0,16},{16,0},{1,17},{17,1},{2,18},{18,2},{3,19},{19,3},{4,20},{20... | collective-permute-start | bytes 1474568 | tf_op jit(solution)/shard_map/ppermute | solution.py:552
  119.3 28.4 %collective-permute-start.14 = (bf16[192,1280]{1,0:T(8,128)(2,1)S(1)}, bf16[192,1280]{1,0:T(8,128)(2,1)}, u32[]{:S(2)}, u32[]{:S(2)}) collective-permute-start(bf16[192,1280]{1,0:T(8,128)(2,1)S(1)} %slice.59), channel_id=1, source_target_pairs={{0,1},{1,0},{2,3},{3,2},{4,5},{5,4},{6,7},{7,6},{8,9},{9,8},{10,11... | collective-permute-start | bytes 1474568 | tf_op jit(solution)/shard_map/ppermute | solution.py:553
  147.7 47.2 %all-to-all-start.1 = ((bf16[4,640,384]{2,1,0:T(8,128)(2,1)}), bf16[4,640,384]{2,1,0:T(8,128)(2,1)}, u32[]{:S(2)}, u32[]{:S(2)}) async-start(bf16[4,640,384]{2,1,0:T(8,128)(2,1)} %cut_columns.3), calls=%async_computation.1 | async-start | bytes 3932160 | tf_op jit(solution)/shard_map/all_to_all | solution.py:456
  153.1 36.1 %collective-permute-start.16 = (bf16[384,1280]{1,0:T(8,128)(2,1)}, bf16[384,1280]{1,0:T(8,128)(2,1)S(1)}, u32[]{:S(2)}, u32[]{:S(2)}) collective-permute-start(bf16[384,1280]{1,0:T(8,128)(2,1)} %collective-permute-done.12.refs_9_.refs_17_), channel_id=1, source_target_pairs={{0,1},{1,0},{2,3},{3,2},{4,5},{5,4},{6,7},{7,6},{8,9},{9,8},{10,11... | collective-permute-start | bytes 2949128 | tf_op jit(solution)/shard_map/ppermute | solution.py:550
  154.6 34.7 %collective-permute-start.18 = (bf16[384,1280]{1,0:T(8,128)(2,1)}, bf16[384,1280]{1,0:T(8,128)(2,1)}, u32[]{:S(2)}, u32[]{:S(2)}) collective-permute-start(bf16[384,1280]{1,0:T(8,128)(2,1)} %collective-permute-done.12.refs_9_.refs_17_), channel_id=1, source_target_pairs={{0,16},{16,0},{1,17},{17,1},{2,18},{18,2},{3,19},{19,3},{4,20},{20... | collective-permute-start | bytes 2949128 | tf_op jit(solution)/shard_map/ppermute | solution.py:549
  160.2 29.0 %collective-permute-start.15 = (bf16[192,1280]{1,0:T(8,128)(2,1)}, bf16[192,1280]{1,0:T(8,128)(2,1)S(1)}, u32[]{:S(2)}, u32[]{:S(2)}) collective-permute-start(bf16[192,1280]{1,0:T(8,128)(2,1)} %slice.60), channel_id=1, source_target_pairs={{0,16},{16,0},{1,17},{17,1},{2,18},{18,2},{3,19},{19,3},{4,20},{20... | collective-permute-start | bytes 1474568 | tf_op jit(solution)/shard_map/ppermute | solution.py:552
  160.7 28.5 %collective-permute-start.19 = (bf16[192,1280]{1,0:T(8,128)(2,1)}, bf16[192,1280]{1,0:T(8,128)(2,1)}, u32[]{:S(2)}, u32[]{:S(2)}) collective-permute-start(bf16[192,1280]{1,0:T(8,128)(2,1)} %slice.62), channel_id=1, source_target_pairs={{0,1},{1,0},{2,3},{3,2},{4,5},{5,4},{6,7},{7,6},{8,9},{9,8},{10,11... | collective-permute-start | bytes 1474568 | tf_op jit(solution)/shard_map/ppermute | solution.py:553
  195.0 48.8 %all-to-all-start.3 = ((bf16[4,640,384]{2,1,0:T(8,128)(2,1)}), bf16[4,640,384]{2,1,0:T(8,128)(2,1)S(1)}, u32[]{:S(2)}, u32[]{:S(2)}) async-start(bf16[4,640,384]{2,1,0:T(8,128)(2,1)} %cut_columns.4), calls=%async_computation.3 | async-start | bytes 3932160 | tf_op jit(solution)/shard_map/all_to_all | solution.py:456
  243.8 32.5 %collective-permute-start.27 = (bf16[4,640,384]{2,1,0:T(8,128)(2,1)S(1)}, bf16[4,640,384]{2,1,0:T(8,128)(2,1)}, u32[]{:S(2)}, u32[]{:S(2)}) collective-permute-start(bf16[4,640,384]{2,1,0:T(8,128)(2,1)S(1)} %all-to-all-done.3.refs_0_), channel_id=1, source_target_pairs={{0,2},{2,0},{1,3},{3,1},{4,6},{6,4},{5,7},{7,5},{8,10},{10,8},{9,1... | collective-permute-start | bytes 5898248 | tf_op jit(solution)/shard_map/ppermute | solution.py:627
  244.0 32.3 %collective-permute-start.26 = (bf16[4,128,1280]{2,1,0:T(8,128)(2,1)}, bf16[4,128,1280]{2,1,0:T(8,128)(2,1)}, u32[]{:S(2)}, u32[]{:S(2)}) collective-permute-start(bf16[4,128,1280]{2,1,0:T(8,128)(2,1)} %constant_dynamic-slice_fusion), channel_id=1, source_target_pairs={{0,17},{1,16},{16,1},{17,0},{2,19},{3,18},{18,3},{19,2},{4,21},{5,... | collective-permute-start | bytes 3932168 | tf_op jit(solution)/shard_map/ppermute | solution.py:598
  246.5 46.9 %all-to-all-start.2 = ((bf16[4,2,384,128]{3,2,1,0:T(8,128)(2,1)}), bf16[4,2,384,128]{3,2,1,0:T(8,128)(2,1)S(1)}, u32[]{:S(2)}, u32[]{:S(2)}) async-start(bf16[4,2,384,128]{3,2,1,0:T(8,128)(2,1)} %bitcast.53), calls=%async_computation.2 | async-start | bytes 1572864 | tf_op jit(solution)/shard_map/all_to_all | solution.py:456
  298.4 26.9 %collective-permute-start.29 = (bf16[384,1280]{1,0:T(8,128)(2,1)}, bf16[384,1280]{1,0:T(8,128)(2,1)S(1)}, u32[]{:S(2)}, u32[]{:S(2)}) collective-permute-start(bf16[384,1280]{1,0:T(8,128)(2,1)} %out_blocks.6), channel_id=1, source_target_pairs={{0,17},{1,16},{16,1},{17,0},{2,19},{3,18},{18,3},{19,2},{4,21},{5,... | collective-permute-start | bytes 2949128 | tf_op jit(solution)/shard_map/ppermute | solution.py:619
  335.8 22.1 %collective-permute-start.31 = (bf16[384,1280]{1,0:T(8,128)(2,1)}, bf16[384,1280]{1,0:T(8,128)(2,1)S(1)}, u32[]{:S(2)}, u32[]{:S(2)}) collective-permute-start(bf16[384,1280]{1,0:T(8,128)(2,1)} %get-tuple-element.153), channel_id=1, source_target_pairs={{0,1},{1,0},{2,3},{3,2},{4,5},{5,4},{6,7},{7,6},{8,9},{9,8},{10,11... | collective-permute-start | bytes 2949128 | tf_op jit(solution)/shard_map/ppermute | solution.py:653
  (38 other events, 566.9 us)

commit v15 on v14

--- a/solution.py
+++ b/solution.py
@@ -605,7 +605,6 @@
                 held_places = project(0, at, 1, 0, early, held_places)
             held_places = project(0, 0, size, len(early), rounds[len(early) :], held_places)
         else:
-            held_places, far_weight = lax.optimization_barrier((held_places, far_weight))
             held_places = project(chunk, 0, size, 0, rounds, held_places)
         if last:
             for earlier in range(len(attended)):

time: 363 us -> 338 us (0.931)
  waiting for transfers between devices: 154 us -> 129 us
    ppermute x1, waiting for transfers between devices: 25 us -> 0.01 us  [per_device_by_heads(): far_weight = lax.ppermute(corner, ('role', 'head'), far_swap)]
  transfers between devices with their start and end apart: 38 -> 38, of which waited for: 17 -> 17; matrix products, arithmetic and copies ran while one was open for 9% -> 10% of each run, Pallas kernels for 29% -> 31%
where the time goes in v15:
time: 338 us; the launch traced here: 336 us
  waiting for transfers between devices  129 us (38%)
  Pallas kernels  108 us (32%)
  starting transfers between devices  56.1 us (17%)
  local copies, waits for them, and re-layouts  21.2 us (6%)
  matrix products  12.7 us (4%)
  other arithmetic  8.98 us (3%)
    ppermute x4, waiting for transfers between devices, per_device_by_heads(): sent['first'] = lax.ppermute(straight[2][:half], 'role', swap)  65.4 us
    pallas_call x4, Pallas kernels, project_heads(): pl.pallas_call(body, in_specs=[in_smem(), in_smem()] + [in_hbm()] * (2 *...  51.7 us
    pallas_call x6, Pallas kernels, out_blocks(): pl.pallas_call(body, grid_spec=pltpu.PrefetchScalarGridSpec(num_scalar_pr...  29.1 us
    all_to_all x5, starting transfers between devices, exchange(): lax.all_to_all(array, 'chip', split_axis=0, concat_axis=0, tiled=True)  24.7 us
    all_to_all x5, waiting for transfers between devices, exchange(): lax.all_to_all(array, 'chip', split_axis=0, concat_axis=0, tiled=True)  22.8 us
    pallas_call x2, Pallas kernels, attend(): pl.pallas_call(body, in_specs=[in_smem()] * 4 + [in_hbm()] * len(arrays),...  16.2 us
    ppermute x3, waiting for transfers between devices, per_device_by_heads(): sent['next'] = lax.ppermute(shard, 'chip', ring)  14 us
    dot_general x1, matrix products, per_device_by_heads(): jnp.dot(hidden_rows, gen_weight, preferred_element_type=jnp.float32)  12.7 us
  transfers between devices with their start and end apart: 38, of which 17 were waited for; matrix products, arithmetic and copies ran while one was open for 10% of the time, Pallas kernels for 31%

profile of v15, /device:TPU:0, one launch (start us, length us, event | category | flops | bytes accessed | tf_op | source)
XLA Modules:
  0.0 336.5 jit_solution(4899080462567932624)
XLA Ops:
  6.2 6.4 %all-to-all-start = ((bf16[4,656,384]{2,1,0:T(8,128)(2,1)}), bf16[4,656,384]{2,1,0:T(8,128)(2,1)S(1)}, u32[]{:S(2)}, u32[]{:S(2)}) async-start(bf16[4,656,384]{2,1,0:T(8,128)(2,1)} %cut_columns.5), calls=%async_computation | async-start | bytes 4030464 | tf_op jit(solution)/shard_map/all_to_all | solution.py:456
  13.0 12.7 %multiply_reduce_fusion = (f32[384]{0:T(512)S(1)}, f32[384,1280]{1,0:T(8,128)}) fusion(bf16[384,5120]{1,0:T(8,128)(2,1)} %param.11, s32[]{:T(128)S(6)} %select_n.48, f32[384]{0:T(512)S(1)} %mul.87, bf16[384,5120]{1,0:T(8,128)(2,1)} %param.9, bf16[5120,1280]{1,0:T(8,128)(2,1)} %param.10, f32[384]{0:T(512)S(1)} %mul.83), kind=kOutput, calls=%fused_computation.5 | convolution fusion | flops 5036604928 | bytes 19993092 | tf_op jit(solution)/shard_map/dot_general | solution.py:474
  47.4 9.1 %collective-permute-done.2.refs_4_ = bf16[384,1280]{1,0:T(8,128)(2,1)} collective-permute-done((bf16[384,1280]{1,0:T(8,128)(2,1)S(1)}, bf16[384,1280]{1,0:T(8,128)(2,1)}, u32[]{:S(2)}, u32[]{:S(2)}) %collective-permute-start.2) | collective-permute-done | bytes 983072 | tf_op jit(solution)/shard_map/ppermute | solution.py:550
  56.5 14.0 %collective-permute-done.3.refs_7_ = bf16[384,1280]{1,0:T(8,128)(2,1)} collective-permute-done((bf16[384,1280]{1,0:T(8,128)(2,1)S(1)}, bf16[384,1280]{1,0:T(8,128)(2,1)}, u32[]{:S(2)}, u32[]{:S(2)}) %collective-permute-start.3) | collective-permute-done | bytes 983072 | tf_op jit(solution)/shard_map/ppermute | solution.py:555
  70.5 9.6 %all-to-all-done.refs_0_ = bf16[4,656,384]{2,1,0:T(8,128)(2,1)S(1)} async-done(((bf16[4,656,384]{2,1,0:T(8,128)(2,1)}), bf16[4,656,384]{2,1,0:T(8,128)(2,1)S(1)}, u32[]{:S(2)}, u32[]{:S(2)}) %all-to-all-start) | async-done | bytes 2015264 | tf_op jit(solution)/shard_map/all_to_all | solution.py:456
  91.1 23.8 %collective-permute-done.5.refs_5_ = bf16[192,1280]{1,0:T(8,128)(2,1)S(1)} collective-permute-done((bf16[192,1280]{1,0:T(8,128)(2,1)}, bf16[192,1280]{1,0:T(8,128)(2,1)S(1)}, u32[]{:S(2)}, u32[]{:S(2)}) %collective-permute-start.5) | collective-permute-done | bytes 491552 | tf_op jit(solution)/shard_map/ppermute | solution.py:552
  120.9 26.8 %collective-permute-done.10.refs_10_ = bf16[192,1280]{1,0:T(8,128)(2,1)} collective-permute-done((bf16[192,1280]{1,0:T(8,128)(2,1)S(1)}, bf16[192,1280]{1,0:T(8,128)(2,1)}, u32[]{:S(2)}, u32[]{:S(2)}) %collective-permute-start.10) | collective-permute-done | bytes 491552 | tf_op jit(solution)/shard_map/ppermute | solution.py:552
  147.7 4.8 %all-to-all-start.1 = ((bf16[4,640,384]{2,1,0:T(8,128)(2,1)}), bf16[4,640,384]{2,1,0:T(8,128)(2,1)}, u32[]{:S(2)}, u32[]{:S(2)}) async-start(bf16[4,640,384]{2,1,0:T(8,128)(2,1)} %cut_columns.3), calls=%async_computation.1 | async-start | bytes 3932160 | tf_op jit(solution)/shard_map/all_to_all | solution.py:456
  164.1 10.3 %project_heads.4 = (bf16[1,2,384,128]{3,2,1,0:T(8,128)(2,1)}, bf16[1,2,2,384,128]{4,3,2,1,0:T(8,128)(2,1)}) custom-call(s32[5]{0:T(128)} %concatenate.9.places_ref, f32[2,1]{1,0:T(2,128)} %get-tuple-element.155.gains_ref, bf16[4,656,384]{2,1,0:T(8,128)(2,1)} %copy-done.2, bf16[4,656,384]{2,1,0:T(8,128)(2,1)} %collective-permute-done.17.refs_1_.refs_2_, ...), custom_call_target="tpu_custom_call" | custom-call | tf_op jit(solution)/shard_map/project_heads/pallas_call | solution.py:257
  174.4 14.8 %collective-permute-done.15.refs_7_.refs_15_ = bf16[192,1280]{1,0:T(8,128)(2,1)S(1)} collective-permute-done((bf16[192,1280]{1,0:T(8,128)(2,1)}, bf16[192,1280]{1,0:T(8,128)(2,1)S(1)}, u32[]{:S(2)}, u32[]{:S(2)}) %collective-permute-start.15) | collective-permute-done | bytes 491552 | tf_op jit(solution)/shard_map/ppermute | solution.py:552
  189.3 5.7 %all-to-all-done.1.refs_0_.refs_1_ = bf16[4,640,384]{2,1,0:T(8,128)(2,1)} async-done(((bf16[4,640,384]{2,1,0:T(8,128)(2,1)}), bf16[4,640,384]{2,1,0:T(8,128)(2,1)}, u32[]{:S(2)}, u32[]{:S(2)}) %all-to-all-start.1) | async-done | bytes 1966112 | tf_op jit(solution)/shard_map/all_to_all | solution.py:456
  204.4 10.3 %project_heads.5 = (bf16[1,2,384,128]{3,2,1,0:T(8,128)(2,1)}, bf16[1,2,2,384,128]{4,3,2,1,0:T(8,128)(2,1)}) custom-call(s32[5]{0:T(128)} %concatenate.9.places_ref, f32[2,1]{1,0:T(2,128)} %get-tuple-element.154.gains_ref, bf16[4,640,384]{2,1,0:T(8,128)(2,1)} %all-to-all-done.1.refs_0_.refs_1_, bf16[4,640,384]{2,1,0:T(8,128)(2,1)} %copy-done.6, ...), custom_call_target="tpu_custom_call" | custom-call | tf_op jit(solution)/shard_map/project_heads/pallas_call | solution.py:257
  215.7 14.1 %project_heads.6 = (bf16[2,2,384,128]{3,2,1,0:T(8,128)(2,1)}, bf16[2,2,2,384,128]{4,3,2,1,0:T(8,128)(2,1)}) custom-call(s32[5]{0:T(128)} %concatenate.9.places_ref, f32[2,2]{1,0:T(2,128)} %bitcast.72, bf16[4,656,384]{2,1,0:T(8,128)(2,1)} %copy-done.2, bf16[4,640,384]{2,1,0:T(8,128)(2,1)} %all-to-all-done.1.refs_0_.refs_1_, ...), custom_call_target="tpu_custom_call" | custom-call | tf_op jit(solution)/shard_map/project_heads/pallas_call | solution.py:257
  234.3 9.9 %attend.2 = bf16[4,2,6,64,128]{4,3,2,1,0:T(8,128)(2,1)} custom-call(s32[3,24,8]{2,1,0:T(8,128)} %fusion.7.slots_ref, s32[3,24]{1,0:T(4,128)} %get-tuple-element.129.counts_ref, s32[24]{0:T(128)} %fusion.11.from_ref, s32[3,4]{1,0:T(4,128)} %reduce_max.9.most_ref, bf16[1,12,64,128]{3,2,1,0:T(8,128)(2,1)} %bitcast.67, bf16[1,2,12,64,128]{4,3,2,1,0:T(8,128)(2,1)} %bitcast.60, ...), custom_call_target="tpu_custom_call" | custom-call | tf_op jit(solution)/shard_map/attend/pallas_call | solution.py:352
  246.8 4.8 %all-to-all-start.2 = ((bf16[4,2,384,128]{3,2,1,0:T(8,128)(2,1)}), bf16[4,2,384,128]{3,2,1,0:T(8,128)(2,1)S(1)}, u32[]{:S(2)}, u32[]{:S(2)}) async-start(bf16[4,2,384,128]{3,2,1,0:T(8,128)(2,1)} %bitcast.53), calls=%async_computation.2 | async-start | bytes 1572864 | tf_op jit(solution)/shard_map/all_to_all | solution.py:456
  251.6 17.0 %project_heads.7 = (bf16[1,4,384,128]{3,2,1,0:T(8,128)(2,1)}, bf16[1,2,4,384,128]{4,3,2,1,0:T(8,128)(2,1)}) custom-call(s32[5]{0:T(128)} %concatenate.9.places_ref, f32[2,1]{1,0:T(2,128)} %get-tuple-element.153.gains_ref, bf16[4,640,384]{2,1,0:T(8,128)(2,1)} %copy-done.7, bf16[4,640,384]{2,1,0:T(8,128)(2,1)} %collective-permute-done.27.refs_1_, ...), custom_call_target="tpu_custom_call" | custom-call | tf_op jit(solution)/shard_map/project_heads/pallas_call | solution.py:257
  272.9 4.1 %out_blocks.6 = bf16[384,1280]{1,0:T(8,128)(2,1)} custom-call(s32[1]{0:T(128)} %bitcast.8.which_ref, s32[1]{0:T(128)} %bitcast.1.sign_ref, bf16[4,2,384,128]{3,2,1,0:T(8,128)(2,1)} %copy-done.4, bf16[4,384,5120]{2,1,0:T(8,128)(2,1)} %bitcast.43), custom_call_target="tpu_custom_call" | custom-call | tf_op jit(solution)/shard_map/out_blocks/pallas_call | solution.py:412
  280.0 6.3 %attend.3 = bf16[4,1,6,64,128]{4,3,2,1,0:T(8,128)(2,1)} custom-call(s32[3,24,8]{2,1,0:T(8,128)} %fusion.7.slots_ref, s32[3,24]{1,0:T(4,128)} %get-tuple-element.129.counts_ref, s32[24]{0:T(128)} %fusion.11.from_ref, s32[3,4]{1,0:T(4,128)} %reduce_max.9.most_ref, bf16[1,24,64,128]{3,2,1,0:T(8,128)(2,1)} %bitcast.65, bf16[1,2,24,64,128]{4,3,2,1,0:T(8,128)(2,1)} %bitcast.59, ...), custom_call_target="tpu_custom_call" | custom-call | tf_op jit(solution)/shard_map/attend/pallas_call | solution.py:352
  286.3 4.8 %all-to-all-start.4 = ((bf16[4,1,384,128]{3,2,1,0:T(8,128)(2,1)}), bf16[4,1,384,128]{3,2,1,0:T(8,128)(2,1)S(1)}, u32[]{:S(2)}, u32[]{:S(2)}) async-start(bf16[4,1,384,128]{3,2,1,0:T(8,128)(2,1)} %bitcast.54), calls=%async_computation.4 | async-start | bytes 786432 | tf_op jit(solution)/shard_map/all_to_all | solution.py:456
  291.8 6.3 %out_blocks.7.refs_0_ = f32[2,384,1280]{2,1,0:T(8,128)} custom-call(s32[2]{0:T(128)} %pad_add_fusion.which_ref, s32[1]{0:T(128)} %bitcast.1.sign_ref, bf16[4,2,384,128]{3,2,1,0:T(8,128)(2,1)} %copy-done.4, bf16[4,384,5120]{2,1,0:T(8,128)(2,1)} %bitcast.44), custom_call_target="tpu_custom_call" | custom-call | tf_op jit(solution)/shard_map/out_blocks/pallas_call | solution.py:412
  298.1 4.1 %all-to-all-done.4.mixed_ref = bf16[4,1,384,128]{3,2,1,0:T(8,128)(2,1)S(1)} async-done(((bf16[4,1,384,128]{3,2,1,0:T(8,128)(2,1)}), bf16[4,1,384,128]{3,2,1,0:T(8,128)(2,1)S(1)}, u32[]{:S(2)}, u32[]{:S(2)}) %all-to-all-start.4) | async-done | bytes 393248 | tf_op jit(solution)/shard_map/all_to_all | solution.py:456
  303.0 5.8 %out_blocks.8 = (bf16[384,1280]{1,0:T(8,128)(2,1)}, bf16[384,1280]{1,0:T(8,128)(2,1)}) custom-call(s32[2]{0:T(128)} %pad_add_fusion.which_ref, s32[1]{0:T(128)} %bitcast.1.sign_ref, bf16[4,1,384,128]{3,2,1,0:T(8,128)(2,1)} %copy-done.10, bf16[4,384,5120]{2,1,0:T(8,128)(2,1)} %bitcast.45, f32[2,384,1280]{2,1,0:T(8,128)} %out_blocks.7.refs_0_), custom_call_target="tpu_custom_call" | custom-call | tf_op jit(solution)/shard_map/out_blocks/pallas_call | solution.py:412
  316.9 5.1 %out_blocks.10 = f32[384,1280]{1,0:T(8,128)} custom-call(s32[1]{0:T(128)} %bitcast.which_ref, s32[1]{0:T(128)} %bitcast.1.sign_ref, bf16[4,2,384,128]{3,2,1,0:T(8,128)(2,1)} %copy-done.4, bf16[4,384,5120]{2,1,0:T(8,128)(2,1)} %bitcast.46, f32[1,384,1280]{2,1,0:T(8,128)} %bitcast.51), custom_call_target="tpu_custom_call" | custom-call | tf_op jit(solution)/shard_map/out_blocks/pallas_call | solution.py:412
  326.0 7.2 %collective-permute-done.31 = bf16[384,1280]{1,0:T(8,128)(2,1)S(1)} collective-permute-done((bf16[384,1280]{1,0:T(8,128)(2,1)}, bf16[384,1280]{1,0:T(8,128)(2,1)S(1)}, u32[]{:S(2)}, u32[]{:S(2)}) %collective-permute-start.31) | collective-permute-done | bytes 983072 | tf_op jit(solution)/shard_map/ppermute | solution.py:652
  (161 shorter events, 98.1 us)
Async XLA Ops:
  6.2 74.0 %all-to-all-start = ((bf16[4,656,384]{2,1,0:T(8,128)(2,1)}), bf16[4,656,384]{2,1,0:T(8,128)(2,1)S(1)}, u32[]{:S(2)}, u32[]{:S(2)}) async-start(bf16[4,656,384]{2,1,0:T(8,128)(2,1)} %cut_columns.5), calls=%async_computation | async-start | bytes 4030464 | tf_op jit(solution)/shard_map/all_to_all | solution.py:456
  34.8 21.7 %collective-permute-start.2 = (bf16[384,1280]{1,0:T(8,128)(2,1)S(1)}, bf16[384,1280]{1,0:T(8,128)(2,1)}, u32[]{:S(2)}, u32[]{:S(2)}) collective-permute-start(bf16[384,1280]{1,0:T(8,128)(2,1)S(1)} %multiply_convert_fusion.refs_2_), channel_id=1, source_target_pairs={{0,1},{1,0},{2,3},{3,2},{4,5},{5,4},{6,7},{7,6},{8,9},{9,8},{10,11... | collective-permute-start | bytes 2949128 | tf_op jit(solution)/shard_map/ppermute | solution.py:550
  36.5 33.9 %collective-permute-start.3 = (bf16[384,1280]{1,0:T(8,128)(2,1)S(1)}, bf16[384,1280]{1,0:T(8,128)(2,1)}, u32[]{:S(2)}, u32[]{:S(2)}) collective-permute-start(bf16[384,1280]{1,0:T(8,128)(2,1)S(1)} %multiply_convert_fusion.refs_2_), channel_id=1, source_target_pairs={{0,4},{4,8},{8,12},{12,0},{1,5},{5,9},{9,13},{13,1},{2,6},{6,10},{... | collective-permute-start | bytes 2949128 | tf_op jit(solution)/shard_map/ppermute | solution.py:555
  38.6 31.9 %collective-permute-start.4 = (bf16[384,1280]{1,0:T(8,128)(2,1)S(1)}, bf16[384,1280]{1,0:T(8,128)(2,1)}, u32[]{:S(2)}, u32[]{:S(2)}) collective-permute-start(bf16[384,1280]{1,0:T(8,128)(2,1)S(1)} %multiply_convert_fusion.refs_2_), channel_id=1, source_target_pairs={{0,16},{16,0},{1,17},{17,1},{2,18},{18,2},{3,19},{19,3},{4,20},{20... | collective-permute-start | bytes 2949128 | tf_op jit(solution)/shard_map/ppermute | solution.py:549
  80.1 34.7 %collective-permute-start.6 = (bf16[384,1280]{1,0:T(8,128)(2,1)}, bf16[384,1280]{1,0:T(8,128)(2,1)S(1)}, u32[]{:S(2)}, u32[]{:S(2)}) collective-permute-start(bf16[384,1280]{1,0:T(8,128)(2,1)} %collective-permute-done.3.refs_7_), channel_id=1, source_target_pairs={{0,1},{1,0},{2,3},{3,2},{4,5},{5,4},{6,7},{7,6},{8,9},{9,8},{10,11... | collective-permute-start | bytes 2949128 | tf_op jit(solution)/shard_map/ppermute | solution.py:550
  81.6 33.2 %collective-permute-start.7 = (bf16[384,1280]{1,0:T(8,128)(2,1)}, bf16[384,1280]{1,0:T(8,128)(2,1)}, u32[]{:S(2)}, u32[]{:S(2)}) collective-permute-start(bf16[384,1280]{1,0:T(8,128)(2,1)} %collective-permute-done.3.refs_7_), channel_id=1, source_target_pairs={{0,4},{4,8},{8,12},{12,0},{1,5},{5,9},{9,13},{13,1},{2,6},{6,10},{... | collective-permute-start | bytes 2949128 | tf_op jit(solution)/shard_map/ppermute | solution.py:555
  81.7 33.2 %collective-permute-start.8 = (bf16[384,1280]{1,0:T(8,128)(2,1)}, bf16[384,1280]{1,0:T(8,128)(2,1)}, u32[]{:S(2)}, u32[]{:S(2)}) collective-permute-start(bf16[384,1280]{1,0:T(8,128)(2,1)} %collective-permute-done.3.refs_7_), channel_id=1, source_target_pairs={{0,16},{16,0},{1,17},{17,1},{2,18},{18,2},{3,19},{19,3},{4,20},{20... | collective-permute-start | bytes 2949128 | tf_op jit(solution)/shard_map/ppermute | solution.py:549
  85.0 29.8 %collective-permute-start.5 = (bf16[192,1280]{1,0:T(8,128)(2,1)}, bf16[192,1280]{1,0:T(8,128)(2,1)S(1)}, u32[]{:S(2)}, u32[]{:S(2)}) collective-permute-start(bf16[192,1280]{1,0:T(8,128)(2,1)} %slice.52), channel_id=1, source_target_pairs={{0,16},{16,0},{1,17},{17,1},{2,18},{18,2},{3,19},{19,3},{4,20},{20... | collective-permute-start | bytes 1474568 | tf_op jit(solution)/shard_map/ppermute | solution.py:552
  87.4 27.5 %collective-permute-start.9 = (bf16[192,1280]{1,0:T(8,128)(2,1)}, bf16[192,1280]{1,0:T(8,128)(2,1)}, u32[]{:S(2)}, u32[]{:S(2)}) collective-permute-start(bf16[192,1280]{1,0:T(8,128)(2,1)} %slice.53), channel_id=1, source_target_pairs={{0,1},{1,0},{2,3},{3,2},{4,5},{5,4},{6,7},{7,6},{8,9},{9,8},{10,11... | collective-permute-start | bytes 1474568 | tf_op jit(solution)/shard_map/ppermute | solution.py:553
  114.9 32.8 %collective-permute-start.11 = (bf16[384,1280]{1,0:T(8,128)(2,1)}, bf16[384,1280]{1,0:T(8,128)(2,1)}, u32[]{:S(2)}, u32[]{:S(2)}) collective-permute-start(bf16[384,1280]{1,0:T(8,128)(2,1)} %collective-permute-done.7.refs_4_.refs_12_), channel_id=1, source_target_pairs={{0,1},{1,0},{2,3},{3,2},{4,5},{5,4},{6,7},{7,6},{8,9},{9,8},{10,11... | collective-permute-start | bytes 2949128 | tf_op jit(solution)/shard_map/ppermute | solution.py:550
  115.5 32.2 %collective-permute-start.12 = (bf16[384,1280]{1,0:T(8,128)(2,1)}, bf16[384,1280]{1,0:T(8,128)(2,1)}, u32[]{:S(2)}, u32[]{:S(2)}) collective-permute-start(bf16[384,1280]{1,0:T(8,128)(2,1)} %collective-permute-done.7.refs_4_.refs_12_), channel_id=1, source_target_pairs={{0,4},{4,8},{8,12},{12,0},{1,5},{5,9},{9,13},{13,1},{2,6},{6,10},{... | collective-permute-start | bytes 2949128 | tf_op jit(solution)/shard_map/ppermute | solution.py:555
  116.1 31.6 %collective-permute-start.13 = (bf16[384,1280]{1,0:T(8,128)(2,1)}, bf16[384,1280]{1,0:T(8,128)(2,1)}, u32[]{:S(2)}, u32[]{:S(2)}) collective-permute-start(bf16[384,1280]{1,0:T(8,128)(2,1)} %collective-permute-done.7.refs_4_.refs_12_), channel_id=1, source_target_pairs={{0,16},{16,0},{1,17},{17,1},{2,18},{18,2},{3,19},{19,3},{4,20},{20... | collective-permute-start | bytes 2949128 | tf_op jit(solution)/shard_map/ppermute | solution.py:549
  117.6 30.0 %collective-permute-start.10 = (bf16[192,1280]{1,0:T(8,128)(2,1)S(1)}, bf16[192,1280]{1,0:T(8,128)(2,1)}, u32[]{:S(2)}, u32[]{:S(2)}) collective-permute-start(bf16[192,1280]{1,0:T(8,128)(2,1)S(1)} %slice.58), channel_id=1, source_target_pairs={{0,16},{16,0},{1,17},{17,1},{2,18},{18,2},{3,19},{19,3},{4,20},{20... | collective-permute-start | bytes 1474568 | tf_op jit(solution)/shard_map/ppermute | solution.py:552
  119.3 28.4 %collective-permute-start.14 = (bf16[192,1280]{1,0:T(8,128)(2,1)S(1)}, bf16[192,1280]{1,0:T(8,128)(2,1)}, u32[]{:S(2)}, u32[]{:S(2)}) collective-permute-start(bf16[192,1280]{1,0:T(8,128)(2,1)S(1)} %slice.59), channel_id=1, source_target_pairs={{0,1},{1,0},{2,3},{3,2},{4,5},{5,4},{6,7},{7,6},{8,9},{9,8},{10,11... | collective-permute-start | bytes 1474568 | tf_op jit(solution)/shard_map/ppermute | solution.py:553
  147.7 47.2 %all-to-all-start.1 = ((bf16[4,640,384]{2,1,0:T(8,128)(2,1)}), bf16[4,640,384]{2,1,0:T(8,128)(2,1)}, u32[]{:S(2)}, u32[]{:S(2)}) async-start(bf16[4,640,384]{2,1,0:T(8,128)(2,1)} %cut_columns.3), calls=%async_computation.1 | async-start | bytes 3932160 | tf_op jit(solution)/shard_map/all_to_all | solution.py:456
  153.1 36.1 %collective-permute-start.16 = (bf16[384,1280]{1,0:T(8,128)(2,1)}, bf16[384,1280]{1,0:T(8,128)(2,1)S(1)}, u32[]{:S(2)}, u32[]{:S(2)}) collective-permute-start(bf16[384,1280]{1,0:T(8,128)(2,1)} %collective-permute-done.12.refs_9_.refs_17_), channel_id=1, source_target_pairs={{0,1},{1,0},{2,3},{3,2},{4,5},{5,4},{6,7},{7,6},{8,9},{9,8},{10,11... | collective-permute-start | bytes 2949128 | tf_op jit(solution)/shard_map/ppermute | solution.py:550
  154.6 34.7 %collective-permute-start.18 = (bf16[384,1280]{1,0:T(8,128)(2,1)}, bf16[384,1280]{1,0:T(8,128)(2,1)}, u32[]{:S(2)}, u32[]{:S(2)}) collective-permute-start(bf16[384,1280]{1,0:T(8,128)(2,1)} %collective-permute-done.12.refs_9_.refs_17_), channel_id=1, source_target_pairs={{0,16},{16,0},{1,17},{17,1},{2,18},{18,2},{3,19},{19,3},{4,20},{20... | collective-permute-start | bytes 2949128 | tf_op jit(solution)/shard_map/ppermute | solution.py:549
  160.2 29.0 %collective-permute-start.15 = (bf16[192,1280]{1,0:T(8,128)(2,1)}, bf16[192,1280]{1,0:T(8,128)(2,1)S(1)}, u32[]{:S(2)}, u32[]{:S(2)}) collective-permute-start(bf16[192,1280]{1,0:T(8,128)(2,1)} %slice.60), channel_id=1, source_target_pairs={{0,16},{16,0},{1,17},{17,1},{2,18},{18,2},{3,19},{19,3},{4,20},{20... | collective-permute-start | bytes 1474568 | tf_op jit(solution)/shard_map/ppermute | solution.py:552
  160.7 28.5 %collective-permute-start.19 = (bf16[192,1280]{1,0:T(8,128)(2,1)}, bf16[192,1280]{1,0:T(8,128)(2,1)}, u32[]{:S(2)}, u32[]{:S(2)}) collective-permute-start(bf16[192,1280]{1,0:T(8,128)(2,1)} %slice.62), channel_id=1, source_target_pairs={{0,1},{1,0},{2,3},{3,2},{4,5},{5,4},{6,7},{7,6},{8,9},{9,8},{10,11... | collective-permute-start | bytes 1474568 | tf_op jit(solution)/shard_map/ppermute | solution.py:553
  195.0 49.2 %all-to-all-start.3 = ((bf16[4,640,384]{2,1,0:T(8,128)(2,1)}), bf16[4,640,384]{2,1,0:T(8,128)(2,1)S(1)}, u32[]{:S(2)}, u32[]{:S(2)}) async-start(bf16[4,640,384]{2,1,0:T(8,128)(2,1)} %cut_columns.4), calls=%async_computation.3 | async-start | bytes 3932160 | tf_op jit(solution)/shard_map/all_to_all | solution.py:456
  244.3 32.8 %collective-permute-start.26 = (bf16[4,128,1280]{2,1,0:T(8,128)(2,1)}, bf16[4,128,1280]{2,1,0:T(8,128)(2,1)}, u32[]{:S(2)}, u32[]{:S(2)}) collective-permute-start(bf16[4,128,1280]{2,1,0:T(8,128)(2,1)} %constant_dynamic-slice_fusion), channel_id=1, source_target_pairs={{0,17},{1,16},{16,1},{17,0},{2,19},{3,18},{18,3},{19,2},{4,21},{5,... | collective-permute-start | bytes 3932168 | tf_op jit(solution)/shard_map/ppermute | solution.py:598
  246.8 25.2 %all-to-all-start.2 = ((bf16[4,2,384,128]{3,2,1,0:T(8,128)(2,1)}), bf16[4,2,384,128]{3,2,1,0:T(8,128)(2,1)S(1)}, u32[]{:S(2)}, u32[]{:S(2)}) async-start(bf16[4,2,384,128]{3,2,1,0:T(8,128)(2,1)} %bitcast.53), calls=%async_computation.2 | async-start | bytes 1572864 | tf_op jit(solution)/shard_map/all_to_all | solution.py:456
  277.0 25.7 %collective-permute-start.29 = (bf16[384,1280]{1,0:T(8,128)(2,1)}, bf16[384,1280]{1,0:T(8,128)(2,1)S(1)}, u32[]{:S(2)}, u32[]{:S(2)}) collective-permute-start(bf16[384,1280]{1,0:T(8,128)(2,1)} %out_blocks.6), channel_id=1, source_target_pairs={{0,17},{1,16},{16,1},{17,0},{2,19},{3,18},{18,3},{19,2},{4,21},{5,... | collective-permute-start | bytes 2949128 | tf_op jit(solution)/shard_map/ppermute | solution.py:618
  312.1 21.1 %collective-permute-start.31 = (bf16[384,1280]{1,0:T(8,128)(2,1)}, bf16[384,1280]{1,0:T(8,128)(2,1)S(1)}, u32[]{:S(2)}, u32[]{:S(2)}) collective-permute-start(bf16[384,1280]{1,0:T(8,128)(2,1)} %get-tuple-element.149), channel_id=1, source_target_pairs={{0,1},{1,0},{2,3},{3,2},{4,5},{5,4},{6,7},{7,6},{8,9},{9,8},{10,11... | collective-permute-start | bytes 2949128 | tf_op jit(solution)/shard_map/ppermute | solution.py:652
  (38 other events, 526.2 us)

commit v16 on v15

--- a/solution.py
+++ b/solution.py
@@ -554,9 +554,9 @@
         if step < chips:
             sent["next"] = lax.ppermute(shard, "chip", ring)
         if phase == 0:
-            sent["weights"] = weights_own.pop()
             sent["cuts"] = cuts[1:]
         if phase == 1:
+            sent["weights"] = weights_own.pop()
             sent["places"] = places
             sent["gains"] = gains
             sent["corner"] = lax.dynamic_slice(
@@ -575,9 +575,9 @@
             sent["places"] = project(0, 1, 1, 0, early, held_places)
         sent, shard = lax.optimization_barrier((sent, shard))
         if phase == 0:
-            weights_own.append(sent["weights"])
             cuts[1:] = sent["cuts"]
         if phase == 1:
+            weights_own.append(sent["weights"])
             gains, corner = sent["gains"], sent["corner"]
         if straight is not None:
             rounds.append(straight + (sent["first"], sent["second"]))

time: 338 us -> 336 us (level)
  waiting for transfers between devices: 129 us -> 118 us
  starting transfers between devices: 56.1 us -> 66 us
    all_to_all x5, waiting for transfers between devices: 22.8 us -> 12.4 us  [exchange(): lax.all_to_all(array, 'chip', split_axis=0, concat_axis=0, tiled=True)]
    ppermute x3, starting transfers between devices: 2.68 us -> 12.9 us  [per_device_by_heads(): sent['next'] = lax.ppermute(shard, 'chip', ring)]
where the time goes in v16:
time: 336 us; the launch traced here: 335 us
  waiting for transfers between devices  118 us (35%)
  Pallas kernels  108 us (32%)
  starting transfers between devices  66 us (20%)
  local copies, waits for them, and re-layouts  21 us (6%)
  matrix products  12.7 us (4%)
  other arithmetic  8.98 us (3%)
    ppermute x4, waiting for transfers between devices, per_device_by_heads(): sent['first'] = lax.ppermute(straight[2][:half], 'role', swap)  64.3 us
    pallas_call x4, Pallas kernels, project_heads(): pl.pallas_call(body, in_specs=[in_smem(), in_smem()] + [in_hbm()] * (2 *...  51.6 us
    pallas_call x6, Pallas kernels, out_blocks(): pl.pallas_call(body, grid_spec=pltpu.PrefetchScalarGridSpec(num_scalar_pr...  29.1 us
    all_to_all x5, starting transfers between devices, exchange(): lax.all_to_all(array, 'chip', split_axis=0, concat_axis=0, tiled=True)  24.3 us
    pallas_call x2, Pallas kernels, attend(): pl.pallas_call(body, in_specs=[in_smem()] * 4 + [in_hbm()] * len(arrays),...  16.2 us
    ppermute x3, waiting for transfers between devices, per_device_by_heads(): sent['next'] = lax.ppermute(shard, 'chip', ring)  14 us
    ppermute x3, starting transfers between devices, per_device_by_heads(): sent['next'] = lax.ppermute(shard, 'chip', ring)  12.9 us
    dot_general x1, matrix products, per_device_by_heads(): jnp.dot(hidden_rows, gen_weight, preferred_element_type=jnp.float32)  12.7 us
  transfers between devices with their start and end apart: 38, of which 17 were waited for; matrix products, arithmetic and copies ran while one was open for 10% of the time, Pallas kernels for 31%

profile of v16, /device:TPU:0, one launch (start us, length us, event | category | flops | bytes accessed | tf_op | source)
XLA Modules:
  0.0 334.9 jit_solution(11479001762910705614)
XLA Ops:
  6.2 6.4 %all-to-all-start = ((bf16[4,656,384]{2,1,0:T(8,128)(2,1)}), bf16[4,656,384]{2,1,0:T(8,128)(2,1)S(1)}, u32[]{:S(2)}, u32[]{:S(2)}) async-start(bf16[4,656,384]{2,1,0:T(8,128)(2,1)} %cut_columns.5), calls=%async_computation | async-start | bytes 4030464 | tf_op jit(solution)/shard_map/all_to_all | solution.py:456
  13.0 12.7 %multiply_reduce_fusion = (f32[384]{0:T(512)S(1)}, f32[384,1280]{1,0:T(8,128)}) fusion(bf16[384,5120]{1,0:T(8,128)(2,1)} %param.11, s32[]{:T(128)S(6)} %select_n.48, f32[384]{0:T(512)S(1)} %mul.87, bf16[384,5120]{1,0:T(8,128)(2,1)} %param.9, bf16[5120,1280]{1,0:T(8,128)(2,1)} %param.10, f32[384]{0:T(512)S(1)} %mul.83), kind=kOutput, calls=%fused_computation.5 | convolution fusion | flops 5036604928 | bytes 19993092 | tf_op jit(solution)/shard_map/dot_general | solution.py:474
  47.4 9.1 %collective-permute-done.2.refs_4_ = bf16[384,1280]{1,0:T(8,128)(2,1)} collective-permute-done((bf16[384,1280]{1,0:T(8,128)(2,1)S(1)}, bf16[384,1280]{1,0:T(8,128)(2,1)}, u32[]{:S(2)}, u32[]{:S(2)}) %collective-permute-start.2) | collective-permute-done | bytes 983072 | tf_op jit(solution)/shard_map/ppermute | solution.py:550
  56.5 14.0 %collective-permute-done.3.refs_7_ = bf16[384,1280]{1,0:T(8,128)(2,1)} collective-permute-done((bf16[384,1280]{1,0:T(8,128)(2,1)S(1)}, bf16[384,1280]{1,0:T(8,128)(2,1)}, u32[]{:S(2)}, u32[]{:S(2)}) %collective-permute-start.3) | collective-permute-done | bytes 983072 | tf_op jit(solution)/shard_map/ppermute | solution.py:555
  72.0 8.3 %collective-permute-start.7 = (bf16[384,1280]{1,0:T(8,128)(2,1)}, bf16[384,1280]{1,0:T(8,128)(2,1)}, u32[]{:S(2)}, u32[]{:S(2)}) collective-permute-start(bf16[384,1280]{1,0:T(8,128)(2,1)} %collective-permute-done.3.refs_7_), channel_id=1, source_target_pairs={{0,4},{4,8},{8,12},{12,0},{1,5},{5,9},{9,13},{13,1},{2,6},{6,10},{... | collective-permute-start | bytes 2949128 | tf_op jit(solution)/shard_map/ppermute | solution.py:555
  89.8 23.1 %collective-permute-done.5.refs_5_ = bf16[192,1280]{1,0:T(8,128)(2,1)S(1)} collective-permute-done((bf16[192,1280]{1,0:T(8,128)(2,1)}, bf16[192,1280]{1,0:T(8,128)(2,1)S(1)}, u32[]{:S(2)}, u32[]{:S(2)}) %collective-permute-start.5) | collective-permute-done | bytes 491552 | tf_op jit(solution)/shard_map/ppermute | solution.py:552
  120.8 26.4 %collective-permute-done.10.refs_10_ = bf16[192,1280]{1,0:T(8,128)(2,1)} collective-permute-done((bf16[192,1280]{1,0:T(8,128)(2,1)S(1)}, bf16[192,1280]{1,0:T(8,128)(2,1)}, u32[]{:S(2)}, u32[]{:S(2)}) %collective-permute-start.10) | collective-permute-done | bytes 491552 | tf_op jit(solution)/shard_map/ppermute | solution.py:552
  147.3 4.4 %all-to-all-start.1 = ((bf16[4,640,384]{2,1,0:T(8,128)(2,1)}), bf16[4,640,384]{2,1,0:T(8,128)(2,1)}, u32[]{:S(2)}, u32[]{:S(2)}) async-start(bf16[4,640,384]{2,1,0:T(8,128)(2,1)} %cut_columns.3), calls=%async_computation.1 | async-start | bytes 3932160 | tf_op jit(solution)/shard_map/all_to_all | solution.py:456
  163.4 10.3 %project_heads.4 = (bf16[1,2,384,128]{3,2,1,0:T(8,128)(2,1)}, bf16[1,2,2,384,128]{4,3,2,1,0:T(8,128)(2,1)}) custom-call(s32[5]{0:T(128)} %concatenate.9.places_ref, f32[2,1]{1,0:T(2,128)} %get-tuple-element.155.gains_ref, bf16[4,656,384]{2,1,0:T(8,128)(2,1)} %copy-done.2, bf16[4,656,384]{2,1,0:T(8,128)(2,1)} %collective-permute-done.17.refs_1_.refs_2_, ...), custom_call_target="tpu_custom_call" | custom-call | tf_op jit(solution)/shard_map/project_heads/pallas_call | solution.py:257
  173.7 14.7 %collective-permute-done.15.refs_7_.refs_15_ = bf16[192,1280]{1,0:T(8,128)(2,1)S(1)} collective-permute-done((bf16[192,1280]{1,0:T(8,128)(2,1)}, bf16[192,1280]{1,0:T(8,128)(2,1)S(1)}, u32[]{:S(2)}, u32[]{:S(2)}) %collective-permute-start.15) | collective-permute-done | bytes 491552 | tf_op jit(solution)/shard_map/ppermute | solution.py:552
  188.4 5.0 %all-to-all-done.1.refs_0_.refs_1_ = bf16[4,640,384]{2,1,0:T(8,128)(2,1)} async-done(((bf16[4,640,384]{2,1,0:T(8,128)(2,1)}), bf16[4,640,384]{2,1,0:T(8,128)(2,1)}, u32[]{:S(2)}, u32[]{:S(2)}) %all-to-all-start.1) | async-done | bytes 1966112 | tf_op jit(solution)/shard_map/all_to_all | solution.py:456
  202.8 10.3 %project_heads.5 = (bf16[1,2,384,128]{3,2,1,0:T(8,128)(2,1)}, bf16[1,2,2,384,128]{4,3,2,1,0:T(8,128)(2,1)}) custom-call(s32[5]{0:T(128)} %concatenate.9.places_ref, f32[2,1]{1,0:T(2,128)} %get-tuple-element.154.gains_ref, bf16[4,640,384]{2,1,0:T(8,128)(2,1)} %all-to-all-done.1.refs_0_.refs_1_, bf16[4,640,384]{2,1,0:T(8,128)(2,1)} %copy-done.6, ...), custom_call_target="tpu_custom_call" | custom-call | tf_op jit(solution)/shard_map/project_heads/pallas_call | solution.py:257
  214.1 14.0 %project_heads.6 = (bf16[2,2,384,128]{3,2,1,0:T(8,128)(2,1)}, bf16[2,2,2,384,128]{4,3,2,1,0:T(8,128)(2,1)}) custom-call(s32[5]{0:T(128)} %concatenate.9.places_ref, f32[2,2]{1,0:T(2,128)} %bitcast.72, bf16[4,656,384]{2,1,0:T(8,128)(2,1)} %copy-done.2, bf16[4,640,384]{2,1,0:T(8,128)(2,1)} %all-to-all-done.1.refs_0_.refs_1_, ...), custom_call_target="tpu_custom_call" | custom-call | tf_op jit(solution)/shard_map/project_heads/pallas_call | solution.py:257
  232.7 9.9 %attend.2 = bf16[4,2,6,64,128]{4,3,2,1,0:T(8,128)(2,1)} custom-call(s32[3,24,8]{2,1,0:T(8,128)} %fusion.7.slots_ref, s32[3,24]{1,0:T(4,128)} %get-tuple-element.129.counts_ref, s32[24]{0:T(128)} %fusion.11.from_ref, s32[3,4]{1,0:T(4,128)} %reduce_max.9.most_ref, bf16[1,12,64,128]{3,2,1,0:T(8,128)(2,1)} %bitcast.67, bf16[1,2,12,64,128]{4,3,2,1,0:T(8,128)(2,1)} %bitcast.60, ...), custom_call_target="tpu_custom_call" | custom-call | tf_op jit(solution)/shard_map/attend/pallas_call | solution.py:352
  245.0 4.8 %all-to-all-start.2 = ((bf16[4,2,384,128]{3,2,1,0:T(8,128)(2,1)}), bf16[4,2,384,128]{3,2,1,0:T(8,128)(2,1)S(1)}, u32[]{:S(2)}, u32[]{:S(2)}) async-start(bf16[4,2,384,128]{3,2,1,0:T(8,128)(2,1)} %bitcast.53), calls=%async_computation.2 | async-start | bytes 1572864 | tf_op jit(solution)/shard_map/all_to_all | solution.py:456
  249.8 17.0 %project_heads.7 = (bf16[1,4,384,128]{3,2,1,0:T(8,128)(2,1)}, bf16[1,2,4,384,128]{4,3,2,1,0:T(8,128)(2,1)}) custom-call(s32[5]{0:T(128)} %concatenate.9.places_ref, f32[2,1]{1,0:T(2,128)} %get-tuple-element.153.gains_ref, bf16[4,640,384]{2,1,0:T(8,128)(2,1)} %copy-done.7, bf16[4,640,384]{2,1,0:T(8,128)(2,1)} %collective-permute-done.27.refs_1_, ...), custom_call_target="tpu_custom_call" | custom-call | tf_op jit(solution)/shard_map/project_heads/pallas_call | solution.py:257
  271.1 4.1 %out_blocks.6 = bf16[384,1280]{1,0:T(8,128)(2,1)} custom-call(s32[1]{0:T(128)} %bitcast.8.which_ref, s32[1]{0:T(128)} %bitcast.1.sign_ref, bf16[4,2,384,128]{3,2,1,0:T(8,128)(2,1)} %copy-done.4, bf16[4,384,5120]{2,1,0:T(8,128)(2,1)} %bitcast.43), custom_call_target="tpu_custom_call" | custom-call | tf_op jit(solution)/shard_map/out_blocks/pallas_call | solution.py:412
  278.2 6.3 %attend.3 = bf16[4,1,6,64,128]{4,3,2,1,0:T(8,128)(2,1)} custom-call(s32[3,24,8]{2,1,0:T(8,128)} %fusion.7.slots_ref, s32[3,24]{1,0:T(4,128)} %get-tuple-element.129.counts_ref, s32[24]{0:T(128)} %fusion.11.from_ref, s32[3,4]{1,0:T(4,128)} %reduce_max.9.most_ref, bf16[1,24,64,128]{3,2,1,0:T(8,128)(2,1)} %bitcast.65, bf16[1,2,24,64,128]{4,3,2,1,0:T(8,128)(2,1)} %bitcast.59, ...), custom_call_target="tpu_custom_call" | custom-call | tf_op jit(solution)/shard_map/attend/pallas_call | solution.py:352
  284.6 4.8 %all-to-all-start.4 = ((bf16[4,1,384,128]{3,2,1,0:T(8,128)(2,1)}), bf16[4,1,384,128]{3,2,1,0:T(8,128)(2,1)S(1)}, u32[]{:S(2)}, u32[]{:S(2)}) async-start(bf16[4,1,384,128]{3,2,1,0:T(8,128)(2,1)} %bitcast.54), calls=%async_computation.4 | async-start | bytes 786432 | tf_op jit(solution)/shard_map/all_to_all | solution.py:456
  290.0 6.3 %out_blocks.7.refs_0_ = f32[2,384,1280]{2,1,0:T(8,128)} custom-call(s32[2]{0:T(128)} %pad_add_fusion.which_ref, s32[1]{0:T(128)} %bitcast.1.sign_ref, bf16[4,2,384,128]{3,2,1,0:T(8,128)(2,1)} %copy-done.4, bf16[4,384,5120]{2,1,0:T(8,128)(2,1)} %bitcast.44), custom_call_target="tpu_custom_call" | custom-call | tf_op jit(solution)/shard_map/out_blocks/pallas_call | solution.py:412
  296.3 4.1 %all-to-all-done.4.mixed_ref = bf16[4,1,384,128]{3,2,1,0:T(8,128)(2,1)S(1)} async-done(((bf16[4,1,384,128]{3,2,1,0:T(8,128)(2,1)}), bf16[4,1,384,128]{3,2,1,0:T(8,128)(2,1)S(1)}, u32[]{:S(2)}, u32[]{:S(2)}) %all-to-all-start.4) | async-done | bytes 393248 | tf_op jit(solution)/shard_map/all_to_all | solution.py:456
  301.2 5.8 %out_blocks.8 = (bf16[384,1280]{1,0:T(8,128)(2,1)}, bf16[384,1280]{1,0:T(8,128)(2,1)}) custom-call(s32[2]{0:T(128)} %pad_add_fusion.which_ref, s32[1]{0:T(128)} %bitcast.1.sign_ref, bf16[4,1,384,128]{3,2,1,0:T(8,128)(2,1)} %copy-done.10, bf16[4,384,5120]{2,1,0:T(8,128)(2,1)} %bitcast.45, f32[2,384,1280]{2,1,0:T(8,128)} %out_blocks.7.refs_0_), custom_call_target="tpu_custom_call" | custom-call | tf_op jit(solution)/shard_map/out_blocks/pallas_call | solution.py:412
  315.3 5.1 %out_blocks.10 = f32[384,1280]{1,0:T(8,128)} custom-call(s32[1]{0:T(128)} %bitcast.which_ref, s32[1]{0:T(128)} %bitcast.1.sign_ref, bf16[4,2,384,128]{3,2,1,0:T(8,128)(2,1)} %copy-done.4, bf16[4,384,5120]{2,1,0:T(8,128)(2,1)} %bitcast.46, f32[1,384,1280]{2,1,0:T(8,128)} %bitcast.51), custom_call_target="tpu_custom_call" | custom-call | tf_op jit(solution)/shard_map/out_blocks/pallas_call | solution.py:412
  324.5 7.0 %collective-permute-done.31 = bf16[384,1280]{1,0:T(8,128)(2,1)S(1)} collective-permute-done((bf16[384,1280]{1,0:T(8,128)(2,1)}, bf16[384,1280]{1,0:T(8,128)(2,1)S(1)}, u32[]{:S(2)}, u32[]{:S(2)}) %collective-permute-start.31) | collective-permute-done | bytes 983072 | tf_op jit(solution)/shard_map/ppermute | solution.py:652
  (161 shorter events, 100.3 us)
Async XLA Ops:
  6.2 106.7 %all-to-all-start = ((bf16[4,656,384]{2,1,0:T(8,128)(2,1)}), bf16[4,656,384]{2,1,0:T(8,128)(2,1)S(1)}, u32[]{:S(2)}, u32[]{:S(2)}) async-start(bf16[4,656,384]{2,1,0:T(8,128)(2,1)} %cut_columns.5), calls=%async_computation | async-start | bytes 4030464 | tf_op jit(solution)/shard_map/all_to_all | solution.py:456
  34.8 21.7 %collective-permute-start.2 = (bf16[384,1280]{1,0:T(8,128)(2,1)S(1)}, bf16[384,1280]{1,0:T(8,128)(2,1)}, u32[]{:S(2)}, u32[]{:S(2)}) collective-permute-start(bf16[384,1280]{1,0:T(8,128)(2,1)S(1)} %multiply_convert_fusion.refs_2_), channel_id=1, source_target_pairs={{0,1},{1,0},{2,3},{3,2},{4,5},{5,4},{6,7},{7,6},{8,9},{9,8},{10,11... | collective-permute-start | bytes 2949128 | tf_op jit(solution)/shard_map/ppermute | solution.py:550
  36.5 33.9 %collective-permute-start.3 = (bf16[384,1280]{1,0:T(8,128)(2,1)S(1)}, bf16[384,1280]{1,0:T(8,128)(2,1)}, u32[]{:S(2)}, u32[]{:S(2)}) collective-permute-start(bf16[384,1280]{1,0:T(8,128)(2,1)S(1)} %multiply_convert_fusion.refs_2_), channel_id=1, source_target_pairs={{0,4},{4,8},{8,12},{12,0},{1,5},{5,9},{9,13},{13,1},{2,6},{6,10},{... | collective-permute-start | bytes 2949128 | tf_op jit(solution)/shard_map/ppermute | solution.py:555
  38.6 31.9 %collective-permute-start.4 = (bf16[384,1280]{1,0:T(8,128)(2,1)S(1)}, bf16[384,1280]{1,0:T(8,128)(2,1)}, u32[]{:S(2)}, u32[]{:S(2)}) collective-permute-start(bf16[384,1280]{1,0:T(8,128)(2,1)S(1)} %multiply_convert_fusion.refs_2_), channel_id=1, source_target_pairs={{0,16},{16,0},{1,17},{17,1},{2,18},{18,2},{3,19},{19,3},{4,20},{20... | collective-permute-start | bytes 2949128 | tf_op jit(solution)/shard_map/ppermute | solution.py:549
  70.5 42.4 %collective-permute-start.6 = (bf16[384,1280]{1,0:T(8,128)(2,1)}, bf16[384,1280]{1,0:T(8,128)(2,1)S(1)}, u32[]{:S(2)}, u32[]{:S(2)}) collective-permute-start(bf16[384,1280]{1,0:T(8,128)(2,1)} %collective-permute-done.3.refs_7_), channel_id=1, source_target_pairs={{0,1},{1,0},{2,3},{3,2},{4,5},{5,4},{6,7},{7,6},{8,9},{9,8},{10,11... | collective-permute-start | bytes 2949128 | tf_op jit(solution)/shard_map/ppermute | solution.py:550
  72.0 40.9 %collective-permute-start.7 = (bf16[384,1280]{1,0:T(8,128)(2,1)}, bf16[384,1280]{1,0:T(8,128)(2,1)}, u32[]{:S(2)}, u32[]{:S(2)}) collective-permute-start(bf16[384,1280]{1,0:T(8,128)(2,1)} %collective-permute-done.3.refs_7_), channel_id=1, source_target_pairs={{0,4},{4,8},{8,12},{12,0},{1,5},{5,9},{9,13},{13,1},{2,6},{6,10},{... | collective-permute-start | bytes 2949128 | tf_op jit(solution)/shard_map/ppermute | solution.py:555
  80.3 32.5 %collective-permute-start.8 = (bf16[384,1280]{1,0:T(8,128)(2,1)}, bf16[384,1280]{1,0:T(8,128)(2,1)}, u32[]{:S(2)}, u32[]{:S(2)}) collective-permute-start(bf16[384,1280]{1,0:T(8,128)(2,1)} %collective-permute-done.3.refs_7_), channel_id=1, source_target_pairs={{0,16},{16,0},{1,17},{17,1},{2,18},{18,2},{3,19},{19,3},{4,20},{20... | collective-permute-start | bytes 2949128 | tf_op jit(solution)/shard_map/ppermute | solution.py:549
  83.7 29.1 %collective-permute-start.5 = (bf16[192,1280]{1,0:T(8,128)(2,1)}, bf16[192,1280]{1,0:T(8,128)(2,1)S(1)}, u32[]{:S(2)}, u32[]{:S(2)}) collective-permute-start(bf16[192,1280]{1,0:T(8,128)(2,1)} %slice.52), channel_id=1, source_target_pairs={{0,16},{16,0},{1,17},{17,1},{2,18},{18,2},{3,19},{19,3},{4,20},{20... | collective-permute-start | bytes 1474568 | tf_op jit(solution)/shard_map/ppermute | solution.py:552
  86.0 26.8 %collective-permute-start.9 = (bf16[192,1280]{1,0:T(8,128)(2,1)}, bf16[192,1280]{1,0:T(8,128)(2,1)}, u32[]{:S(2)}, u32[]{:S(2)}) collective-permute-start(bf16[192,1280]{1,0:T(8,128)(2,1)} %slice.53), channel_id=1, source_target_pairs={{0,1},{1,0},{2,3},{3,2},{4,5},{5,4},{6,7},{7,6},{8,9},{9,8},{10,11... | collective-permute-start | bytes 1474568 | tf_op jit(solution)/shard_map/ppermute | solution.py:553
  112.9 34.4 %collective-permute-start.11 = (bf16[384,1280]{1,0:T(8,128)(2,1)}, bf16[384,1280]{1,0:T(8,128)(2,1)}, u32[]{:S(2)}, u32[]{:S(2)}) collective-permute-start(bf16[384,1280]{1,0:T(8,128)(2,1)} %collective-permute-done.7.refs_4_.refs_12_), channel_id=1, source_target_pairs={{0,1},{1,0},{2,3},{3,2},{4,5},{5,4},{6,7},{7,6},{8,9},{9,8},{10,11... | collective-permute-start | bytes 2949128 | tf_op jit(solution)/shard_map/ppermute | solution.py:550
  113.5 33.8 %collective-permute-start.12 = (bf16[384,1280]{1,0:T(8,128)(2,1)}, bf16[384,1280]{1,0:T(8,128)(2,1)}, u32[]{:S(2)}, u32[]{:S(2)}) collective-permute-start(bf16[384,1280]{1,0:T(8,128)(2,1)} %collective-permute-done.7.refs_4_.refs_12_), channel_id=1, source_target_pairs={{0,4},{4,8},{8,12},{12,0},{1,5},{5,9},{9,13},{13,1},{2,6},{6,10},{... | collective-permute-start | bytes 2949128 | tf_op jit(solution)/shard_map/ppermute | solution.py:555
  116.1 31.2 %collective-permute-start.13 = (bf16[384,1280]{1,0:T(8,128)(2,1)}, bf16[384,1280]{1,0:T(8,128)(2,1)}, u32[]{:S(2)}, u32[]{:S(2)}) collective-permute-start(bf16[384,1280]{1,0:T(8,128)(2,1)} %collective-permute-done.7.refs_4_.refs_12_), channel_id=1, source_target_pairs={{0,16},{16,0},{1,17},{17,1},{2,18},{18,2},{3,19},{19,3},{4,20},{20... | collective-permute-start | bytes 2949128 | tf_op jit(solution)/shard_map/ppermute | solution.py:549
  117.6 29.7 %collective-permute-start.10 = (bf16[192,1280]{1,0:T(8,128)(2,1)S(1)}, bf16[192,1280]{1,0:T(8,128)(2,1)}, u32[]{:S(2)}, u32[]{:S(2)}) collective-permute-start(bf16[192,1280]{1,0:T(8,128)(2,1)S(1)} %slice.58), channel_id=1, source_target_pairs={{0,16},{16,0},{1,17},{17,1},{2,18},{18,2},{3,19},{19,3},{4,20},{20... | collective-permute-start | bytes 1474568 | tf_op jit(solution)/shard_map/ppermute | solution.py:552
  119.2 28.0 %collective-permute-start.14 = (bf16[192,1280]{1,0:T(8,128)(2,1)S(1)}, bf16[192,1280]{1,0:T(8,128)(2,1)}, u32[]{:S(2)}, u32[]{:S(2)}) collective-permute-start(bf16[192,1280]{1,0:T(8,128)(2,1)S(1)} %slice.59), channel_id=1, source_target_pairs={{0,1},{1,0},{2,3},{3,2},{4,5},{5,4},{6,7},{7,6},{8,9},{9,8},{10,11... | collective-permute-start | bytes 1474568 | tf_op jit(solution)/shard_map/ppermute | solution.py:553
  147.3 46.1 %all-to-all-start.1 = ((bf16[4,640,384]{2,1,0:T(8,128)(2,1)}), bf16[4,640,384]{2,1,0:T(8,128)(2,1)}, u32[]{:S(2)}, u32[]{:S(2)}) async-start(bf16[4,640,384]{2,1,0:T(8,128)(2,1)} %cut_columns.3), calls=%async_computation.1 | async-start | bytes 3932160 | tf_op jit(solution)/shard_map/all_to_all | solution.py:456
  152.4 36.0 %collective-permute-start.16 = (bf16[384,1280]{1,0:T(8,128)(2,1)}, bf16[384,1280]{1,0:T(8,128)(2,1)S(1)}, u32[]{:S(2)}, u32[]{:S(2)}) collective-permute-start(bf16[384,1280]{1,0:T(8,128)(2,1)} %collective-permute-done.12.refs_9_.refs_17_), channel_id=1, source_target_pairs={{0,1},{1,0},{2,3},{3,2},{4,5},{5,4},{6,7},{7,6},{8,9},{9,8},{10,11... | collective-permute-start | bytes 2949128 | tf_op jit(solution)/shard_map/ppermute | solution.py:550
  153.8 34.6 %collective-permute-start.18 = (bf16[384,1280]{1,0:T(8,128)(2,1)}, bf16[384,1280]{1,0:T(8,128)(2,1)}, u32[]{:S(2)}, u32[]{:S(2)}) collective-permute-start(bf16[384,1280]{1,0:T(8,128)(2,1)} %collective-permute-done.12.refs_9_.refs_17_), channel_id=1, source_target_pairs={{0,16},{16,0},{1,17},{17,1},{2,18},{18,2},{3,19},{19,3},{4,20},{20... | collective-permute-start | bytes 2949128 | tf_op jit(solution)/shard_map/ppermute | solution.py:549
  159.4 29.0 %collective-permute-start.15 = (bf16[192,1280]{1,0:T(8,128)(2,1)}, bf16[192,1280]{1,0:T(8,128)(2,1)S(1)}, u32[]{:S(2)}, u32[]{:S(2)}) collective-permute-start(bf16[192,1280]{1,0:T(8,128)(2,1)} %slice.60), channel_id=1, source_target_pairs={{0,16},{16,0},{1,17},{17,1},{2,18},{18,2},{3,19},{19,3},{4,20},{20... | collective-permute-start | bytes 1474568 | tf_op jit(solution)/shard_map/ppermute | solution.py:552
  159.9 28.5 %collective-permute-start.19 = (bf16[192,1280]{1,0:T(8,128)(2,1)}, bf16[192,1280]{1,0:T(8,128)(2,1)}, u32[]{:S(2)}, u32[]{:S(2)}) collective-permute-start(bf16[192,1280]{1,0:T(8,128)(2,1)} %slice.62), channel_id=1, source_target_pairs={{0,1},{1,0},{2,3},{3,2},{4,5},{5,4},{6,7},{7,6},{8,9},{9,8},{10,11... | collective-permute-start | bytes 1474568 | tf_op jit(solution)/shard_map/ppermute | solution.py:553
  193.4 49.2 %all-to-all-start.3 = ((bf16[4,640,384]{2,1,0:T(8,128)(2,1)}), bf16[4,640,384]{2,1,0:T(8,128)(2,1)S(1)}, u32[]{:S(2)}, u32[]{:S(2)}) async-start(bf16[4,640,384]{2,1,0:T(8,128)(2,1)} %cut_columns.4), calls=%async_computation.3 | async-start | bytes 3932160 | tf_op jit(solution)/shard_map/all_to_all | solution.py:456
  242.7 32.6 %collective-permute-start.26 = (bf16[4,128,1280]{2,1,0:T(8,128)(2,1)}, bf16[4,128,1280]{2,1,0:T(8,128)(2,1)}, u32[]{:S(2)}, u32[]{:S(2)}) collective-permute-start(bf16[4,128,1280]{2,1,0:T(8,128)(2,1)} %constant_dynamic-slice_fusion), channel_id=1, source_target_pairs={{0,17},{1,16},{16,1},{17,0},{2,19},{3,18},{18,3},{19,2},{4,21},{5,... | collective-permute-start | bytes 3932168 | tf_op jit(solution)/shard_map/ppermute | solution.py:598
  245.0 25.3 %all-to-all-start.2 = ((bf16[4,2,384,128]{3,2,1,0:T(8,128)(2,1)}), bf16[4,2,384,128]{3,2,1,0:T(8,128)(2,1)S(1)}, u32[]{:S(2)}, u32[]{:S(2)}) async-start(bf16[4,2,384,128]{3,2,1,0:T(8,128)(2,1)} %bitcast.53), calls=%async_computation.2 | async-start | bytes 1572864 | tf_op jit(solution)/shard_map/all_to_all | solution.py:456
  275.3 25.9 %collective-permute-start.29 = (bf16[384,1280]{1,0:T(8,128)(2,1)}, bf16[384,1280]{1,0:T(8,128)(2,1)S(1)}, u32[]{:S(2)}, u32[]{:S(2)}) collective-permute-start(bf16[384,1280]{1,0:T(8,128)(2,1)} %out_blocks.6), channel_id=1, source_target_pairs={{0,17},{1,16},{16,1},{17,0},{2,19},{3,18},{18,3},{19,2},{4,21},{5,... | collective-permute-start | bytes 2949128 | tf_op jit(solution)/shard_map/ppermute | solution.py:618
  310.4 21.1 %collective-permute-start.31 = (bf16[384,1280]{1,0:T(8,128)(2,1)}, bf16[384,1280]{1,0:T(8,128)(2,1)S(1)}, u32[]{:S(2)}, u32[]{:S(2)}) collective-permute-start(bf16[384,1280]{1,0:T(8,128)(2,1)} %get-tuple-element.149), channel_id=1, source_target_pairs={{0,1},{1,0},{2,3},{3,2},{4,5},{5,4},{6,7},{7,6},{8,9},{9,8},{10,11... | collective-permute-start | bytes 2949128 | tf_op jit(solution)/shard_map/ppermute | solution.py:652
  (38 other events, 493.4 us)
